TPU v7x, 32 devices: a whole 2x2x4 slice. The times are simulated.
32 devices in a mesh: dp: 4 (over y, core), tensor: 8 (over z, x).
Axes of the slice: x: 2, y: 2, z: 4, core: 2. Of those that a mesh axis runs over, the one named last changes fastest.
Arguments:
- layer_inputs: bfloat16 [4, 1536, 2048], P(None, 'dp'), may hold values from -6 to 6
- history: bfloat16 [3, 1536, 2048], P(None, None, 'dp'), may hold values from -6 to 6
- seq_ids: int32 [1536], P('dp'), may hold values from -1 to 14, as said below
- norms_master: float32 [9, 2048], P(None, 'dp'), may hold values from -4 to 4
- norms_first: float32 [9, 2048], P(None, 'dp'), may hold values from -1 to 1
- norms_second: float32 [9, 2048], P(None, 'dp'), may hold values from 0 to 1
- attend_in_master: float32 [3, 2048, 2048], P(None, 'dp', 'tensor'), may hold values from -1 to 1
- attend_in_first: float32 [3, 2048, 2048], P(None, 'dp', 'tensor'), may hold values from -1 to 1
- attend_in_second: float32 [3, 2048, 2048], P(None, 'dp', 'tensor'), may hold values from 0 to 1
- attend_out_master: float32 [2048, 2048], P('tensor', 'dp'), may hold values from -4 to 4
- attend_out_first: float32 [2048, 2048], P('tensor', 'dp'), may hold values from -1 to 1
- attend_out_second: float32 [2048, 2048], P('tensor', 'dp'), may hold values from 0 to 1
- expand_master: float32 [2048, 8192], P('dp', 'tensor'), may hold values from -1 to 1
- expand_first: float32 [2048, 8192], P('dp', 'tensor'), may hold values from -1 to 1
- expand_second: float32 [2048, 8192], P('dp', 'tensor'), may hold values from 0 to 1
- project_master: float32 [8192, 2048], P('tensor', 'dp'), may hold values from -1 to 1
- project_first: float32 [8192, 2048], P('tensor', 'dp'), may hold values from -1 to 1
- project_second: float32 [8192, 2048], P('tensor', 'dp'), may hold values from 0 to 1
- mixer_in_master: float32 [2048, 36], P('dp'), may hold values from -0.125 to 0.125
- mixer_in_first: float32 [2048, 36], P('dp'), may hold values from -1 to 1
- mixer_in_second: float32 [2048, 36], P('dp'), may hold values from 0 to 1
- mixer_out_master: float32 [16, 36], P('dp'), may hold values from -1 to 1
- mixer_out_first: float32 [16, 36], P('dp'), may hold values from -1 to 1
- mixer_out_second: float32 [16, 36], P('dp'), may hold values from 0 to 1
- next_cotangent: bfloat16 [4, 1536, 2048], P(None, 'dp'), may hold values from -16 to 16
- grad_entry: bfloat16 [1536, 2048], P(None, 'dp'), may hold values from -16 to 16
Outputs:
- next_inputs: bfloat16 [4, 1536, 2048], P(None, 'dp')
- new_entry: bfloat16 [1536, 2048], P(None, 'dp')
- grad_inputs: bfloat16 [4, 1536, 2048], P(None, 'dp')
- grad_history: bfloat16 [3, 1536, 2048], P(None, None, 'dp')
- norms_new: float32 [9, 2048], P(None, 'dp')
- norms_first_new: float32 [9, 2048], P(None, 'dp')
- norms_second_new: float32 [9, 2048], P(None, 'dp')
- attend_in_new: float32 [3, 2048, 2048], P(None, 'dp', 'tensor')
- attend_in_first_new: float32 [3, 2048, 2048], P(None, 'dp', 'tensor')
- attend_in_second_new: float32 [3, 2048, 2048], P(None, 'dp', 'tensor')
- attend_in_copy: bfloat16 [3, 2048, 2048], P(None, 'dp', 'tensor')
- attend_out_new: float32 [2048, 2048], P('tensor', 'dp')
- attend_out_first_new: float32 [2048, 2048], P('tensor', 'dp')
- attend_out_second_new: float32 [2048, 2048], P('tensor', 'dp')
- attend_out_copy: bfloat16 [2048, 2048], P('tensor', 'dp')
- expand_new: float32 [2048, 8192], P('dp', 'tensor')
- expand_first_new: float32 [2048, 8192], P('dp', 'tensor')
- expand_second_new: float32 [2048, 8192], P('dp', 'tensor')
- expand_copy: bfloat16 [2048, 8192], P('dp', 'tensor')
- project_new: float32 [8192, 2048], P('tensor', 'dp')
- project_first_new: float32 [8192, 2048], P('tensor', 'dp')
- project_second_new: float32 [8192, 2048], P('tensor', 'dp')
- project_copy: bfloat16 [8192, 2048], P('tensor', 'dp')
- mixer_in_new: float32 [2048, 36], P('dp')
- mixer_in_first_new: float32 [2048, 36], P('dp')
- mixer_in_second_new: float32 [2048, 36], P('dp')
- mixer_in_copy: bfloat16 [2048, 36], P('dp')
- mixer_out_new: float32 [16, 36], P('dp')
- mixer_out_first_new: float32 [16, 36], P('dp')
- mixer_out_second_new: float32 [16, 36], P('dp')
- mixer_out_copy: bfloat16 [16, 36], P('dp')
- grad_norm: float32 [], replicated
Inputs may be any that keep to these rules, and one draw needn't show every extreme that they name: `seq_ids`: slots 384 k to 384 (k + 1) - 1 form bucket k. In a bucket the ids of real tokens come first, never fall, and lie in 4 k to 4 k + 2; equal ids are consecutive; the rest of the bucket is padding with id -1. The share of real tokens rises from about a third in bucket 0 to all of the last bucket.
All inputs are finite; a program needn't handle non-finite values.
Results may differ from a plain program's by a relative error of at most 0.018.
The roundings to bfloat16 on the way count: a program that leaves them out, or rounds other values in their place, can miss the bound.
Values may be sent and summed in bfloat16 or wider, within the bound.
No kernel may reach another device: no remote copies, remote signals or barrier semaphores. Data moves between devices by JAX's collectives and lax.ppermute only.
A program may use at most 256 MiB of HBM per device.

v0:
```python
import math

import jax
import jax.numpy as jnp
from jax import lax
from jax.sharding import PartitionSpec as P

D = 2048
HDIM = 128
FF = 8192
MIXH = 36
ROT = 32
STEP = 10


norm_epsilon = 1e-05
mixer_epsilon = 1e-06
clip_level = 1.0
beta_first = 0.9
beta_second = 0.95
adam_epsilon = 1e-08
weight_decay = 0.1


def exact_gelu(values):
    return jax.nn.gelu(values, approximate=False)


def gelu_grad(values, upstream):
    unused, pullback = jax.vjp(exact_gelu, values)
    return pullback(upstream)[0]


def rotate(vectors, cosine, sine_table):
    half = ROT // 2
    first_half = vectors[..., :half]
    second_half = vectors[..., half:ROT]
    return jnp.concatenate(
        [
            first_half * cosine - second_half * sine_table,
            second_half * cosine + first_half * sine_table,
            vectors[..., ROT:],
        ],
        axis=-1,
    )


def angles(bucket_ids):
    same_seq = bucket_ids[:, None] == bucket_ids[None, :]
    order = jnp.arange(bucket_ids.shape[0])
    earlier = order[None, :] < order[:, None]
    position = jnp.sum(jnp.where(same_seq & earlier, 1, 0), axis=1).astype(jnp.float32)
    freqs = 10000.0 ** (-2.0 * jnp.arange(ROT // 2).astype(jnp.float32) / ROT)
    angle = position[:, None] * freqs[None, :]
    allowed = same_seq & (order[None, :] <= order[:, None])
    return (jnp.cos(angle), jnp.sin(angle), allowed)


def score_block(query, key_rows, allowed):
    head_scale = HDIM ** (-0.5)
    scores = (
        jnp.einsum("hqd,hkd->hqk", query, key_rows, preferred_element_type=jnp.float32) * head_scale
    )
    return jnp.where(allowed[None], scores, -1e30)


def norm_back(grad_rows, unit_rows, inverse_rows, gain_rows):
    scaled = grad_rows * gain_rows
    mean_scaled = jnp.mean(scaled, axis=-1, keepdims=True)
    mean_cross = jnp.mean(scaled * unit_rows, axis=-1, keepdims=True)
    return inverse_rows * (scaled - mean_scaled - unit_rows * mean_cross)


def contract_rows(left, right):
    return lax.dot_general(
        left, right, (((0,), (0,)), ((), ())), preferred_element_type=jnp.float32
    )


def contract_cols(left, right):
    return lax.dot_general(
        left, right, (((1,), (1,)), ((), ())), preferred_element_type=jnp.float32
    )


def adam_step(master, first_moment, second_moment, gradient, factor, step_rate, decay_rate):
    scaled = gradient * factor
    first_new = beta_first * first_moment + (1.0 - beta_first) * scaled
    second_new = beta_second * second_moment + (1.0 - beta_second) * scaled * scaled
    first_hat = first_new / (1.0 - beta_first**STEP)
    second_hat = second_new / (1.0 - beta_second**STEP)
    master_new = master - step_rate * (
        first_hat / (jnp.sqrt(second_hat) + adam_epsilon) + decay_rate * master
    )
    return (master_new, first_new, second_new)


def body(
    layer_inputs,
    history,
    seq_ids,
    norms_master,
    norms_first,
    norms_second,
    attend_in_master,
    attend_in_first,
    attend_in_second,
    attend_out_master,
    attend_out_first,
    attend_out_second,
    expand_master,
    expand_first,
    expand_second,
    project_master,
    project_first,
    project_second,
    mixer_in_master,
    mixer_in_first,
    mixer_in_second,
    mixer_out_master,
    mixer_out_first,
    mixer_out_second,
    next_cotangent,
    grad_entry,
):
    tensor_size = lax.axis_size("tensor")
    tokens_here = layer_inputs.shape[1]
    bf16_type = jnp.bfloat16
    float_type = jnp.float32
    fetched = (
        lax.all_gather(norms_master.astype(bf16_type), "dp", axis=1, tiled=True),
        lax.all_gather(attend_in_master.astype(bf16_type), "dp", axis=1, tiled=True),
        lax.all_gather(attend_out_master.astype(bf16_type), "dp", axis=1, tiled=True),
        lax.all_gather(expand_master.astype(bf16_type), "dp", axis=0, tiled=True),
        lax.all_gather(project_master.astype(bf16_type), "dp", axis=1, tiled=True),
        lax.all_gather(mixer_in_master.astype(bf16_type), "dp", axis=0, tiled=True),
        lax.all_gather(mixer_out_master.astype(bf16_type), "dp", axis=0, tiled=True),
    )
    (
        norms_low,
        attend_in_low,
        attend_out_low,
        expand_low,
        project_low,
        mixer_in_low,
        mixer_out_low,
    ) = fetched
    norm_vals = norms_low.astype(float_type)
    gain_rows = norm_vals[0:4][:, None, :]
    input_vals = layer_inputs.astype(float_type)
    centred = input_vals - jnp.mean(input_vals, axis=-1, keepdims=True)
    inverse = lax.rsqrt(jnp.mean(centred * centred, axis=-1, keepdims=True) + norm_epsilon)
    unit_vals = centred * inverse
    normed = (unit_vals * gain_rows + norm_vals[4:8][:, None, :]).astype(bf16_type)
    proj = jnp.einsum("ctd,cde->cte", normed[0:3], attend_in_low, preferred_element_type=float_type)
    local_heads = proj.shape[2] // HDIM
    split_heads = jnp.transpose(proj.reshape(3, tokens_here, local_heads, HDIM), (0, 2, 1, 3))
    cosine, sine_table, allowed = angles(seq_ids)
    query = rotate(split_heads[0], cosine, sine_table).astype(bf16_type)
    key_rows = rotate(split_heads[1], cosine, sine_table).astype(bf16_type)
    value_rows = split_heads[2].astype(bf16_type)
    scores = score_block(query, key_rows, allowed)
    row_max = jnp.max(scores, axis=-1, keepdims=True)
    log_total = jnp.log(jnp.sum(jnp.exp(scores - row_max), axis=-1, keepdims=True)) + row_max
    prob_low = jnp.exp(scores - log_total).astype(bf16_type)
    heads_mixed = jnp.einsum(
        "hqk,hkd->qhd", prob_low, value_rows, preferred_element_type=float_type
    )
    heads_out = heads_mixed.reshape(tokens_here, local_heads * HDIM).astype(bf16_type)
    upper = jnp.dot(normed[3], expand_low, preferred_element_type=float_type)
    hidden = exact_gelu(upper).astype(bf16_type)
    partial_branch = jnp.dot(
        heads_out, attend_out_low, preferred_element_type=float_type
    ) + jnp.dot(hidden, project_low, preferred_element_type=float_type)
    branch = lax.psum(partial_branch, "tensor")
    valid = (seq_ids >= 0).astype(float_type)[:, None]
    newest = input_vals[3] + valid * branch
    new_entry = lax.all_to_all(
        newest.astype(bf16_type), "dp", split_axis=1, concat_axis=0, tiled=True
    )
    stored = lax.all_to_all(history, "dp", split_axis=1, concat_axis=2, tiled=True).astype(
        float_type
    )
    mix_scale = lax.rsqrt(jnp.mean(newest * newest, axis=-1, keepdims=True) + mixer_epsilon)
    mix_normed = (newest * mix_scale * norm_vals[8]).astype(bf16_type)
    mix_pre = jnp.dot(mix_normed, mixer_in_low, preferred_element_type=float_type)
    mix_act = exact_gelu(mix_pre).astype(bf16_type)
    layer_count = stored.shape[0] + 1
    mix_weights = contract_cols(mix_act, mixer_out_low).reshape(tokens_here, 4, layer_count)
    layers = [stored[layer_index] for layer_index in range(layer_count - 1)] + [newest]
    next_vals = mix_weights[:, :, 0].T[:, :, None] * layers[0][None]
    for layer_index in range(1, layer_count):
        next_vals = (
            next_vals + mix_weights[:, :, layer_index].T[:, :, None] * layers[layer_index][None]
        )
    next_inputs = next_vals.astype(bf16_type)
    grad_out = next_cotangent.astype(float_type)
    entry_back = lax.all_to_all(grad_entry, "dp", split_axis=0, concat_axis=1, tiled=True).astype(
        float_type
    )
    weight_terms = jnp.stack(
        [jnp.sum(grad_out * layer_vals[None], axis=-1) for layer_vals in layers], axis=-1
    )
    grad_weights = (
        jnp.transpose(weight_terms, (1, 0, 2))
        .reshape(tokens_here, 4 * layer_count)
        .astype(bf16_type)
    )
    layer_grads = [
        jnp.sum(mix_weights[:, :, layer_index].T[:, :, None] * grad_out, axis=0)
        for layer_index in range(layer_count)
    ]
    grad_history = lax.all_to_all(
        jnp.stack(layer_grads[:-1]).astype(bf16_type), "dp", split_axis=2, concat_axis=1, tiled=True
    )
    grad_mixer_out = contract_rows(grad_weights, mix_act)
    grad_mix_act = jnp.dot(grad_weights, mixer_out_low, preferred_element_type=float_type)
    grad_mix_pre = gelu_grad(mix_pre, grad_mix_act).astype(bf16_type)
    grad_mixer_in = contract_rows(mix_normed, grad_mix_pre)
    grad_mix_normed = contract_cols(grad_mix_pre, mixer_in_low)
    scaled_mix = grad_mix_normed * norm_vals[8]
    grad_newest = (
        layer_grads[-1]
        + entry_back
        + mix_scale * scaled_mix
        - newest * mix_scale**3 * jnp.mean(scaled_mix * newest, axis=-1, keepdims=True)
    )
    share_rows = tokens_here // tensor_size
    share_start = lax.axis_index("tensor") * share_rows
    mixer_gain = jnp.sum(
        lax.dynamic_slice_in_dim(grad_mix_normed * newest * mix_scale, share_start, share_rows, 0),
        axis=0,
    )
    grad_branch = (valid * grad_newest).astype(bf16_type)
    grad_attend_out = contract_rows(heads_out, grad_branch)
    grad_project = contract_rows(hidden, grad_branch)
    grad_heads = contract_cols(grad_branch, attend_out_low).astype(bf16_type)
    grad_hidden = contract_cols(grad_branch, project_low)
    grad_upper = gelu_grad(upper, grad_hidden).astype(bf16_type)
    grad_expand = contract_rows(normed[3], grad_upper)
    grad_normed_ffn = contract_cols(grad_upper, expand_low)
    head_scale = HDIM ** (-0.5)
    grad_heads_split = jnp.transpose(grad_heads.reshape(tokens_here, local_heads, HDIM), (1, 0, 2))
    prob = jnp.exp(score_block(query, key_rows, allowed) - log_total)
    grad_prob = jnp.einsum(
        "hqd,hkd->hqk", grad_heads_split, value_rows, preferred_element_type=float_type
    )
    row_delta = jnp.sum(prob * grad_prob, axis=-1, keepdims=True)
    grad_scores = (prob * (grad_prob - row_delta)).astype(bf16_type)
    grad_query = (
        jnp.einsum("hqk,hkd->hqd", grad_scores, key_rows, preferred_element_type=float_type)
        * head_scale
    )
    grad_key = (
        jnp.einsum("hqk,hqd->hkd", grad_scores, query, preferred_element_type=float_type)
        * head_scale
    )
    grad_value = jnp.einsum(
        "hqk,hqd->hkd", prob_low, grad_heads_split, preferred_element_type=float_type
    )
    grad_split = jnp.stack(
        [rotate(grad_query, cosine, -sine_table), rotate(grad_key, cosine, -sine_table), grad_value]
    ).astype(bf16_type)
    grad_proj = jnp.transpose(grad_split, (0, 2, 1, 3)).reshape(3, tokens_here, local_heads * HDIM)
    grad_attend_in = jnp.einsum(
        "ctd,cte->cde", normed[0:3], grad_proj, preferred_element_type=float_type
    )
    grad_normed_attn = jnp.einsum(
        "cte,cde->ctd", grad_proj, attend_in_low, preferred_element_type=float_type
    )
    grad_normed = jnp.concatenate([grad_normed_attn, grad_normed_ffn[None]], axis=0)
    gain_part = jnp.sum(grad_normed * unit_vals, axis=1)
    bias_part = jnp.sum(grad_normed, axis=1)
    norm_part = jnp.concatenate([gain_part, bias_part, mixer_gain[None]], axis=0)
    summed_grads = lax.psum(grad_normed, "tensor")
    back_full = norm_back(summed_grads, unit_vals, inverse, gain_rows)
    grad_inputs = back_full.at[3].add(grad_newest).astype(bf16_type)
    norm_total = lax.psum(norm_part, ("dp", "tensor"))
    norm_cols = norms_master.shape[1]
    norm_grad = lax.dynamic_slice_in_dim(norm_total, lax.axis_index("dp") * norm_cols, norm_cols, 1)
    reduced = (
        lax.psum_scatter(grad_attend_in, "dp", scatter_dimension=1, tiled=True),
        lax.psum_scatter(grad_attend_out, "dp", scatter_dimension=1, tiled=True),
        lax.psum_scatter(grad_expand, "dp", scatter_dimension=0, tiled=True),
        lax.psum_scatter(grad_project, "dp", scatter_dimension=1, tiled=True),
        lax.psum_scatter(grad_mixer_in, "dp", scatter_dimension=0, tiled=True),
        lax.psum_scatter(grad_mixer_out, "dp", scatter_dimension=0, tiled=True),
    )
    shard_squares = sum((jnp.sum(gradient * gradient) for gradient in reduced[0:4]))
    shared_squares = (
        jnp.sum(norm_grad * norm_grad)
        + jnp.sum(reduced[4] * reduced[4])
        + jnp.sum(reduced[5] * reduced[5])
    )
    total_squares = lax.psum(shard_squares + shared_squares / tensor_size, ("dp", "tensor"))
    grad_norm = jnp.sqrt(total_squares)
    factor = jnp.minimum(1.0, clip_level / grad_norm)
    wide_rate = 2.0 / math.sqrt(D)
    norms_out = adam_step(norms_master, norms_first, norms_second, norm_grad, factor, 1.0, 0.0)
    attend_in_out = adam_step(
        attend_in_master,
        attend_in_first,
        attend_in_second,
        reduced[0],
        factor,
        wide_rate,
        weight_decay,
    )
    attend_out_out = adam_step(
        attend_out_master,
        attend_out_first,
        attend_out_second,
        reduced[1],
        factor,
        wide_rate,
        weight_decay,
    )
    expand_out = adam_step(
        expand_master, expand_first, expand_second, reduced[2], factor, wide_rate, weight_decay
    )
    project_out = adam_step(
        project_master,
        project_first,
        project_second,
        reduced[3],
        factor,
        2.0 / math.sqrt(FF),
        weight_decay,
    )
    mixer_in_out = adam_step(
        mixer_in_master,
        mixer_in_first,
        mixer_in_second,
        reduced[4],
        factor,
        wide_rate,
        weight_decay,
    )
    mixer_out_out = adam_step(
        mixer_out_master,
        mixer_out_first,
        mixer_out_second,
        reduced[5],
        factor,
        2.0 / math.sqrt(MIXH),
        weight_decay,
    )
    return (
        next_inputs,
        new_entry,
        grad_inputs,
        grad_history,
        norms_out[0],
        norms_out[1],
        norms_out[2],
        attend_in_out[0],
        attend_in_out[1],
        attend_in_out[2],
        attend_in_out[0].astype(bf16_type),
        attend_out_out[0],
        attend_out_out[1],
        attend_out_out[2],
        attend_out_out[0].astype(bf16_type),
        expand_out[0],
        expand_out[1],
        expand_out[2],
        expand_out[0].astype(bf16_type),
        project_out[0],
        project_out[1],
        project_out[2],
        project_out[0].astype(bf16_type),
        mixer_in_out[0],
        mixer_in_out[1],
        mixer_in_out[2],
        mixer_in_out[0].astype(bf16_type),
        mixer_out_out[0],
        mixer_out_out[1],
        mixer_out_out[2],
        mixer_out_out[0].astype(bf16_type),
        grad_norm,
    )


def solution(mesh):
    in_specs = (
        P(None, "dp", None),
        P(None, None, "dp"),
        P("dp"),
        P(None, "dp"),
        P(None, "dp"),
        P(None, "dp"),
        P(None, "dp", "tensor"),
        P(None, "dp", "tensor"),
        P(None, "dp", "tensor"),
        P("tensor", "dp"),
        P("tensor", "dp"),
        P("tensor", "dp"),
        P("dp", "tensor"),
        P("dp", "tensor"),
        P("dp", "tensor"),
        P("tensor", "dp"),
        P("tensor", "dp"),
        P("tensor", "dp"),
        P("dp", None),
        P("dp", None),
        P("dp", None),
        P("dp", None),
        P("dp", None),
        P("dp", None),
        P(None, "dp", None),
        P(None, "dp"),
    )
    out_specs = (
        P(None, "dp", None),
        P(None, "dp"),
        P(None, "dp", None),
        P(None, None, "dp"),
        P(None, "dp"),
        P(None, "dp"),
        P(None, "dp"),
        P(None, "dp", "tensor"),
        P(None, "dp", "tensor"),
        P(None, "dp", "tensor"),
        P(None, "dp", "tensor"),
        P("tensor", "dp"),
        P("tensor", "dp"),
        P("tensor", "dp"),
        P("tensor", "dp"),
        P("dp", "tensor"),
        P("dp", "tensor"),
        P("dp", "tensor"),
        P("dp", "tensor"),
        P("tensor", "dp"),
        P("tensor", "dp"),
        P("tensor", "dp"),
        P("tensor", "dp"),
        P("dp", None),
        P("dp", None),
        P("dp", None),
        P("dp", None),
        P("dp", None),
        P("dp", None),
        P("dp", None),
        P("dp", None),
        P(),
    )
    return jax.shard_map(body, mesh=mesh, in_specs=in_specs, out_specs=out_specs, check_vma=False)
```

profile of v0, /device:TPU:0, one launch (start us, length us, event | category | flops | bytes accessed | tf_op | source)
XLA Modules:
  0.0 1306.8 jit_solution(16019210338437415168)
XLA Ops:
  14.0 4.5 all-to-all-start.2
  20.3 4.2 convert_reduce_fusion
  24.5 4.6 multiply_reduce_fusion.2
  29.1 28.1 %all_gather.21 = bf16[9,2048]{1,0:T(8,128)(2,1)S(1)} all-gather(bf16[9,512]{1,0:T(8,128)(2,1)S(1)} %convert_element_type.149), channel_id=1, replica_groups=mesh['dp'=4,'tensor'=8] {'dp'}, dimensions={1}, use_global_device_ids=true | all-gather | bytes 46080 | tf_op jit(solution)/shard_map/all_gather | solution.py:131
  59.0 9.5 copy.217
  68.6 6.2 add_convert_fusion.1
  74.7 5.1 fusion.72
  84.1 5.3 all-to-all-start
  89.6 6.2 all-gather.10.cloned.1.call-done
  95.8 9.4 multiply_convert_fusion.2
  105.2 49.4 %all-gather.12.cloned.1.call-done = bf16[1024,2048]{1,0:T(8,128)(2,1)} async-done(((bf16[1024,512]{1,0:T(8,128)(2,1)}), bf16[1024,2048]{1,0:T(8,128)(2,1)}) %all-gather.12.cloned.1.call-update) | async-done | bytes 4194320 | tf_op jit(solution)/shard_map/all_gather | solution.py:135
  154.6 4.2 fusion.65
  158.8 20.3 %all-gather.8.cloned.1.call-done = bf16[256,2048]{1,0:T(8,128)(2,1)} async-done(((bf16[256,512]{1,0:T(8,128)(2,1)}), bf16[256,2048]{1,0:T(8,128)(2,1)}) %all-gather.8.cloned.1.call-update) | async-done | bytes 1048592 | tf_op jit(solution)/shard_map/all_gather | solution.py:133
  183.6 9.0 convert_element_type.147
  193.4 5.5 all-gather
  198.9 6.0 all_gather.26
  209.3 4.1 copy.218
  214.7 3.8 fusion.61
  218.5 3.9 copy.219
  229.5 3.7 copy.224
  239.1 72.9 %all-reduce.5.cloned.1.call-done = f32[384,2048]{1,0:T(8,128)} async-done(((f32[384,2048]{1,0:T(8,128)}), f32[384,2048]{1,0:T(8,128)}) %all-reduce.5.cloned.1.call-update) | async-done | bytes 3145744 | tf_op jit(solution)/shard_map/psum | solution.py:175
  312.0 4.4 fusion.57
  324.0 22.1 %fusion.5 = (bf16[384,2048]{1,0:T(8,128)(2,1)}, bf16[4,384]{1,0:T(4,128)(2,1)S(1)}, bf16[4,384]{1,0:T(4,128)(2,1)S(1)}, bf16[4,384]{1,0:T(4,128)(2,1)S(1)}, bf16...) fusion(bf16[4,384,2048]{2,1,0:T(8,128)(2,1)} %param.52, ...), kind=kLoop, calls=%fused_computation.13 | loop fusion | flops 75491328 | bytes 33067008 | tf_op jit(solution)/shard_map/reduce_sum | solution.py:210
  364.3 5.9 add_convert_fusion.2
  372.5 5.0 fusion.67
  377.5 10.1 pad_maximum_fusion
  394.6 7.3 fusion.73
  403.8 380.8 %all-reduce.7.cloned.1.call-done = f32[4,384,2048]{2,1,0:T(8,128)} async-done(((f32[4,384,2048]{2,1,0:T(8,128)}), f32[4,384,2048]{2,1,0:T(8,128)}) %all-reduce.7.cloned.1.call-update) | async-done | bytes 12582928 | tf_op jit(solution)/shard_map/psum | solution.py:275
  784.6 12.4 multiply_reduce_fusion.3
  797.8 7.0 fusion.20
  806.4 5.6 fusion.69
  814.7 4.6 all-to-all-start.1
  819.4 3.6 pad_maximum_fusion.1
  823.0 10.2 copy.241
  833.2 16.2 %all-to-all-done.1 = bf16[384,4,512]{2,0,1:T(8,128)(2,1)} async-done(((bf16[384,4,512]{2,0,1:T(8,128)(2,1)}), bf16[384,4,512]{2,0,1:T(8,128)(2,1)}, u32[]{:S(2)}, u32[]{:S(2)}) %all-to-all-start.1) | async-done | bytes 1572896 | tf_op jit(solution)/shard_map/all_to_all | solution.py:178
  849.4 5.3 all-to-all-start.3
  856.1 104.7 %all-reduce = f32[16,36]{1,0:T(8,128)S(1)} all-reduce(f32[16,36]{1,0:T(8,128)S(1)} %fusion.71), channel_id=7, replica_groups=mesh['dp'=4,'tensor'=8] {'dp'}, use_global_device_ids=true, to_apply=%region_35.36.clone | all-reduce | flops 576 | bytes 4608
  962.9 5.6 copy.242
  968.6 6.9 copy.243
  981.0 13.7 %subtract_multiply_fusion = f32[4,384,2048]{2,1,0:T(8,128)} fusion(f32[4,384,2048]{2,1,0:T(8,128)} %all-reduce.7.cloned.1.call-done, bf16[4,384,2048]{2,1,0:T(8,128)(2,1)} %param.28, f32[4,384]{1,0:T(4,128)S(1)} %broadcast_multiply_fusion, f32[4,384]{1,0:T(4,128)S(1)} %broadcast_multiply_fusion.1, f32[4,2048]{1,0:T(4,128)S(1)} %copy-done.52, ...), kind=kLoop, calls=%fused_computation.18 | loop fusion | flops 25165824 | bytes 31514624 | tf_op jit(solution)/shard_map/mul | solution.py:71
  994.7 4.1 fusion.8
  998.8 75.3 %all-reduce.9.cloned.1.call-done = f32[9,2048]{1,0:T(8,128)} async-done(((f32[9,2048]{1,0:T(8,128)}), f32[9,2048]{1,0:T(8,128)}) %all-reduce.9.cloned.1.call-update) | async-done | bytes 73744 | tf_op jit(solution)/shard_map/psum | solution.py:278
  1077.3 70.2 %reduce-scatter.10.cloned.1.call-done = f32[512,1024]{1,0:T(8,128)} async-done(((f32[2048,1024]{1,0:T(8,128)}), f32[512,1024]{1,0:T(8,128)}) %reduce-scatter.10.cloned.1.call-update) | async-done | bytes 2097168 | tf_op jit(solution)/shard_map/reduce_scatter | solution.py:284
  1150.9 70.8 %reduce-scatter.12.cloned.1.call-done = f32[1024,512]{1,0:T(8,128)} async-done(((f32[1024,2048]{1,0:T(8,128)}), f32[1024,512]{1,0:T(8,128)}) %reduce-scatter.12.cloned.1.call-update) | async-done | bytes 2097168 | tf_op jit(solution)/shard_map/reduce_scatter | solution.py:285
  1225.2 8.4 convert_element_type.184
  1233.7 39.3 %psum.31 = f32[]{:T(128)} all-reduce(f32[]{:T(128)S(6)} %add.256), channel_id=1, replica_groups=mesh['dp'=4,'tensor'=8] {'dp','tensor'}, use_global_device_ids=true, to_apply=%region_37.38 | all-reduce | flops 1 | bytes 8 | tf_op jit(solution)/shard_map/psum | solution.py:295
  1285.5 4.5 fusion.48
  1291.6 4.2 fusion.50
  (296 shorter events, 110.0 us)
Async XLA Ops:
  7.2 67.5 %all-gather.6.cloned.1.call-start = ((), (), s32[]{:S(2)}) async-start(), calls=%async_computation.9 | async-start | bytes 3932160 | tf_op jit(solution)/shard_map/all_gather | solution.py:132
  9.8 86.0 %all-gather.10.cloned.1.call-start = ((), (), s32[]{:S(2)}) async-start(), calls=%async_computation.11 | async-start | bytes 5242880 | tf_op jit(solution)/shard_map/all_gather | solution.py:134
  12.8 141.8 %all-gather.12.cloned.1.call-start = ((), (), s32[]{:S(2)}) async-start(), calls=%async_computation.12 | async-start | bytes 5242880 | tf_op jit(solution)/shard_map/all_gather | solution.py:135
  14.0 70.1 %all-to-all-start.2 = ((bf16[4,384,512]{2,1,0:T(8,128)(2,1)}), bf16[4,384,512]{2,1,0:T(8,128)(2,1)}, u32[]{:S(2)}, u32[]{:S(2)}) async-start(bf16[4,384,512]{2,1,0:T(8,128)(2,1)} %bitcast.173), calls=%async_computation.2 | async-start | bytes 3145728 | tf_op jit(solution)/shard_map/all_to_all | solution.py:198
  18.5 160.6 %all-gather.8.cloned.1.call-start = ((), (), s32[]{:S(2)}) async-start(), calls=%async_computation.10 | async-start | bytes 1310720 | tf_op jit(solution)/shard_map/all_gather | solution.py:133
  29.1 39.4 %copy-start.64 = (f32[4,384]{1,0:T(4,128)}, f32[4,384]{1,0:T(4,128)S(1)}, u32[]{:S(2)}) copy-start(f32[4,384]{1,0:T(4,128)S(1)} %add_rsqrt_fusion) | copy-start | bytes 18436
  57.2 11.3 slice-start
  57.2 11.3 copy-start.51
  58.2 22.4 %copy-start.30 = (f32[384,16]{1,0:T(8,128)}, f32[384,16]{1,0:T(8,128)S(1)}, u32[]{:S(2)}) copy-start(f32[384,16]{1,0:T(8,128)S(1)} %copy.213) | copy-start | bytes 73732
  59.0 9.5 slice-start.1
  84.1 125.2 %all-to-all-start = ((bf16[3,1536,512]{2,0,1:T(4,128)(2,1)}), bf16[3,1536,512]{2,0,1:T(4,128)(2,1)}, u32[]{:S(2)}, u32[]{:S(2)}) async-start(bf16[3,1536,512]{2,0,1:T(4,128)(2,1)} %copy.217), calls=%async_computation | async-start | bytes 12582912 | tf_op jit(solution)/shard_map/all_to_all | solution.py:181
  89.4 222.6 %all-reduce.5.cloned.1.call-start = ((), (), s32[]{:S(2)}) async-start(), calls=%async_computation.13 | async-start | bytes 6291456 | tf_op jit(solution)/shard_map/psum | solution.py:175
  182.7 601.9 %all-reduce.7.cloned.1.call-start = ((), (), s32[]{:S(2)}) async-start(), calls=%async_computation.14 | async-start | bytes 25165824 | tf_op jit(solution)/shard_map/psum | solution.py:275
  183.5 9.0 copy-start.55
  183.5 9.1 copy-start.66
  183.6 9.9 copy-start.80
  183.6 21.3 %copy-start.72 = (s32[384]{0:T(512)S(1)}, s32[384]{0:T(512)}, u32[]{:S(2)}) copy-start(s32[384]{0:T(512)} %param.30) | copy-start | bytes 4612
  364.3 5.9 copy-start.83
  372.1 5.4 copy-start.5
  387.9 573.5 %reduce-scatter.14.cloned.1.call-start = ((), (), s32[]{:S(2)}) async-start(), calls=%async_computation.20 | async-start | bytes 409600 | tf_op jit(solution)/shard_map/reduce_scatter | solution.py:286
  390.9 584.5 %reduce-scatter.8.cloned.1.call-start = ((), (), s32[]{:S(2)}) async-start(), calls=%async_computation.17 | async-start | bytes 2621440 | tf_op jit(solution)/shard_map/reduce_scatter | solution.py:283
  394.5 582.7 %reduce-scatter.6.cloned.1.call-start = ((), (), s32[]{:S(2)}) async-start(), calls=%async_computation.16 | async-start | bytes 7864320 | tf_op jit(solution)/shard_map/reduce_scatter | solution.py:282
  401.8 382.8 %copy-start.52 = (f32[4,2048]{1,0:T(4,128)S(1)}, f32[4,2048]{1,0:T(4,128)}, u32[]{:S(2)}) copy-start(f32[4,2048]{1,0:T(4,128)} %copy-done.51) | copy-start | bytes 98308
  401.8 382.8 %copy-start.65 = (f32[4,384]{1,0:T(4,128)S(1)}, f32[4,384]{1,0:T(4,128)}, u32[]{:S(2)}) copy-start(f32[4,384]{1,0:T(4,128)} %copy-done.64) | copy-start | bytes 18436
  401.9 672.2 %all-reduce.9.cloned.1.call-start = ((), (), s32[]{:S(2)}) async-start(), calls=%async_computation.15 | async-start | bytes 262144 | tf_op jit(solution)/shard_map/psum | solution.py:278
  403.8 394.0 %copy-start.45 = (bf16[384,1024]{1,0:T(8,128)(2,1)S(1)}, bf16[384,1024]{1,0:T(8,128)(2,1)}, u32[]{:S(2)}) copy-start(bf16[384,1024]{1,0:T(8,128)(2,1)} %copy-done.44) | copy-start | bytes 2359300
  797.7 349.8 %reduce-scatter.10.cloned.1.call-start = ((), (), s32[]{:S(2)}) async-start(), calls=%async_computation.18 | async-start | bytes 10485760 | tf_op jit(solution)/shard_map/reduce_scatter | solution.py:284
  804.8 416.9 %reduce-scatter.12.cloned.1.call-start = ((), (), s32[]{:S(2)}) async-start(), calls=%async_computation.19 | async-start | bytes 10485760 | tf_op jit(solution)/shard_map/reduce_scatter | solution.py:285
  814.7 34.7 %all-to-all-start.1 = ((bf16[384,4,512]{2,0,1:T(8,128)(2,1)}), bf16[384,4,512]{2,0,1:T(8,128)(2,1)}, u32[]{:S(2)}, u32[]{:S(2)}) async-start(bf16[384,4,512]{2,0,1:T(8,128)(2,1)} %bitcast.166), calls=%async_computation.1 | async-start | bytes 3145728 | tf_op jit(solution)/shard_map/all_to_all | solution.py:178
  833.2 21.5 %copy-start.84 = (u32[32]{0:T(128)S(1)}, u32[32]{0:T(128)}, u32[]{:S(2)}) copy-start(u32[32]{0:T(128)} %constant.54) | copy-start | bytes 388
  833.2 22.7 %copy-start.63 = (bf16[384,36]{0,1:T(8,128)(2,1)S(1)}, bf16[384,36]{0,1:T(8,128)(2,1)}, u32[]{:S(2)}) copy-start(bf16[384,36]{0,1:T(8,128)(2,1)} %copy-done.62) | copy-start | bytes 82948
  833.2 22.7 %copy-start.73 = (bf16[384,16]{0,1:T(8,128)(2,1)S(1)}, bf16[384,16]{0,1:T(8,128)(2,1)}, u32[]{:S(2)}) copy-start(bf16[384,16]{0,1:T(8,128)(2,1)} %convert_element_type.178) | copy-start | bytes 36868
  849.4 113.5 %all-to-all-start.3 = ((bf16[3,384,2048]{1,0,2:T(4,128)(2,1)}), bf16[3,384,2048]{1,0,2:T(4,128)(2,1)}, u32[]{:S(2)}, u32[]{:S(2)}) async-start(bf16[3,384,2048]{1,0,2:T(4,128)(2,1)} %copy.241), calls=%async_computation.3 | async-start | bytes 12582912 | tf_op jit(solution)/shard_map/all_to_all | solution.py:213
  981.0 13.7 %copy-start.8 = (f32[384,2048]{1,0:T(8,128)S(1)}, f32[384,2048]{1,0:T(8,128)}, u32[]{:S(2)}) copy-start(f32[384,2048]{1,0:T(8,128)} %get-tuple-element.86) | copy-start | bytes 9437188
  1225.1 48.6 %copy-start.81 = (f32[4,36]{1,0:T(4,128)S(1)}, f32[4,36]{1,0:T(4,128)}, u32[]{:S(2)}) copy-start(f32[4,36]{1,0:T(4,128)} %param.49) | copy-start | bytes 1732
  1225.1 48.6 %copy-start.82 = (f32[4,36]{1,0:T(4,128)S(1)}, f32[4,36]{1,0:T(4,128)}, u32[]{:S(2)}) copy-start(f32[4,36]{1,0:T(4,128)} %param.50) | copy-start | bytes 1732
  1225.1 49.9 %copy-start.59 = (f32[9,512]{1,0:T(8,128)S(1)}, f32[9,512]{1,0:T(8,128)}, u32[]{:S(2)}) copy-start(f32[9,512]{1,0:T(8,128)} %param.31) | copy-start | bytes 55300
  1225.1 49.9 %copy-start.74 = (f32[9,512]{1,0:T(8,128)S(1)}, f32[9,512]{1,0:T(8,128)}, u32[]{:S(2)}) copy-start(f32[9,512]{1,0:T(8,128)} %param.32) | copy-start | bytes 55300
  1225.1 51.4 %copy-start.54 = (f32[512,36]{0,1:T(8,128)S(1)}, f32[512,36]{0,1:T(8,128)}, u32[]{:S(2)}) copy-start(f32[512,36]{0,1:T(8,128)} %reduce-scatter.14.cloned.1.call-done) | copy-start | bytes 221188
  1225.2 51.4 %copy-start.56 = (f32[512,36]{0,1:T(8,128)S(1)}, f32[512,36]{0,1:T(8,128)}, u32[]{:S(2)}) copy-start(f32[512,36]{0,1:T(8,128)} %param.46) | copy-start | bytes 221188
  1225.2 51.4 %copy-start.67 = (f32[512,36]{0,1:T(8,128)S(1)}, f32[512,36]{0,1:T(8,128)}, u32[]{:S(2)}) copy-start(f32[512,36]{0,1:T(8,128)} %param.47) | copy-start | bytes 221188
  1225.2 51.4 %copy-start.68 = (f32[512,36]{0,1:T(8,128)S(1)}, f32[512,36]{0,1:T(8,128)}, u32[]{:S(2)}) copy-start(f32[512,36]{0,1:T(8,128)} %param.48) | copy-start | bytes 221188
  1225.2 52.1 %copy-start.28 = (f32[256,512]{1,0:T(8,128)S(1)}, f32[256,512]{1,0:T(8,128)}, u32[]{:S(2)}) copy-start(f32[256,512]{1,0:T(8,128)} %param.37) | copy-start | bytes 1572868
  1225.2 52.1 %copy-start.29 = (f32[256,512]{1,0:T(8,128)S(1)}, f32[256,512]{1,0:T(8,128)}, u32[]{:S(2)}) copy-start(f32[256,512]{1,0:T(8,128)} %reduce-scatter.8.cloned.1.call-done) | copy-start | bytes 1572868
  1225.2 52.1 %copy-start.53 = (f32[256,512]{1,0:T(8,128)S(1)}, f32[256,512]{1,0:T(8,128)}, u32[]{:S(2)}) copy-start(f32[256,512]{1,0:T(8,128)} %param.38) | copy-start | bytes 1572868
  1225.2 54.8 %copy-start.41 = (f32[3,512,256]{2,1,0:T(8,128)S(1)}, f32[3,512,256]{2,1,0:T(8,128)}, u32[]{:S(2)}) copy-start(f32[3,512,256]{2,1,0:T(8,128)} %param.35) | copy-start | bytes 4718596
  1280.1 5.4 copy-start.24
  1285.5 6.0 copy-start.26
  (55 other events, 139.6 us)
Sparse Core Ops, SparseCore 0:
  10.2 47.5 all-gather.5
  59.9 35.8 all-gather.9
  97.9 56.6 all-gather.11
  156.6 22.4 all-gather.7
  183.1 128.8 all-reduce.4
  388.0 396.5 all-reduce.6
  787.7 19.5 reduce-scatter.13
  810.5 41.1 reduce-scatter.7
  854.3 90.2 reduce-scatter.5
  951.5 122.4 all-reduce.8
  1076.8 70.7 reduce-scatter.9
  1150.0 71.6 reduce-scatter.11
where the time goes:
time: 1320 us; the launch traced here: 1310 us
  waiting for transfers between devices  762 us (58%)
  blocking collectives  184 us (14%)
  other arithmetic  153 us (12%)
  local copies, waits for them, and re-layouts  94.1 us (7%)
  matrix products  70.9 us (5%)
  between operations  22.8 us (2%)
  starting transfers between devices  20.4 us (2%)
    psum x1, waiting for transfers between devices, body(): summed_grads = lax.psum(grad_normed, 'tensor')  381 us
    unnamed x1, blocking collectives  105 us
    psum x1, waiting for transfers between devices, body(): norm_total = lax.psum(norm_part, ('dp', 'tensor'))  75.3 us
    psum x1, waiting for transfers between devices, body(): branch = lax.psum(partial_branch, 'tensor')  72.9 us
    reduce_scatter x1, waiting for transfers between devices, body(): lax.psum_scatter(grad_project, 'dp', scatter_dimension=1, tiled=True)  70.8 us
    reduce_scatter x1, waiting for transfers between devices, body(): lax.psum_scatter(grad_expand, 'dp', scatter_dimension=0, tiled=True)  70.2 us
    all_gather x1, waiting for transfers between devices, body(): lax.all_gather(project_master.astype(bf16_type), 'dp', axis=1, tiled=True)  49.4 us
    psum x1, blocking collectives, body(): lax.psum(shard_squares + shared_squares / tensor_size, ('dp', 'tensor'))  39.3 us
  transfers between devices with their start and end apart: 16, of which 9 were waited for; matrix products, arithmetic and copies ran while one was open for 15% of the time, Pallas kernels for 0%

commit v1 on v0

--- a/solution.py
+++ b/solution.py
@@ -93,6 +93,83 @@
         first_hat / (jnp.sqrt(second_hat) + adam_epsilon) + decay_rate * master
     )
     return (master_new, first_new, second_new)
+
+
+def bits_of(size):
+    return [1 << index for index in range(size.bit_length() - 1)]
+
+
+def swap(values, axis, mask):
+    size = lax.axis_size(axis)
+    return lax.ppermute(values, axis, [(source, source ^ mask) for source in range(size)])
+
+
+def gather_pieces(piece, axis):
+    size = lax.axis_size(axis)
+    pieces = {0: piece}
+    for bit in reversed(bits_of(size)):
+        for known in list(pieces):
+            pieces[known | bit] = swap(pieces[known], axis, bit)
+    return [pieces[index] for index in range(size)]
+
+
+def exchange_pieces(pieces, axis):
+    return [pieces[0]] + [swap(pieces[mask], axis, mask) for mask in range(1, len(pieces))]
+
+
+def reduce_pieces(pieces, axis, send_type):
+    kept = dict(enumerate(pieces))
+    for bit in bits_of(len(pieces)):
+        for index in sorted(kept, reverse=True):
+            if index & bit:
+                moved = swap(kept.pop(index).astype(send_type), axis, bit)
+                kept[index ^ bit] = kept[index ^ bit].astype(jnp.float32) + moved.astype(jnp.float32)
+    return kept[0]
+
+
+def butterfly(values, axis):
+    for bit in bits_of(lax.axis_size(axis)):
+        values = values + swap(values, axis, bit)
+    return values
+
+
+def share_index(axis):
+    size = lax.axis_size(axis)
+    here = lax.axis_index(axis)
+    place = 0
+    for bit in bits_of(size):
+        place = place * 2 + (here & bit) // bit
+    return place
+
+
+def scatter_rows(values, axis, row_axis):
+    here = lax.axis_index(axis)
+    low_type = values.dtype
+    for bit in bits_of(lax.axis_size(axis)):
+        half = values.shape[row_axis] // 2
+        side = (here & bit) // bit
+        kept = lax.dynamic_slice_in_dim(values, side * half, half, row_axis)
+        given = lax.dynamic_slice_in_dim(values, (1 - side) * half, half, row_axis)
+        moved = swap(given.astype(low_type), axis, bit)
+        values = kept.astype(jnp.float32) + moved.astype(jnp.float32)
+        if bit * 2 < lax.axis_size(axis):
+            values = values.astype(low_type)
+    return values
+
+
+def gather_rows(values, axis, row_axis):
+    here = lax.axis_index(axis)
+    for bit in reversed(bits_of(lax.axis_size(axis))):
+        side = (here & bit) // bit
+        moved = swap(values, axis, bit)
+        half = values.shape[row_axis]
+        shape = list(values.shape)
+        shape[row_axis] = half * 2
+        joined = lax.dynamic_update_slice_in_dim(
+            jnp.zeros(shape, values.dtype), values, side * half, row_axis
+        )
+        values = lax.dynamic_update_slice_in_dim(joined, moved, (1 - side) * half, row_axis)
+    return values
 
 
 def body(
@@ -123,36 +200,87 @@
     next_cotangent,
     grad_entry,
 ):
-    tensor_size = lax.axis_size("tensor")
-    tokens_here = layer_inputs.shape[1]
     bf16_type = jnp.bfloat16
     float_type = jnp.float32
-    fetched = (
-        lax.all_gather(norms_master.astype(bf16_type), "dp", axis=1, tiled=True),
-        lax.all_gather(attend_in_master.astype(bf16_type), "dp", axis=1, tiled=True),
-        lax.all_gather(attend_out_master.astype(bf16_type), "dp", axis=1, tiled=True),
-        lax.all_gather(expand_master.astype(bf16_type), "dp", axis=0, tiled=True),
-        lax.all_gather(project_master.astype(bf16_type), "dp", axis=1, tiled=True),
-        lax.all_gather(mixer_in_master.astype(bf16_type), "dp", axis=0, tiled=True),
-        lax.all_gather(mixer_out_master.astype(bf16_type), "dp", axis=0, tiled=True),
-    )
-    (
-        norms_low,
-        attend_in_low,
-        attend_out_low,
-        expand_low,
-        project_low,
-        mixer_in_low,
-        mixer_out_low,
-    ) = fetched
-    norm_vals = norms_low.astype(float_type)
-    gain_rows = norm_vals[0:4][:, None, :]
+    tensor_size = lax.axis_size("tensor")
+    owners = lax.axis_size("dp")
+    me = lax.axis_index("dp")
+    tokens_here = layer_inputs.shape[1]
+    share_rows = tokens_here // tensor_size
+    share_start = share_index("tensor") * share_rows
+    cols = norms_master.shape[1]
+    mixers = mixer_out_master.shape[0]
+
+    def own_rows(values, axis):
+        return lax.dynamic_slice_in_dim(values, share_start, share_rows, axis)
+
+    def block_of(values, index):
+        return lax.dynamic_slice_in_dim(values, (me ^ index) * cols, cols, values.ndim - 1)
+
+    def reorder(pieces):
+        stacked = jnp.stack(pieces)
+        return jnp.concatenate(
+            [lax.dynamic_index_in_dim(stacked, me ^ index, 0, False) for index in range(owners)],
+            axis=-1,
+        )
+
+    def split(values):
+        return [values[..., index * cols : (index + 1) * cols] for index in range(owners)]
+
+    small = jnp.concatenate(
+        [
+            norms_master,
+            mixer_in_master.T,
+            jnp.pad(mixer_out_master, ((0, 0), (0, cols - MIXH))),
+        ],
+        axis=0,
+    ).astype(bf16_type)
+    small_pieces = gather_pieces(small, "dp")
+    attend_in_pieces = gather_pieces(attend_in_master.astype(bf16_type), "dp")
+    expand_pieces = gather_pieces(expand_master.astype(bf16_type), "dp")
+    project_pieces = gather_pieces(project_master.astype(bf16_type), "dp")
+    attend_out_pieces = gather_pieces(attend_out_master.astype(bf16_type), "dp")
+
+    stacked_entry = jnp.concatenate([history, grad_entry[None]], axis=0)
+    early_rows = [
+        lax.dynamic_slice_in_dim(
+            stacked_entry, (me ^ index) * tokens_here + share_start, share_rows, 1
+        )
+        for index in range(owners)
+    ]
+    early = reorder(exchange_pieces(early_rows, "dp"))
+    stored_share = early[:-1]
+    entry_back = early[-1].astype(float_type)
+    stored = gather_rows(stored_share, "tensor", 1)
+
+    norm_pieces = [piece[0:9].astype(float_type) for piece in small_pieces]
+    small_whole = reorder([piece[0 : 9 + MIXH] for piece in small_pieces])
+    norm_vals = small_whole[0:9].astype(float_type)
+    mixer_in_low = small_whole[9:]
+    mixer_out_stack = jnp.stack([piece[9 + MIXH :, 0:MIXH] for piece in small_pieces])
+    mixer_out_low = jnp.concatenate(
+        [lax.dynamic_index_in_dim(mixer_out_stack, me ^ index, 0, False) for index in range(owners)]
+    )
+
     input_vals = layer_inputs.astype(float_type)
-    centred = input_vals - jnp.mean(input_vals, axis=-1, keepdims=True)
+    mean_vals = jnp.mean(input_vals, axis=-1, keepdims=True)
+    centred = input_vals - mean_vals
     inverse = lax.rsqrt(jnp.mean(centred * centred, axis=-1, keepdims=True) + norm_epsilon)
-    unit_vals = centred * inverse
-    normed = (unit_vals * gain_rows + norm_vals[4:8][:, None, :]).astype(bf16_type)
-    proj = jnp.einsum("ctd,cde->cte", normed[0:3], attend_in_low, preferred_element_type=float_type)
+    normed_pieces = [
+        (
+            (block_of(layer_inputs, index).astype(float_type) - mean_vals)
+            * inverse
+            * norm_pieces[index][0:4][:, None, :]
+            + norm_pieces[index][4:8][:, None, :]
+        ).astype(bf16_type)
+        for index in range(owners)
+    ]
+    proj = sum(
+        jnp.einsum(
+            "ctd,cde->cte", normed[0:3], weights, preferred_element_type=float_type
+        )
+        for normed, weights in zip(normed_pieces, attend_in_pieces)
+    )
     local_heads = proj.shape[2] // HDIM
     split_heads = jnp.transpose(proj.reshape(3, tokens_here, local_heads, HDIM), (0, 2, 1, 3))
     cosine, sine_table, allowed = angles(seq_ids)
@@ -167,78 +295,125 @@
         "hqk,hkd->qhd", prob_low, value_rows, preferred_element_type=float_type
     )
     heads_out = heads_mixed.reshape(tokens_here, local_heads * HDIM).astype(bf16_type)
-    upper = jnp.dot(normed[3], expand_low, preferred_element_type=float_type)
+    upper = sum(
+        jnp.dot(normed[3], weights, preferred_element_type=float_type)
+        for normed, weights in zip(normed_pieces, expand_pieces)
+    )
     hidden = exact_gelu(upper).astype(bf16_type)
-    partial_branch = jnp.dot(
-        heads_out, attend_out_low, preferred_element_type=float_type
-    ) + jnp.dot(hidden, project_low, preferred_element_type=float_type)
-    branch = lax.psum(partial_branch, "tensor")
-    valid = (seq_ids >= 0).astype(float_type)[:, None]
-    newest = input_vals[3] + valid * branch
-    new_entry = lax.all_to_all(
-        newest.astype(bf16_type), "dp", split_axis=1, concat_axis=0, tiled=True
-    )
-    stored = lax.all_to_all(history, "dp", split_axis=1, concat_axis=2, tiled=True).astype(
-        float_type
-    )
+    partial_branch = jnp.concatenate(
+        [
+            (
+                jnp.dot(heads_out, out_weights, preferred_element_type=float_type)
+                + jnp.dot(hidden, weights, preferred_element_type=float_type)
+            ).astype(bf16_type)
+            for out_weights, weights in zip(attend_out_pieces, project_pieces)
+        ],
+        axis=-1,
+    )
+    branch = reorder(split(scatter_rows(partial_branch, "tensor", 0)))
+
+    valid = (own_rows(seq_ids, 0) >= 0).astype(float_type)[:, None]
+    input_share = own_rows(layer_inputs, 1).astype(float_type)
+    newest = input_share[3] + valid * branch
     mix_scale = lax.rsqrt(jnp.mean(newest * newest, axis=-1, keepdims=True) + mixer_epsilon)
     mix_normed = (newest * mix_scale * norm_vals[8]).astype(bf16_type)
-    mix_pre = jnp.dot(mix_normed, mixer_in_low, preferred_element_type=float_type)
+    mix_pre = contract_cols(mix_normed, mixer_in_low)
     mix_act = exact_gelu(mix_pre).astype(bf16_type)
     layer_count = stored.shape[0] + 1
-    mix_weights = contract_cols(mix_act, mixer_out_low).reshape(tokens_here, 4, layer_count)
-    layers = [stored[layer_index] for layer_index in range(layer_count - 1)] + [newest]
-    next_vals = mix_weights[:, :, 0].T[:, :, None] * layers[0][None]
-    for layer_index in range(1, layer_count):
-        next_vals = (
-            next_vals + mix_weights[:, :, layer_index].T[:, :, None] * layers[layer_index][None]
-        )
-    next_inputs = next_vals.astype(bf16_type)
-    grad_out = next_cotangent.astype(float_type)
-    entry_back = lax.all_to_all(grad_entry, "dp", split_axis=0, concat_axis=1, tiled=True).astype(
-        float_type
-    )
+    mix_share = contract_cols(mix_act, mixer_out_low)
+    mix_weights = mix_share.reshape(share_rows, 4, layer_count)
+    layers = [stored_share[index].astype(float_type) for index in range(layer_count - 1)] + [newest]
+    grad_out = own_rows(next_cotangent, 1).astype(float_type)
     weight_terms = jnp.stack(
         [jnp.sum(grad_out * layer_vals[None], axis=-1) for layer_vals in layers], axis=-1
     )
     grad_weights = (
         jnp.transpose(weight_terms, (1, 0, 2))
-        .reshape(tokens_here, 4 * layer_count)
+        .reshape(share_rows, 4 * layer_count)
         .astype(bf16_type)
     )
-    layer_grads = [
-        jnp.sum(mix_weights[:, :, layer_index].T[:, :, None] * grad_out, axis=0)
-        for layer_index in range(layer_count)
-    ]
-    grad_history = lax.all_to_all(
-        jnp.stack(layer_grads[:-1]).astype(bf16_type), "dp", split_axis=2, concat_axis=1, tiled=True
-    )
+    newest_back = jnp.sum(mix_weights[:, :, layer_count - 1].T[:, :, None] * grad_out, axis=0)
     grad_mixer_out = contract_rows(grad_weights, mix_act)
     grad_mix_act = jnp.dot(grad_weights, mixer_out_low, preferred_element_type=float_type)
     grad_mix_pre = gelu_grad(mix_pre, grad_mix_act).astype(bf16_type)
-    grad_mixer_in = contract_rows(mix_normed, grad_mix_pre)
-    grad_mix_normed = contract_cols(grad_mix_pre, mixer_in_low)
+    grad_mixer_in = contract_rows(grad_mix_pre, mix_normed)
+    grad_mix_normed = jnp.dot(grad_mix_pre, mixer_in_low, preferred_element_type=float_type)
     scaled_mix = grad_mix_normed * norm_vals[8]
     grad_newest = (
-        layer_grads[-1]
+        newest_back
         + entry_back
         + mix_scale * scaled_mix
         - newest * mix_scale**3 * jnp.mean(scaled_mix * newest, axis=-1, keepdims=True)
     )
-    share_rows = tokens_here // tensor_size
-    share_start = lax.axis_index("tensor") * share_rows
-    mixer_gain = jnp.sum(
-        lax.dynamic_slice_in_dim(grad_mix_normed * newest * mix_scale, share_start, share_rows, 0),
-        axis=0,
-    )
-    grad_branch = (valid * grad_newest).astype(bf16_type)
-    grad_attend_out = contract_rows(heads_out, grad_branch)
-    grad_project = contract_rows(hidden, grad_branch)
-    grad_heads = contract_cols(grad_branch, attend_out_low).astype(bf16_type)
-    grad_hidden = contract_cols(grad_branch, project_low)
+    mixer_gain = jnp.sum(grad_mix_normed * newest * mix_scale, axis=0)
+    branch_share = (valid * grad_newest).astype(bf16_type)
+    grad_branch = split(
+        gather_rows(
+            jnp.concatenate([block_of(branch_share, index) for index in range(owners)], axis=-1),
+            "tensor",
+            0,
+        )
+    )
+
+    newest_low = gather_rows(newest.astype(bf16_type), "tensor", 0)
+    mix_whole = gather_rows(mix_share, "tensor", 0).reshape(tokens_here, 4, layer_count)
+    layers_low = [stored[index] for index in range(layer_count - 1)] + [newest_low]
+    next_inputs = sum(
+        mix_whole[:, :, index].T[:, :, None] * layers_low[index].astype(float_type)[None]
+        for index in range(layer_count)
+    ).astype(bf16_type)
+    entry_pieces = exchange_pieces(
+        [block_of(newest_low, index) for index in range(owners)], "dp"
+    )
+    history_pieces = exchange_pieces(
+        [
+            jnp.stack(
+                [
+                    jnp.sum(
+                        mix_whole[:, :, layer].T[:, :, None]
+                        * block_of(next_cotangent, index).astype(float_type),
+                        axis=0,
+                    )
+                    for layer in range(layer_count - 1)
+                ]
+            ).astype(bf16_type)
+            for index in range(owners)
+        ],
+        "dp",
+    )
+    new_entry = jnp.zeros(grad_entry.shape, bf16_type)
+    grad_history = jnp.zeros(history.shape, bf16_type)
+    for index in range(owners):
+        first_row = (me ^ index) * tokens_here
+        new_entry = lax.dynamic_update_slice_in_dim(new_entry, entry_pieces[index], first_row, 0)
+        grad_history = lax.dynamic_update_slice_in_dim(
+            grad_history, history_pieces[index], first_row, 1
+        )
+
+    grad_heads = sum(
+        contract_cols(grads, weights) for grads, weights in zip(grad_branch, attend_out_pieces)
+    ).astype(bf16_type)
+    grad_hidden = sum(
+        contract_cols(grads, weights) for grads, weights in zip(grad_branch, project_pieces)
+    )
     grad_upper = gelu_grad(upper, grad_hidden).astype(bf16_type)
-    grad_expand = contract_rows(normed[3], grad_upper)
-    grad_normed_ffn = contract_cols(grad_upper, expand_low)
+    grad_project = reduce_pieces(
+        [contract_rows(hidden, grads) for grads in grad_branch], "dp", bf16_type
+    )
+    grad_attend_out = reduce_pieces(
+        [contract_rows(heads_out, grads) for grads in grad_branch], "dp", bf16_type
+    )
+    grad_expand = reduce_pieces(
+        [contract_rows(normed[3], grad_upper) for normed in normed_pieces], "dp", bf16_type
+    )
+    summed_ffn = scatter_rows(
+        jnp.concatenate(
+            [contract_cols(grad_upper, weights).astype(bf16_type) for weights in expand_pieces],
+            axis=-1,
+        ),
+        "tensor",
+        0,
+    )
     head_scale = HDIM ** (-0.5)
     grad_heads_split = jnp.transpose(grad_heads.reshape(tokens_here, local_heads, HDIM), (1, 0, 2))
     prob = jnp.exp(score_block(query, key_rows, allowed) - log_total)
@@ -258,41 +433,95 @@
     grad_value = jnp.einsum(
         "hqk,hqd->hkd", prob_low, grad_heads_split, preferred_element_type=float_type
     )
-    grad_split = jnp.stack(
-        [rotate(grad_query, cosine, -sine_table), rotate(grad_key, cosine, -sine_table), grad_value]
-    ).astype(bf16_type)
-    grad_proj = jnp.transpose(grad_split, (0, 2, 1, 3)).reshape(3, tokens_here, local_heads * HDIM)
-    grad_attend_in = jnp.einsum(
-        "ctd,cte->cde", normed[0:3], grad_proj, preferred_element_type=float_type
-    )
-    grad_normed_attn = jnp.einsum(
-        "cte,cde->ctd", grad_proj, attend_in_low, preferred_element_type=float_type
-    )
-    grad_normed = jnp.concatenate([grad_normed_attn, grad_normed_ffn[None]], axis=0)
-    gain_part = jnp.sum(grad_normed * unit_vals, axis=1)
-    bias_part = jnp.sum(grad_normed, axis=1)
-    norm_part = jnp.concatenate([gain_part, bias_part, mixer_gain[None]], axis=0)
-    summed_grads = lax.psum(grad_normed, "tensor")
-    back_full = norm_back(summed_grads, unit_vals, inverse, gain_rows)
-    grad_inputs = back_full.at[3].add(grad_newest).astype(bf16_type)
-    norm_total = lax.psum(norm_part, ("dp", "tensor"))
-    norm_cols = norms_master.shape[1]
-    norm_grad = lax.dynamic_slice_in_dim(norm_total, lax.axis_index("dp") * norm_cols, norm_cols, 1)
-    reduced = (
-        lax.psum_scatter(grad_attend_in, "dp", scatter_dimension=1, tiled=True),
-        lax.psum_scatter(grad_attend_out, "dp", scatter_dimension=1, tiled=True),
-        lax.psum_scatter(grad_expand, "dp", scatter_dimension=0, tiled=True),
-        lax.psum_scatter(grad_project, "dp", scatter_dimension=1, tiled=True),
-        lax.psum_scatter(grad_mixer_in, "dp", scatter_dimension=0, tiled=True),
-        lax.psum_scatter(grad_mixer_out, "dp", scatter_dimension=0, tiled=True),
-    )
-    shard_squares = sum((jnp.sum(gradient * gradient) for gradient in reduced[0:4]))
+    grad_proj = [
+        jnp.transpose(grads, (1, 0, 2)).reshape(tokens_here, local_heads * HDIM).astype(bf16_type)
+        for grads in (
+            rotate(grad_query, cosine, -sine_table),
+            rotate(grad_key, cosine, -sine_table),
+            grad_value,
+        )
+    ]
+    grad_attend_in = [
+        reduce_pieces(
+            [contract_rows(normed[index], grad_proj[index]) for normed in normed_pieces],
+            "dp",
+            bf16_type,
+        )
+        for index in range(3)
+    ]
+    summed = [
+        scatter_rows(
+            jnp.concatenate(
+                [
+                    contract_cols(grad_proj[index], weights[index]).astype(bf16_type)
+                    for weights in attend_in_pieces
+                ],
+                axis=-1,
+            ),
+            "tensor",
+            0,
+        )
+        for index in range(3)
+    ] + [summed_ffn]
+    unit_share = (input_share - own_rows(mean_vals, 1)) * own_rows(inverse, 1)
+    inverse_share = own_rows(inverse, 1)
+    gain_parts = []
+    bias_parts = []
+    grad_inputs = []
+    for index in range(4):
+        grad_rows = reorder(split(summed[index]))
+        gain_parts.append(jnp.sum(grad_rows * unit_share[index], axis=0))
+        bias_parts.append(jnp.sum(grad_rows, axis=0))
+        back = norm_back(grad_rows, unit_share[index], inverse_share[index], norm_vals[index][None])
+        if index == 3:
+            back = back + grad_newest
+        grad_inputs.append(gather_rows(back.astype(bf16_type), "tensor", 0))
+    grad_inputs = jnp.stack(grad_inputs)
+
+    early_pack = jnp.concatenate(
+        [
+            grad_mixer_in,
+            jnp.pad(
+                grad_mixer_out.reshape(owners, mixers * MIXH), ((0, 0), (0, cols - mixers * MIXH))
+            ).reshape(1, owners * cols),
+            mixer_gain[None],
+        ],
+        axis=0,
+    )
+    late_pack = jnp.stack(gain_parts + bias_parts)
+    early_sum = butterfly(
+        reduce_pieces([block_of(early_pack, index) for index in range(owners)], "dp", float_type),
+        "tensor",
+    )
+    late_sum = butterfly(
+        reduce_pieces([block_of(late_pack, index) for index in range(owners)], "dp", float_type),
+        "tensor",
+    )
+    norm_grad = jnp.concatenate([late_sum, early_sum[MIXH + 1 :]], axis=0)
+    grad_mixer_in = early_sum[0:MIXH].T
+    grad_mixer_out = early_sum[MIXH, 0 : mixers * MIXH].reshape(mixers, MIXH)
+    shard_squares = sum(
+        (
+            jnp.sum(gradient * gradient)
+            for gradient in grad_attend_in + [grad_attend_out, grad_expand, grad_project]
+        )
+    )
     shared_squares = (
         jnp.sum(norm_grad * norm_grad)
-        + jnp.sum(reduced[4] * reduced[4])
-        + jnp.sum(reduced[5] * reduced[5])
-    )
-    total_squares = lax.psum(shard_squares + shared_squares / tensor_size, ("dp", "tensor"))
+        + jnp.sum(grad_mixer_in * grad_mixer_in)
+        + jnp.sum(grad_mixer_out * grad_mixer_out)
+    )
+    total_squares = butterfly(
+        butterfly((shard_squares + shared_squares / tensor_size).reshape(1, 1), "dp"), "tensor"
+    )[0, 0]
+    reduced = (
+        jnp.stack(grad_attend_in),
+        grad_attend_out,
+        grad_expand,
+        grad_project,
+        grad_mixer_in,
+        grad_mixer_out,
+    )
     grad_norm = jnp.sqrt(total_squares)
     factor = jnp.minimum(1.0, clip_level / grad_norm)
     wide_rate = 2.0 / math.sqrt(D)

time: 1320 us -> 731 us (0.55)
  waiting for transfers between devices: 762 us -> 268 us
  blocking collectives: 184 us -> 0 us
  starting transfers between devices: 20.4 us -> 130 us
  other arithmetic: 153 us -> 119 us
  matrix products: 70.9 us -> 102 us
    psum x3 -> x0, waiting for transfers between devices: 529 us -> none  [the longest x1 381 us: body(): summed_grads = lax.psum(grad_normed, 'tensor')]
    ppermute x0 -> x98, waiting for transfers between devices: none -> 268 us  [swap(): lax.ppermute(values, axis, [(source, source ^ mask) for source in range(s...]
    reduce_scatter x5 -> x0, waiting for transfers between devices: 141 us -> none  [the longest x1 70.8 us: body(): lax.psum_scatter(grad_project, 'dp', scatter_dimension=1, tiled=True)]
    ppermute x0 -> x98, starting transfers between devices: none -> 130 us  [swap(): lax.ppermute(values, axis, [(source, source ^ mask) for source in range(s...]
    unnamed x1 -> x0, blocking collectives: 105 us -> none
    all_gather x4 -> x0, waiting for transfers between devices: 75.9 us -> none  [the longest x1 49.4 us: body(): lax.all_gather(project_master.astype(bf16_type), 'dp', axis=1, tiled=True)]
    all_gather x3 -> x0, blocking collectives: 39.6 us -> none  [the longest x1 28.1 us: body(): lax.all_gather(norms_master.astype(bf16_type), 'dp', axis=1, tiled=True)]
    psum x1 -> x0, blocking collectives: 39.3 us -> none  [body(): lax.psum(shard_squares + shared_squares / tensor_size, ('dp', 'tensor'))]
  transfers between devices with their start and end apart: 16 -> 98, of which waited for: 9 -> 42; matrix products, arithmetic and copies ran while one was open for 15% -> 40% of each run, Pallas kernels for 0% -> 0%
where the time goes in v1:
time: 731 us; the launch traced here: 722 us
  waiting for transfers between devices  268 us (37%)
  starting transfers between devices  130 us (18%)
  other arithmetic  119 us (16%)
  matrix products  102 us (14%)
  local copies, waits for them, and re-layouts  88 us (12%)
  between operations  14.9 us (2%)
    ppermute x98, waiting for transfers between devices, swap(): lax.ppermute(values, axis, [(source, source ^ mask) for source in range(s...  268 us
    ppermute x98, starting transfers between devices, swap(): lax.ppermute(values, axis, [(source, source ^ mask) for source in range(s...  130 us
    dot_general x26, matrix products, contract_rows(): lax.dot_general(left, right, (((0,), (0,)), ((), ())), preferred_element_...  36.3 us
    dot_general x26, matrix products, contract_cols(): lax.dot_general(left, right, (((1,), (1,)), ((), ())), preferred_element_...  30.5 us
    dynamic_update_slice x24, local copies, waits for them, and re-layouts, gather_rows(): lax.dynamic_update_slice_in_dim(joined, moved, (1 - side) * half, row_axis)  21.3 us
    dynamic_update_slice x17, local copies, waits for them, and re-layouts, gather_rows(): lax.dynamic_update_slice_in_dim(jnp.zeros(shape, values.dtype), values, s...  17.4 us
  transfers between devices with their start and end apart: 98, of which 42 were waited for; matrix products, arithmetic and copies ran while one was open for 40% of the time, Pallas kernels for 0%

profile of v1, /device:TPU:0, one launch (start us, length us, event | category | flops | bytes accessed | tf_op | source)
XLA Modules:
  0.0 722.1 jit_solution(16530843449184296532)
XLA Ops:
  14.8 3.7 convert_reduce_fusion
  18.5 4.6 fusion.1
  42.5 4.7 add_convert_fusion.1
  55.9 15.9 %collective-permute-done.3 = bf16[3,512,256]{1,2,0:T(8,128)(2,1)S(1)} collective-permute-done((bf16[3,512,256]{1,2,0:T(8,128)(2,1)S(1)}, bf16[3,512,256]{1,2,0:T(8,128)(2,1)S(1)}, u32[]{:S(2)}, u32[]{:S(2)}) %collective-permute-start.3) | collective-permute-done | bytes 786464 | tf_op jit(solution)/shard_map/ppermute | solution.py:104
  90.4 9.1 %collective-permute-done.11 = bf16[256,512]{1,0:T(8,128)(2,1)} collective-permute-done((bf16[256,512]{1,0:T(8,128)(2,1)}, bf16[256,512]{1,0:T(8,128)(2,1)}, u32[]{:S(2)}, u32[]{:S(2)}) %collective-permute-start.11) | collective-permute-done | bytes 262176 | tf_op jit(solution)/shard_map/ppermute | solution.py:104
  102.9 6.2 multiply_convert_fusion
  120.7 7.4 %collective-permute-done.24 = bf16[3,48,2048]{2,1,0:T(8,128)(2,1)S(1)} collective-permute-done((bf16[3,48,2048]{2,1,0:T(8,128)(2,1)S(1)}, bf16[3,48,2048]{2,1,0:T(8,128)(2,1)S(1)}, u32[]{:S(2)}, u32[]{:S(2)}) %collective-permute-start.24) | collective-permute-done | bytes 589856 | tf_op jit(solution)/shard_map/ppermute | solution.py:104
  129.1 9.6 %collective-permute-done.15 = bf16[192,2048]{1,0:T(8,128)(2,1)S(1)} collective-permute-done((bf16[192,2048]{1,0:T(8,128)(2,1)S(1)}, bf16[192,2048]{1,0:T(8,128)(2,1)S(1)}, u32[]{:S(2)}, u32[]{:S(2)}) %collective-permute-start.15) | collective-permute-done | bytes 786464 | tf_op jit(solution)/shard_map/ppermute | solution.py:104
  143.5 13.7 %collective-permute-done.25 = bf16[3,96,2048]{2,1,0:T(8,128)(2,1)S(1)} collective-permute-done((bf16[3,96,2048]{2,1,0:T(8,128)(2,1)S(1)}, bf16[3,96,2048]{2,1,0:T(8,128)(2,1)S(1)}, u32[]{:S(2)}, u32[]{:S(2)}) %collective-permute-start.25) | collective-permute-done | bytes 1179680 | tf_op jit(solution)/shard_map/ppermute | solution.py:104
  159.8 3.8 collective-permute-done.16
  163.7 3.4 collective-permute-start.17
  169.8 6.2 collective-permute-done.17
  198.1 4.0 collective-permute-start.19
  216.7 6.9 fusion.11
  240.8 8.2 %collective-permute-done.73 = f32[38,512]{1,0:T(8,128)S(1)} collective-permute-done((f32[38,512]{1,0:T(8,128)S(1)}, f32[38,512]{1,0:T(8,128)S(1)}, u32[]{:S(2)}, u32[]{:S(2)}) %collective-permute-start.73) | collective-permute-done | bytes 77856 | tf_op jit(solution)/shard_map/ppermute | solution.py:104
  249.0 3.2 collective-permute-start.74
  258.8 4.3 collective-permute-done.34
  269.7 4.1 fusion.25
  274.0 11.3 %collective-permute-done.62 = bf16[3,384,512]{2,1,0:T(8,128)(2,1)S(1)} collective-permute-done((bf16[3,384,512]{2,1,0:T(8,128)(2,1)S(1)}, bf16[3,384,512]{2,1,0:T(8,128)(2,1)S(1)}, u32[]{:S(2)}, u32[]{:S(2)}) %collective-permute-start.62) | collective-permute-done | bytes 1179680 | tf_op jit(solution)/shard_map/ppermute | solution.py:104
  285.4 10.4 %collective-permute-done.35 = bf16[192,2048]{1,0:T(8,128)(2,1)S(1)} collective-permute-done((bf16[192,2048]{1,0:T(8,128)(2,1)S(1)}, bf16[192,2048]{1,0:T(8,128)(2,1)S(1)}, u32[]{:S(2)}, u32[]{:S(2)}) %collective-permute-start.35) | collective-permute-done | bytes 786464 | tf_op jit(solution)/shard_map/ppermute | solution.py:104
  331.5 4.6 add_convert_fusion.8
  361.6 5.9 add_convert_fusion
  378.9 4.8 collective-permute-done.77
  386.7 5.0 collective-permute-done.80
  394.8 4.3 collective-permute-done.83
  413.3 13.2 %collective-permute-done.54 = bf16[192,2048]{1,0:T(8,128)(2,1)} collective-permute-done((bf16[192,2048]{1,0:T(8,128)(2,1)}, bf16[192,2048]{1,0:T(8,128)(2,1)}, u32[]{:S(2)}, u32[]{:S(2)}) %collective-permute-start.54) | collective-permute-done | bytes 786464 | tf_op jit(solution)/shard_map/ppermute | solution.py:104
  428.1 14.5 %collective-permute-done.48 = bf16[192,2048]{1,0:T(8,128)(2,1)} collective-permute-done((bf16[192,2048]{1,0:T(8,128)(2,1)}, bf16[192,2048]{1,0:T(8,128)(2,1)}, u32[]{:S(2)}, u32[]{:S(2)}) %collective-permute-start.48) | collective-permute-done | bytes 786464 | tf_op jit(solution)/shard_map/ppermute | solution.py:104
  457.0 6.2 collective-permute-done.37
  464.7 7.0 collective-permute-done.55
  471.7 3.2 collective-permute-start.44
  475.1 7.8 %collective-permute-done.49 = bf16[96,2048]{1,0:T(8,128)(2,1)S(1)} collective-permute-done((bf16[96,2048]{1,0:T(8,128)(2,1)S(1)}, bf16[96,2048]{1,0:T(8,128)(2,1)S(1)}, u32[]{:S(2)}, u32[]{:S(2)}) %collective-permute-start.49) | collective-permute-done | bytes 393248 | tf_op jit(solution)/shard_map/ppermute | solution.py:104
  486.2 12.6 %collective-permute-done.38 = bf16[48,2048]{1,0:T(8,128)(2,1)S(1)} collective-permute-done((bf16[48,2048]{1,0:T(8,128)(2,1)S(1)}, bf16[48,2048]{1,0:T(8,128)(2,1)S(1)}, u32[]{:S(2)}, u32[]{:S(2)}) %collective-permute-start.38) | collective-permute-done | bytes 196640 | tf_op jit(solution)/shard_map/ppermute | solution.py:104
  498.8 8.3 %collective-permute-done.56 = bf16[48,2048]{1,0:T(8,128)(2,1)S(1)} collective-permute-done((bf16[48,2048]{1,0:T(8,128)(2,1)S(1)}, bf16[48,2048]{1,0:T(8,128)(2,1)S(1)}, u32[]{:S(2)}, u32[]{:S(2)}) %collective-permute-start.56) | collective-permute-done | bytes 196640 | tf_op jit(solution)/shard_map/ppermute | solution.py:104
  507.2 3.4 collective-permute-done.50
  533.1 4.7 collective-permute-done.67
  551.0 7.2 collective-permute-done.51
  560.0 9.8 %collective-permute-done.45 = bf16[48,2048]{1,0:T(8,128)(2,1)S(1)} collective-permute-done((bf16[48,2048]{1,0:T(8,128)(2,1)}, bf16[48,2048]{1,0:T(8,128)(2,1)S(1)}, u32[]{:S(2)}, u32[]{:S(2)}) %collective-permute-start.45) | collective-permute-done | bytes 196640 | tf_op jit(solution)/shard_map/ppermute | solution.py:104
  571.6 6.3 collective-permute-done.39
  578.0 11.5 %collective-permute-done.58 = bf16[96,2048]{1,0:T(8,128)(2,1)S(1)} collective-permute-done((bf16[96,2048]{1,0:T(8,128)(2,1)S(1)}, bf16[96,2048]{1,0:T(8,128)(2,1)S(1)}, u32[]{:S(2)}, u32[]{:S(2)}) %collective-permute-start.58) | collective-permute-done | bytes 393248 | tf_op jit(solution)/shard_map/ppermute | solution.py:104
  592.1 8.6 %collective-permute-done.52 = bf16[96,2048]{1,0:T(8,128)(2,1)S(1)} collective-permute-done((bf16[96,2048]{1,0:T(8,128)(2,1)S(1)}, bf16[96,2048]{1,0:T(8,128)(2,1)S(1)}, u32[]{:S(2)}, u32[]{:S(2)}) %collective-permute-start.52) | collective-permute-done | bytes 393248 | tf_op jit(solution)/shard_map/ppermute | solution.py:104
  603.7 7.2 %collective-permute-done.46 = bf16[96,2048]{1,0:T(8,128)(2,1)S(1)} collective-permute-done((bf16[96,2048]{1,0:T(8,128)(2,1)S(1)}, bf16[96,2048]{1,0:T(8,128)(2,1)S(1)}, u32[]{:S(2)}, u32[]{:S(2)}) %collective-permute-start.46) | collective-permute-done | bytes 393248 | tf_op jit(solution)/shard_map/ppermute | solution.py:104
  614.0 4.7 collective-permute-done.40
  623.0 4.2 multiply_reduce_fusion.1
  628.7 4.0 multiply_reduce_fusion
  639.7 38.5 %collective-permute-start.95 = (f32[1,1]{1,0:T(1,128)}, f32[1,1]{1,0:T(1,128)}, u32[]{:S(2)}, u32[]{:S(2)}) collective-permute-start(f32[1,1]{1,0:T(1,128)} %add.792), channel_id=1, source_target_pairs={{0,1},{1,0},{2,3},{3,2},{4,5},{5,4},{6,7},{7,6},{8,9},{9,8},{10,11... | collective-permute-start | bytes 20 | tf_op jit(solution)/shard_map/ppermute | solution.py:104
  691.8 8.9 %fusion.140 = (bf16[512,1024]{1,0:T(8,128)(2,1)}, f32[512,1024]{1,0:T(8,128)}, f32[512,1024]{1,0:T(8,128)}, f32[512,1024]{1,0:T(8,128)}) fusion(f32[512,1024]{1,0:T(8,128)} %param.38, f32[]{:T(128)S(6)} %min.3, bf16[512,1024]{1,0:T(8,128)(2,1)} %collective-permute-done.89, f32[512,1024]{1,0:T(8,128)} %get-tuple-element.259, ...), kind=kLoop, calls=%fused_computation.607 | loop fusion | flops 11010048 | bytes 17825796 | tf_op jit(solution)/shard_map/convert_element_type | solution.py:596
  700.8 5.8 fusion.138
  706.7 3.3 fusion.144
  (867 shorter events, 340.7 us)
Async XLA Ops:
  3.7 34.5 %collective-permute-start.2 = (bf16[49,512]{1,0:T(8,128)(2,1)}, bf16[49,512]{1,0:T(8,128)(2,1)}, u32[]{:S(2)}, u32[]{:S(2)}) collective-permute-start(bf16[49,512]{1,0:T(8,128)(2,1)} %fusion.100), channel_id=1, source_target_pairs={{0,16},{8,24},{16,0},{24,8},{1,17},{9,25},{17,1},{25,9},{2,18},{10... | collective-permute-start | bytes 150536 | tf_op jit(solution)/shard_map/ppermute | solution.py:104
  6.6 30.5 %collective-permute-start = (bf16[49,512]{1,0:T(8,128)(2,1)}, bf16[49,512]{1,0:T(8,128)(2,1)}, u32[]{:S(2)}, u32[]{:S(2)}) collective-permute-start(bf16[49,512]{1,0:T(8,128)(2,1)} %fusion.100), channel_id=1, source_target_pairs={{0,8},{8,0},{16,24},{24,16},{1,9},{9,1},{17,25},{25,17},{2,10},{10... | collective-permute-start | bytes 150536 | tf_op jit(solution)/shard_map/ppermute | solution.py:104
  8.4 64.9 %collective-permute-start.7 = (bf16[512,1024]{1,0:T(8,128)(2,1)S(1)}, bf16[512,1024]{1,0:T(8,128)(2,1)}, u32[]{:S(2)}, u32[]{:S(2)}) collective-permute-start(bf16[512,1024]{1,0:T(8,128)(2,1)S(1)} %convert_element_type.568), channel_id=1, source_target_pairs={{0,16},{8,24},{16,0},{24,8},{1,17},{9,25},{17,1},{25,9},{2,18},{10... | collective-permute-start | bytes 3145736 | tf_op jit(solution)/shard_map/ppermute | solution.py:104
  8.6 69.5 %collective-permute-start.6 = (bf16[512,1024]{1,0:T(8,128)(2,1)S(1)}, bf16[512,1024]{1,0:T(8,128)(2,1)}, u32[]{:S(2)}, u32[]{:S(2)}) collective-permute-start(bf16[512,1024]{1,0:T(8,128)(2,1)S(1)} %convert_element_type.568), channel_id=1, source_target_pairs={{0,8},{8,0},{16,24},{24,16},{1,9},{9,1},{17,25},{25,17},{2,10},{10... | collective-permute-start | bytes 3145736 | tf_op jit(solution)/shard_map/ppermute | solution.py:104
  11.1 40.3 %collective-permute-start.23 = (bf16[4,48,512]{2,1,0:T(8,128)(2,1)}, bf16[4,48,512]{2,1,0:T(8,128)(2,1)}, u32[]{:S(2)}, u32[]{:S(2)}) collective-permute-start(bf16[4,48,512]{2,1,0:T(8,128)(2,1)} %get-tuple-element.121), channel_id=1, source_target_pairs={{0,24},{8,16},{16,8},{24,0},{1,25},{9,17},{17,9},{25,1},{2,26},{10... | collective-permute-start | bytes 589832 | tf_op jit(solution)/shard_map/ppermute | solution.py:104
  51.4 20.4 %collective-permute-start.3 = (bf16[3,512,256]{1,2,0:T(8,128)(2,1)S(1)}, bf16[3,512,256]{1,2,0:T(8,128)(2,1)S(1)}, u32[]{:S(2)}, u32[]{:S(2)}) collective-permute-start(bf16[3,512,256]{1,2,0:T(8,128)(2,1)S(1)} %copy.99), channel_id=1, source_target_pairs={{0,16},{8,24},{16,0},{24,8},{1,17},{9,25},{17,1},{25,9},{2,18},{10... | collective-permute-start | bytes 2359304 | tf_op jit(solution)/shard_map/ppermute | solution.py:104
  53.2 49.2 %collective-permute-start.12 = (bf16[1024,512]{1,0:T(8,128)(2,1)}, bf16[1024,512]{1,0:T(8,128)(2,1)}, u32[]{:S(2)}, u32[]{:S(2)}) collective-permute-start(bf16[1024,512]{1,0:T(8,128)(2,1)} %convert_element_type.570), channel_id=1, source_target_pairs={{0,16},{8,24},{16,0},{24,8},{1,17},{9,25},{17,1},{25,9},{2,18},{10... | collective-permute-start | bytes 3145736 | tf_op jit(solution)/shard_map/ppermute | solution.py:104
  55.9 58.0 %collective-permute-start.10 = (bf16[1024,512]{1,0:T(8,128)(2,1)}, bf16[1024,512]{1,0:T(8,128)(2,1)}, u32[]{:S(2)}, u32[]{:S(2)}) collective-permute-start(bf16[1024,512]{1,0:T(8,128)(2,1)} %convert_element_type.570), channel_id=1, source_target_pairs={{0,8},{8,0},{16,24},{24,16},{1,9},{9,1},{17,25},{25,17},{2,10},{10... | collective-permute-start | bytes 3145736 | tf_op jit(solution)/shard_map/ppermute | solution.py:104
  73.3 26.2 %collective-permute-start.11 = (bf16[256,512]{1,0:T(8,128)(2,1)}, bf16[256,512]{1,0:T(8,128)(2,1)}, u32[]{:S(2)}, u32[]{:S(2)}) collective-permute-start(bf16[256,512]{1,0:T(8,128)(2,1)} %convert_element_type.567), channel_id=1, source_target_pairs={{0,16},{8,24},{16,0},{24,8},{1,17},{9,25},{17,1},{25,9},{2,18},{10... | collective-permute-start | bytes 786440 | tf_op jit(solution)/shard_map/ppermute | solution.py:104
  78.1 39.5 %collective-permute-start.9 = (bf16[256,512]{1,0:T(8,128)(2,1)}, bf16[256,512]{1,0:T(8,128)(2,1)}, u32[]{:S(2)}, u32[]{:S(2)}) collective-permute-start(bf16[256,512]{1,0:T(8,128)(2,1)} %convert_element_type.567), channel_id=1, source_target_pairs={{0,8},{8,0},{16,24},{24,16},{1,9},{9,1},{17,25},{25,17},{2,10},{10... | collective-permute-start | bytes 786440 | tf_op jit(solution)/shard_map/ppermute | solution.py:104
  81.1 21.3 %collective-permute-start.8 = (bf16[512,1024]{1,0:T(8,128)(2,1)}, bf16[512,1024]{1,0:T(8,128)(2,1)}, u32[]{:S(2)}, u32[]{:S(2)}) collective-permute-start(bf16[512,1024]{1,0:T(8,128)(2,1)} %collective-permute-done.7), channel_id=1, source_target_pairs={{0,8},{8,0},{16,24},{24,16},{1,9},{9,1},{17,25},{25,17},{2,10},{10... | collective-permute-start | bytes 3145736 | tf_op jit(solution)/shard_map/ppermute | solution.py:104
  99.6 28.6 %collective-permute-start.24 = (bf16[3,48,2048]{2,1,0:T(8,128)(2,1)S(1)}, bf16[3,48,2048]{2,1,0:T(8,128)(2,1)S(1)}, u32[]{:S(2)}, u32[]{:S(2)}) collective-permute-start(bf16[3,48,2048]{2,1,0:T(8,128)(2,1)S(1)} %copy-done.133), channel_id=1, source_target_pairs={{0,4},{1,5},{2,6},{3,7},{4,0},{5,1},{6,2},{7,3},{8,12},{9,13},{10,... | collective-permute-start | bytes 1769480 | tf_op jit(solution)/shard_map/ppermute | solution.py:104
  119.2 19.6 %collective-permute-start.15 = (bf16[192,2048]{1,0:T(8,128)(2,1)S(1)}, bf16[192,2048]{1,0:T(8,128)(2,1)S(1)}, u32[]{:S(2)}, u32[]{:S(2)}) collective-permute-start(bf16[192,2048]{1,0:T(8,128)(2,1)S(1)} %constant_dynamic-slice_fusion.37), channel_id=1, source_target_pairs={{0,1},{1,0},{2,3},{3,2},{4,5},{5,4},{6,7},{7,6},{8,9},{9,8},{10,11... | collective-permute-start | bytes 2359304 | tf_op jit(solution)/shard_map/ppermute | solution.py:104
  128.2 29.0 %collective-permute-start.25 = (bf16[3,96,2048]{2,1,0:T(8,128)(2,1)S(1)}, bf16[3,96,2048]{2,1,0:T(8,128)(2,1)S(1)}, u32[]{:S(2)}, u32[]{:S(2)}) collective-permute-start(bf16[3,96,2048]{2,1,0:T(8,128)(2,1)S(1)} %constant_dynamic-update-slice_fusion.38), channel_id=1, source_target_pairs={{0,2},{1,3},{2,0},{3,1},{4,6},{5,7},{6,4},{7,5},{8,10},{9,11},{10,... | collective-permute-start | bytes 3538952 | tf_op jit(solution)/shard_map/ppermute | solution.py:104
  139.1 24.5 %collective-permute-start.16 = (bf16[96,2048]{1,0:T(8,128)(2,1)S(1)}, bf16[96,2048]{1,0:T(8,128)(2,1)S(1)}, u32[]{:S(2)}, u32[]{:S(2)}) collective-permute-start(bf16[96,2048]{1,0:T(8,128)(2,1)S(1)} %constant_dynamic-slice_fusion.36), channel_id=1, source_target_pairs={{0,2},{1,3},{2,0},{3,1},{4,6},{5,7},{6,4},{7,5},{8,10},{9,11},{10,... | collective-permute-start | bytes 1179656 | tf_op jit(solution)/shard_map/ppermute | solution.py:104
  158.3 108.8 %collective-permute-start.26 = (bf16[3,192,2048]{2,1,0:T(8,128)(2,1)}, bf16[3,192,2048]{2,1,0:T(8,128)(2,1)}, u32[]{:S(2)}, u32[]{:S(2)}) collective-permute-start(bf16[3,192,2048]{2,1,0:T(8,128)(2,1)} %constant_dynamic-update-slice_fusion.36), channel_id=1, source_target_pairs={{0,1},{1,0},{2,3},{3,2},{4,5},{5,4},{6,7},{7,6},{8,9},{9,8},{10,11... | collective-permute-start | bytes 7077896 | tf_op jit(solution)/shard_map/ppermute | solution.py:104
  178.2 18.5 %collective-permute-start.18 = (f32[48,16]{0,1:T(8,128)}, f32[48,16]{0,1:T(8,128)}, u32[]{:S(2)}, u32[]{:S(2)}) collective-permute-start(f32[48,16]{0,1:T(8,128)} %fusion.123), channel_id=1, source_target_pairs={{0,4},{1,5},{2,6},{3,7},{4,0},{5,1},{6,2},{7,3},{8,12},{9,13},{10,... | collective-permute-start | bytes 9224 | tf_op jit(solution)/shard_map/ppermute | solution.py:104
  186.8 45.9 %collective-permute-start.27 = (bf16[48,2048]{1,0:T(8,128)(2,1)}, bf16[48,2048]{1,0:T(8,128)(2,1)}, u32[]{:S(2)}, u32[]{:S(2)}) collective-permute-start(bf16[48,2048]{1,0:T(8,128)(2,1)} %get-tuple-element.113), channel_id=1, source_target_pairs={{0,4},{1,5},{2,6},{3,7},{4,0},{5,1},{6,2},{7,3},{8,12},{9,13},{10,... | collective-permute-start | bytes 589832 | tf_op jit(solution)/shard_map/ppermute | solution.py:104
  195.2 42.6 %collective-permute-start.33 = (bf16[48,2048]{1,0:T(8,128)(2,1)}, bf16[48,2048]{1,0:T(8,128)(2,1)}, u32[]{:S(2)}, u32[]{:S(2)}) collective-permute-start(bf16[48,2048]{1,0:T(8,128)(2,1)} %get-tuple-element.211), channel_id=1, source_target_pairs={{0,4},{1,5},{2,6},{3,7},{4,0},{5,1},{6,2},{7,3},{8,12},{9,13},{10,... | collective-permute-start | bytes 589832 | tf_op jit(solution)/shard_map/ppermute | solution.py:104
  228.5 45.3 %collective-permute-start.60 = (bf16[3,384,512]{2,1,0:T(8,128)(2,1)S(1)}, bf16[3,384,512]{2,1,0:T(8,128)(2,1)S(1)}, u32[]{:S(2)}, u32[]{:S(2)}) collective-permute-start(bf16[3,384,512]{2,1,0:T(8,128)(2,1)S(1)} %pad_maximum_fusion.6), channel_id=1, source_target_pairs={{0,8},{8,0},{16,24},{24,16},{1,9},{9,1},{17,25},{25,17},{2,10},{10... | collective-permute-start | bytes 3538952 | tf_op jit(solution)/shard_map/ppermute | solution.py:104
  230.3 43.6 %collective-permute-start.61 = (bf16[3,384,512]{2,1,0:T(8,128)(2,1)S(1)}, bf16[3,384,512]{2,1,0:T(8,128)(2,1)S(1)}, u32[]{:S(2)}, u32[]{:S(2)}) collective-permute-start(bf16[3,384,512]{2,1,0:T(8,128)(2,1)S(1)} %pad_maximum_fusion.7), channel_id=1, source_target_pairs={{0,16},{8,24},{16,0},{24,8},{1,17},{9,25},{17,1},{25,9},{2,18},{10... | collective-permute-start | bytes 3538952 | tf_op jit(solution)/shard_map/ppermute | solution.py:104
  237.7 20.3 %collective-permute-start.28 = (bf16[96,2048]{1,0:T(8,128)(2,1)}, bf16[96,2048]{1,0:T(8,128)(2,1)S(1)}, u32[]{:S(2)}, u32[]{:S(2)}) collective-permute-start(bf16[96,2048]{1,0:T(8,128)(2,1)} %constant_dynamic-update-slice_fusion.32), channel_id=1, source_target_pairs={{0,2},{1,3},{2,0},{3,1},{4,6},{5,7},{6,4},{7,5},{8,10},{9,11},{10,... | collective-permute-start | bytes 1179656 | tf_op jit(solution)/shard_map/ppermute | solution.py:104
  258.0 27.3 %collective-permute-start.62 = (bf16[3,384,512]{2,1,0:T(8,128)(2,1)S(1)}, bf16[3,384,512]{2,1,0:T(8,128)(2,1)S(1)}, u32[]{:S(2)}, u32[]{:S(2)}) collective-permute-start(bf16[3,384,512]{2,1,0:T(8,128)(2,1)S(1)} %pad_maximum_fusion.8), channel_id=1, source_target_pairs={{0,24},{8,16},{16,8},{24,0},{1,25},{9,17},{17,9},{25,1},{2,26},{10... | collective-permute-start | bytes 3538952 | tf_op jit(solution)/shard_map/ppermute | solution.py:104
  263.1 81.6 %collective-permute-start.29 = (bf16[192,2048]{1,0:T(8,128)(2,1)}, bf16[192,2048]{1,0:T(8,128)(2,1)}, u32[]{:S(2)}, u32[]{:S(2)}) collective-permute-start(bf16[192,2048]{1,0:T(8,128)(2,1)} %constant_dynamic-update-slice_fusion.30), channel_id=1, source_target_pairs={{0,1},{1,0},{2,3},{3,2},{4,5},{5,4},{6,7},{7,6},{8,9},{9,8},{10,11... | collective-permute-start | bytes 2359304 | tf_op jit(solution)/shard_map/ppermute | solution.py:104
  267.1 28.8 %collective-permute-start.35 = (bf16[192,2048]{1,0:T(8,128)(2,1)S(1)}, bf16[192,2048]{1,0:T(8,128)(2,1)S(1)}, u32[]{:S(2)}, u32[]{:S(2)}) collective-permute-start(bf16[192,2048]{1,0:T(8,128)(2,1)S(1)} %constant_dynamic-update-slice_fusion.21), channel_id=1, source_target_pairs={{0,1},{1,0},{2,3},{3,2},{4,5},{5,4},{6,7},{7,6},{8,9},{9,8},{10,11... | collective-permute-start | bytes 2359304 | tf_op jit(solution)/shard_map/ppermute | solution.py:104
  346.6 28.4 %collective-permute-start.30 = (bf16[384,512]{1,0:T(8,128)(2,1)S(1)}, bf16[384,512]{1,0:T(8,128)(2,1)S(1)}, u32[]{:S(2)}, u32[]{:S(2)}) collective-permute-start(bf16[384,512]{1,0:T(8,128)(2,1)S(1)} %get-tuple-element.133), channel_id=1, source_target_pairs={{0,8},{8,0},{16,24},{24,16},{1,9},{9,1},{17,25},{25,17},{2,10},{10... | collective-permute-start | bytes 1179656 | tf_op jit(solution)/shard_map/ppermute | solution.py:104
  346.7 29.9 %collective-permute-start.31 = (bf16[384,512]{1,0:T(8,128)(2,1)S(1)}, bf16[384,512]{1,0:T(8,128)(2,1)S(1)}, u32[]{:S(2)}, u32[]{:S(2)}) collective-permute-start(bf16[384,512]{1,0:T(8,128)(2,1)S(1)} %get-tuple-element.132), channel_id=1, source_target_pairs={{0,16},{8,24},{16,0},{24,8},{1,17},{9,25},{17,1},{25,9},{2,18},{10... | collective-permute-start | bytes 1179656 | tf_op jit(solution)/shard_map/ppermute | solution.py:104
  348.3 29.0 %collective-permute-start.32 = (bf16[384,512]{1,0:T(8,128)(2,1)S(1)}, bf16[384,512]{1,0:T(8,128)(2,1)S(1)}, u32[]{:S(2)}, u32[]{:S(2)}) collective-permute-start(bf16[384,512]{1,0:T(8,128)(2,1)S(1)} %get-tuple-element.131), channel_id=1, source_target_pairs={{0,24},{8,16},{16,8},{24,0},{1,25},{9,17},{17,9},{25,1},{2,26},{10... | collective-permute-start | bytes 1179656 | tf_op jit(solution)/shard_map/ppermute | solution.py:104
  372.0 37.3 %collective-permute-start.42 = (bf16[192,2048]{1,0:T(8,128)(2,1)}, bf16[192,2048]{1,0:T(8,128)(2,1)}, u32[]{:S(2)}, u32[]{:S(2)}) collective-permute-start(bf16[192,2048]{1,0:T(8,128)(2,1)} %constant_dynamic-slice_fusion.14), channel_id=1, source_target_pairs={{0,1},{1,0},{2,3},{3,2},{4,5},{5,4},{6,7},{7,6},{8,9},{9,8},{10,11... | collective-permute-start | bytes 2359304 | tf_op jit(solution)/shard_map/ppermute | solution.py:104
  376.6 35.0 %collective-permute-start.36 = (bf16[192,2048]{1,0:T(8,128)(2,1)}, bf16[192,2048]{1,0:T(8,128)(2,1)}, u32[]{:S(2)}, u32[]{:S(2)}) collective-permute-start(bf16[192,2048]{1,0:T(8,128)(2,1)} %constant_dynamic-slice_fusion.18), channel_id=1, source_target_pairs={{0,1},{1,0},{2,3},{3,2},{4,5},{5,4},{6,7},{7,6},{8,9},{9,8},{10,11... | collective-permute-start | bytes 2359304 | tf_op jit(solution)/shard_map/ppermute | solution.py:104
  377.3 49.2 %collective-permute-start.54 = (bf16[192,2048]{1,0:T(8,128)(2,1)}, bf16[192,2048]{1,0:T(8,128)(2,1)}, u32[]{:S(2)}, u32[]{:S(2)}) collective-permute-start(bf16[192,2048]{1,0:T(8,128)(2,1)} %constant_dynamic-slice_fusion.8), channel_id=1, source_target_pairs={{0,1},{1,0},{2,3},{3,2},{4,5},{5,4},{6,7},{7,6},{8,9},{9,8},{10,11... | collective-permute-start | bytes 2359304 | tf_op jit(solution)/shard_map/ppermute | solution.py:104
  404.0 38.6 %collective-permute-start.48 = (bf16[192,2048]{1,0:T(8,128)(2,1)}, bf16[192,2048]{1,0:T(8,128)(2,1)}, u32[]{:S(2)}, u32[]{:S(2)}) collective-permute-start(bf16[192,2048]{1,0:T(8,128)(2,1)} %constant_dynamic-slice_fusion.11), channel_id=1, source_target_pairs={{0,1},{1,0},{2,3},{3,2},{4,5},{5,4},{6,7},{7,6},{8,9},{9,8},{10,11... | collective-permute-start | bytes 2359304 | tf_op jit(solution)/shard_map/ppermute | solution.py:104
  405.8 40.5 %collective-permute-start.88 = (bf16[512,1024]{1,0:T(8,128)(2,1)}, bf16[512,1024]{1,0:T(8,128)(2,1)}, u32[]{:S(2)}, u32[]{:S(2)}) collective-permute-start(bf16[512,1024]{1,0:T(8,128)(2,1)} %convolution_convert_fusion.2), channel_id=1, source_target_pairs={{0,8},{8,0},{16,24},{24,16},{1,9},{9,1},{17,25},{25,17},{2,10},{10... | collective-permute-start | bytes 3145736 | tf_op jit(solution)/shard_map/ppermute | solution.py:104
  409.3 211.7 %collective-permute-start.87 = (bf16[512,1024]{1,0:T(8,128)(2,1)}, bf16[512,1024]{1,0:T(8,128)(2,1)}, u32[]{:S(2)}, u32[]{:S(2)}) collective-permute-start(bf16[512,1024]{1,0:T(8,128)(2,1)} %convolution_convert_fusion.3), channel_id=1, source_target_pairs={{0,8},{8,0},{16,24},{24,16},{1,9},{9,1},{17,25},{25,17},{2,10},{10... | collective-permute-start | bytes 3145736 | tf_op jit(solution)/shard_map/ppermute | solution.py:104
  411.6 37.8 %collective-permute-start.91 = (bf16[1024,512]{1,0:T(8,128)(2,1)}, bf16[1024,512]{1,0:T(8,128)(2,1)S(1)}, u32[]{:S(2)}, u32[]{:S(2)}) collective-permute-start(bf16[1024,512]{1,0:T(8,128)(2,1)} %convolution_convert_fusion), channel_id=1, source_target_pairs={{0,8},{8,0},{16,24},{24,16},{1,9},{9,1},{17,25},{25,17},{2,10},{10... | collective-permute-start | bytes 3145736 | tf_op jit(solution)/shard_map/ppermute | solution.py:104
  426.5 201.5 %collective-permute-start.90 = (bf16[1024,512]{1,0:T(8,128)(2,1)}, bf16[1024,512]{1,0:T(8,128)(2,1)}, u32[]{:S(2)}, u32[]{:S(2)}) collective-permute-start(bf16[1024,512]{1,0:T(8,128)(2,1)} %convolution_convert_fusion.1), channel_id=1, source_target_pairs={{0,8},{8,0},{16,24},{24,16},{1,9},{9,1},{17,25},{25,17},{2,10},{10... | collective-permute-start | bytes 3145736 | tf_op jit(solution)/shard_map/ppermute | solution.py:104
  446.3 17.0 %collective-permute-start.37 = (bf16[96,2048]{1,0:T(8,128)(2,1)S(1)}, bf16[96,2048]{1,0:T(8,128)(2,1)S(1)}, u32[]{:S(2)}, u32[]{:S(2)}) collective-permute-start(bf16[96,2048]{1,0:T(8,128)(2,1)S(1)} %constant_dynamic-slice_fusion.17), channel_id=1, source_target_pairs={{0,2},{1,3},{2,0},{3,1},{4,6},{5,7},{6,4},{7,5},{8,10},{9,11},{10,... | collective-permute-start | bytes 1179656 | tf_op jit(solution)/shard_map/ppermute | solution.py:104
  449.4 22.3 %collective-permute-start.55 = (bf16[96,2048]{1,0:T(8,128)(2,1)S(1)}, bf16[96,2048]{1,0:T(8,128)(2,1)S(1)}, u32[]{:S(2)}, u32[]{:S(2)}) collective-permute-start(bf16[96,2048]{1,0:T(8,128)(2,1)S(1)} %constant_dynamic-slice_fusion.7), channel_id=1, source_target_pairs={{0,2},{1,3},{2,0},{3,1},{4,6},{5,7},{6,4},{7,5},{8,10},{9,11},{10,... | collective-permute-start | bytes 1179656 | tf_op jit(solution)/shard_map/ppermute | solution.py:104
  454.8 28.1 %collective-permute-start.49 = (bf16[96,2048]{1,0:T(8,128)(2,1)S(1)}, bf16[96,2048]{1,0:T(8,128)(2,1)S(1)}, u32[]{:S(2)}, u32[]{:S(2)}) collective-permute-start(bf16[96,2048]{1,0:T(8,128)(2,1)S(1)} %constant_dynamic-slice_fusion.10), channel_id=1, source_target_pairs={{0,2},{1,3},{2,0},{3,1},{4,6},{5,7},{6,4},{7,5},{8,10},{9,11},{10,... | collective-permute-start | bytes 1179656 | tf_op jit(solution)/shard_map/ppermute | solution.py:104
  463.3 158.4 %collective-permute-start.89 = (bf16[512,1024]{1,0:T(8,128)(2,1)}, bf16[512,1024]{1,0:T(8,128)(2,1)}, u32[]{:S(2)}, u32[]{:S(2)}) collective-permute-start(bf16[512,1024]{1,0:T(8,128)(2,1)} %add_convert_fusion.6), channel_id=1, source_target_pairs={{0,16},{8,24},{16,0},{24,8},{1,17},{9,25},{17,1},{25,9},{2,18},{10... | collective-permute-start | bytes 3145736 | tf_op jit(solution)/shard_map/ppermute | solution.py:104
  484.8 22.4 %collective-permute-start.56 = (bf16[48,2048]{1,0:T(8,128)(2,1)S(1)}, bf16[48,2048]{1,0:T(8,128)(2,1)S(1)}, u32[]{:S(2)}, u32[]{:S(2)}) collective-permute-start(bf16[48,2048]{1,0:T(8,128)(2,1)S(1)} %constant_dynamic-slice_fusion.6), channel_id=1, source_target_pairs={{0,4},{1,5},{2,6},{3,7},{4,0},{5,1},{6,2},{7,3},{8,12},{9,13},{10,... | collective-permute-start | bytes 589832 | tf_op jit(solution)/shard_map/ppermute | solution.py:104
  527.5 18.9 %collective-permute-start.57 = (bf16[48,2048]{1,0:T(8,128)(2,1)}, bf16[48,2048]{1,0:T(8,128)(2,1)}, u32[]{:S(2)}, u32[]{:S(2)}) collective-permute-start(bf16[48,2048]{1,0:T(8,128)(2,1)} %get-tuple-element.105), channel_id=1, source_target_pairs={{0,4},{1,5},{2,6},{3,7},{4,0},{5,1},{6,2},{7,3},{8,12},{9,13},{10,... | collective-permute-start | bytes 589832 | tf_op jit(solution)/shard_map/ppermute | solution.py:104
  542.5 86.2 %collective-permute-start.92 = (bf16[1024,512]{1,0:T(8,128)(2,1)}, bf16[1024,512]{1,0:T(8,128)(2,1)S(1)}, u32[]{:S(2)}, u32[]{:S(2)}) collective-permute-start(bf16[1024,512]{1,0:T(8,128)(2,1)} %add_convert_fusion.5), channel_id=1, source_target_pairs={{0,16},{8,24},{16,0},{24,8},{1,17},{9,25},{17,1},{25,9},{2,18},{10... | collective-permute-start | bytes 3145736 | tf_op jit(solution)/shard_map/ppermute | solution.py:104
  618.7 92.9 %collective-permute-start.59 = (bf16[192,2048]{1,0:T(8,128)(2,1)}, bf16[192,2048]{1,0:T(8,128)(2,1)}, u32[]{:S(2)}, u32[]{:S(2)}) collective-permute-start(bf16[192,2048]{1,0:T(8,128)(2,1)} %constant_dynamic-update-slice_fusion.3), channel_id=1, source_target_pairs={{0,1},{1,0},{2,3},{3,2},{4,5},{5,4},{6,7},{7,6},{8,9},{9,8},{10,11... | collective-permute-start | bytes 2359304 | tf_op jit(solution)/shard_map/ppermute | solution.py:104
  621.0 92.5 %collective-permute-start.53 = (bf16[192,2048]{1,0:T(8,128)(2,1)}, bf16[192,2048]{1,0:T(8,128)(2,1)}, u32[]{:S(2)}, u32[]{:S(2)}) collective-permute-start(bf16[192,2048]{1,0:T(8,128)(2,1)} %constant_dynamic-update-slice_fusion.7), channel_id=1, source_target_pairs={{0,1},{1,0},{2,3},{3,2},{4,5},{5,4},{6,7},{7,6},{8,9},{9,8},{10,11... | collective-permute-start | bytes 2359304 | tf_op jit(solution)/shard_map/ppermute | solution.py:104
  621.6 93.2 %collective-permute-start.47 = (bf16[192,2048]{1,0:T(8,128)(2,1)}, bf16[192,2048]{1,0:T(8,128)(2,1)}, u32[]{:S(2)}, u32[]{:S(2)}) collective-permute-start(bf16[192,2048]{1,0:T(8,128)(2,1)} %constant_dynamic-update-slice_fusion.11), channel_id=1, source_target_pairs={{0,1},{1,0},{2,3},{3,2},{4,5},{5,4},{6,7},{7,6},{8,9},{9,8},{10,11... | collective-permute-start | bytes 2359304 | tf_op jit(solution)/shard_map/ppermute | solution.py:104
  628.0 88.1 %collective-permute-start.41 = (bf16[192,2048]{1,0:T(8,128)(2,1)}, bf16[192,2048]{1,0:T(8,128)(2,1)}, u32[]{:S(2)}, u32[]{:S(2)}) collective-permute-start(bf16[192,2048]{1,0:T(8,128)(2,1)} %copy-done.50), channel_id=1, source_target_pairs={{0,1},{1,0},{2,3},{3,2},{4,5},{5,4},{6,7},{7,6},{8,9},{9,8},{10,11... | collective-permute-start | bytes 2359304 | tf_op jit(solution)/shard_map/ppermute | solution.py:104
  639.7 39.6 %collective-permute-start.95 = (f32[1,1]{1,0:T(1,128)}, f32[1,1]{1,0:T(1,128)}, u32[]{:S(2)}, u32[]{:S(2)}) collective-permute-start(f32[1,1]{1,0:T(1,128)} %add.792), channel_id=1, source_target_pairs={{0,1},{1,0},{2,3},{3,2},{4,5},{5,4},{6,7},{7,6},{8,9},{9,8},{10,11... | collective-permute-start | bytes 20 | tf_op jit(solution)/shard_map/ppermute | solution.py:104
  (238 other events, 2202.9 us)

commit v2 on v0

v2 whole, which is shorter than its diff:
```python
import functools
import math

import jax
import jax.numpy as jnp
from jax import lax
from jax.experimental import pallas as pl
from jax.experimental.pallas import tpu as pltpu
from jax.sharding import PartitionSpec as P

D = 2048
HDIM = 128
FF = 8192
MIXH = 36
ROT = 32
STEP = 10


norm_epsilon = 1e-05
mixer_epsilon = 1e-06
clip_level = 1.0
beta_first = 0.9
beta_second = 0.95
adam_epsilon = 1e-08
weight_decay = 0.1


def exact_gelu(values):
    return jax.nn.gelu(values, approximate=False)


def gelu_grad(values, upstream):
    unused, pullback = jax.vjp(exact_gelu, values)
    return pullback(upstream)[0]


def rotate(vectors, cosine, sine_table):
    half = ROT // 2
    first_half = vectors[..., :half]
    second_half = vectors[..., half:ROT]
    return jnp.concatenate(
        [
            first_half * cosine - second_half * sine_table,
            second_half * cosine + first_half * sine_table,
            vectors[..., ROT:],
        ],
        axis=-1,
    )


def angles(bucket_ids):
    same_seq = bucket_ids[:, None] == bucket_ids[None, :]
    order = jnp.arange(bucket_ids.shape[0])
    earlier = order[None, :] < order[:, None]
    position = jnp.sum(jnp.where(same_seq & earlier, 1, 0), axis=1).astype(jnp.float32)
    freqs = 10000.0 ** (-2.0 * jnp.arange(ROT // 2).astype(jnp.float32) / ROT)
    angle = position[:, None] * freqs[None, :]
    allowed = same_seq & (order[None, :] <= order[:, None])
    return (jnp.cos(angle), jnp.sin(angle), allowed)


def score_block(query, key_rows, allowed):
    head_scale = HDIM ** (-0.5)
    scores = (
        jnp.einsum("hqd,hkd->hqk", query, key_rows, preferred_element_type=jnp.float32) * head_scale
    )
    return jnp.where(allowed[None], scores, -1e30)


def norm_back(grad_rows, unit_rows, inverse_rows, gain_rows):
    scaled = grad_rows * gain_rows
    mean_scaled = jnp.mean(scaled, axis=-1, keepdims=True)
    mean_cross = jnp.mean(scaled * unit_rows, axis=-1, keepdims=True)
    return inverse_rows * (scaled - mean_scaled - unit_rows * mean_cross)


def contract_rows(left, right):
    return lax.dot_general(
        left, right, (((0,), (0,)), ((), ())), preferred_element_type=jnp.float32
    )


def contract_cols(left, right):
    return lax.dot_general(
        left, right, (((1,), (1,)), ((), ())), preferred_element_type=jnp.float32
    )


def adam_step(master, first_moment, second_moment, gradient, factor, step_rate, decay_rate):
    scaled = gradient * factor
    first_new = beta_first * first_moment + (1.0 - beta_first) * scaled
    second_new = beta_second * second_moment + (1.0 - beta_second) * scaled * scaled
    first_hat = first_new / (1.0 - beta_first**STEP)
    second_hat = second_new / (1.0 - beta_second**STEP)
    master_new = master - step_rate * (
        first_hat / (jnp.sqrt(second_hat) + adam_epsilon) + decay_rate * master
    )
    return (master_new, first_new, second_new)


def gelu_parts(values):
    upper_share = 0.5 * (1.0 + lax.erf(values * math.sqrt(0.5)))
    density = jnp.exp(-0.5 * values * values) * (1.0 / math.sqrt(2.0 * math.pi))
    return upper_share, density


def bits_of(size):
    return [1 << index for index in range(size.bit_length() - 1)]


def feature_order(owners):
    order = [0]
    for bit in reversed(bits_of(owners)):
        order = order + [index | bit for index in order]
    return order


def swap(values, axis, mask):
    size = lax.axis_size(axis)
    return lax.ppermute(values, axis, [(source, source ^ mask) for source in range(size)])


def sync(plain, steps):
    held = [vars(item) for item in steps]
    names = [
        [name for name in ("values", "terms", "given") if item.get(name) is not None]
        for item in held
    ]
    plain, inner = lax.optimization_barrier(
        (
            list(plain),
            [[item[name] for name in kinds] for item, kinds in zip(held, names)],
        )
    )
    for item, kinds, values in zip(steps, names, inner):
        for name, value in zip(kinds, values):
            setattr(item, name, value)
    return plain


def gather_half(piece, axis, dim):
    for bit in reversed(bits_of(lax.axis_size(axis))[1:]):
        piece = jnp.concatenate([piece, swap(piece, axis, bit)], axis=dim)
    return piece


def halve(values, dim):
    half = values.shape[dim] // 2
    return (
        lax.slice_in_dim(values, 0, half, axis=dim),
        lax.slice_in_dim(values, half, 2 * half, axis=dim),
    )


class Reduce:
    def __init__(self, kept, given, axis, dim):
        self.terms, self.given, self.axis, self.dim = [kept], given, axis, dim

    def near(self):
        self.terms.append(swap(self.given, self.axis, 1))
        self.given = None

    def prepare(self):
        half = self.terms[-1].shape[self.dim] // 2
        self.given = sum(
            lax.slice_in_dim(term, half, 2 * half, axis=self.dim).astype(jnp.float32)
            for term in self.terms
        ).astype(jnp.bfloat16)

    def far(self):
        for bit in bits_of(lax.axis_size(self.axis))[1:]:
            if self.given is None:
                self.prepare()
            self.terms.append(swap(self.given, self.axis, bit))
            self.given = None

    def squares(self):
        own = self.terms[-1].shape[self.dim]
        return square_sum(
            sum(
                lax.slice_in_dim(term, 0, own, axis=self.dim).astype(jnp.float32)
                for term in self.terms
            )
        )


class Halves:
    def __init__(self, values, axis):
        self.values, self.axis = values, axis

    def hop(self, bit):
        kept, given = halve(self.values, 1)
        self.values = kept + swap(given, self.axis, bit)

    def near(self):
        self.hop(1)

    def far(self):
        for bit in bits_of(lax.axis_size(self.axis))[1:]:
            self.hop(bit)

    def rows(self, axis, bits):
        for bit in bits:
            self.values = self.values + swap(self.values, axis, bit)


def step_both(scatter, stage, gather, gather_stage):
    for bit in scatter.order[stage]:
        kept, given = scatter.split(bit)
        both = jnp.stack([given, gather.values])
        moved = swap(both, scatter.axis, bit)
        scatter.add(kept, moved[0])
        gather.values = gather.join(moved[1], bit)


def square_sum(values):
    return jnp.sum(values * values)


def share_index(axis):
    here = lax.axis_index(axis)
    place = 0
    for bit in bits_of(lax.axis_size(axis)):
        place = place * 2 + (here & bit) // bit
    return place


def unfold_rows(values, axis, dim):
    count = len(bits_of(lax.axis_size(axis)))
    shape = values.shape
    return values.reshape(
        shape[:dim] + (2,) * count + (shape[dim] >> count,) + shape[dim + 1 :]
    )


def fold_rows(values, axis, dim):
    count = len(bits_of(lax.axis_size(axis)))
    shape = values.shape
    return values.reshape(shape[:dim] + (-1,) + shape[dim + count + 1 :])


class Scatter:
    def __init__(self, values, axis, order):
        self.values, self.axis, self.order = unfold_rows(values, axis, 0), axis, list(order)
        self.places = bits_of(lax.axis_size(axis))

    def split(self, bit):
        dim = self.places.index(bit)
        self.places = [place for place in self.places if place != bit]
        side = (lax.axis_index(self.axis) & bit) // bit
        return (
            lax.dynamic_index_in_dim(self.values, side, dim, False),
            lax.dynamic_index_in_dim(self.values, 1 - side, dim, False),
        )

    def add(self, kept, moved):
        values = kept.astype(jnp.float32) + moved.astype(jnp.float32)
        self.values = values.astype(jnp.bfloat16) if self.places else values

    def step(self, stage):
        for bit in self.order[stage]:
            kept, given = self.split(bit)
            self.add(kept, swap(given, self.axis, bit))


class Gather:
    def __init__(self, values, axis, order, dim=0):
        self.values, self.axis, self.order, self.dim = values, axis, list(order), dim
        self.places = []

    def step(self, stage):
        for bit in self.order[stage]:
            moved = swap(self.values, self.axis, bit)
            self.values = self.join(moved, bit)

    def join(self, moved, bit):
        known = self.places + [bit]
        self.places = [place for place in bits_of(lax.axis_size(self.axis)) if place in known]
        dim = self.dim + self.places.index(bit)
        side = (lax.axis_index(self.axis) & bit) // bit
        shape = list(moved.shape)
        shape.insert(dim, 2)
        return jnp.where(
            lax.broadcasted_iota(jnp.int32, shape, dim) == side,
            jnp.expand_dims(self.values, dim),
            jnp.expand_dims(moved, dim),
        )

    def result(self):
        return fold_rows(self.values, self.axis, self.dim)


def stages_of(axis):
    bits = bits_of(lax.axis_size(axis))
    near = len(bits) - 2
    return bits[:near], bits[near : near + 1], bits[near + 1 :]


def adam_kernel(rates, count, flip, factor_ref, *refs):
    term_refs, (master_ref, first_ref, second_ref) = refs[:count], refs[count : count + 3]
    new_ref, first_new_ref, second_new_ref, copy_ref = refs[count + 3 :]
    gradient = sum(term_ref[...].astype(jnp.float32) for term_ref in term_refs)
    if flip:
        gradient = gradient[0].T
    master_new, first_new, second_new = adam_step(
        master_ref[...], first_ref[...], second_ref[...], gradient, factor_ref[0], *rates
    )
    new_ref[...] = master_new
    first_new_ref[...] = first_new
    second_new_ref[...] = second_new
    copy_ref[...] = master_new.astype(jnp.bfloat16)


def adam_call(terms, master, first_moment, second_moment, factor, rates, grid, block, spot):
    flip = spot is not None
    own = pl.BlockSpec(block, lambda *steps: steps[: len(grid)])
    if flip:
        term_specs = [
            pl.BlockSpec((1,) + master.shape[::-1], lambda *steps: (spot, 0, 0)) for term in terms
        ]
    else:
        term_specs = [own] * len(terms)
    wide = jax.ShapeDtypeStruct(master.shape, jnp.float32)
    return pl.pallas_call(
        functools.partial(adam_kernel, rates, len(terms), flip),
        grid=grid,
        in_specs=[pl.BlockSpec(memory_space=pltpu.SMEM)] + term_specs + [own] * 3,
        out_specs=[own] * 4,
        out_shape=[wide, wide, wide, jax.ShapeDtypeStruct(master.shape, jnp.bfloat16)],
        compiler_params=pltpu.CompilerParams(vmem_limit_bytes=60 << 20),
        cost_estimate=pl.CostEstimate(
            flops=20 * master.size, bytes_accessed=32 * master.size, transcendentals=0
        ),
    )(factor.reshape(1), *terms, master, first_moment, second_moment)


def lane_block(place_ref, index, cols):
    return pl.ds(pl.multiple_of(place_ref[index] * cols, cols), cols)


def norm_kernel(owners, place_ref, inputs_ref, gains_ref, biases_ref, kept_ref, given_ref):
    cols = inputs_ref.shape[2] // owners
    values = inputs_ref[0].astype(jnp.float32)
    mean_vals = jnp.mean(values, axis=-1, keepdims=True)
    centred = values - mean_vals
    inverse = lax.rsqrt(jnp.mean(centred * centred, axis=-1, keepdims=True) + norm_epsilon)
    for index in range(owners):
        block = inputs_ref[0, :, lane_block(place_ref, index, cols)].astype(jnp.float32)
        spot = slice(index * cols, (index + 1) * cols)
        normed = (block - mean_vals) * inverse * gains_ref[0, :, spot] + biases_ref[0, :, spot]
        target = kept_ref if index < owners // 2 else given_ref
        near = index % (owners // 2)
        target[0, :, near * cols : (near + 1) * cols] = normed.astype(jnp.bfloat16)


def norm_forward(layer_inputs, gains, biases, place, owners):
    count, tokens, width = layer_inputs.shape
    tile = 128
    half = pl.BlockSpec((1, tile, width // 2), lambda c, i, place_ref: (c, i, 0))
    row = pl.BlockSpec((1, 1, width), lambda c, i, place_ref: (c, 0, 0))
    shape = jax.ShapeDtypeStruct((count, tokens, width // 2), jnp.bfloat16)
    return pl.pallas_call(
        functools.partial(norm_kernel, owners),
        grid_spec=pltpu.PrefetchScalarGridSpec(
            num_scalar_prefetch=1,
            grid=(count, tokens // tile),
            in_specs=[
                pl.BlockSpec((1, tile, width), lambda c, i, place_ref: (c, i, 0)),
                row,
                row,
            ],
            out_specs=[half, half],
        ),
        out_shape=[shape, shape],
        compiler_params=pltpu.CompilerParams(vmem_limit_bytes=56 << 20),
        cost_estimate=pl.CostEstimate(
            flops=10 * count * tokens * width,
            bytes_accessed=4 * count * tokens * width,
            transcendentals=0,
        ),
    )(place, layer_inputs, gains[:, None, :], biases[:, None, :])


def turn(values, cosine, sine_low, sine_high):
    width = values.shape[-1]
    return (
        values * cosine
        + pltpu.roll(values, width - ROT // 2, 1) * sine_low
        + pltpu.roll(values, ROT // 2, 1) * sine_high
    )


def masked_probs(query, key_rows, ids_col, ids_row):
    tokens = query.shape[0]
    scores = lax.dot_general(
        query, key_rows, (((1,), (1,)), ((), ())), preferred_element_type=jnp.float32
    ) * (HDIM ** (-0.5))
    here = lax.broadcasted_iota(jnp.int32, (tokens, tokens), 0)
    there = lax.broadcasted_iota(jnp.int32, (tokens, tokens), 1)
    scores = jnp.where((ids_col == ids_row) & (there <= here), scores, -1e30)
    row_max = jnp.max(scores, axis=-1, keepdims=True)
    log_total = jnp.log(jnp.sum(jnp.exp(scores - row_max), axis=-1, keepdims=True)) + row_max
    return jnp.exp(scores - log_total)


def attend_kernel(proj_ref, cos_ref, low_ref, high_ref, col_ref, row_ref, turned_ref, heads_ref):
    tables = (cos_ref[...], low_ref[...], high_ref[...])
    query = turn(proj_ref[0], *tables).astype(jnp.bfloat16)
    key_rows = turn(proj_ref[1], *tables).astype(jnp.bfloat16)
    value_rows = proj_ref[2].astype(jnp.bfloat16)
    turned_ref[0] = query
    turned_ref[1] = key_rows
    turned_ref[2] = value_rows
    prob = masked_probs(query, key_rows, col_ref[...], row_ref[...]).astype(jnp.bfloat16)
    heads_ref[...] = jnp.dot(prob, value_rows, preferred_element_type=jnp.float32).astype(
        jnp.bfloat16
    )


def attend_back_kernel(
    turned_ref, grads_ref, cos_ref, low_ref, high_ref, col_ref, row_ref, back_ref
):
    query, key_rows, value_rows = turned_ref[0], turned_ref[1], turned_ref[2]
    grads = grads_ref[...]
    prob = masked_probs(query, key_rows, col_ref[...], row_ref[...])
    grad_prob = contract_cols(grads, value_rows)
    row_delta = jnp.sum(prob * grad_prob, axis=-1, keepdims=True)
    grad_scores = (prob * (grad_prob - row_delta)).astype(jnp.bfloat16)
    tables = (cos_ref[...], -low_ref[...], -high_ref[...])
    head_scale = HDIM ** (-0.5)
    grad_query = jnp.dot(grad_scores, key_rows, preferred_element_type=jnp.float32) * head_scale
    grad_key = contract_rows(grad_scores, query) * head_scale
    back_ref[0] = turn(grad_query, *tables).astype(jnp.bfloat16)
    back_ref[1] = turn(grad_key, *tables).astype(jnp.bfloat16)
    back_ref[2] = contract_rows(prob.astype(jnp.bfloat16), grads).astype(jnp.bfloat16)


def attend_specs(tokens):
    table = pl.BlockSpec((tokens, HDIM), lambda head: (0, 0))
    heads = pl.BlockSpec((tokens, HDIM), lambda head: (0, head))
    triple = pl.BlockSpec((3, tokens, HDIM), lambda head: (0, 0, head))
    shared = [
        table,
        table,
        table,
        pl.BlockSpec((tokens, 1), lambda head: (0, 0)),
        pl.BlockSpec((1, tokens), lambda head: (0, 0)),
    ]
    return heads, triple, shared


def attend(proj, tables, ids):
    tokens, width = proj.shape[1:]
    heads, triple, shared = attend_specs(tokens)
    return pl.pallas_call(
        attend_kernel,
        grid=(width // HDIM,),
        in_specs=[triple] + shared,
        out_specs=[triple, heads],
        out_shape=[
            jax.ShapeDtypeStruct((3, tokens, width), jnp.bfloat16),
            jax.ShapeDtypeStruct((tokens, width), jnp.bfloat16),
        ],
        compiler_params=pltpu.CompilerParams(vmem_limit_bytes=32 << 20),
        cost_estimate=pl.CostEstimate(
            flops=4 * tokens * tokens * width,
            bytes_accessed=20 * tokens * width,
            transcendentals=2 * tokens * tokens,
        ),
    )(proj, *tables, ids[:, None], ids[None, :])


def attend_back(turned, grads, tables, ids):
    tokens, width = grads.shape
    heads, triple, shared = attend_specs(tokens)
    return pl.pallas_call(
        attend_back_kernel,
        grid=(width // HDIM,),
        in_specs=[triple, heads] + shared,
        out_specs=triple,
        out_shape=jax.ShapeDtypeStruct((3, tokens, width), jnp.bfloat16),
        compiler_params=pltpu.CompilerParams(vmem_limit_bytes=32 << 20),
        cost_estimate=pl.CostEstimate(
            flops=10 * tokens * tokens * width,
            bytes_accessed=14 * tokens * width,
            transcendentals=2 * tokens * tokens,
        ),
    )(turned, grads, *tables, ids[:, None], ids[None, :])


def mix_kernel(
    branch_ref,
    inputs_ref,
    stored_ref,
    entry_ref,
    cotangent_ref,
    valid_ref,
    gain_ref,
    mixer_in_ref,
    mixer_out_ref,
    newest_ref,
    grad_newest_ref,
    sent_kept_ref,
    sent_given_ref,
    mixer_in_grad_ref,
    mixer_out_grad_ref,
    gain_grad_ref,
):
    valid = valid_ref[...]
    gain = gain_ref[...]
    newest = inputs_ref[...].astype(jnp.float32) + valid * branch_ref[...]
    newest_ref[...] = newest.astype(jnp.bfloat16)
    rows, width = newest.shape
    scale = lax.rsqrt(jnp.mean(newest * newest, axis=-1, keepdims=True) + mixer_epsilon)
    normed = (newest * scale * gain).astype(jnp.bfloat16)
    mix_pre = contract_cols(normed, mixer_in_ref[...])
    phi, density = gelu_parts(mix_pre)
    mix_act = (mix_pre * phi).astype(jnp.bfloat16)
    weights = contract_cols(mix_act, mixer_out_ref[...])
    count = stored_ref.shape[0] + 1
    total = weights.shape[1]
    lane = lax.broadcasted_iota(jnp.int32, (rows, total), 1)
    grad_weights = jnp.zeros((rows, total), jnp.float32)
    newest_back = jnp.zeros((rows, width), jnp.float32)
    for outer in range(total // count):
        upstream = cotangent_ref[outer].astype(jnp.float32)
        for inner in range(count):
            layer = newest if inner == count - 1 else stored_ref[inner].astype(jnp.float32)
            dots = jnp.sum(upstream * layer, axis=-1, keepdims=True)
            grad_weights = jnp.where(lane == outer * count + inner, dots, grad_weights)
        last = outer * count + count - 1
        newest_back = newest_back + weights[:, last : last + 1] * upstream
    grad_weights = grad_weights.astype(jnp.bfloat16)
    mixer_out_grad_ref[...] = contract_rows(grad_weights, mix_act)
    grad_act = jnp.dot(grad_weights, mixer_out_ref[...], preferred_element_type=jnp.float32)
    grad_pre = ((phi + mix_pre * density) * grad_act).astype(jnp.bfloat16)
    mixer_in_grad_ref[...] = contract_rows(grad_pre, normed)
    grad_normed = jnp.dot(grad_pre, mixer_in_ref[...], preferred_element_type=jnp.float32)
    gain_grad_ref[...] = jnp.sum(grad_normed * newest * scale, axis=0, keepdims=True)
    scaled = grad_normed * gain
    grad_newest = (
        newest_back
        + entry_ref[...].astype(jnp.float32)
        + scale * scaled
        - newest * (scale * scale * scale) * jnp.mean(scaled * newest, axis=-1, keepdims=True)
    )
    grad_newest_ref[...] = grad_newest
    sent = (valid * grad_newest).astype(jnp.bfloat16)
    sent_kept_ref[...] = sent[:, 0 : width // 2]
    sent_given_ref[:, 0 : width // 2] = sent[:, width // 2 :]
    high = weights.astype(jnp.bfloat16)
    rest = (weights - high.astype(jnp.float32)).astype(jnp.bfloat16)
    blank = jnp.zeros((rows, 128 - 2 * total), jnp.bfloat16)
    sent_given_ref[:, width // 2 :] = jnp.concatenate([high, rest, blank], axis=1)


def mix(branch, inputs, stored, entry, cotangent, valid, gain, mixer_in, mixer_out):
    rows, width = branch.shape
    hidden_units = mixer_in.shape[0]
    total = mixer_out.shape[0]
    return pl.pallas_call(
        mix_kernel,
        out_shape=[
            jax.ShapeDtypeStruct((rows, width), jnp.bfloat16),
            jax.ShapeDtypeStruct((rows, width), jnp.float32),
            jax.ShapeDtypeStruct((rows, width // 2), jnp.bfloat16),
            jax.ShapeDtypeStruct((rows, width // 2 + 128), jnp.bfloat16),
            jax.ShapeDtypeStruct((hidden_units, width), jnp.float32),
            jax.ShapeDtypeStruct((total, hidden_units), jnp.float32),
            jax.ShapeDtypeStruct((1, width), jnp.float32),
        ],
        compiler_params=pltpu.CompilerParams(vmem_limit_bytes=32 << 20),
        cost_estimate=pl.CostEstimate(
            flops=60 * rows * width, bytes_accessed=30 * rows * width, transcendentals=0
        ),
    )(branch, inputs, stored, entry, cotangent, valid, gain, mixer_in, mixer_out)


def history_kernel(owners, count, place_ref, weights_ref, cotangent_ref, *back_refs):
    cols = back_refs[0].shape[2]
    weights = weights_ref[...]
    for index in range(owners):
        spot = lane_block(place_ref, index, cols)
        upstream = [
            cotangent_ref[outer, :, spot].astype(jnp.float32)
            for outer in range(cotangent_ref.shape[0])
        ]
        for layer in range(count - 1):
            back_refs[index][layer] = sum(
                weights[:, outer * count + layer : outer * count + layer + 1] * upstream[outer]
                for outer in range(len(upstream))
            ).astype(jnp.bfloat16)


def history_back(weights, cotangent, place, owners):
    outer, tokens, width = cotangent.shape
    total = weights.shape[1]
    count = total // outer
    tile = 128
    return pl.pallas_call(
        functools.partial(history_kernel, owners, count),
        grid_spec=pltpu.PrefetchScalarGridSpec(
            num_scalar_prefetch=1,
            grid=(tokens // tile,),
            in_specs=[
                pl.BlockSpec((tile, total), lambda i, place_ref: (i, 0)),
                pl.BlockSpec((outer, tile, width), lambda i, place_ref: (0, i, 0)),
            ],
            out_specs=[
                pl.BlockSpec((count - 1, tile, width // owners), lambda i, place_ref: (0, i, 0))
            ]
            * owners,
        ),
        out_shape=[
            jax.ShapeDtypeStruct((count - 1, tokens, width // owners), jnp.bfloat16)
        ]
        * owners,
        compiler_params=pltpu.CompilerParams(vmem_limit_bytes=56 << 20),
        cost_estimate=pl.CostEstimate(
            flops=8 * outer * tokens * width,
            bytes_accessed=14 * tokens * width,
            transcendentals=0,
        ),
    )(place, weights, cotangent)


def next_kernel(owners, place_ref, weights_ref, newest_ref, *refs):
    stored_refs, next_ref = refs[:-1], refs[-1]
    cols = newest_ref.shape[1] // owners
    weights = weights_ref[...]
    count = len(stored_refs) + 1
    for index in range(owners):
        spot = slice(index * cols, (index + 1) * cols)
        layers = [stored_ref[:, spot].astype(jnp.float32) for stored_ref in stored_refs]
        layers.append(newest_ref[:, spot].astype(jnp.float32))
        for outer in range(next_ref.shape[0]):
            next_ref[outer, :, lane_block(place_ref, index, cols)] = sum(
                weights[:, outer * count + layer : outer * count + layer + 1] * layers[layer]
                for layer in range(count)
            ).astype(jnp.bfloat16)


def next_layer(weights, stored, newest, place, owners):
    tokens, width = newest.shape
    total = weights.shape[1]
    count = len(stored) + 1
    outer = total // count
    tile = 128
    return pl.pallas_call(
        functools.partial(next_kernel, owners),
        grid_spec=pltpu.PrefetchScalarGridSpec(
            num_scalar_prefetch=1,
            grid=(tokens // tile,),
            in_specs=[
                pl.BlockSpec((tile, total), lambda i, place_ref: (i, 0)),
            ]
            + [pl.BlockSpec((tile, width), lambda i, place_ref: (i, 0))] * count,
            out_specs=pl.BlockSpec((outer, tile, width), lambda i, place_ref: (0, i, 0)),
        ),
        out_shape=jax.ShapeDtypeStruct((outer, tokens, width), jnp.bfloat16),
        compiler_params=pltpu.CompilerParams(vmem_limit_bytes=32 << 20),
        cost_estimate=pl.CostEstimate(
            flops=8 * outer * tokens * width,
            bytes_accessed=16 * tokens * width,
            transcendentals=0,
        ),
    )(place, weights, newest, *stored)


def sums_kernel(owners, place_ref, grads_ref, inputs_ref, sums_ref):
    cols = inputs_ref.shape[2] // owners
    values = inputs_ref[0].astype(jnp.float32)
    mean_vals = jnp.mean(values, axis=-1, keepdims=True)
    centred = values - mean_vals
    inverse = lax.rsqrt(jnp.mean(centred * centred, axis=-1, keepdims=True) + norm_epsilon)

    @pl.when(pl.program_id(1) == 0)
    def clear():
        sums_ref[...] = jnp.zeros_like(sums_ref)

    for index in range(owners):
        spot = lane_block(place_ref, index, cols)
        unit = (inputs_ref[0, :, spot].astype(jnp.float32) - mean_vals) * inverse
        grads = grads_ref[0, :, index * cols : (index + 1) * cols].astype(jnp.float32)
        near = slice(index * cols, (index + 1) * cols)
        sums_ref[0, 0:1, near] += jnp.sum(grads * unit, axis=0, keepdims=True)
        sums_ref[0, 1:2, near] += jnp.sum(grads, axis=0, keepdims=True)


def norm_sums(grads, layer_inputs, first, place, owners):
    count, tokens, width = grads.shape
    tile = 128
    return pl.pallas_call(
        functools.partial(sums_kernel, owners),
        grid_spec=pltpu.PrefetchScalarGridSpec(
            num_scalar_prefetch=1,
            grid=(count, tokens // tile),
            in_specs=[
                pl.BlockSpec((1, tile, width), lambda c, i, place_ref: (c, i, 0)),
                pl.BlockSpec((1, tile, width), lambda c, i, place_ref: (c + first, i, 0)),
            ],
            out_specs=pl.BlockSpec((1, 2, width), lambda c, i, place_ref: (c, 0, 0)),
        ),
        out_shape=jax.ShapeDtypeStruct((count, 2, width), jnp.float32),
        compiler_params=pltpu.CompilerParams(vmem_limit_bytes=32 << 20),
        cost_estimate=pl.CostEstimate(
            flops=12 * count * tokens * width,
            bytes_accessed=4 * count * tokens * width,
            transcendentals=0,
        ),
    )(place, grads, layer_inputs)


def back_kernel(owners, place_ref, grads_ref, inputs_ref, gain_ref, extra_ref, out_ref):
    cols = inputs_ref.shape[1] // owners
    values = inputs_ref[...].astype(jnp.float32)
    centred = values - jnp.mean(values, axis=-1, keepdims=True)
    inverse = lax.rsqrt(jnp.mean(centred * centred, axis=-1, keepdims=True) + norm_epsilon)
    back = norm_back(grads_ref[...], centred * inverse, inverse, gain_ref[...])
    if extra_ref is not None:
        back = back + extra_ref[...]
    for index in range(owners):
        spot = slice(index * cols, (index + 1) * cols)
        out_ref[:, lane_block(place_ref, index, cols)] = back[:, spot].astype(jnp.bfloat16)


def back_share(grads, inputs, gain, extra, place, owners):
    rows, width = grads.shape
    kernel = functools.partial(back_kernel, owners)
    if extra is None:
        kernel = lambda place_ref, grads_ref, inputs_ref, gain_ref, out_ref: back_kernel(
            owners, place_ref, grads_ref, inputs_ref, gain_ref, None, out_ref
        )
    whole = pl.BlockSpec((rows, width), lambda i, place_ref: (0, 0))
    given = [grads, inputs, gain] + ([] if extra is None else [extra])
    return pl.pallas_call(
        kernel,
        grid_spec=pltpu.PrefetchScalarGridSpec(
            num_scalar_prefetch=1,
            grid=(1,),
            in_specs=[whole, whole, pl.BlockSpec((1, width), lambda i, place_ref: (0, 0))]
            + ([] if extra is None else [whole]),
            out_specs=whole,
        ),
        out_shape=jax.ShapeDtypeStruct((rows, width), jnp.bfloat16),
        compiler_params=pltpu.CompilerParams(vmem_limit_bytes=32 << 20),
        cost_estimate=pl.CostEstimate(
            flops=15 * rows * width, bytes_accessed=10 * rows * width, transcendentals=0
        ),
    )(place, *given)


def body(
    layer_inputs,
    history,
    seq_ids,
    norms_master,
    norms_first,
    norms_second,
    attend_in_master,
    attend_in_first,
    attend_in_second,
    attend_out_master,
    attend_out_first,
    attend_out_second,
    expand_master,
    expand_first,
    expand_second,
    project_master,
    project_first,
    project_second,
    mixer_in_master,
    mixer_in_first,
    mixer_in_second,
    mixer_out_master,
    mixer_out_first,
    mixer_out_second,
    next_cotangent,
    grad_entry,
):
    bf16_type = jnp.bfloat16
    float_type = jnp.float32
    tensor_size = lax.axis_size("tensor")
    owners = lax.axis_size("dp")
    me = lax.axis_index("dp")
    order = feature_order(owners)
    place = jnp.stack([me ^ index for index in order]).astype(jnp.int32)
    tokens_here, width = layer_inputs.shape[1:]
    share_rows = tokens_here // tensor_size
    share_start = share_index("tensor") * share_rows
    cols = norms_master.shape[1]
    mixers = mixer_out_master.shape[0]

    def own_rows(values, axis):
        return lax.dynamic_slice_in_dim(values, share_start, share_rows, axis)

    def reorder(values):
        return jnp.concatenate(
            [
                lax.dynamic_slice_in_dim(values, (me ^ index) * cols, cols, values.ndim - 1)
                for index in order
            ],
            axis=-1,
        )


    near, side_bits, far = stages_of("tensor")
    out_first = (near, side_bits, far)
    in_first = (side_bits, far, near)
    back_order = (far, side_bits, near)
    cross_order = (near, far, side_bits)

    small = jnp.concatenate(
        [
            norms_master,
            mixer_in_master.T,
            jnp.pad(mixer_out_master, ((0, 0), (0, cols - MIXH))),
        ],
        axis=0,
    ).astype(bf16_type)
    small_half = gather_half(small, "dp", 1)
    attend_low = jnp.concatenate(
        [attend_in_master.astype(bf16_type), attend_out_master.astype(bf16_type).T[None]], axis=0
    )
    small_half, attend_low, history_late, entry_late, expand_late = sync(
        [small_half, attend_low, history, grad_entry, expand_master], []
    )
    attend_kept = gather_half(attend_low, "dp", 1)
    early_rows = [
        jnp.concatenate(
            [
                lax.dynamic_slice_in_dim(
                    values, (me ^ index) * tokens_here + share_start, share_rows, 1
                )
                for values in (history_late, entry_late[None])
            ],
            axis=0,
        )
        for index in order
    ]
    early_rows = [
        rows if index == 0 else swap(rows, "dp", index) for rows, index in zip(early_rows, order)
    ]
    expand_low = expand_late.astype(bf16_type)
    small_given = swap(small_half, "dp", 1)
    small_whole = jnp.concatenate([small_half, small_given], axis=1)
    norm_vals = small_whole[0:9].astype(float_type)
    mixer_in_low = small_whole[9 : 9 + MIXH]
    out_rows = small_whole[9 + MIXH :]
    mixer_out_low = jnp.zeros((owners, mixers, MIXH), bf16_type)
    for spot, index in enumerate(order):
        mixer_out_low = lax.dynamic_update_index_in_dim(
            mixer_out_low, out_rows[:, spot * cols : spot * cols + MIXH], me ^ index, 0
        )
    mixer_out_low = mixer_out_low.reshape(owners * mixers, MIXH)
    normed_kept, normed_given = norm_forward(
        layer_inputs, norm_vals[0:4], norm_vals[4:8], place, owners
    )
    early_rows, attend_kept, normed_kept, normed_given, expand_low, project_late = sync(
        [early_rows, attend_kept, normed_kept, normed_given, expand_low, project_master], []
    )

    early = jnp.concatenate(early_rows, axis=-1)
    stored_share = early[:-1]
    layer_count = stored_share.shape[0] + 1
    stored_most = Gather(stored_share[:-1], "tensor", back_order, 1)
    stored_last = Gather(stored_share[-1:], "tensor", cross_order, 1)
    expand_kept = gather_half(expand_low, "dp", 0)
    attend_given = swap(attend_kept, "dp", 1)
    stored_most.step(0)
    stored_last.step(0)
    proj_kept = jnp.einsum(
        "ctd,cde->cte", normed_kept[0:3], attend_kept[0:3], preferred_element_type=float_type
    )
    cosine, sine_table, unused = angles(seq_ids)
    half = ROT // 2
    tables = (
        jnp.concatenate([cosine, cosine, jnp.ones((tokens_here, HDIM - ROT), float_type)], 1),
        jnp.pad(-sine_table, ((0, 0), (0, HDIM - half))),
        jnp.pad(sine_table, ((0, 0), (half, HDIM - ROT))),
    )
    project_low = project_late.astype(bf16_type)
    expand_kept, attend_given, proj_kept, project_low, tables, layer_late, cotangent_late = sync(
        [
            expand_kept,
            attend_given,
            proj_kept,
            project_low,
            tables,
            layer_inputs,
            next_cotangent,
        ],
        [stored_most, stored_last],
    )

    project_kept = gather_half(project_low, "dp", 1)
    expand_given = swap(expand_kept, "dp", 1)
    stored_most.step(1)
    stored_last.step(1)
    proj = proj_kept + jnp.einsum(
        "ctd,cde->cte", normed_given[0:3], attend_given[0:3], preferred_element_type=float_type
    )
    turned, heads_out = attend(proj, tables, seq_ids)
    upper_kept = jnp.dot(normed_kept[3], expand_kept, preferred_element_type=float_type)
    valid = (own_rows(seq_ids, 0) >= 0).astype(float_type)[:, None]
    input_share = reorder(own_rows(layer_late, 1))
    cotangent_share = reorder(own_rows(cotangent_late, 1))
    (
        project_kept,
        expand_given,
        turned,
        heads_out,
        upper_kept,
        input_share,
        cotangent_share,
    ) = sync(
        [
            project_kept,
            expand_given,
            turned,
            heads_out,
            upper_kept,
            input_share,
            cotangent_share,
        ],
        [stored_most, stored_last],
    )

    out_kept, out_given = attend_kept[3], attend_given[3]
    project_given = swap(project_kept, "dp", 1)
    upper = upper_kept + jnp.dot(normed_given[3], expand_given, preferred_element_type=float_type)
    hidden = exact_gelu(upper).astype(bf16_type)
    branch_kept = Scatter(
        (
            contract_cols(heads_out, out_kept)
            + jnp.dot(hidden, project_kept, preferred_element_type=float_type)
        ).astype(bf16_type),
        "tensor",
        out_first,
    )
    branch_given = Scatter(
        (
            contract_cols(heads_out, out_given)
            + jnp.dot(hidden, project_given, preferred_element_type=float_type)
        ).astype(bf16_type),
        "tensor",
        in_first,
    )
    for stage in range(2):
        branch_kept.step(stage)
        branch_given.step(stage)
    (upper,) = sync([upper], [branch_kept, branch_given])
    branch_kept.step(2)
    branch_given.step(2)
    branch = jnp.concatenate([branch_kept.values, branch_given.values], axis=-1)
    phi, density = gelu_parts(upper)
    slope = phi + upper * density
    branch, slope = sync([branch, slope], [])

    newest, grad_newest, sent_kept, sent_given, grad_mixer_in, grad_mixer_out, mixer_gain = mix(
        branch,
        input_share[3],
        stored_share,
        early[-1],
        cotangent_share,
        valid,
        norm_vals[8:9],
        mixer_in_low,
        mixer_out_low,
    )
    grad_kept = Gather(sent_kept, "tensor", back_order)
    grad_given = Gather(sent_given, "tensor", cross_order)
    for stage in range(3):
        grad_kept.step(stage)
        grad_given.step(stage)
    grad_kept = grad_kept.result()
    received = grad_given.result()
    grad_given = received[:, 0 : width // 2]
    mix_low = received[:, width // 2 :]
    mix_total = 4 * layer_count
    mix_weights = mix_low[:, 0:mix_total].astype(float_type) + mix_low[
        :, mix_total : 2 * mix_total
    ].astype(float_type)
    newest_all = Gather(newest, "tensor", back_order)
    grad_kept, grad_given, mix_weights = sync(
        [grad_kept, grad_given, mix_weights], [newest_all, stored_last, stored_most]
    )

    history_pieces = list(history_back(mix_weights, cotangent_late, place, owners))

    def send_far(pieces, which):
        for spot in which:
            pieces[spot] = swap(pieces[spot], "dp", order[spot])

    far_spots = [spot for spot in range(owners) if order[spot] > 1]
    near_spots = [spot for spot in range(owners) if order[spot] == 1]
    first_far, last_far = far_spots[: len(far_spots) // 2], far_spots[len(far_spots) // 2 :]
    stored_pair = [
        Gather(stored_most.values[index : index + 1], "tensor", back_order, 1)
        for index in range(layer_count - 2)
    ]
    for item in stored_pair:
        item.places = list(stored_most.places)
    for item in stored_pair[:1]:
        item.step(2)
    stored_last.step(2)
    newest_all.step(0)
    grad_hidden = contract_cols(grad_kept, project_kept) + contract_cols(grad_given, project_given)
    grad_upper = (slope * grad_hidden).astype(bf16_type)
    grad_normed_ffn = jnp.concatenate(
        [
            contract_cols(grad_upper, expand_kept).astype(bf16_type),
            contract_cols(grad_upper, expand_given).astype(bf16_type),
        ],
        axis=-1,
    )
    grad_project = Reduce(
        contract_rows(hidden, grad_kept).astype(bf16_type),
        contract_rows(hidden, grad_given).astype(bf16_type),
        "dp",
        1,
    )
    (
        history_pieces,
        grad_normed_ffn,
        grad_upper,
        grad_kept,
        grad_given,
        out_kept,
        out_given,
    ) = sync(
        [history_pieces, grad_normed_ffn, grad_upper, grad_kept, grad_given, out_kept, out_given],
        [newest_all, stored_last, grad_project] + stored_pair,
    )

    newest_all.step(1)
    for item in stored_pair[1:]:
        item.step(2)
    send_far(history_pieces, near_spots)
    grad_project.near()
    grad_heads = (
        jnp.dot(grad_kept, out_kept, preferred_element_type=float_type)
        + jnp.dot(grad_given, out_given, preferred_element_type=float_type)
    ).astype(bf16_type)
    grad_proj = attend_back(turned, grad_heads, tables, seq_ids)
    grad_normed_attend = [
        jnp.concatenate(
            [
                contract_cols(grad_proj[index], weights[index]).astype(bf16_type)
                for weights in (attend_kept, attend_given)
            ],
            axis=-1,
        )
        for index in range(3)
    ]
    attend_grads = [
        jnp.concatenate(
            [
                jnp.einsum(
                    "ctd,cte->cde", normed[0:3], grad_proj, preferred_element_type=float_type
                ).astype(bf16_type),
                contract_rows(grads, heads_out).astype(bf16_type)[None],
            ],
            axis=0,
        )
        for normed, grads in ((normed_kept, grad_kept), (normed_given, grad_given))
    ]
    grad_attend = Reduce(*attend_grads, "dp", 1)
    grad_expand = Reduce(
        contract_rows(normed_kept[3], grad_upper).astype(bf16_type),
        contract_rows(normed_given[3], grad_upper).astype(bf16_type),
        "dp",
        0,
    )
    grad_normed_attend, grad_normed_ffn, history_pieces, layer_late = sync(
        [grad_normed_attend, grad_normed_ffn, history_pieces, layer_late],
        [grad_attend, grad_expand, grad_project, newest_all] + stored_pair,
    )

    summed = [
        Scatter(grad_normed_attend[index], "tensor", out_first) for index in range(3)
    ] + [Scatter(grad_normed_ffn, "tensor", in_first)]
    summed[0].step(0)
    summed[3].step(0)
    send_far(history_pieces, first_far)
    grad_attend.near()
    grad_expand.near()
    sums = [
        norm_sums(grads[None], layer_late, index, place, owners)[0]
        for index, grads in enumerate(grad_normed_attend + [grad_normed_ffn])
    ]
    sums, history_pieces = sync(
        [sums, history_pieces], summed + [newest_all, grad_project, grad_attend, grad_expand]
    )

    norm_pack = jnp.stack(sums)
    own_rows_out = jnp.stack(
        [
            lax.dynamic_index_in_dim(
                grad_mixer_out.reshape(owners, mixers * MIXH), me ^ index, 0, False
            )
            for index in order
        ]
    )
    pack = Halves(
        jnp.concatenate(
            [
                norm_pack[:, 0],
                norm_pack[:, 1],
                mixer_gain,
                grad_mixer_in,
                jnp.pad(own_rows_out, ((0, 0), (0, cols - mixers * MIXH))).reshape(1, width),
            ],
            axis=0,
        ),
        "dp",
    )
    pack.near()
    summed[1].step(0)
    summed[3].step(1)
    summed[3].step(2)
    summed[0].step(1)
    send_far(history_pieces, last_far)
    grad_project.prepare()
    (history_pieces,) = sync(
        [history_pieces], summed + [grad_project, grad_expand, grad_attend, pack]
    )

    def back(index):
        return Gather(
            back_share(
                summed[index].values,
                input_share[index],
                norm_vals[index][None],
                grad_newest if index == 3 else None,
                place,
                owners,
            ),
            "tensor",
            back_order,
        )

    gathered = [None, None, None, back(3)]
    summed[2].step(0)
    summed[1].step(1)
    step_both(summed[0], 2, gathered[3], 0)
    grad_project.far()
    grad_expand.prepare()
    pack.far()
    sync([], summed[0:3] + [gathered[3], grad_expand, grad_project, grad_attend, newest_all, pack])

    gathered[0] = back(0)
    newest_all.step(2)
    step_both(summed[2], 1, gathered[3], 1)
    step_both(summed[1], 2, gathered[0], 0)
    grad_expand.far()
    grad_attend.prepare()
    pack.rows("tensor", near)
    (project_squares,) = sync(
        [grad_project.squares()],
        summed[1:3] + [gathered[0], gathered[3], newest_all, grad_attend, grad_expand, pack],
    )

    gathered[1] = back(1)
    gathered[3].step(2)
    step_both(summed[2], 2, gathered[1], 0)
    gathered[0].step(1)
    grad_attend.far()
    pack.rows("tensor", side_bits)
    newest_whole = newest_all.result()
    newest_stored = [item.result()[0] for item in stored_pair] + [stored_last.result()[0]]
    expand_squares, newest_whole, newest_stored, mix_weights = sync(
        [grad_expand.squares(), newest_whole, newest_stored, mix_weights],
        [summed[2], gathered[0], gathered[1], gathered[3], grad_attend, pack],
    )

    gathered[2] = back(2)
    gathered[0].step(2)
    gathered[2].step(0)
    gathered[1].step(1)
    pack.rows("tensor", far)
    entry_pieces = [newest_whole[:, spot * cols : (spot + 1) * cols] for spot in range(owners)]
    send_far(entry_pieces, first_far)
    next_inputs = next_layer(mix_weights, newest_stored, newest_whole, place, owners)
    attend_squares, entry_pieces, next_inputs = sync(
        [grad_attend.squares(), entry_pieces, next_inputs],
        [gathered[0], gathered[1], gathered[2], pack],
    )

    gathered[1].step(2)
    gathered[2].step(1)
    send_far(entry_pieces, last_far)
    send_far(entry_pieces, near_spots)
    own_pack = pack.values
    norm_grad = own_pack[0:9]
    grad_mixer_in = own_pack[9 : 9 + MIXH].T
    grad_mixer_out = own_pack[9 + MIXH, 0 : mixers * MIXH].reshape(mixers, MIXH)
    shared_squares = (
        square_sum(norm_grad) + square_sum(grad_mixer_in) + square_sum(grad_mixer_out)
    )
    shard_squares = project_squares + expand_squares + attend_squares
    total_squares = (shard_squares + shared_squares / tensor_size).reshape(1, 1)
    for axis, bits in (
        ("dp", bits_of(owners)[:1]),
        ("tensor", side_bits + far),
        ("dp", bits_of(owners)[1:]),
        ("tensor", near),
    ):
        for bit in bits:
            total_squares = total_squares + swap(total_squares, axis, bit)
    total_squares, entry_pieces = sync(
        [total_squares, entry_pieces], [gathered[1], gathered[2]]
    )
    total_squares = total_squares[0, 0]

    gathered[2].step(2)
    grad_norm = jnp.sqrt(total_squares)
    factor = jnp.minimum(1.0, clip_level / grad_norm)
    wide_rate = 2.0 / math.sqrt(D)
    wide = (wide_rate, weight_decay)
    norms_out = adam_step(norms_master, norms_first, norms_second, norm_grad, factor, 1.0, 0.0)
    mixer_in_out = adam_step(
        mixer_in_master,
        mixer_in_first,
        mixer_in_second,
        grad_mixer_in,
        factor,
        wide_rate,
        weight_decay,
    )
    mixer_out_out = adam_step(
        mixer_out_master,
        mixer_out_first,
        mixer_out_second,
        grad_mixer_out,
        factor,
        2.0 / math.sqrt(MIXH),
        weight_decay,
    )
    parts, rows, units = attend_in_master.shape
    attend_in_out = adam_call(
        grad_attend.terms,
        attend_in_master,
        attend_in_first,
        attend_in_second,
        factor,
        wide,
        (parts, 1, 1),
        (1, rows, units),
        None,
    )
    attend_out_out = adam_call(
        grad_attend.terms,
        attend_out_master,
        attend_out_first,
        attend_out_second,
        factor,
        wide,
        (1, 1),
        attend_out_master.shape,
        parts,
    )
    rows, units = expand_master.shape
    expand_out = adam_call(
        grad_expand.terms,
        expand_master,
        expand_first,
        expand_second,
        factor,
        wide,
        (4, 1),
        (rows // 4, units),
        None,
    )
    rows, units = project_master.shape
    project_out = adam_call(
        grad_project.terms,
        project_master,
        project_first,
        project_second,
        factor,
        (2.0 / math.sqrt(FF), weight_decay),
        (4, 1),
        (rows // 4, units),
        None,
    )
    new_entry = jnp.zeros(grad_entry.shape, bf16_type)
    grad_history = jnp.zeros(history.shape, bf16_type)
    for spot, index in enumerate(order):
        first_row = (me ^ index) * tokens_here
        new_entry = lax.dynamic_update_slice_in_dim(new_entry, entry_pieces[spot], first_row, 0)
        grad_history = lax.dynamic_update_slice_in_dim(
            grad_history, history_pieces[spot], first_row, 1
        )
    grad_inputs = jnp.zeros(layer_inputs.shape, bf16_type)
    for index in (3, 0, 1, 2):
        grad_inputs = lax.dynamic_update_index_in_dim(
            grad_inputs, gathered[index].result(), index, 0
        )
    return (
        next_inputs,
        new_entry,
        grad_inputs,
        grad_history,
        norms_out[0],
        norms_out[1],
        norms_out[2],
        attend_in_out[0],
        attend_in_out[1],
        attend_in_out[2],
        attend_in_out[3],
        attend_out_out[0],
        attend_out_out[1],
        attend_out_out[2],
        attend_out_out[3],
        expand_out[0],
        expand_out[1],
        expand_out[2],
        expand_out[3],
        project_out[0],
        project_out[1],
        project_out[2],
        project_out[3],
        mixer_in_out[0],
        mixer_in_out[1],
        mixer_in_out[2],
        mixer_in_out[0].astype(bf16_type),
        mixer_out_out[0],
        mixer_out_out[1],
        mixer_out_out[2],
        mixer_out_out[0].astype(bf16_type),
        grad_norm,
    )


def solution(mesh):
    in_specs = (
        P(None, "dp", None),
        P(None, None, "dp"),
        P("dp"),
        P(None, "dp"),
        P(None, "dp"),
        P(None, "dp"),
        P(None, "dp", "tensor"),
        P(None, "dp", "tensor"),
        P(None, "dp", "tensor"),
        P("tensor", "dp"),
        P("tensor", "dp"),
        P("tensor", "dp"),
        P("dp", "tensor"),
        P("dp", "tensor"),
        P("dp", "tensor"),
        P("tensor", "dp"),
        P("tensor", "dp"),
        P("tensor", "dp"),
        P("dp", None),
        P("dp", None),
        P("dp", None),
        P("dp", None),
        P("dp", None),
        P("dp", None),
        P(None, "dp", None),
        P(None, "dp"),
    )
    out_specs = (
        P(None, "dp", None),
        P(None, "dp"),
        P(None, "dp", None),
        P(None, None, "dp"),
        P(None, "dp"),
        P(None, "dp"),
        P(None, "dp"),
        P(None, "dp", "tensor"),
        P(None, "dp", "tensor"),
        P(None, "dp", "tensor"),
        P(None, "dp", "tensor"),
        P("tensor", "dp"),
        P("tensor", "dp"),
        P("tensor", "dp"),
        P("tensor", "dp"),
        P("dp", "tensor"),
        P("dp", "tensor"),
        P("dp", "tensor"),
        P("dp", "tensor"),
        P("tensor", "dp"),
        P("tensor", "dp"),
        P("tensor", "dp"),
        P("tensor", "dp"),
        P("dp", None),
        P("dp", None),
        P("dp", None),
        P("dp", None),
        P("dp", None),
        P("dp", None),
        P("dp", None),
        P("dp", None),
        P(),
    )
    return jax.shard_map(body, mesh=mesh, in_specs=in_specs, out_specs=out_specs, check_vma=False)
```

time: 1320 us -> 518 us (0.39)
  waiting for transfers between devices: 762 us -> 185 us
  blocking collectives: 184 us -> 0 us
  other arithmetic: 153 us -> 67.3 us
  Pallas kernels: 0 us -> 74 us
  starting transfers between devices: 20.4 us -> 80.3 us
  matrix products: 70.9 us -> 29.3 us
  local copies, waits for them, and re-layouts: 94.1 us -> 64.8 us
    psum x3 -> x0, waiting for transfers between devices: 529 us -> none  [the longest x1 381 us: body(): summed_grads = lax.psum(grad_normed, 'tensor')]
    ppermute x0 -> x75, waiting for transfers between devices: none -> 185 us  [swap(): lax.ppermute(values, axis, [(source, source ^ mask) for source in range(s...]
    reduce_scatter x5 -> x0, waiting for transfers between devices: 141 us -> none  [the longest x1 70.8 us: body(): lax.psum_scatter(grad_project, 'dp', scatter_dimension=1, tiled=True)]
    unnamed x1 -> x0, blocking collectives: 105 us -> none
    ppermute x0 -> x75, starting transfers between devices: none -> 80.3 us  [swap(): lax.ppermute(values, axis, [(source, source ^ mask) for source in range(s...]
    all_gather x4 -> x0, waiting for transfers between devices: 75.9 us -> none  [the longest x1 49.4 us: body(): lax.all_gather(project_master.astype(bf16_type), 'dp', axis=1, tiled=True)]
    pallas_call x0 -> x18, Pallas kernels: none -> 74 us  [the longest x4 25.4 us: adam_call(): pl.pallas_call(functools.partial(adam_kernel, rates, len(terms), flip), g...]
    reduce_sum x14 -> x6, other arithmetic: 58 us -> 7.89 us  [square_sum(): return jnp.sum(values * values)]
  transfers between devices with their start and end apart: 16 -> 75, of which waited for: 9 -> 31; matrix products, arithmetic and copies ran while one was open for 15% -> 21% of each run, Pallas kernels for 0% -> 13%
where the time goes in v2:
time: 518 us; the launch traced here: 513 us
  waiting for transfers between devices  185 us (36%)
  starting transfers between devices  80.3 us (16%)
  Pallas kernels  74 us (14%)
  other arithmetic  67.3 us (13%)
  local copies, waits for them, and re-layouts  64.8 us (13%)
  matrix products  29.3 us (6%)
  between operations  11.8 us (2%)
    ppermute x75, waiting for transfers between devices, swap(): lax.ppermute(values, axis, [(source, source ^ mask) for source in range(s...  185 us
    ppermute x75, starting transfers between devices, swap(): lax.ppermute(values, axis, [(source, source ^ mask) for source in range(s...  80.3 us
    pallas_call x4, Pallas kernels, adam_call(): pl.pallas_call(functools.partial(adam_kernel, rates, len(terms), flip), g...  25.4 us
    unnamed x224, local copies, waits for them, and re-layouts  22.3 us
    select_n x27, other arithmetic, join(): jnp.where(lax.broadcasted_iota(jnp.int32, shape, dim) == side, jnp.expand...  20.1 us
    pallas_call x1, Pallas kernels, norm_forward(): pl.pallas_call(functools.partial(norm_kernel, owners), grid_spec=pltpu.Pr...  12.6 us
    dot_general x6, matrix products, contract_rows(): lax.dot_general(left, right, (((0,), (0,)), ((), ())), preferred_element_...  11.6 us
    pallas_call x4, Pallas kernels, norm_sums(): pl.pallas_call(functools.partial(sums_kernel, owners), grid_spec=pltpu.Pr...  11.4 us
  transfers between devices with their start and end apart: 75, of which 31 were waited for; matrix products, arithmetic and copies ran while one was open for 21% of the time, Pallas kernels for 13%

profile of v2, /device:TPU:0, one launch (start us, length us, event | category | flops | bytes accessed | tf_op | source)
XLA Modules:
  0.0 513.0 jit_solution(10561810187213124276)
XLA Ops:
  3.0 3.0 collective-permute-start
  21.0 12.6 %shard_map.497 = (bf16[4,384,1024]{2,1,0:T(8,128)(2,1)}, bf16[4,384,1024]{2,1,0:T(8,128)(2,1)}) custom-call(s32[4]{0:T(128)} %pad_add_fusion.place_ref, bf16[4,384,2048]{2,1,0:T(8,128)(2,1)} %inputs_ref.5, f32[4,1,2048]{2,1,0:T(1,128)} %copy.89.gains_ref, f32[4,1,2048]{2,1,0:T(1,128)} %copy.90.biases_ref), custom_call_target="tpu_custom_call" | custom-call | flops 31457280 | bytes 12582912 | tf_op jit(solution)/shard_map/pallas_call | solution.py:362
  33.6 14.0 %collective-permute-done.4 = bf16[4,512,256]{2,1,0:T(8,128)(2,1)S(1)} collective-permute-done((bf16[4,512,256]{2,1,0:T(8,128)(2,1)}, bf16[4,512,256]{2,1,0:T(8,128)(2,1)S(1)}, u32[]{:S(2)}, u32[]{:S(2)}) %collective-permute-start.4) | collective-permute-done | bytes 1048608 | tf_op jit(solution)/shard_map/ppermute | solution.py:120
  53.1 2.7 collective-permute-start.8
  57.2 16.6 %collective-permute-done.8 = bf16[2,48,2048]{2,1,0:T(8,128)(2,1)S(1)} collective-permute-done((bf16[2,48,2048]{2,1,0:T(8,128)(2,1)S(1)}, bf16[2,48,2048]{2,1,0:T(8,128)(2,1)S(1)}, u32[]{:S(2)}, u32[]{:S(2)}) %collective-permute-start.8) | collective-permute-done | bytes 393248 | tf_op jit(solution)/shard_map/ppermute | solution.py:120
  76.4 3.4 collective-permute-start.13
  80.6 3.0 constant_dynamic-slice_fusion.15
  87.1 15.2 %collective-permute-done.13 = bf16[1,2,48,2048]{3,2,1,0:T(8,128)(2,1)S(1)} collective-permute-done((bf16[1,2,48,2048]{3,2,1,0:T(8,128)(2,1)S(1)}, bf16[1,2,48,2048]{3,2,1,0:T(8,128)(2,1)S(1)}, u32[]{:S(2)}, u32[]{:S(2)}) %collective-permute-start.13) | collective-permute-done | bytes 393248 | tf_op jit(solution)/shard_map/ppermute | solution.py:120
  107.1 3.9 fusion.2
  115.0 3.4 collective-permute-start.17
  119.2 4.7 collective-permute-done.14
  124.0 3.5 collective-permute-start.15
  128.9 4.7 collective-permute-done.15
  133.6 5.7 %collective-permute-done.18 = bf16[2,48,1024]{2,1,0:T(8,128)(2,1)S(1)} collective-permute-done((bf16[2,48,1024]{2,1,0:T(8,128)(2,1)S(1)}, bf16[2,48,1024]{2,1,0:T(8,128)(2,1)S(1)}, u32[]{:S(2)}, u32[]{:S(2)}) %collective-permute-start.18) | collective-permute-done | bytes 196640 | tf_op jit(solution)/shard_map/ppermute | solution.py:120
  144.1 3.5 collective-permute-done.19
  152.3 9.0 %collective-permute-done.21 = bf16[48,1024]{1,0:T(8,128)(2,1)S(1)} collective-permute-done((bf16[48,1024]{1,0:T(8,128)(2,1)S(1)}, bf16[48,1024]{1,0:T(8,128)(2,1)S(1)}, u32[]{:S(2)}, u32[]{:S(2)}) %collective-permute-start.21) | collective-permute-done | bytes 98336 | tf_op jit(solution)/shard_map/ppermute | solution.py:120
  164.1 7.4 %collective-permute-done.22 = bf16[2,48,1024]{2,1,0:T(8,128)(2,1)S(1)} collective-permute-done((bf16[2,48,1024]{2,1,0:T(8,128)(2,1)S(1)}, bf16[2,48,1024]{2,1,0:T(8,128)(2,1)S(1)}, u32[]{:S(2)}, u32[]{:S(2)}) %collective-permute-start.22) | collective-permute-done | bytes 196640 | tf_op jit(solution)/shard_map/ppermute | solution.py:120
  189.3 2.7 convolution_convert_fusion.3.refs_0_
  192.0 2.8 convolution_convert_fusion.2
  200.5 8.0 %shard_map.500 = (bf16[3,384,512]{2,1,0:T(8,128)(2,1)}, bf16[3,384,512]{2,1,0:T(8,128)(2,1)}, bf16[3,384,512]{2,1,0:T(8,128)(2,1)}, bf16[3,384,512]{2,1,0:T(8,128)(2,1)}) custom-call(s32[4]{0:T(128)} %pad_add_fusion.place_ref, f32[384,16]{1,0:T(8,128)} %convert_add_fusion.14.weights_ref, bf16[4,384,2048]{2,1,0:T(8,128)(2,1)} %cotangent_ref), custom_call_target="tpu_custom_call" | custom-call | flops 25165824 | bytes 11010048 | tf_op jit(solution)/shard_map/pallas_call | solution.py:600
  208.8 3.5 collective-permute-done.28
  225.8 2.6 convolution_convert_fusion.1.refs_0_
  228.4 2.6 convolution_convert_fusion
  238.9 6.2 %collective-permute-done.32 = bf16[2,48,2048]{2,1,0:T(8,128)(2,1)S(1)} collective-permute-done((bf16[2,48,2048]{2,1,0:T(8,128)(2,1)S(1)}, bf16[2,48,2048]{2,1,0:T(8,128)(2,1)S(1)}, u32[]{:S(2)}, u32[]{:S(2)}) %collective-permute-start.32) | collective-permute-done | bytes 393248 | tf_op jit(solution)/shard_map/ppermute | solution.py:120
  246.1 7.5 %collective-permute-done.33 = bf16[1,2,2,48,2048]{4,3,2,1,0:T(8,128)(2,1)S(1)} collective-permute-done((bf16[1,2,2,48,2048]{4,3,2,1,0:T(8,128)(2,1)S(1)}, bf16[1,2,2,48,2048]{4,3,2,1,0:T(8,128)(2,1)S(1)}, u32[]{:S(2)}, u32[]{:S(2)}) %collective-permute-start.33) | collective-permute-done | bytes 786464 | tf_op jit(solution)/shard_map/ppermute | solution.py:120
  261.0 2.8 copy-done
  265.2 2.8 shard_map.502
  268.0 2.8 shard_map.503
  270.8 2.8 shard_map.504
  273.7 3.0 shard_map.505
  279.9 8.2 %collective-permute-done.34 = bf16[3,384,512]{2,1,0:T(8,128)(2,1)S(1)} collective-permute-done((bf16[3,384,512]{2,1,0:T(8,128)(2,1)}, bf16[3,384,512]{2,1,0:T(8,128)(2,1)S(1)}, u32[]{:S(2)}, u32[]{:S(2)}) %collective-permute-start.34) | collective-permute-done | bytes 1179680 | tf_op jit(solution)/shard_map/ppermute | solution.py:120
  295.3 4.6 concatenate.92
  302.9 10.5 %collective-permute-done.42 = bf16[2,48,2048]{2,1,0:T(8,128)(2,1)} collective-permute-done((bf16[2,48,2048]{2,1,0:T(8,128)(2,1)}, bf16[2,48,2048]{2,1,0:T(8,128)(2,1)}, u32[]{:S(2)}, u32[]{:S(2)}) %collective-permute-start.42) | collective-permute-done | bytes 393248 | tf_op jit(solution)/shard_map/ppermute | solution.py:120
  315.9 4.3 collective-permute-done.43
  322.9 2.6 collective-permute-start.46
  325.9 2.6 collective-permute-start.48
  334.2 18.3 %collective-permute-done.49 = f32[46,512]{1,0:T(8,128)S(1)} collective-permute-done((f32[46,512]{1,0:T(8,128)S(1)}, f32[46,512]{1,0:T(8,128)S(1)}, u32[]{:S(2)}, u32[]{:S(2)}) %collective-permute-start.49) | collective-permute-done | bytes 94240 | tf_op jit(solution)/shard_map/ppermute | solution.py:120
  364.0 12.3 %collective-permute-done.54 = f32[46,512]{1,0:T(8,128)S(1)} collective-permute-done((f32[46,512]{1,0:T(8,128)S(1)}, f32[46,512]{1,0:T(8,128)S(1)}, u32[]{:S(2)}, u32[]{:S(2)}) %collective-permute-start.54) | collective-permute-done | bytes 94240 | tf_op jit(solution)/shard_map/ppermute | solution.py:120
  376.5 4.9 collective-permute-done.51
  393.3 11.0 %collective-permute-done.59 = f32[46,512]{1,0:T(8,128)S(1)} collective-permute-done((f32[46,512]{1,0:T(8,128)S(1)}, f32[46,512]{1,0:T(8,128)S(1)}, u32[]{:S(2)}, u32[]{:S(2)}) %collective-permute-start.59) | collective-permute-done | bytes 94240 | tf_op jit(solution)/shard_map/ppermute | solution.py:120
  407.1 4.0 collective-permute-done.58.refs_2_
  420.8 3.5 dynamic_update_slice.58
  428.4 6.9 %shard_map.509 = bf16[4,384,2048]{2,1,0:T(8,128)(2,1)} custom-call(s32[4]{0:T(128)S(1)} %copy-done.16, f32[384,16]{1,0:T(8,128)S(1)} %copy-done.9, bf16[384,2048]{1,0:T(8,128)(2,1)S(1)} %bitcast.298, bf16[384,2048]{1,0:T(8,128)(2,1)S(1)} %bitcast.311, bf16[384,2048]{1,0:T(8,128)(2,1)S(1)} %bitcast.312, bf16[384,2048]{1,0:T(8,128)(2,1)S(1)} %bitcast.310), custom_call_target="tpu_custom_call" | custom-call | flops 25165824 | bytes 12582912 | tf_op jit(solution)/shard_map/pallas_call | solution.py:649
  460.9 2.8 collective-permute-start.68
  480.1 3.3 shard_map.512
  483.5 6.8 %shard_map.511 = (f32[3,512,256]{2,1,0:T(8,128)}, f32[3,512,256]{2,1,0:T(8,128)}, f32[3,512,256]{2,1,0:T(8,128)}, bf16[3,512,256]{2,1,0:T(8,128)(2,1)}) custom-call(f32[1]{0:T(128)} %bitcast.122.factor_ref, bf16[4,1024,256]{2,1,0:T(8,128)(2,1)} %pad_maximum_fusion.3.refs_0_, bf16[4,1024,256]{2,1,0:T(8,128)(2,1)} %collective-permute-done.37.refs_1_, ...), custom_call_target="tpu_custom_call" | custom-call | flops 7864320 | bytes 12582912 | tf_op jit(solution)/shard_map/pallas_call | solution.py:324
  490.3 7.6 %shard_map.513 = (f32[512,1024]{1,0:T(8,128)}, f32[512,1024]{1,0:T(8,128)}, f32[512,1024]{1,0:T(8,128)}, bf16[512,1024]{1,0:T(8,128)(2,1)}) custom-call(f32[1]{0:T(128)} %bitcast.122.factor_ref, bf16[1024,1024]{1,0:T(8,128)(2,1)} %convolution_convert_fusion.1.refs_0_, bf16[1024,1024]{1,0:T(8,128)(2,1)} %collective-permute-done.38.refs_1_, ...), custom_call_target="tpu_custom_call" | custom-call | flops 10485760 | bytes 16777216 | tf_op jit(solution)/shard_map/pallas_call | solution.py:324
  497.9 7.7 %shard_map.514 = (f32[1024,512]{1,0:T(8,128)}, f32[1024,512]{1,0:T(8,128)}, f32[1024,512]{1,0:T(8,128)}, bf16[1024,512]{1,0:T(8,128)(2,1)}) custom-call(f32[1]{0:T(128)} %bitcast.122.factor_ref, bf16[1024,1024]{1,0:T(8,128)(2,1)} %convolution_convert_fusion.3.refs_0_, bf16[1024,1024]{1,0:T(8,128)(2,1)} %copy-done.29, bf16[1024,512]{1,0:T(8,128)(2,1)} %copy-done.40, ...), custom_call_target="tpu_custom_call" | custom-call | flops 10485760 | bytes 16777216 | tf_op jit(solution)/shard_map/pallas_call | solution.py:324
  (564 shorter events, 212.9 us)
Async XLA Ops:
  14.4 34.6 %collective-permute-start.1 = (bf16[4,48,512]{2,1,0:T(8,128)(2,1)S(1)}, bf16[4,48,512]{2,1,0:T(8,128)(2,1)S(1)}, u32[]{:S(2)}, u32[]{:S(2)}) collective-permute-start(bf16[4,48,512]{2,1,0:T(8,128)(2,1)S(1)} %pad_maximum_fusion.18), channel_id=1, source_target_pairs={{0,16},{8,24},{16,0},{24,8},{1,17},{9,25},{17,1},{25,9},{2,18},{10... | collective-permute-start | bytes 589832 | tf_op jit(solution)/shard_map/ppermute | solution.py:120
  14.6 34.5 %collective-permute-start.2 = (bf16[4,48,512]{2,1,0:T(8,128)(2,1)S(1)}, bf16[4,48,512]{2,1,0:T(8,128)(2,1)S(1)}, u32[]{:S(2)}, u32[]{:S(2)}) collective-permute-start(bf16[4,48,512]{2,1,0:T(8,128)(2,1)S(1)} %pad_maximum_fusion.19), channel_id=1, source_target_pairs={{0,8},{8,0},{16,24},{24,16},{1,9},{9,1},{17,25},{25,17},{2,10},{10... | collective-permute-start | bytes 589832 | tf_op jit(solution)/shard_map/ppermute | solution.py:120
  14.7 34.4 %collective-permute-start.3 = (bf16[4,48,512]{2,1,0:T(8,128)(2,1)S(1)}, bf16[4,48,512]{2,1,0:T(8,128)(2,1)S(1)}, u32[]{:S(2)}, u32[]{:S(2)}) collective-permute-start(bf16[4,48,512]{2,1,0:T(8,128)(2,1)S(1)} %pad_maximum_fusion.20), channel_id=1, source_target_pairs={{0,24},{8,16},{16,8},{24,0},{1,25},{9,17},{17,9},{25,1},{2,26},{10... | collective-permute-start | bytes 589832 | tf_op jit(solution)/shard_map/ppermute | solution.py:120
  16.8 30.7 %collective-permute-start.4 = (bf16[4,512,256]{2,1,0:T(8,128)(2,1)}, bf16[4,512,256]{2,1,0:T(8,128)(2,1)S(1)}, u32[]{:S(2)}, u32[]{:S(2)}) collective-permute-start(bf16[4,512,256]{2,1,0:T(8,128)(2,1)} %pad_maximum_fusion.9), channel_id=1, source_target_pairs={{0,16},{8,24},{16,0},{24,8},{1,17},{9,25},{17,1},{25,9},{2,18},{10... | collective-permute-start | bytes 3145736 | tf_op jit(solution)/shard_map/ppermute | solution.py:120
  49.1 24.8 %collective-permute-start.6 = (bf16[512,1024]{1,0:T(8,128)(2,1)S(1)}, bf16[512,1024]{1,0:T(8,128)(2,1)S(1)}, u32[]{:S(2)}, u32[]{:S(2)}) collective-permute-start(bf16[512,1024]{1,0:T(8,128)(2,1)S(1)} %convert_element_type.368), channel_id=1, source_target_pairs={{0,16},{8,24},{16,0},{24,8},{1,17},{9,25},{17,1},{25,9},{2,18},{10... | collective-permute-start | bytes 3145736 | tf_op jit(solution)/shard_map/ppermute | solution.py:120
  49.5 24.6 %collective-permute-start.7 = (bf16[4,1024,256]{2,1,0:T(8,128)(2,1)S(1)}, bf16[4,1024,256]{2,1,0:T(8,128)(2,1)S(1)}, u32[]{:S(2)}, u32[]{:S(2)}) collective-permute-start(bf16[4,1024,256]{2,1,0:T(8,128)(2,1)S(1)} %pad_maximum_fusion), channel_id=1, source_target_pairs={{0,8},{8,0},{16,24},{24,16},{1,9},{9,1},{17,25},{25,17},{2,10},{10... | collective-permute-start | bytes 6291464 | tf_op jit(solution)/shard_map/ppermute | solution.py:120
  53.1 20.6 %collective-permute-start.8 = (bf16[2,48,2048]{2,1,0:T(8,128)(2,1)S(1)}, bf16[2,48,2048]{2,1,0:T(8,128)(2,1)S(1)}, u32[]{:S(2)}, u32[]{:S(2)}) collective-permute-start(bf16[2,48,2048]{2,1,0:T(8,128)(2,1)S(1)} %slice.329), channel_id=1, source_target_pairs={{0,4},{1,5},{2,6},{3,7},{4,0},{5,1},{6,2},{7,3},{8,12},{9,13},{10,... | collective-permute-start | bytes 1179656 | tf_op jit(solution)/shard_map/ppermute | solution.py:120
  74.2 31.3 %collective-permute-start.10 = (bf16[1024,512]{1,0:T(8,128)(2,1)S(1)}, bf16[1024,512]{1,0:T(8,128)(2,1)S(1)}, u32[]{:S(2)}, u32[]{:S(2)}) collective-permute-start(bf16[1024,512]{1,0:T(8,128)(2,1)S(1)} %convert_element_type.369), channel_id=1, source_target_pairs={{0,16},{8,24},{16,0},{24,8},{1,17},{9,25},{17,1},{25,9},{2,18},{10... | collective-permute-start | bytes 3145736 | tf_op jit(solution)/shard_map/ppermute | solution.py:120
  75.7 30.0 %collective-permute-start.11 = (bf16[1024,1024]{1,0:T(8,128)(2,1)S(1)}, bf16[1024,1024]{1,0:T(8,128)(2,1)S(1)}, u32[]{:S(2)}, u32[]{:S(2)}) collective-permute-start(bf16[1024,1024]{1,0:T(8,128)(2,1)S(1)} %pad_maximum_fusion.1), channel_id=1, source_target_pairs={{0,8},{8,0},{16,24},{24,16},{1,9},{9,1},{17,25},{25,17},{2,10},{10... | collective-permute-start | bytes 6291464 | tf_op jit(solution)/shard_map/ppermute | solution.py:120
  75.7 28.4 %collective-permute-start.12 = (bf16[2,2,48,2048]{3,2,1,0:T(8,128)(2,1)S(1)}, bf16[2,2,48,2048]{3,2,1,0:T(8,128)(2,1)S(1)}, u32[]{:S(2)}, u32[]{:S(2)}) collective-permute-start(bf16[2,2,48,2048]{3,2,1,0:T(8,128)(2,1)S(1)} %broadcast_select_fusion.14), channel_id=1, source_target_pairs={{0,2},{1,3},{2,0},{3,1},{4,6},{5,7},{6,4},{7,5},{8,10},{9,11},{10,... | collective-permute-start | bytes 2359304 | tf_op jit(solution)/shard_map/ppermute | solution.py:120
  76.4 25.9 %collective-permute-start.13 = (bf16[1,2,48,2048]{3,2,1,0:T(8,128)(2,1)S(1)}, bf16[1,2,48,2048]{3,2,1,0:T(8,128)(2,1)S(1)}, u32[]{:S(2)}, u32[]{:S(2)}) collective-permute-start(bf16[1,2,48,2048]{3,2,1,0:T(8,128)(2,1)S(1)} %broadcast_select_fusion.22), channel_id=1, source_target_pairs={{0,4},{1,5},{2,6},{3,7},{4,0},{5,1},{6,2},{7,3},{8,12},{9,13},{10,... | collective-permute-start | bytes 1179656 | tf_op jit(solution)/shard_map/ppermute | solution.py:120
  198.8 16.1 %collective-permute-start.29 = (bf16[1,2,2,48,2048]{4,3,2,1,0:T(8,128)(2,1)}, bf16[1,2,2,48,2048]{4,3,2,1,0:T(8,128)(2,1)}, u32[]{:S(2)}, u32[]{:S(2)}) collective-permute-start(bf16[1,2,2,48,2048]{4,3,2,1,0:T(8,128)(2,1)} %get-tuple-element.471), channel_id=1, source_target_pairs={{0,1},{1,0},{2,3},{3,2},{4,5},{5,4},{6,7},{7,6},{8,9},{9,8},{10,11... | collective-permute-start | bytes 2359304 | tf_op jit(solution)/shard_map/ppermute | solution.py:120
  231.1 23.9 %collective-permute-start.31 = (bf16[1024,1024]{1,0:T(8,128)(2,1)S(1)}, bf16[1024,1024]{1,0:T(8,128)(2,1)S(1)}, u32[]{:S(2)}, u32[]{:S(2)}) collective-permute-start(bf16[1024,1024]{1,0:T(8,128)(2,1)S(1)} %copy-done.106), channel_id=1, source_target_pairs={{0,8},{8,0},{16,24},{24,16},{1,9},{9,1},{17,25},{25,17},{2,10},{10... | collective-permute-start | bytes 6291464 | tf_op jit(solution)/shard_map/ppermute | solution.py:120
  233.4 21.5 %collective-permute-start.30 = (bf16[3,384,512]{2,1,0:T(8,128)(2,1)S(1)}, bf16[3,384,512]{2,1,0:T(8,128)(2,1)S(1)}, u32[]{:S(2)}, u32[]{:S(2)}) collective-permute-start(bf16[3,384,512]{2,1,0:T(8,128)(2,1)S(1)} %copy-done.107), channel_id=1, source_target_pairs={{0,8},{8,0},{16,24},{24,16},{1,9},{9,1},{17,25},{25,17},{2,10},{10... | collective-permute-start | bytes 3538952 | tf_op jit(solution)/shard_map/ppermute | solution.py:120
  234.3 19.3 %collective-permute-start.33 = (bf16[1,2,2,48,2048]{4,3,2,1,0:T(8,128)(2,1)S(1)}, bf16[1,2,2,48,2048]{4,3,2,1,0:T(8,128)(2,1)S(1)}, u32[]{:S(2)}, u32[]{:S(2)}) collective-permute-start(bf16[1,2,2,48,2048]{4,3,2,1,0:T(8,128)(2,1)S(1)} %copy-done.53), channel_id=1, source_target_pairs={{0,1},{1,0},{2,3},{3,2},{4,5},{5,4},{6,7},{7,6},{8,9},{9,8},{10,11... | collective-permute-start | bytes 2359304 | tf_op jit(solution)/shard_map/ppermute | solution.py:120
  255.0 33.1 %collective-permute-start.37 = (bf16[4,1024,256]{2,1,0:T(8,128)(2,1)}, bf16[4,1024,256]{2,1,0:T(8,128)(2,1)}, u32[]{:S(2)}, u32[]{:S(2)}) collective-permute-start(bf16[4,1024,256]{2,1,0:T(8,128)(2,1)} %pad_maximum_fusion.4), channel_id=1, source_target_pairs={{0,8},{8,0},{16,24},{24,16},{1,9},{9,1},{17,25},{25,17},{2,10},{10... | collective-permute-start | bytes 6291464 | tf_op jit(solution)/shard_map/ppermute | solution.py:120
  255.1 33.1 %collective-permute-start.38 = (bf16[1024,1024]{1,0:T(8,128)(2,1)}, bf16[1024,1024]{1,0:T(8,128)(2,1)}, u32[]{:S(2)}, u32[]{:S(2)}) collective-permute-start(bf16[1024,1024]{1,0:T(8,128)(2,1)} %convolution_convert_fusion), channel_id=1, source_target_pairs={{0,8},{8,0},{16,24},{24,16},{1,9},{9,1},{17,25},{25,17},{2,10},{10... | collective-permute-start | bytes 6291464 | tf_op jit(solution)/shard_map/ppermute | solution.py:120
  256.9 19.8 %collective-permute-start.35 = (bf16[2,2,48,2048]{3,2,1,0:T(8,128)(2,1)}, bf16[2,2,48,2048]{3,2,1,0:T(8,128)(2,1)}, u32[]{:S(2)}, u32[]{:S(2)}) collective-permute-start(bf16[2,2,48,2048]{3,2,1,0:T(8,128)(2,1)} %dynamic-slice_bitcast_fusion.2), channel_id=1, source_target_pairs={{0,1},{1,0},{2,3},{3,2},{4,5},{5,4},{6,7},{7,6},{8,9},{9,8},{10,11... | collective-permute-start | bytes 2359304 | tf_op jit(solution)/shard_map/ppermute | solution.py:120
  259.2 19.1 %collective-permute-start.36 = (bf16[2,2,48,2048]{3,2,0,1:T(8,128)(2,1)}, bf16[2,2,48,2048]{3,2,0,1:T(8,128)(2,1)}, u32[]{:S(2)}, u32[]{:S(2)}) collective-permute-start(bf16[2,2,48,2048]{3,2,0,1:T(8,128)(2,1)} %bitcast.293), channel_id=1, source_target_pairs={{0,2},{1,3},{2,0},{3,1},{4,6},{5,7},{6,4},{7,5},{8,10},{9,11},{10,... | collective-permute-start | bytes 2359304 | tf_op jit(solution)/shard_map/ppermute | solution.py:120
  260.9 27.2 %collective-permute-start.34 = (bf16[3,384,512]{2,1,0:T(8,128)(2,1)}, bf16[3,384,512]{2,1,0:T(8,128)(2,1)S(1)}, u32[]{:S(2)}, u32[]{:S(2)}) collective-permute-start(bf16[3,384,512]{2,1,0:T(8,128)(2,1)} %get-tuple-element.312), channel_id=1, source_target_pairs={{0,16},{8,24},{16,0},{24,8},{1,17},{9,25},{17,1},{25,9},{2,18},{10... | collective-permute-start | bytes 3538952 | tf_op jit(solution)/shard_map/ppermute | solution.py:120
  288.1 33.6 %collective-permute-start.39 = (bf16[3,384,512]{2,1,0:T(8,128)(2,1)}, bf16[3,384,512]{2,1,0:T(8,128)(2,1)}, u32[]{:S(2)}, u32[]{:S(2)}) collective-permute-start(bf16[3,384,512]{2,1,0:T(8,128)(2,1)} %get-tuple-element.325), channel_id=1, source_target_pairs={{0,24},{8,16},{16,8},{24,0},{1,25},{9,17},{17,9},{25,1},{2,26},{10... | collective-permute-start | bytes 3538952 | tf_op jit(solution)/shard_map/ppermute | solution.py:120
  289.1 25.7 %collective-permute-start.40 = (bf16[2,48,2048]{2,1,0:T(8,128)(2,1)}, bf16[2,48,2048]{2,1,0:T(8,128)(2,1)}, u32[]{:S(2)}, u32[]{:S(2)}) collective-permute-start(bf16[2,48,2048]{2,1,0:T(8,128)(2,1)} %dynamic-slice_bitcast_fusion.5), channel_id=1, source_target_pairs={{0,2},{1,3},{2,0},{3,1},{4,6},{5,7},{6,4},{7,5},{8,10},{9,11},{10,... | collective-permute-start | bytes 1179656 | tf_op jit(solution)/shard_map/ppermute | solution.py:120
  290.4 29.9 %collective-permute-start.41 = (bf16[2,2,48,2048]{3,2,1,0:T(8,128)(2,1)}, bf16[2,2,48,2048]{3,2,1,0:T(8,128)(2,1)}, u32[]{:S(2)}, u32[]{:S(2)}) collective-permute-start(bf16[2,2,48,2048]{3,2,1,0:T(8,128)(2,1)} %dynamic-slice_bitcast_fusion.1), channel_id=1, source_target_pairs={{0,1},{1,0},{2,3},{3,2},{4,5},{5,4},{6,7},{7,6},{8,9},{9,8},{10,11... | collective-permute-start | bytes 2359304 | tf_op jit(solution)/shard_map/ppermute | solution.py:120
  292.9 20.4 %collective-permute-start.42 = (bf16[2,48,2048]{2,1,0:T(8,128)(2,1)}, bf16[2,48,2048]{2,1,0:T(8,128)(2,1)}, u32[]{:S(2)}, u32[]{:S(2)}) collective-permute-start(bf16[2,48,2048]{2,1,0:T(8,128)(2,1)} %dynamic-slice_bitcast_fusion.4), channel_id=1, source_target_pairs={{0,4},{1,5},{2,6},{3,7},{4,0},{5,1},{6,2},{7,3},{8,12},{9,13},{10,... | collective-permute-start | bytes 1179656 | tf_op jit(solution)/shard_map/ppermute | solution.py:120
  322.8 29.8 %collective-permute-start.45 = (bf16[2,48,2048]{2,1,0:T(8,128)(2,1)S(1)}, bf16[2,48,2048]{2,1,0:T(8,128)(2,1)S(1)}, u32[]{:S(2)}, u32[]{:S(2)}) collective-permute-start(bf16[2,48,2048]{2,1,0:T(8,128)(2,1)S(1)} %pad_maximum_fusion.14), channel_id=1, source_target_pairs={{0,4},{1,5},{2,6},{3,7},{4,0},{5,1},{6,2},{7,3},{8,12},{9,13},{10,... | collective-permute-start | bytes 1179656 | tf_op jit(solution)/shard_map/ppermute | solution.py:120
  322.9 29.7 %collective-permute-start.46 = (bf16[2,48,2048]{2,1,0:T(8,128)(2,1)S(1)}, bf16[2,48,2048]{2,1,0:T(8,128)(2,1)S(1)}, u32[]{:S(2)}, u32[]{:S(2)}) collective-permute-start(bf16[2,48,2048]{2,1,0:T(8,128)(2,1)S(1)} %dynamic-slice_bitcast_fusion.3), channel_id=1, source_target_pairs={{0,2},{1,3},{2,0},{3,1},{4,6},{5,7},{6,4},{7,5},{8,10},{9,11},{10,... | collective-permute-start | bytes 1179656 | tf_op jit(solution)/shard_map/ppermute | solution.py:120
  325.6 27.3 %collective-permute-start.47 = (bf16[2,2,48,2048]{3,2,1,0:T(8,128)(2,1)S(1)}, bf16[2,2,48,2048]{3,2,1,0:T(8,128)(2,1)S(1)}, u32[]{:S(2)}, u32[]{:S(2)}) collective-permute-start(bf16[2,2,48,2048]{3,2,1,0:T(8,128)(2,1)S(1)} %dynamic-slice_bitcast_fusion), channel_id=1, source_target_pairs={{0,1},{1,0},{2,3},{3,2},{4,5},{5,4},{6,7},{7,6},{8,9},{9,8},{10,11... | collective-permute-start | bytes 2359304 | tf_op jit(solution)/shard_map/ppermute | solution.py:120
  325.9 27.3 %collective-permute-start.48 = (bf16[1024,512]{1,0:T(8,128)(2,1)S(1)}, bf16[1024,512]{1,0:T(8,128)(2,1)S(1)}, u32[]{:S(2)}, u32[]{:S(2)}) collective-permute-start(bf16[1024,512]{1,0:T(8,128)(2,1)S(1)} %add_convert_fusion.2), channel_id=1, source_target_pairs={{0,16},{8,24},{16,0},{24,8},{1,17},{9,25},{17,1},{25,9},{2,18},{10... | collective-permute-start | bytes 3145736 | tf_op jit(solution)/shard_map/ppermute | solution.py:120
  328.6 23.9 %collective-permute-start.49 = (f32[46,512]{1,0:T(8,128)S(1)}, f32[46,512]{1,0:T(8,128)S(1)}, u32[]{:S(2)}, u32[]{:S(2)}) collective-permute-start(f32[46,512]{1,0:T(8,128)S(1)} %slice.298), channel_id=1, source_target_pairs={{0,16},{8,24},{16,0},{24,8},{1,17},{9,25},{17,1},{25,9},{2,18},{10... | collective-permute-start | bytes 282632 | tf_op jit(solution)/shard_map/ppermute | solution.py:120
  354.8 21.5 %collective-permute-start.50 = (bf16[2,48,2048]{2,1,0:T(8,128)(2,1)S(1)}, bf16[2,48,2048]{2,1,0:T(8,128)(2,1)S(1)}, u32[]{:S(2)}, u32[]{:S(2)}) collective-permute-start(bf16[2,48,2048]{2,1,0:T(8,128)(2,1)S(1)} %pad_maximum_fusion.15), channel_id=1, source_target_pairs={{0,4},{1,5},{2,6},{3,7},{4,0},{5,1},{6,2},{7,3},{8,12},{9,13},{10,... | collective-permute-start | bytes 1179656 | tf_op jit(solution)/shard_map/ppermute | solution.py:120
  355.6 25.8 %collective-permute-start.51 = (bf16[2,2,48,2048]{3,2,1,0:T(8,128)(2,1)S(1)}, bf16[2,2,48,2048]{3,2,1,0:T(8,128)(2,1)S(1)}, u32[]{:S(2)}, u32[]{:S(2)}) collective-permute-start(bf16[2,2,48,2048]{3,2,1,0:T(8,128)(2,1)S(1)} %pad_maximum_fusion.12), channel_id=1, source_target_pairs={{0,2},{1,3},{2,0},{3,1},{4,6},{5,7},{6,4},{7,5},{8,10},{9,11},{10,... | collective-permute-start | bytes 2359304 | tf_op jit(solution)/shard_map/ppermute | solution.py:120
  357.4 24.4 %collective-permute-start.52 = (bf16[2,2,48,2048]{3,2,1,0:T(8,128)(2,1)S(1)}, bf16[2,2,48,2048]{3,2,1,0:T(8,128)(2,1)S(1)}, u32[]{:S(2)}, u32[]{:S(2)}) collective-permute-start(bf16[2,2,48,2048]{3,2,1,0:T(8,128)(2,1)S(1)} %copy-done.51), channel_id=1, source_target_pairs={{0,1},{1,0},{2,3},{3,2},{4,5},{5,4},{6,7},{7,6},{8,9},{9,8},{10,11... | collective-permute-start | bytes 2359304 | tf_op jit(solution)/shard_map/ppermute | solution.py:120
  359.1 22.9 %collective-permute-start.53 = (bf16[512,1024]{1,0:T(8,128)(2,1)S(1)}, bf16[512,1024]{1,0:T(8,128)(2,1)S(1)}, u32[]{:S(2)}, u32[]{:S(2)}) collective-permute-start(bf16[512,1024]{1,0:T(8,128)(2,1)S(1)} %add_convert_fusion.1), channel_id=1, source_target_pairs={{0,16},{8,24},{16,0},{24,8},{1,17},{9,25},{17,1},{25,9},{2,18},{10... | collective-permute-start | bytes 3145736 | tf_op jit(solution)/shard_map/ppermute | solution.py:120
  360.8 15.5 %collective-permute-start.54 = (f32[46,512]{1,0:T(8,128)S(1)}, f32[46,512]{1,0:T(8,128)S(1)}, u32[]{:S(2)}, u32[]{:S(2)}) collective-permute-start(f32[46,512]{1,0:T(8,128)S(1)} %slice_add_fusion.1), channel_id=1, source_target_pairs={{0,1},{1,0},{2,3},{3,2},{4,5},{5,4},{6,7},{7,6},{8,9},{9,8},{10,11... | collective-permute-start | bytes 282632 | tf_op jit(solution)/shard_map/ppermute | solution.py:120
  383.6 21.3 %collective-permute-start.55 = (bf16[2,48,2048]{2,1,0:T(8,128)(2,1)S(1)}, bf16[2,48,2048]{2,1,0:T(8,128)(2,1)S(1)}, u32[]{:S(2)}, u32[]{:S(2)}) collective-permute-start(bf16[2,48,2048]{2,1,0:T(8,128)(2,1)S(1)} %pad_maximum_fusion.16), channel_id=1, source_target_pairs={{0,4},{1,5},{2,6},{3,7},{4,0},{5,1},{6,2},{7,3},{8,12},{9,13},{10,... | collective-permute-start | bytes 1179656 | tf_op jit(solution)/shard_map/ppermute | solution.py:120
  385.8 20.1 %collective-permute-start.56 = (bf16[2,48,2048]{2,1,0:T(8,128)(2,1)S(1)}, bf16[2,48,2048]{2,1,0:T(8,128)(2,1)S(1)}, u32[]{:S(2)}, u32[]{:S(2)}) collective-permute-start(bf16[2,48,2048]{2,1,0:T(8,128)(2,1)S(1)} %broadcast_select_fusion.18), channel_id=1, source_target_pairs={{0,2},{1,3},{2,0},{3,1},{4,6},{5,7},{6,4},{7,5},{8,10},{9,11},{10,... | collective-permute-start | bytes 1179656 | tf_op jit(solution)/shard_map/ppermute | solution.py:120
  387.6 19.3 %collective-permute-start.57 = (bf16[2,2,48,2048]{3,2,1,0:T(8,128)(2,1)S(1)}, bf16[2,2,48,2048]{3,2,1,0:T(8,128)(2,1)S(1)}, u32[]{:S(2)}, u32[]{:S(2)}) collective-permute-start(bf16[2,2,48,2048]{3,2,1,0:T(8,128)(2,1)S(1)} %broadcast_select_fusion.11), channel_id=1, source_target_pairs={{0,1},{1,0},{2,3},{3,2},{4,5},{5,4},{6,7},{7,6},{8,9},{9,8},{10,11... | collective-permute-start | bytes 2359304 | tf_op jit(solution)/shard_map/ppermute | solution.py:120
  389.2 21.9 %collective-permute-start.58 = (bf16[4,512,256]{2,1,0:T(8,128)(2,1)S(1)}, bf16[4,512,256]{2,1,0:T(8,128)(2,1)S(1)}, u32[]{:S(2)}, u32[]{:S(2)}) collective-permute-start(bf16[4,512,256]{2,1,0:T(8,128)(2,1)S(1)} %add_convert_fusion), channel_id=1, source_target_pairs={{0,16},{8,24},{16,0},{24,8},{1,17},{9,25},{17,1},{25,9},{2,18},{10... | collective-permute-start | bytes 3145736 | tf_op jit(solution)/shard_map/ppermute | solution.py:120
  412.3 28.0 %collective-permute-start.60 = (bf16[384,512]{1,0:T(8,128)(2,1)}, bf16[384,512]{1,0:T(8,128)(2,1)}, u32[]{:S(2)}, u32[]{:S(2)}) collective-permute-start(bf16[384,512]{1,0:T(8,128)(2,1)} %get-tuple-element.465), channel_id=1, source_target_pairs={{0,16},{8,24},{16,0},{24,8},{1,17},{9,25},{17,1},{25,9},{2,18},{10... | collective-permute-start | bytes 1179656 | tf_op jit(solution)/shard_map/ppermute | solution.py:120
  413.8 24.9 %collective-permute-start.61 = (bf16[2,2,48,2048]{3,2,1,0:T(8,128)(2,1)}, bf16[2,2,48,2048]{3,2,1,0:T(8,128)(2,1)}, u32[]{:S(2)}, u32[]{:S(2)}) collective-permute-start(bf16[2,2,48,2048]{3,2,1,0:T(8,128)(2,1)} %broadcast_select_fusion.10), channel_id=1, source_target_pairs={{0,1},{1,0},{2,3},{3,2},{4,5},{5,4},{6,7},{7,6},{8,9},{9,8},{10,11... | collective-permute-start | bytes 2359304 | tf_op jit(solution)/shard_map/ppermute | solution.py:120
  414.2 23.1 %collective-permute-start.62 = (bf16[2,48,2048]{2,1,0:T(8,128)(2,1)}, bf16[2,48,2048]{2,1,0:T(8,128)(2,1)}, u32[]{:S(2)}, u32[]{:S(2)}) collective-permute-start(bf16[2,48,2048]{2,1,0:T(8,128)(2,1)} %broadcast_select_fusion.17), channel_id=1, source_target_pairs={{0,2},{1,3},{2,0},{3,1},{4,6},{5,7},{6,4},{7,5},{8,10},{9,11},{10,... | collective-permute-start | bytes 1179656 | tf_op jit(solution)/shard_map/ppermute | solution.py:120
  415.4 20.9 %collective-permute-start.63 = (bf16[48,2048]{1,0:T(8,128)(2,1)S(1)}, bf16[48,2048]{1,0:T(8,128)(2,1)}, u32[]{:S(2)}, u32[]{:S(2)}) collective-permute-start(bf16[48,2048]{1,0:T(8,128)(2,1)S(1)} %shard_map.510), channel_id=1, source_target_pairs={{0,4},{1,5},{2,6},{3,7},{4,0},{5,1},{6,2},{7,3},{8,12},{9,13},{10,... | collective-permute-start | bytes 589832 | tf_op jit(solution)/shard_map/ppermute | solution.py:120
  417.7 17.6 %collective-permute-start.64 = (f32[46,512]{1,0:T(8,128)}, f32[46,512]{1,0:T(8,128)}, u32[]{:S(2)}, u32[]{:S(2)}) collective-permute-start(f32[46,512]{1,0:T(8,128)} %add.469), channel_id=1, source_target_pairs={{0,4},{1,5},{2,6},{3,7},{4,0},{5,1},{6,2},{7,3},{8,12},{9,13},{10,... | collective-permute-start | bytes 282632 | tf_op jit(solution)/shard_map/ppermute | solution.py:120
  441.0 28.3 %collective-permute-start.73 = (bf16[2,48,2048]{2,1,0:T(8,128)(2,1)S(1)}, bf16[2,48,2048]{2,1,0:T(8,128)(2,1)}, u32[]{:S(2)}, u32[]{:S(2)}) collective-permute-start(bf16[2,48,2048]{2,1,0:T(8,128)(2,1)S(1)} %broadcast_select_fusion.16), channel_id=1, source_target_pairs={{0,2},{1,3},{2,0},{3,1},{4,6},{5,7},{6,4},{7,5},{8,10},{9,11},{10,... | collective-permute-start | bytes 1179656 | tf_op jit(solution)/shard_map/ppermute | solution.py:120
  443.4 27.1 %collective-permute-start.72 = (bf16[2,2,48,2048]{3,2,1,0:T(8,128)(2,1)S(1)}, bf16[2,2,48,2048]{3,2,1,0:T(8,128)(2,1)}, u32[]{:S(2)}, u32[]{:S(2)}) collective-permute-start(bf16[2,2,48,2048]{3,2,1,0:T(8,128)(2,1)S(1)} %broadcast_select_fusion.9), channel_id=1, source_target_pairs={{0,1},{1,0},{2,3},{3,2},{4,5},{5,4},{6,7},{7,6},{8,9},{9,8},{10,11... | collective-permute-start | bytes 2359304 | tf_op jit(solution)/shard_map/ppermute | solution.py:120
  449.0 22.7 %collective-permute-start.70 = (bf16[384,512]{1,0:T(8,128)(2,1)}, bf16[384,512]{1,0:T(8,128)(2,1)S(1)}, u32[]{:S(2)}, u32[]{:S(2)}) collective-permute-start(bf16[384,512]{1,0:T(8,128)(2,1)} %get-tuple-element.405), channel_id=1, source_target_pairs={{0,8},{8,0},{16,24},{24,16},{1,9},{9,1},{17,25},{25,17},{2,10},{10... | collective-permute-start | bytes 1179656 | tf_op jit(solution)/shard_map/ppermute | solution.py:120
  449.5 23.0 %collective-permute-start.71 = (bf16[384,512]{1,0:T(8,128)(2,1)}, bf16[384,512]{1,0:T(8,128)(2,1)}, u32[]{:S(2)}, u32[]{:S(2)}) collective-permute-start(bf16[384,512]{1,0:T(8,128)(2,1)} %get-tuple-element.406), channel_id=1, source_target_pairs={{0,24},{8,16},{16,8},{24,0},{1,25},{9,17},{17,9},{25,1},{2,26},{10... | collective-permute-start | bytes 1179656 | tf_op jit(solution)/shard_map/ppermute | solution.py:120
  472.5 35.7 %collective-permute-start.74 = (bf16[2,2,48,2048]{3,2,1,0:T(8,128)(2,1)S(1)}, bf16[2,2,48,2048]{3,2,1,0:T(8,128)(2,1)}, u32[]{:S(2)}, u32[]{:S(2)}) collective-permute-start(bf16[2,2,48,2048]{3,2,1,0:T(8,128)(2,1)S(1)} %broadcast_select_fusion.8), channel_id=1, source_target_pairs={{0,1},{1,0},{2,3},{3,2},{4,5},{5,4},{6,7},{7,6},{8,9},{9,8},{10,11... | collective-permute-start | bytes 2359304 | tf_op jit(solution)/shard_map/ppermute | solution.py:120
  (135 other events, 1073.7 us)

commit v3 on v2

--- a/solution.py
+++ b/solution.py
@@ -123,7 +123,7 @@
 def sync(plain, steps):
     held = [vars(item) for item in steps]
     names = [
-        [name for name in ("values", "terms", "given") if item.get(name) is not None]
+        [name for name in ("values", "terms", "given", "moved") if item.get(name) is not None]
         for item in held
     ]
     plain, inner = lax.optimization_barrier(
@@ -174,14 +174,15 @@
             self.terms.append(swap(self.given, self.axis, bit))
             self.given = None
 
+    def own(self):
+        own = self.terms[-1].shape[self.dim]
+        return sum(
+            lax.slice_in_dim(term, 0, own, axis=self.dim).astype(jnp.float32)
+            for term in self.terms
+        )
+
     def squares(self):
-        own = self.terms[-1].shape[self.dim]
-        return square_sum(
-            sum(
-                lax.slice_in_dim(term, 0, own, axis=self.dim).astype(jnp.float32)
-                for term in self.terms
-            )
-        )
+        return square_sum(self.own())
 
 
 class Halves:
@@ -206,11 +207,10 @@
 
 def step_both(scatter, stage, gather, gather_stage):
     for bit in scatter.order[stage]:
-        kept, given = scatter.split(bit)
-        both = jnp.stack([given, gather.values])
-        moved = swap(both, scatter.axis, bit)
-        scatter.add(kept, moved[0])
-        gather.values = gather.join(moved[1], bit)
+        given = scatter.split(bit)
+        gather.settle()
+        moved = swap(jnp.stack([given, gather.values]), scatter.axis, bit)
+        scatter.moved, gather.moved, gather.bit = moved[0], moved[1], bit
 
 
 def square_sum(values):
@@ -243,50 +243,70 @@
     def __init__(self, values, axis, order):
         self.values, self.axis, self.order = unfold_rows(values, axis, 0), axis, list(order)
         self.places = bits_of(lax.axis_size(axis))
+        self.moved = None
 
     def split(self, bit):
+        self.settle()
         dim = self.places.index(bit)
         self.places = [place for place in self.places if place != bit]
         side = (lax.axis_index(self.axis) & bit) // bit
-        return (
-            lax.dynamic_index_in_dim(self.values, side, dim, False),
-            lax.dynamic_index_in_dim(self.values, 1 - side, dim, False),
-        )
-
-    def add(self, kept, moved):
-        values = kept.astype(jnp.float32) + moved.astype(jnp.float32)
-        self.values = values.astype(jnp.bfloat16) if self.places else values
+        given = lax.dynamic_index_in_dim(self.values, 1 - side, dim, False)
+        self.values = lax.dynamic_index_in_dim(self.values, side, dim, False)
+        return given
+
+    def settle(self):
+        if self.moved is not None:
+            values = self.values.astype(jnp.float32) + self.moved.astype(jnp.float32)
+            self.values = values.astype(jnp.bfloat16) if self.places else values
+            self.moved = None
 
     def step(self, stage):
         for bit in self.order[stage]:
-            kept, given = self.split(bit)
-            self.add(kept, swap(given, self.axis, bit))
+            self.moved = swap(self.split(bit), self.axis, bit)
+
+    def result(self):
+        self.settle()
+        return self.values
 
 
 class Gather:
     def __init__(self, values, axis, order, dim=0):
         self.values, self.axis, self.order, self.dim = values, axis, list(order), dim
-        self.places = []
+        self.places, self.moved, self.bit = [], None, None
 
     def step(self, stage):
         for bit in self.order[stage]:
-            moved = swap(self.values, self.axis, bit)
-            self.values = self.join(moved, bit)
-
-    def join(self, moved, bit):
-        known = self.places + [bit]
+            self.settle()
+            self.moved, self.bit = swap(self.values, self.axis, bit), bit
+
+    def settle(self):
+        if self.moved is None:
+            return
+        known = self.places + [self.bit]
         self.places = [place for place in bits_of(lax.axis_size(self.axis)) if place in known]
-        dim = self.dim + self.places.index(bit)
-        side = (lax.axis_index(self.axis) & bit) // bit
-        shape = list(moved.shape)
+        dim = self.dim + self.places.index(self.bit)
+        side = (lax.axis_index(self.axis) & self.bit) // self.bit
+        shape = list(self.moved.shape)
         shape.insert(dim, 2)
-        return jnp.where(
+        self.values = jnp.where(
             lax.broadcasted_iota(jnp.int32, shape, dim) == side,
             jnp.expand_dims(self.values, dim),
-            jnp.expand_dims(moved, dim),
+            jnp.expand_dims(self.moved, dim),
         )
+        self.moved = None
+
+    def place_last(self, whole, index):
+        spot = bits_of(lax.axis_size(self.axis)).index(self.bit)
+        side = (lax.axis_index(self.axis) & self.bit) // self.bit
+        for values, at in ((self.values, side), (self.moved, 1 - side)):
+            block = jnp.expand_dims(values, spot)[None]
+            starts = [0] * block.ndim
+            starts[0], starts[spot + 1] = index, at
+            whole = lax.dynamic_update_slice(whole, block, starts)
+        return whole
 
     def result(self):
+        self.settle()
         return fold_rows(self.values, self.axis, self.dim)
 
 
@@ -294,6 +314,122 @@
     bits = bits_of(lax.axis_size(axis))
     near = len(bits) - 2
     return bits[:near], bits[near : near + 1], bits[near + 1 :]
+
+
+def light():
+    return pl.CostEstimate(flops=1, bytes_accessed=1, transcendentals=0)
+
+
+def join_kernel(*refs):
+    out_ref = refs[-1]
+    cols = refs[0].shape[-1]
+    for index, ref in enumerate(refs[:-1]):
+        out_ref[:, :, index * cols : (index + 1) * cols] = ref[...]
+
+
+def join_blocks(blocks):
+    shape = blocks[0].shape
+    return pl.pallas_call(
+        join_kernel,
+        out_shape=jax.ShapeDtypeStruct(
+            shape[:-1] + (shape[-1] * len(blocks),), blocks[0].dtype
+        ),
+        cost_estimate=light(),
+    )(*blocks)
+
+
+def outer_kernel(pairs, *refs):
+    for left, right, target in pairs:
+        left_ref, right_ref = refs[left], refs[right]
+        value = contract_rows(left_ref[...].reshape(left_ref.shape[-2:]), right_ref[...])
+        refs[target][...] = value.astype(jnp.bfloat16)
+
+
+def outer_call(operands, specs, pairs, grid, out_rows, out_cols, tile):
+    out = pl.BlockSpec((tile, out_cols), lambda i: (i, 0))
+    shape = jax.ShapeDtypeStruct((out_rows, out_cols), jnp.bfloat16)
+    return pl.pallas_call(
+        functools.partial(outer_kernel, pairs),
+        grid=grid,
+        in_specs=specs,
+        out_specs=[out, out],
+        out_shape=[shape, shape],
+        compiler_params=pltpu.CompilerParams(vmem_limit_bytes=16 << 20),
+        cost_estimate=light(),
+    )(*operands)
+
+
+def project_grads(hidden, kept, given):
+    tokens, units = hidden.shape
+    tile = 256
+    whole = pl.BlockSpec(kept.shape, lambda i: (0, 0))
+    return outer_call(
+        (hidden, kept, given),
+        [pl.BlockSpec((tokens, tile), lambda i: (0, i)), whole, whole],
+        ((0, 1, 3), (0, 2, 4)),
+        (units // tile,),
+        units,
+        kept.shape[1],
+        tile,
+    )
+
+
+def expand_grads(kept, given, upper):
+    count, tokens, width = kept.shape
+    tile = 256
+    part = pl.BlockSpec((1, tokens, tile), lambda i: (count - 1, 0, i))
+    return outer_call(
+        (kept, given, upper),
+        [part, part, pl.BlockSpec(upper.shape, lambda i: (0, 0))],
+        ((0, 2, 3), (1, 2, 4)),
+        (width // tile,),
+        width,
+        upper.shape[1],
+        tile,
+    )
+
+
+def attend_grads_kernel(
+    kept_ref, given_ref, back_ref, out_kept_ref, out_given_ref, heads_ref, *outs
+):
+    last = pl.program_id(0) == pl.num_programs(0) - 1
+    for left_ref, other_ref, target_ref in (
+        (kept_ref, out_kept_ref, outs[0]),
+        (given_ref, out_given_ref, outs[1]),
+    ):
+
+        @pl.when(jnp.logical_not(last))
+        def inner(left_ref=left_ref, target_ref=target_ref):
+            target_ref[0] = contract_rows(left_ref[0], back_ref[0]).astype(jnp.bfloat16)
+
+        @pl.when(last)
+        def outer(other_ref=other_ref, target_ref=target_ref):
+            target_ref[0] = contract_rows(other_ref[...], heads_ref[...]).astype(jnp.bfloat16)
+
+
+def attend_grads_call(kept, given, back, out_kept, out_given, heads):
+    count, tokens, width = kept.shape
+    units = heads.shape[1]
+    part = pl.BlockSpec((1, tokens, width), lambda c: (jnp.minimum(c, count - 2), 0, 0))
+    whole = pl.BlockSpec((tokens, width), lambda c: (0, 0))
+    out = pl.BlockSpec((1, width, units), lambda c: (c, 0, 0))
+    shape = jax.ShapeDtypeStruct((count, width, units), jnp.bfloat16)
+    return pl.pallas_call(
+        attend_grads_kernel,
+        grid=(count,),
+        in_specs=[
+            part,
+            part,
+            pl.BlockSpec((1, tokens, units), lambda c: (jnp.minimum(c, count - 2), 0, 0)),
+            whole,
+            whole,
+            pl.BlockSpec((tokens, units), lambda c: (0, 0)),
+        ],
+        out_specs=[out, out],
+        out_shape=[shape, shape],
+        compiler_params=pltpu.CompilerParams(vmem_limit_bytes=20 << 20),
+        cost_estimate=light(),
+    )(kept, given, back, out_kept, out_given, heads)
 
 
 def adam_kernel(rates, count, flip, factor_ref, *refs):
@@ -327,10 +463,8 @@
         in_specs=[pl.BlockSpec(memory_space=pltpu.SMEM)] + term_specs + [own] * 3,
         out_specs=[own] * 4,
         out_shape=[wide, wide, wide, jax.ShapeDtypeStruct(master.shape, jnp.bfloat16)],
-        compiler_params=pltpu.CompilerParams(vmem_limit_bytes=60 << 20),
-        cost_estimate=pl.CostEstimate(
-            flops=20 * master.size, bytes_accessed=32 * master.size, transcendentals=0
-        ),
+        compiler_params=pltpu.CompilerParams(vmem_limit_bytes=20 << 20),
+        cost_estimate=light(),
     )(factor.reshape(1), *terms, master, first_moment, second_moment)
 
 
@@ -372,12 +506,8 @@
             out_specs=[half, half],
         ),
         out_shape=[shape, shape],
-        compiler_params=pltpu.CompilerParams(vmem_limit_bytes=56 << 20),
-        cost_estimate=pl.CostEstimate(
-            flops=10 * count * tokens * width,
-            bytes_accessed=4 * count * tokens * width,
-            transcendentals=0,
-        ),
+        compiler_params=pltpu.CompilerParams(vmem_limit_bytes=14 << 20),
+        cost_estimate=light(),
     )(place, layer_inputs, gains[:, None, :], biases[:, None, :])
 
 
@@ -461,12 +591,8 @@
             jax.ShapeDtypeStruct((3, tokens, width), jnp.bfloat16),
             jax.ShapeDtypeStruct((tokens, width), jnp.bfloat16),
         ],
-        compiler_params=pltpu.CompilerParams(vmem_limit_bytes=32 << 20),
-        cost_estimate=pl.CostEstimate(
-            flops=4 * tokens * tokens * width,
-            bytes_accessed=20 * tokens * width,
-            transcendentals=2 * tokens * tokens,
-        ),
+        compiler_params=pltpu.CompilerParams(vmem_limit_bytes=16 << 20),
+        cost_estimate=light(),
     )(proj, *tables, ids[:, None], ids[None, :])
 
 
@@ -479,12 +605,8 @@
         in_specs=[triple, heads] + shared,
         out_specs=triple,
         out_shape=jax.ShapeDtypeStruct((3, tokens, width), jnp.bfloat16),
-        compiler_params=pltpu.CompilerParams(vmem_limit_bytes=32 << 20),
-        cost_estimate=pl.CostEstimate(
-            flops=10 * tokens * tokens * width,
-            bytes_accessed=14 * tokens * width,
-            transcendentals=2 * tokens * tokens,
-        ),
+        compiler_params=pltpu.CompilerParams(vmem_limit_bytes=20 << 20),
+        cost_estimate=light(),
     )(turned, grads, *tables, ids[:, None], ids[None, :])
 
 
@@ -570,14 +692,17 @@
             jax.ShapeDtypeStruct((1, width), jnp.float32),
         ],
         compiler_params=pltpu.CompilerParams(vmem_limit_bytes=32 << 20),
-        cost_estimate=pl.CostEstimate(
-            flops=60 * rows * width, bytes_accessed=30 * rows * width, transcendentals=0
-        ),
+        cost_estimate=light(),
     )(branch, inputs, stored, entry, cotangent, valid, gain, mixer_in, mixer_out)
 
 
 def history_kernel(owners, count, place_ref, weights_ref, cotangent_ref, *back_refs):
     cols = back_refs[0].shape[2]
+    spots = [
+        (target_ref, layer)
+        for target_ref in back_refs
+        for layer in range(target_ref.shape[0])
+    ]
     weights = weights_ref[...]
     for index in range(owners):
         spot = lane_block(place_ref, index, cols)
@@ -586,7 +711,8 @@
             for outer in range(cotangent_ref.shape[0])
         ]
         for layer in range(count - 1):
-            back_refs[index][layer] = sum(
+            target_ref, near = spots[index * (count - 1) + layer]
+            target_ref[near] = sum(
                 weights[:, outer * count + layer : outer * count + layer + 1] * upstream[outer]
                 for outer in range(len(upstream))
             ).astype(jnp.bfloat16)
@@ -596,6 +722,9 @@
     outer, tokens, width = cotangent.shape
     total = weights.shape[1]
     count = total // outer
+    cuts = []
+    for index in feature_order(owners):
+        cuts += [count - 2, 1] if index > 1 else [count - 1]
     tile = 128
     return pl.pallas_call(
         functools.partial(history_kernel, owners, count),
@@ -607,20 +736,16 @@
                 pl.BlockSpec((outer, tile, width), lambda i, place_ref: (0, i, 0)),
             ],
             out_specs=[
-                pl.BlockSpec((count - 1, tile, width // owners), lambda i, place_ref: (0, i, 0))
-            ]
-            * owners,
+                pl.BlockSpec((layers, tile, width // owners), lambda i, place_ref: (0, i, 0))
+                for layers in cuts
+            ],
         ),
         out_shape=[
-            jax.ShapeDtypeStruct((count - 1, tokens, width // owners), jnp.bfloat16)
-        ]
-        * owners,
-        compiler_params=pltpu.CompilerParams(vmem_limit_bytes=56 << 20),
-        cost_estimate=pl.CostEstimate(
-            flops=8 * outer * tokens * width,
-            bytes_accessed=14 * tokens * width,
-            transcendentals=0,
-        ),
+            jax.ShapeDtypeStruct((layers, tokens, width // owners), jnp.bfloat16)
+            for layers in cuts
+        ],
+        compiler_params=pltpu.CompilerParams(vmem_limit_bytes=20 << 20),
+        cost_estimate=light(),
     )(place, weights, cotangent)
 
 
@@ -658,12 +783,8 @@
             out_specs=pl.BlockSpec((outer, tile, width), lambda i, place_ref: (0, i, 0)),
         ),
         out_shape=jax.ShapeDtypeStruct((outer, tokens, width), jnp.bfloat16),
-        compiler_params=pltpu.CompilerParams(vmem_limit_bytes=32 << 20),
-        cost_estimate=pl.CostEstimate(
-            flops=8 * outer * tokens * width,
-            bytes_accessed=16 * tokens * width,
-            transcendentals=0,
-        ),
+        compiler_params=pltpu.CompilerParams(vmem_limit_bytes=24 << 20),
+        cost_estimate=light(),
     )(place, weights, newest, *stored)
 
 
@@ -702,12 +823,8 @@
             out_specs=pl.BlockSpec((1, 2, width), lambda c, i, place_ref: (c, 0, 0)),
         ),
         out_shape=jax.ShapeDtypeStruct((count, 2, width), jnp.float32),
-        compiler_params=pltpu.CompilerParams(vmem_limit_bytes=32 << 20),
-        cost_estimate=pl.CostEstimate(
-            flops=12 * count * tokens * width,
-            bytes_accessed=4 * count * tokens * width,
-            transcendentals=0,
-        ),
+        compiler_params=pltpu.CompilerParams(vmem_limit_bytes=12 << 20),
+        cost_estimate=light(),
     )(place, grads, layer_inputs)
 
 
@@ -743,10 +860,8 @@
             out_specs=whole,
         ),
         out_shape=jax.ShapeDtypeStruct((rows, width), jnp.bfloat16),
-        compiler_params=pltpu.CompilerParams(vmem_limit_bytes=32 << 20),
-        cost_estimate=pl.CostEstimate(
-            flops=15 * rows * width, bytes_accessed=10 * rows * width, transcendentals=0
-        ),
+        compiler_params=pltpu.CompilerParams(vmem_limit_bytes=12 << 20),
+        cost_estimate=light(),
     )(place, *given)
 
 
@@ -810,29 +925,13 @@
     back_order = (far, side_bits, near)
     cross_order = (near, far, side_bits)
 
-    small = jnp.concatenate(
-        [
-            norms_master,
-            mixer_in_master.T,
-            jnp.pad(mixer_out_master, ((0, 0), (0, cols - MIXH))),
-        ],
-        axis=0,
-    ).astype(bf16_type)
-    small_half = gather_half(small, "dp", 1)
-    attend_low = jnp.concatenate(
-        [attend_in_master.astype(bf16_type), attend_out_master.astype(bf16_type).T[None]], axis=0
-    )
-    small_half, attend_low, history_late, entry_late, expand_late = sync(
-        [small_half, attend_low, history, grad_entry, expand_master], []
-    )
-    attend_kept = gather_half(attend_low, "dp", 1)
     early_rows = [
         jnp.concatenate(
             [
                 lax.dynamic_slice_in_dim(
                     values, (me ^ index) * tokens_here + share_start, share_rows, 1
                 )
-                for values in (history_late, entry_late[None])
+                for values in (history, grad_entry[None])
             ],
             axis=0,
         )
@@ -841,34 +940,40 @@
     early_rows = [
         rows if index == 0 else swap(rows, "dp", index) for rows, index in zip(early_rows, order)
     ]
-    expand_low = expand_late.astype(bf16_type)
-    small_given = swap(small_half, "dp", 1)
-    small_whole = jnp.concatenate([small_half, small_given], axis=1)
-    norm_vals = small_whole[0:9].astype(float_type)
-    mixer_in_low = small_whole[9 : 9 + MIXH]
-    out_rows = small_whole[9 + MIXH :]
-    mixer_out_low = jnp.zeros((owners, mixers, MIXH), bf16_type)
-    for spot, index in enumerate(order):
-        mixer_out_low = lax.dynamic_update_index_in_dim(
-            mixer_out_low, out_rows[:, spot * cols : spot * cols + MIXH], me ^ index, 0
-        )
-    mixer_out_low = mixer_out_low.reshape(owners * mixers, MIXH)
-    normed_kept, normed_given = norm_forward(
-        layer_inputs, norm_vals[0:4], norm_vals[4:8], place, owners
-    )
-    early_rows, attend_kept, normed_kept, normed_given, expand_low, project_late = sync(
-        [early_rows, attend_kept, normed_kept, normed_given, expand_low, project_master], []
-    )
-
-    early = jnp.concatenate(early_rows, axis=-1)
+    norms_half = gather_half(norms_master.astype(bf16_type), "dp", 1)
+    attend_low = jnp.concatenate(
+        [attend_in_master.astype(bf16_type), attend_out_master.astype(bf16_type).T[None]], axis=0
+    )
+    norms_half, attend_low, early_rows, expand_late, mixer_in_late, mixer_out_late = sync(
+        [norms_half, attend_low, early_rows, expand_master, mixer_in_master, mixer_out_master], []
+    )
+
+    attend_kept = gather_half(attend_low, "dp", 1)
+    early = join_blocks(early_rows)
     stored_share = early[:-1]
     layer_count = stored_share.shape[0] + 1
     stored_most = Gather(stored_share[:-1], "tensor", back_order, 1)
     stored_last = Gather(stored_share[-1:], "tensor", cross_order, 1)
+    stored_most.step(0)
+    stored_last.step(0)
+    expand_low = expand_late.astype(bf16_type)
+    norms_given = swap(norms_half, "dp", 1)
+    norm_vals = jnp.concatenate([norms_half, norms_given], axis=1).astype(float_type)
+    normed_kept, normed_given = norm_forward(
+        layer_inputs, norm_vals[0:4], norm_vals[4:8], place, owners
+    )
+    attend_kept, normed_kept, normed_given, expand_low, project_late = sync(
+        [attend_kept, normed_kept, normed_given, expand_low, project_master],
+        [stored_most, stored_last],
+    )
+
+    small = jnp.concatenate(
+        [mixer_in_late.T, jnp.pad(mixer_out_late, ((0, 0), (0, cols - MIXH)))], axis=0
+    ).astype(bf16_type)
+    small_half = gather_half(small, "dp", 1)
     expand_kept = gather_half(expand_low, "dp", 0)
     attend_given = swap(attend_kept, "dp", 1)
-    stored_most.step(0)
-    stored_last.step(0)
+    stored_most.step(1)
     proj_kept = jnp.einsum(
         "ctd,cde->cte", normed_kept[0:3], attend_kept[0:3], preferred_element_type=float_type
     )
@@ -880,8 +985,18 @@
         jnp.pad(sine_table, ((0, 0), (half, HDIM - ROT))),
     )
     project_low = project_late.astype(bf16_type)
-    expand_kept, attend_given, proj_kept, project_low, tables, layer_late, cotangent_late = sync(
+    (
+        small_half,
+        expand_kept,
+        attend_given,
+        proj_kept,
+        project_low,
+        tables,
+        layer_late,
+        cotangent_late,
+    ) = sync(
         [
+            small_half,
             expand_kept,
             attend_given,
             proj_kept,
@@ -893,10 +1008,27 @@
         [stored_most, stored_last],
     )
 
+    small_whole = jnp.concatenate([small_half, swap(small_half, "dp", 1)], axis=1)
+    mixer_in_low = small_whole[0:MIXH]
+    out_rows = small_whole[MIXH:]
+    mixer_out_low = jnp.zeros((owners, mixers, MIXH), bf16_type)
+    for spot, index in enumerate(order):
+        mixer_out_low = lax.dynamic_update_index_in_dim(
+            mixer_out_low, out_rows[:, spot * cols : spot * cols + MIXH], me ^ index, 0
+        )
+    mixer_out_low = mixer_out_low.reshape(owners * mixers, MIXH)
     project_kept = gather_half(project_low, "dp", 1)
     expand_given = swap(expand_kept, "dp", 1)
-    stored_most.step(1)
     stored_last.step(1)
+    stored_most.settle()
+    stored_pair = [
+        Gather(stored_most.values[index : index + 1], "tensor", back_order, 1)
+        for index in range(layer_count - 2)
+    ]
+    for item in stored_pair:
+        item.places = list(stored_most.places)
+    for item in stored_pair[:1]:
+        item.step(2)
     proj = proj_kept + jnp.einsum(
         "ctd,cde->cte", normed_given[0:3], attend_given[0:3], preferred_element_type=float_type
     )
@@ -906,6 +1038,8 @@
     input_share = reorder(own_rows(layer_late, 1))
     cotangent_share = reorder(own_rows(cotangent_late, 1))
     (
+        mixer_in_low,
+        mixer_out_low,
         project_kept,
         expand_given,
         turned,
@@ -915,6 +1049,8 @@
         cotangent_share,
     ) = sync(
         [
+            mixer_in_low,
+            mixer_out_low,
             project_kept,
             expand_given,
             turned,
@@ -923,13 +1059,15 @@
             input_share,
             cotangent_share,
         ],
-        [stored_most, stored_last],
+        [stored_last] + stored_pair,
     )
 
     out_kept, out_given = attend_kept[3], attend_given[3]
     project_given = swap(project_kept, "dp", 1)
     upper = upper_kept + jnp.dot(normed_given[3], expand_given, preferred_element_type=float_type)
+    phi, density = gelu_parts(upper)
     hidden = exact_gelu(upper).astype(bf16_type)
+    slope = phi + upper * density
     branch_kept = Scatter(
         (
             contract_cols(heads_out, out_kept)
@@ -946,15 +1084,10 @@
         "tensor",
         in_first,
     )
-    for stage in range(2):
+    for stage in range(3):
         branch_kept.step(stage)
         branch_given.step(stage)
-    (upper,) = sync([upper], [branch_kept, branch_given])
-    branch_kept.step(2)
-    branch_given.step(2)
-    branch = jnp.concatenate([branch_kept.values, branch_given.values], axis=-1)
-    phi, density = gelu_parts(upper)
-    slope = phi + upper * density
+    branch = jnp.concatenate([branch_kept.result(), branch_given.result()], axis=-1)
     branch, slope = sync([branch, slope], [])
 
     newest, grad_newest, sent_kept, sent_given, grad_mixer_in, grad_mixer_out, mixer_gain = mix(
@@ -983,10 +1116,15 @@
     ].astype(float_type)
     newest_all = Gather(newest, "tensor", back_order)
     grad_kept, grad_given, mix_weights = sync(
-        [grad_kept, grad_given, mix_weights], [newest_all, stored_last, stored_most]
-    )
-
-    history_pieces = list(history_back(mix_weights, cotangent_late, place, owners))
+        [grad_kept, grad_given, mix_weights], [newest_all, stored_last] + stored_pair
+    )
+
+    history_pieces = history_back(mix_weights, cotangent_late, place, owners)
+    history_pieces = list(history_pieces)
+    history_front, history_last = [], []
+    for index in order:
+        history_front.append(history_pieces.pop(0))
+        history_last.append(history_pieces.pop(0) if index > 1 else None)
 
     def send_far(pieces, which):
         for spot in which:
@@ -995,13 +1133,7 @@
     far_spots = [spot for spot in range(owners) if order[spot] > 1]
     near_spots = [spot for spot in range(owners) if order[spot] == 1]
     first_far, last_far = far_spots[: len(far_spots) // 2], far_spots[len(far_spots) // 2 :]
-    stored_pair = [
-        Gather(stored_most.values[index : index + 1], "tensor", back_order, 1)
-        for index in range(layer_count - 2)
-    ]
-    for item in stored_pair:
-        item.places = list(stored_most.places)
-    for item in stored_pair[:1]:
+    for item in stored_pair[1:]:
         item.step(2)
     stored_last.step(2)
     newest_all.step(0)
@@ -1014,14 +1146,10 @@
         ],
         axis=-1,
     )
-    grad_project = Reduce(
-        contract_rows(hidden, grad_kept).astype(bf16_type),
-        contract_rows(hidden, grad_given).astype(bf16_type),
-        "dp",
-        1,
-    )
+    grad_project = Reduce(*project_grads(hidden, grad_kept, grad_given), "dp", 1)
     (
-        history_pieces,
+        history_front,
+        history_last,
         grad_normed_ffn,
         grad_upper,
         grad_kept,
@@ -1029,14 +1157,24 @@
         out_kept,
         out_given,
     ) = sync(
-        [history_pieces, grad_normed_ffn, grad_upper, grad_kept, grad_given, out_kept, out_given],
+        [
+            history_front,
+            history_last,
+            grad_normed_ffn,
+            grad_upper,
+            grad_kept,
+            grad_given,
+            out_kept,
+            out_given,
+        ],
         [newest_all, stored_last, grad_project] + stored_pair,
     )
 
+    summed = [None, None, None, Scatter(grad_normed_ffn, "tensor", in_first)]
+    summed[3].step(0)
     newest_all.step(1)
-    for item in stored_pair[1:]:
-        item.step(2)
-    send_far(history_pieces, near_spots)
+    send_far(history_front, first_far)
+    send_far(history_front, near_spots)
     grad_project.near()
     grad_heads = (
         jnp.dot(grad_kept, out_kept, preferred_element_type=float_type)
@@ -1053,46 +1191,64 @@
         )
         for index in range(3)
     ]
-    attend_grads = [
-        jnp.concatenate(
-            [
-                jnp.einsum(
-                    "ctd,cte->cde", normed[0:3], grad_proj, preferred_element_type=float_type
-                ).astype(bf16_type),
-                contract_rows(grads, heads_out).astype(bf16_type)[None],
-            ],
-            axis=0,
-        )
-        for normed, grads in ((normed_kept, grad_kept), (normed_given, grad_given))
-    ]
-    grad_attend = Reduce(*attend_grads, "dp", 1)
-    grad_expand = Reduce(
-        contract_rows(normed_kept[3], grad_upper).astype(bf16_type),
-        contract_rows(normed_given[3], grad_upper).astype(bf16_type),
+    grad_attend = Reduce(
+        *attend_grads_call(normed_kept, normed_given, grad_proj, grad_kept, grad_given, heads_out),
         "dp",
-        0,
-    )
-    grad_normed_attend, grad_normed_ffn, history_pieces, layer_late = sync(
-        [grad_normed_attend, grad_normed_ffn, history_pieces, layer_late],
-        [grad_attend, grad_expand, grad_project, newest_all] + stored_pair,
-    )
-
-    summed = [
-        Scatter(grad_normed_attend[index], "tensor", out_first) for index in range(3)
-    ] + [Scatter(grad_normed_ffn, "tensor", in_first)]
+        1,
+    )
+    grad_expand = Reduce(*expand_grads(normed_kept, normed_given, grad_upper), "dp", 0)
+    grad_normed_attend, grad_normed_ffn, history_front, history_last, layer_late = sync(
+        [grad_normed_attend, grad_normed_ffn, history_front, history_last, layer_late],
+        [grad_attend, grad_expand, grad_project, newest_all, summed[3]] + stored_pair,
+    )
+
+    for index in range(3):
+        summed[index] = Scatter(grad_normed_attend[index], "tensor", out_first)
     summed[0].step(0)
-    summed[3].step(0)
-    send_far(history_pieces, first_far)
+    summed[3].step(1)
+    send_far(history_front, last_far)
     grad_attend.near()
     grad_expand.near()
+    all_grads = list(enumerate(grad_normed_attend + [grad_normed_ffn]))
     sums = [
-        norm_sums(grads[None], layer_late, index, place, owners)[0]
-        for index, grads in enumerate(grad_normed_attend + [grad_normed_ffn])
+        norm_sums(grads[None], layer_late, index, place, owners)[0] for index, grads in all_grads[:2]
     ]
-    sums, history_pieces = sync(
-        [sums, history_pieces], summed + [newest_all, grad_project, grad_attend, grad_expand]
-    )
-
+    grad_project.prepare()
+    sums, all_grads[2:], history_front, history_last = sync(
+        [sums, [grads for index, grads in all_grads[2:]], history_front, history_last],
+        summed + [newest_all, grad_project, grad_attend, grad_expand],
+    )
+
+    sums = sums + [
+        norm_sums(grads[None], layer_late, index + 2, place, owners)[0]
+        for index, grads in enumerate(all_grads[2:])
+    ]
+    summed[1].step(0)
+    summed[3].step(2)
+    summed[0].step(1)
+    grad_project.far()
+    sums, history_front, history_last = sync(
+        [sums, history_front, history_last], summed + [grad_project, grad_expand, grad_attend]
+    )
+
+    def back(index):
+        return Gather(
+            back_share(
+                summed[index].result(),
+                input_share[index],
+                norm_vals[index][None],
+                grad_newest if index == 3 else None,
+                place,
+                owners,
+            ),
+            "tensor",
+            back_order,
+        )
+
+    gathered = [None, None, None, back(3)]
+    summed[2].step(0)
+    summed[1].step(1)
+    step_both(summed[0], 2, gathered[3], 0)
     norm_pack = jnp.stack(sums)
     own_rows_out = jnp.stack(
         [
@@ -1115,39 +1271,12 @@
         ),
         "dp",
     )
-    pack.near()
-    summed[1].step(0)
-    summed[3].step(1)
-    summed[3].step(2)
-    summed[0].step(1)
-    send_far(history_pieces, last_far)
-    grad_project.prepare()
-    (history_pieces,) = sync(
-        [history_pieces], summed + [grad_project, grad_expand, grad_attend, pack]
-    )
-
-    def back(index):
-        return Gather(
-            back_share(
-                summed[index].values,
-                input_share[index],
-                norm_vals[index][None],
-                grad_newest if index == 3 else None,
-                place,
-                owners,
-            ),
-            "tensor",
-            back_order,
-        )
-
-    gathered = [None, None, None, back(3)]
-    summed[2].step(0)
-    summed[1].step(1)
-    step_both(summed[0], 2, gathered[3], 0)
-    grad_project.far()
+    send_far(history_last, far_spots)
     grad_expand.prepare()
-    pack.far()
-    sync([], summed[0:3] + [gathered[3], grad_expand, grad_project, grad_attend, newest_all, pack])
+    project_squares, history_last = sync(
+        [grad_project.squares(), history_last],
+        summed[0:3] + [gathered[3], grad_expand, grad_project, grad_attend, newest_all, pack],
+    )
 
     gathered[0] = back(0)
     newest_all.step(2)
@@ -1155,9 +1284,21 @@
     step_both(summed[1], 2, gathered[0], 0)
     grad_expand.far()
     grad_attend.prepare()
-    pack.rows("tensor", near)
-    (project_squares,) = sync(
-        [grad_project.squares()],
+    pack.near()
+    pack.far()
+    grad_inputs = jnp.zeros(
+        (4,) + (2,) * len(bits_of(tensor_size)) + (share_rows, width), bf16_type
+    )
+    grad_history = jnp.zeros(history.shape, bf16_type)
+    for spot, index in enumerate(order):
+        first_row = (me ^ index) * tokens_here
+        for pieces, layer in ((history_front, 0), (history_last, layer_count - 2)):
+            if pieces[spot] is not None:
+                grad_history = lax.dynamic_update_slice(
+                    grad_history, pieces[spot], (layer, first_row, 0)
+                )
+    grad_history, grad_inputs = sync(
+        [grad_history, grad_inputs],
         summed[1:3] + [gathered[0], gathered[3], newest_all, grad_attend, grad_expand, pack],
     )
 
@@ -1166,11 +1307,12 @@
     step_both(summed[2], 2, gathered[1], 0)
     gathered[0].step(1)
     grad_attend.far()
-    pack.rows("tensor", side_bits)
+    pack.rows("tensor", near)
     newest_whole = newest_all.result()
     newest_stored = [item.result()[0] for item in stored_pair] + [stored_last.result()[0]]
-    expand_squares, newest_whole, newest_stored, mix_weights = sync(
-        [grad_expand.squares(), newest_whole, newest_stored, mix_weights],
+    next_inputs = next_layer(mix_weights, newest_stored, newest_whole, place, owners)
+    expand_squares, newest_whole, next_inputs = sync(
+        [grad_expand.squares(), newest_whole, next_inputs],
         [summed[2], gathered[0], gathered[1], gathered[3], grad_attend, pack],
     )
 
@@ -1178,19 +1320,17 @@
     gathered[0].step(2)
     gathered[2].step(0)
     gathered[1].step(1)
+    pack.rows("tensor", side_bits)
     pack.rows("tensor", far)
     entry_pieces = [newest_whole[:, spot * cols : (spot + 1) * cols] for spot in range(owners)]
     send_far(entry_pieces, first_far)
-    next_inputs = next_layer(mix_weights, newest_stored, newest_whole, place, owners)
-    attend_squares, entry_pieces, next_inputs = sync(
-        [grad_attend.squares(), entry_pieces, next_inputs],
+    grad_inputs = gathered[3].place_last(grad_inputs, 3)
+    shard_squares = project_squares + expand_squares + grad_attend.squares()
+    shard_squares, entry_pieces, grad_inputs = sync(
+        [shard_squares, entry_pieces, grad_inputs],
         [gathered[0], gathered[1], gathered[2], pack],
     )
 
-    gathered[1].step(2)
-    gathered[2].step(1)
-    send_far(entry_pieces, last_far)
-    send_far(entry_pieces, near_spots)
     own_pack = pack.values
     norm_grad = own_pack[0:9]
     grad_mixer_in = own_pack[9 : 9 + MIXH].T
@@ -1198,8 +1338,7 @@
     shared_squares = (
         square_sum(norm_grad) + square_sum(grad_mixer_in) + square_sum(grad_mixer_out)
     )
-    shard_squares = project_squares + expand_squares + attend_squares
-    total_squares = (shard_squares + shared_squares / tensor_size).reshape(1, 1)
+    total_squares = jnp.full((1, 128), shard_squares + shared_squares / tensor_size)
     for axis, bits in (
         ("dp", bits_of(owners)[:1]),
         ("tensor", side_bits + far),
@@ -1208,8 +1347,13 @@
     ):
         for bit in bits:
             total_squares = total_squares + swap(total_squares, axis, bit)
-    total_squares, entry_pieces = sync(
-        [total_squares, entry_pieces], [gathered[1], gathered[2]]
+    gathered[1].step(2)
+    gathered[2].step(1)
+    send_far(entry_pieces, last_far)
+    send_far(entry_pieces, near_spots)
+    grad_inputs = gathered[0].place_last(grad_inputs, 0)
+    total_squares, entry_pieces, grad_inputs = sync(
+        [total_squares, entry_pieces, grad_inputs], [gathered[1], gathered[2]]
     )
     total_squares = total_squares[0, 0]
 
@@ -1237,17 +1381,15 @@
         2.0 / math.sqrt(MIXH),
         weight_decay,
     )
-    parts, rows, units = attend_in_master.shape
-    attend_in_out = adam_call(
-        grad_attend.terms,
+    parts = attend_in_master.shape[0]
+    attend_in_out = adam_step(
         attend_in_master,
         attend_in_first,
         attend_in_second,
+        grad_attend.own()[0:parts],
         factor,
-        wide,
-        (parts, 1, 1),
-        (1, rows, units),
-        None,
+        wide_rate,
+        weight_decay,
     )
     attend_out_out = adam_call(
         grad_attend.terms,
@@ -1260,43 +1402,31 @@
         attend_out_master.shape,
         parts,
     )
-    rows, units = expand_master.shape
-    expand_out = adam_call(
-        grad_expand.terms,
+    expand_out = adam_step(
         expand_master,
         expand_first,
         expand_second,
+        grad_expand.own(),
         factor,
-        wide,
-        (4, 1),
-        (rows // 4, units),
-        None,
-    )
-    rows, units = project_master.shape
-    project_out = adam_call(
-        grad_project.terms,
+        wide_rate,
+        weight_decay,
+    )
+    project_out = adam_step(
         project_master,
         project_first,
         project_second,
+        grad_project.own(),
         factor,
-        (2.0 / math.sqrt(FF), weight_decay),
-        (4, 1),
-        (rows // 4, units),
-        None,
+        2.0 / math.sqrt(FF),
+        weight_decay,
     )
     new_entry = jnp.zeros(grad_entry.shape, bf16_type)
-    grad_history = jnp.zeros(history.shape, bf16_type)
     for spot, index in enumerate(order):
         first_row = (me ^ index) * tokens_here
         new_entry = lax.dynamic_update_slice_in_dim(new_entry, entry_pieces[spot], first_row, 0)
-        grad_history = lax.dynamic_update_slice_in_dim(
-            grad_history, history_pieces[spot], first_row, 1
-        )
-    grad_inputs = jnp.zeros(layer_inputs.shape, bf16_type)
-    for index in (3, 0, 1, 2):
-        grad_inputs = lax.dynamic_update_index_in_dim(
-            grad_inputs, gathered[index].result(), index, 0
-        )
+    for index in (1, 2):
+        grad_inputs = gathered[index].place_last(grad_inputs, index)
+    grad_inputs = grad_inputs.reshape(layer_inputs.shape)
     return (
         next_inputs,
         new_entry,
@@ -1308,7 +1438,7 @@
         attend_in_out[0],
         attend_in_out[1],
         attend_in_out[2],
-        attend_in_out[3],
+        attend_in_out[0].astype(bf16_type),
         attend_out_out[0],
         attend_out_out[1],
         attend_out_out[2],
@@ -1316,11 +1446,11 @@
         expand_out[0],
         expand_out[1],
         expand_out[2],
-        expand_out[3],
+        expand_out[0].astype(bf16_type),
         project_out[0],
         project_out[1],
         project_out[2],
-        project_out[3],
+        project_out[0].astype(bf16_type),
         mixer_in_out[0],
         mixer_in_out[1],
         mixer_in_out[2],

time: 518 us -> 465 us (0.90)
  waiting for transfers between devices: 185 us -> 163 us
  Pallas kernels: 74 us -> 57.1 us
  matrix products: 29.3 us -> 13.6 us
    ppermute x75 -> x79, waiting for transfers between devices: 185 us -> 163 us  [swap(): lax.ppermute(values, axis, [(source, source ^ mask) for source in range(s...]
    pallas_call x4 -> x1, Pallas kernels: 25.4 us -> 3.29 us  [adam_call(): pl.pallas_call(functools.partial(adam_kernel, rates, len(terms), flip), g...]
    pallas_call x0 -> x4, Pallas kernels: none -> 14.3 us  [the longest x2 7.49 us: outer_call(): pl.pallas_call(functools.partial(outer_kernel, pairs), grid=grid, in_spec...]
    dot_general x8 -> x0, matrix products: 14 us -> none  [the longest x6 11.6 us: contract_rows(): lax.dot_general(left, right, (((0,), (0,)), ((), ())), preferred_element_...]
    dynamic_update_slice x7 -> x13, local copies, waits for them, and re-layouts: 7.68 us -> 18.8 us  [the longest x7 10.1 us: place_last(): whole = lax.dynamic_update_slice(whole, block, starts)]
    select_n x27 -> x23, other arithmetic: 20.1 us -> 10.7 us  [settle(): jnp.where(lax.broadcasted_iota(jnp.int32, shape, dim) == side, jnp.expand...]
    convert_element_type x14 -> x17, other arithmetic: 11.5 us -> 20.8 us  [the longest x1 6.51 us: body(): expand_out[0].astype(bf16_type)]
    pallas_call x1, Pallas kernels: 12.6 us -> 6.65 us  [norm_forward(): pl.pallas_call(functools.partial(norm_kernel, owners), grid_spec=pltpu.Pr...]
  transfers between devices with their start and end apart: 75 -> 79, of which waited for: 31 -> 31; matrix products, arithmetic and copies ran while one was open for 21% -> 25% of each run, Pallas kernels for 13% -> 10%
where the time goes in v3:
time: 465 us; the launch traced here: 461 us
  waiting for transfers between devices  163 us (35%)
  starting transfers between devices  82.4 us (18%)
  local copies, waits for them, and re-layouts  69.3 us (15%)
  other arithmetic  67 us (14%)
  Pallas kernels  57.1 us (12%)
  matrix products  13.6 us (3%)
  between operations  9.01 us (2%)
    ppermute x79, waiting for transfers between devices, swap(): lax.ppermute(values, axis, [(source, source ^ mask) for source in range(s...  163 us
    ppermute x79, starting transfers between devices, swap(): lax.ppermute(values, axis, [(source, source ^ mask) for source in range(s...  82.4 us
    unnamed x300, local copies, waits for them, and re-layouts  20.8 us
    pallas_call x4, Pallas kernels, norm_sums(): pl.pallas_call(functools.partial(sums_kernel, owners), grid_spec=pltpu.Pr...  11.4 us
    select_n x23, other arithmetic, settle(): jnp.where(lax.broadcasted_iota(jnp.int32, shape, dim) == side, jnp.expand...  10.7 us
    reduce_sum x6, other arithmetic, square_sum(): return jnp.sum(values * values)  10.6 us
    dynamic_update_slice x7, local copies, waits for them, and re-layouts, place_last(): whole = lax.dynamic_update_slice(whole, block, starts)  10.1 us
  transfers between devices with their start and end apart: 79, of which 31 were waited for; matrix products, arithmetic and copies ran while one was open for 25% of the time, Pallas kernels for 10%

profile of v3, /device:TPU:0, one launch (start us, length us, event | category | flops | bytes accessed | tf_op | source)
XLA Modules:
  0.0 461.0 jit_solution(6152259416229921305)
XLA Ops:
  1.6 3.0 collective-permute-start
  22.5 2.9 collective-permute-start.7
  27.0 2.8 copy-done
  29.8 6.6 %shard_map.497 = (bf16[4,384,1024]{2,1,0:T(8,128)(2,1)S(1)}, bf16[4,384,1024]{2,1,0:T(8,128)(2,1)S(1)}) custom-call(s32[4]{0:T(128)S(1)} %pad_add_fusion.place_ref, bf16[4,384,2048]{2,1,0:T(8,128)(2,1)S(1)} %copy-done, f32[4,1,2048]{2,1,0:T(1,128)S(1)} %copy.83.gains_ref, f32[4,1,2048]{2,1,0:T(1,128)S(1)} %copy.84.biases_ref), custom_call_target="tpu_custom_call" | custom-call | flops 1 | bytes 1 | tf_op jit(solution)/shard_map/pallas_call | solution.py:496
  36.5 6.3 %collective-permute-done.5 = bf16[4,512,256]{2,1,0:T(8,128)(2,1)} collective-permute-done((bf16[4,512,256]{2,1,0:T(8,128)(2,1)}, bf16[4,512,256]{2,1,0:T(8,128)(2,1)}, u32[]{:S(2)}, u32[]{:S(2)}) %collective-permute-start.5) | collective-permute-done | bytes 1048608 | tf_op jit(solution)/shard_map/ppermute | solution.py:120
  50.2 21.3 %collective-permute-done.9 = bf16[512,1024]{1,0:T(8,128)(2,1)S(1)} collective-permute-done((bf16[512,1024]{1,0:T(8,128)(2,1)S(1)}, bf16[512,1024]{1,0:T(8,128)(2,1)S(1)}, u32[]{:S(2)}, u32[]{:S(2)}) %collective-permute-start.9) | collective-permute-done | bytes 1048608 | tf_op jit(solution)/shard_map/ppermute | solution.py:120
  74.6 2.7 collective-permute-start.15
  79.9 3.0 constant_dynamic-slice_fusion.13
  87.2 11.4 %collective-permute-done.13 = bf16[1024,512]{1,0:T(8,128)(2,1)S(1)} collective-permute-done((bf16[1024,512]{1,0:T(8,128)(2,1)S(1)}, bf16[1024,512]{1,0:T(8,128)(2,1)S(1)}, u32[]{:S(2)}, u32[]{:S(2)}) %collective-permute-start.13) | collective-permute-done | bytes 1048608 | tf_op jit(solution)/shard_map/ppermute | solution.py:120
  100.5 4.9 %fusion.8 = (f32[384,1024]{1,0:T(8,128)}, bf16[384,1024]{1,0:T(8,128)(2,1)S(1)}) fusion(f32[384,1024]{1,0:T(8,128)S(1)} %fusion.26, f32[384,1024]{1,0:T(8,128)S(1)} %fusion.24), kind=kLoop, calls=%fused_computation.29 | loop fusion | flops 29097984 | bytes 5505024 | tf_op jit(solution)/shard_map/add | solution.py:1070
  113.1 5.0 %collective-permute-done.17 = bf16[2,2,48,1024]{3,2,1,0:T(8,128)(2,1)S(1)} collective-permute-done((bf16[2,2,48,1024]{3,2,1,0:T(8,128)(2,1)S(1)}, bf16[2,2,48,1024]{3,2,1,0:T(8,128)(2,1)S(1)}, u32[]{:S(2)}, u32[]{:S(2)}) %collective-permute-start.17) | collective-permute-done | bytes 393248 | tf_op jit(solution)/shard_map/ppermute | solution.py:120
  120.1 2.6 collective-permute-done.21
  125.3 2.8 collective-permute-done.18
  129.4 7.0 %collective-permute-done.22 = bf16[2,48,1024]{2,1,0:T(8,128)(2,1)S(1)} collective-permute-done((bf16[2,48,1024]{2,1,0:T(8,128)(2,1)S(1)}, bf16[2,48,1024]{2,1,0:T(8,128)(2,1)S(1)}, u32[]{:S(2)}, u32[]{:S(2)}) %collective-permute-start.22) | collective-permute-done | bytes 196640 | tf_op jit(solution)/shard_map/ppermute | solution.py:120
  137.5 3.7 collective-permute-done.23
  146.6 6.1 %collective-permute-done.24 = bf16[48,1024]{1,0:T(8,128)(2,1)} collective-permute-done((bf16[48,1024]{1,0:T(8,128)(2,1)S(1)}, bf16[48,1024]{1,0:T(8,128)(2,1)}, u32[]{:S(2)}, u32[]{:S(2)}) %collective-permute-start.24) | collective-permute-done | bytes 98336 | tf_op jit(solution)/shard_map/ppermute | solution.py:120
  157.0 4.8 %collective-permute-done.25 = bf16[2,48,1024]{2,1,0:T(8,128)(2,1)S(1)} collective-permute-done((bf16[2,48,1024]{2,1,0:T(8,128)(2,1)S(1)}, bf16[2,48,1024]{2,1,0:T(8,128)(2,1)S(1)}, u32[]{:S(2)}, u32[]{:S(2)}) %collective-permute-start.25) | collective-permute-done | bytes 196640 | tf_op jit(solution)/shard_map/ppermute | solution.py:120
  166.8 3.0 collective-permute-done.26
  172.7 5.2 %shard_map.501 = (bf16[3,384,512]{2,1,0:T(8,128)(2,1)S(1)}, bf16[2,384,512]{2,1,0:T(8,128)(2,1)S(1)}, bf16[1,384,512]{2,1,0:T(8,128)(2,1)}, bf16[3,384,512]{2,1,...) custom-call(s32[4]{0:T(128)S(1)} %pad_add_fusion.place_ref, ...), custom_call_target="tpu_custom_call" | custom-call | flops 1 | bytes 1 | tf_op jit(solution)/shard_map/pallas_call | solution.py:729
  182.5 3.5 shard_map.502
  193.8 3.6 collective-permute-done.31
  209.8 4.7 %shard_map.504 = (bf16[4,1024,256]{2,1,0:T(8,128)(2,1)S(1)}, bf16[4,1024,256]{2,1,0:T(8,128)(2,1)}) custom-call(bf16[4,384,1024]{2,1,0:T(8,128)(2,1)S(1)} %copy-done.6, bf16[4,384,1024]{2,1,0:T(8,128)(2,1)S(1)} %copy-done.8, bf16[3,384,256]{2,1,0:T(8,128)(2,1)S(1)} %shard_map.503.back_ref, bf16[384,1024]{1,0:T(8,128)(2,1)S(1)} %bitcast_select_fusion.5.refs_1_.out_kept_ref, ...), custom_call_target="tpu_custom_call" | custom-call | flops 1 | bytes 1 | tf_op jit(solution)/shard_map/pallas_call | solution.py:417
  214.5 4.0 shard_map.505
  218.7 11.9 %collective-permute-done.37 = bf16[2,2,48,2048]{3,2,1,0:T(8,128)(2,1)S(1)} collective-permute-done((bf16[2,2,48,2048]{3,2,1,0:T(8,128)(2,1)S(1)}, bf16[2,2,48,2048]{3,2,1,0:T(8,128)(2,1)S(1)}, u32[]{:S(2)}, u32[]{:S(2)}) %collective-permute-start.37) | collective-permute-done | bytes 786464 | tf_op jit(solution)/shard_map/ppermute | solution.py:120
  236.2 2.8 copy-done.1
  240.4 3.0 shard_map.506
  243.5 2.8 shard_map.507
  246.8 9.1 %collective-permute-done.40 = bf16[2,48,2048]{2,1,0:T(8,128)(2,1)} collective-permute-done((bf16[2,48,2048]{2,1,0:T(8,128)(2,1)}, bf16[2,48,2048]{2,1,0:T(8,128)(2,1)}, u32[]{:S(2)}, u32[]{:S(2)}) %collective-permute-start.40) | collective-permute-done | bytes 393248 | tf_op jit(solution)/shard_map/ppermute | solution.py:120
  264.2 2.8 shard_map.508
  267.0 2.8 shard_map.509
  269.8 12.5 %collective-permute-done.45 = bf16[48,2048]{1,0:T(8,128)(2,1)S(1)} collective-permute-done((bf16[48,2048]{1,0:T(8,128)(2,1)S(1)}, bf16[48,2048]{1,0:T(8,128)(2,1)S(1)}, u32[]{:S(2)}, u32[]{:S(2)}) %collective-permute-start.45) | collective-permute-done | bytes 196640 | tf_op jit(solution)/shard_map/ppermute | solution.py:120
  292.9 2.6 add_convert_fusion.1
  295.5 2.6 broadcast_in_dim.513
  300.7 2.7 multiply_reduce_fusion.2
  303.5 4.4 collective-permute-done.49
  331.1 16.1 %collective-permute-done.57 = f32[46,512]{1,0:T(8,128)S(1)} collective-permute-done((f32[46,512]{1,0:T(8,128)S(1)}, f32[46,512]{1,0:T(8,128)S(1)}, u32[]{:S(2)}, u32[]{:S(2)}) %collective-permute-start.57) | collective-permute-done | bytes 94240 | tf_op jit(solution)/shard_map/ppermute | solution.py:120
  358.6 6.6 %shard_map.512 = bf16[4,384,2048]{2,1,0:T(8,128)(2,1)} custom-call(s32[4]{0:T(128)S(1)} %pad_add_fusion.place_ref, f32[384,16]{1,0:T(8,128)S(1)} %convert_add_fusion.12.weights_ref, bf16[384,2048]{1,0:T(8,128)(2,1)S(1)} %get-tuple-element.508.newest_ref, bf16[384,2048]{1,0:T(8,128)(2,1)S(1)} %get-tuple-element.656.refs_0_, ...), custom_call_target="tpu_custom_call" | custom-call | flops 1 | bytes 1 | tf_op jit(solution)/shard_map/pallas_call | solution.py:774
  365.2 4.9 %collective-permute-done.62 = f32[46,512]{1,0:T(8,128)S(1)} collective-permute-done((f32[46,512]{1,0:T(8,128)S(1)}, f32[46,512]{1,0:T(8,128)S(1)}, u32[]{:S(2)}, u32[]{:S(2)}) %collective-permute-start.62) | collective-permute-done | bytes 94240 | tf_op jit(solution)/shard_map/ppermute | solution.py:120
  370.3 3.8 collective-permute-done.61.refs_2_
  383.9 3.5 broadcast_in_dim.563
  389.2 3.4 collective-permute-done.67
  392.6 3.1 collective-permute-start.68
  395.7 3.6 multiply_reduce_fusion
  421.3 7.1 %collective-permute-done.73 = f32[1,128]{1,0:T(1,128)S(1)} collective-permute-done((f32[1,128]{1,0:T(1,128)S(1)}, f32[1,128]{1,0:T(1,128)S(1)}, u32[]{:S(2)}, u32[]{:S(2)}) %collective-permute-start.73) | collective-permute-done | bytes 544 | tf_op jit(solution)/shard_map/ppermute | solution.py:120
  438.6 6.5 %fusion.59 = (bf16[512,1024]{1,0:T(8,128)(2,1)}, f32[512,1024]{1,0:T(8,128)}, f32[512,1024]{1,0:T(8,128)}, f32[512,1024]{1,0:T(8,128)}) fusion(f32[512,1024]{1,0:T(8,128)S(1)} %copy-done.55, f32[]{:T(128)} %min.3, bf16[512,1024]{1,0:T(8,128)(2,1)} %copy-done.70, bf16[1024,1024]{1,0:T(8,128)(2,1)} %collective-permute-done.42, ...), kind=kLoop, calls=%fused_computation.302 | loop fusion | flops 11534336 | bytes 16777220 | tf_op jit(solution)/shard_map/convert_element_type | solution.py:1449
  446.0 3.4 fusion.61
  449.5 3.3 shard_map.515
  453.7 3.8 fusion.57
  (648 shorter events, 202.4 us)
Async XLA Ops:
  16.8 26.0 %collective-permute-start.5 = (bf16[4,512,256]{2,1,0:T(8,128)(2,1)}, bf16[4,512,256]{2,1,0:T(8,128)(2,1)}, u32[]{:S(2)}, u32[]{:S(2)}) collective-permute-start(bf16[4,512,256]{2,1,0:T(8,128)(2,1)} %pad_maximum_fusion.7), channel_id=1, source_target_pairs={{0,16},{8,24},{16,0},{24,8},{1,17},{9,25},{17,1},{25,9},{2,18},{10... | collective-permute-start | bytes 3145736 | tf_op jit(solution)/shard_map/ppermute | solution.py:120
  22.5 21.7 %collective-permute-start.7 = (bf16[2,48,2048]{2,1,0:T(8,128)(2,1)S(1)}, bf16[2,48,2048]{2,1,0:T(8,128)(2,1)S(1)}, u32[]{:S(2)}, u32[]{:S(2)}) collective-permute-start(bf16[2,48,2048]{2,1,0:T(8,128)(2,1)S(1)} %slice.340), channel_id=1, source_target_pairs={{0,4},{1,5},{2,6},{3,7},{4,0},{5,1},{6,2},{7,3},{8,12},{9,13},{10,... | collective-permute-start | bytes 1179656 | tf_op jit(solution)/shard_map/ppermute | solution.py:120
  25.4 18.8 %collective-permute-start.8 = (bf16[1,48,2048]{2,1,0:T(8,128)(2,1)S(1)}, bf16[1,48,2048]{2,1,0:T(8,128)(2,1)S(1)}, u32[]{:S(2)}, u32[]{:S(2)}) collective-permute-start(bf16[1,48,2048]{2,1,0:T(8,128)(2,1)S(1)} %get-tuple-element.323), channel_id=1, source_target_pairs={{0,1},{1,0},{2,3},{3,2},{4,5},{5,4},{6,7},{7,6},{8,9},{9,8},{10,11... | collective-permute-start | bytes 589832 | tf_op jit(solution)/shard_map/ppermute | solution.py:120
  44.2 27.5 %collective-permute-start.10 = (bf16[4,1024,256]{2,1,0:T(8,128)(2,1)S(1)}, bf16[4,1024,256]{2,1,0:T(8,128)(2,1)S(1)}, u32[]{:S(2)}, u32[]{:S(2)}) collective-permute-start(bf16[4,1024,256]{2,1,0:T(8,128)(2,1)S(1)} %pad_maximum_fusion), channel_id=1, source_target_pairs={{0,8},{8,0},{16,24},{24,16},{1,9},{9,1},{17,25},{25,17},{2,10},{10... | collective-permute-start | bytes 6291464 | tf_op jit(solution)/shard_map/ppermute | solution.py:120
  46.2 25.3 %collective-permute-start.9 = (bf16[512,1024]{1,0:T(8,128)(2,1)S(1)}, bf16[512,1024]{1,0:T(8,128)(2,1)S(1)}, u32[]{:S(2)}, u32[]{:S(2)}) collective-permute-start(bf16[512,1024]{1,0:T(8,128)(2,1)S(1)} %convert_element_type.337), channel_id=1, source_target_pairs={{0,16},{8,24},{16,0},{24,8},{1,17},{9,25},{17,1},{25,9},{2,18},{10... | collective-permute-start | bytes 3145736 | tf_op jit(solution)/shard_map/ppermute | solution.py:120
  47.8 23.9 %collective-permute-start.11 = (bf16[2,2,48,2048]{3,2,1,0:T(8,128)(2,1)S(1)}, bf16[2,2,48,2048]{3,2,1,0:T(8,128)(2,1)S(1)}, u32[]{:S(2)}, u32[]{:S(2)}) collective-permute-start(bf16[2,2,48,2048]{3,2,1,0:T(8,128)(2,1)S(1)} %broadcast_select_fusion.7), channel_id=1, source_target_pairs={{0,2},{1,3},{2,0},{3,1},{4,6},{5,7},{6,4},{7,5},{8,10},{9,11},{10,... | collective-permute-start | bytes 2359304 | tf_op jit(solution)/shard_map/ppermute | solution.py:120
  71.7 27.2 %collective-permute-start.14 = (bf16[1024,1024]{1,0:T(8,128)(2,1)S(1)}, bf16[1024,1024]{1,0:T(8,128)(2,1)S(1)}, u32[]{:S(2)}, u32[]{:S(2)}) collective-permute-start(bf16[1024,1024]{1,0:T(8,128)(2,1)S(1)} %pad_maximum_fusion.1), channel_id=1, source_target_pairs={{0,8},{8,0},{16,24},{24,16},{1,9},{9,1},{17,25},{25,17},{2,10},{10... | collective-permute-start | bytes 6291464 | tf_op jit(solution)/shard_map/ppermute | solution.py:120
  73.3 25.2 %collective-permute-start.13 = (bf16[1024,512]{1,0:T(8,128)(2,1)S(1)}, bf16[1024,512]{1,0:T(8,128)(2,1)S(1)}, u32[]{:S(2)}, u32[]{:S(2)}) collective-permute-start(bf16[1024,512]{1,0:T(8,128)(2,1)S(1)} %convert_element_type.338), channel_id=1, source_target_pairs={{0,16},{8,24},{16,0},{24,8},{1,17},{9,25},{17,1},{25,9},{2,18},{10... | collective-permute-start | bytes 3145736 | tf_op jit(solution)/shard_map/ppermute | solution.py:120
  74.6 24.3 %collective-permute-start.15 = (bf16[1,2,48,2048]{3,2,1,0:T(8,128)(2,1)S(1)}, bf16[1,2,48,2048]{3,2,1,0:T(8,128)(2,1)S(1)}, u32[]{:S(2)}, u32[]{:S(2)}) collective-permute-start(bf16[1,2,48,2048]{3,2,1,0:T(8,128)(2,1)S(1)} %broadcast_select_fusion.16), channel_id=1, source_target_pairs={{0,4},{1,5},{2,6},{3,7},{4,0},{5,1},{6,2},{7,3},{8,12},{9,13},{10,... | collective-permute-start | bytes 1179656 | tf_op jit(solution)/shard_map/ppermute | solution.py:120
  78.5 20.4 %collective-permute-start.16 = (bf16[1,2,2,48,2048]{4,3,2,1,0:T(8,128)(2,1)S(1)}, bf16[1,2,2,48,2048]{4,3,2,1,0:T(8,128)(2,1)S(1)}, u32[]{:S(2)}, u32[]{:S(2)}) collective-permute-start(bf16[1,2,2,48,2048]{4,3,2,1,0:T(8,128)(2,1)S(1)} %get-tuple-element.484), channel_id=1, source_target_pairs={{0,1},{1,0},{2,3},{3,2},{4,5},{5,4},{6,7},{7,6},{8,9},{9,8},{10,11... | collective-permute-start | bytes 2359304 | tf_op jit(solution)/shard_map/ppermute | solution.py:120
  180.7 16.7 %collective-permute-start.31 = (bf16[1,2,2,48,2048]{4,3,2,1,0:T(8,128)(2,1)S(1)}, bf16[1,2,2,48,2048]{4,3,2,1,0:T(8,128)(2,1)S(1)}, u32[]{:S(2)}, u32[]{:S(2)}) collective-permute-start(bf16[1,2,2,48,2048]{4,3,2,1,0:T(8,128)(2,1)S(1)} %broadcast_select_fusion.6), channel_id=1, source_target_pairs={{0,2},{1,3},{2,0},{3,1},{4,6},{5,7},{6,4},{7,5},{8,10},{9,11},{10,... | collective-permute-start | bytes 2359304 | tf_op jit(solution)/shard_map/ppermute | solution.py:120
  181.4 16.0 %collective-permute-start.32 = (bf16[1,2,2,48,2048]{4,3,2,1,0:T(8,128)(2,1)S(1)}, bf16[1,2,2,48,2048]{4,3,2,1,0:T(8,128)(2,1)S(1)}, u32[]{:S(2)}, u32[]{:S(2)}) collective-permute-start(bf16[1,2,2,48,2048]{4,3,2,1,0:T(8,128)(2,1)S(1)} %copy-done.74), channel_id=1, source_target_pairs={{0,1},{1,0},{2,3},{3,2},{4,5},{5,4},{6,7},{7,6},{8,9},{9,8},{10,11... | collective-permute-start | bytes 2359304 | tf_op jit(solution)/shard_map/ppermute | solution.py:120
  201.1 17.6 %collective-permute-start.33 = (bf16[2,384,512]{2,1,0:T(8,128)(2,1)S(1)}, bf16[2,384,512]{2,1,0:T(8,128)(2,1)S(1)}, u32[]{:S(2)}, u32[]{:S(2)}) collective-permute-start(bf16[2,384,512]{2,1,0:T(8,128)(2,1)S(1)} %get-tuple-element.369), channel_id=1, source_target_pairs={{0,16},{8,24},{16,0},{24,8},{1,17},{9,25},{17,1},{25,9},{2,18},{10... | collective-permute-start | bytes 2359304 | tf_op jit(solution)/shard_map/ppermute | solution.py:120
  202.0 28.6 %collective-permute-start.34 = (bf16[3,384,512]{2,1,0:T(8,128)(2,1)S(1)}, bf16[3,384,512]{2,1,0:T(8,128)(2,1)S(1)}, u32[]{:S(2)}, u32[]{:S(2)}) collective-permute-start(bf16[3,384,512]{2,1,0:T(8,128)(2,1)S(1)} %get-tuple-element.370), channel_id=1, source_target_pairs={{0,8},{8,0},{16,24},{24,16},{1,9},{9,1},{17,25},{25,17},{2,10},{10... | collective-permute-start | bytes 3538952 | tf_op jit(solution)/shard_map/ppermute | solution.py:120
  202.0 28.6 %collective-permute-start.35 = (bf16[1024,1024]{1,0:T(8,128)(2,1)S(1)}, bf16[1024,1024]{1,0:T(8,128)(2,1)S(1)}, u32[]{:S(2)}, u32[]{:S(2)}) collective-permute-start(bf16[1024,1024]{1,0:T(8,128)(2,1)S(1)} %get-tuple-element.380), channel_id=1, source_target_pairs={{0,8},{8,0},{16,24},{24,16},{1,9},{9,1},{17,25},{25,17},{2,10},{10... | collective-permute-start | bytes 6291464 | tf_op jit(solution)/shard_map/ppermute | solution.py:120
  203.2 27.4 %collective-permute-start.37 = (bf16[2,2,48,2048]{3,2,1,0:T(8,128)(2,1)S(1)}, bf16[2,2,48,2048]{3,2,1,0:T(8,128)(2,1)S(1)}, u32[]{:S(2)}, u32[]{:S(2)}) collective-permute-start(bf16[2,2,48,2048]{3,2,1,0:T(8,128)(2,1)S(1)} %get-tuple-element.599), channel_id=1, source_target_pairs={{0,2},{1,3},{2,0},{3,1},{4,6},{5,7},{6,4},{7,5},{8,10},{9,11},{10,... | collective-permute-start | bytes 2359304 | tf_op jit(solution)/shard_map/ppermute | solution.py:120
  230.6 25.3 %collective-permute-start.41 = (bf16[4,1024,256]{2,1,0:T(8,128)(2,1)}, bf16[4,1024,256]{2,1,0:T(8,128)(2,1)}, u32[]{:S(2)}, u32[]{:S(2)}) collective-permute-start(bf16[4,1024,256]{2,1,0:T(8,128)(2,1)} %get-tuple-element.405), channel_id=1, source_target_pairs={{0,8},{8,0},{16,24},{24,16},{1,9},{9,1},{17,25},{25,17},{2,10},{10... | collective-permute-start | bytes 6291464 | tf_op jit(solution)/shard_map/ppermute | solution.py:120
  230.7 25.3 %collective-permute-start.42 = (bf16[1024,1024]{1,0:T(8,128)(2,1)}, bf16[1024,1024]{1,0:T(8,128)(2,1)}, u32[]{:S(2)}, u32[]{:S(2)}) collective-permute-start(bf16[1024,1024]{1,0:T(8,128)(2,1)} %get-tuple-element.407), channel_id=1, source_target_pairs={{0,8},{8,0},{16,24},{24,16},{1,9},{9,1},{17,25},{25,17},{2,10},{10... | collective-permute-start | bytes 6291464 | tf_op jit(solution)/shard_map/ppermute | solution.py:120
  231.2 24.8 %collective-permute-start.38 = (bf16[2,384,512]{2,1,0:T(8,128)(2,1)}, bf16[2,384,512]{2,1,0:T(8,128)(2,1)}, u32[]{:S(2)}, u32[]{:S(2)}) collective-permute-start(bf16[2,384,512]{2,1,0:T(8,128)(2,1)} %get-tuple-element.395), channel_id=1, source_target_pairs={{0,24},{8,16},{16,8},{24,0},{1,25},{9,17},{17,9},{25,1},{2,26},{10... | collective-permute-start | bytes 2359304 | tf_op jit(solution)/shard_map/ppermute | solution.py:120
  233.4 22.6 %collective-permute-start.39 = (bf16[2,2,48,2048]{3,2,1,0:T(8,128)(2,1)}, bf16[2,2,48,2048]{3,2,1,0:T(8,128)(2,1)}, u32[]{:S(2)}, u32[]{:S(2)}) collective-permute-start(bf16[2,2,48,2048]{3,2,1,0:T(8,128)(2,1)} %get-tuple-element.597), channel_id=1, source_target_pairs={{0,1},{1,0},{2,3},{3,2},{4,5},{5,4},{6,7},{7,6},{8,9},{9,8},{10,11... | collective-permute-start | bytes 2359304 | tf_op jit(solution)/shard_map/ppermute | solution.py:120
  235.4 20.5 %collective-permute-start.40 = (bf16[2,48,2048]{2,1,0:T(8,128)(2,1)}, bf16[2,48,2048]{2,1,0:T(8,128)(2,1)}, u32[]{:S(2)}, u32[]{:S(2)}) collective-permute-start(bf16[2,48,2048]{2,1,0:T(8,128)(2,1)} %get-tuple-element.619), channel_id=1, source_target_pairs={{0,4},{1,5},{2,6},{3,7},{4,0},{5,1},{6,2},{7,3},{8,12},{9,13},{10,... | collective-permute-start | bytes 1179656 | tf_op jit(solution)/shard_map/ppermute | solution.py:120
  257.7 24.7 %collective-permute-start.43 = (bf16[2,48,2048]{2,1,0:T(8,128)(2,1)S(1)}, bf16[2,48,2048]{2,1,0:T(8,128)(2,1)S(1)}, u32[]{:S(2)}, u32[]{:S(2)}) collective-permute-start(bf16[2,48,2048]{2,1,0:T(8,128)(2,1)S(1)} %get-tuple-element.617), channel_id=1, source_target_pairs={{0,2},{1,3},{2,0},{3,1},{4,6},{5,7},{6,4},{7,5},{8,10},{9,11},{10,... | collective-permute-start | bytes 1179656 | tf_op jit(solution)/shard_map/ppermute | solution.py:120
  257.8 25.2 %collective-permute-start.46 = (bf16[1024,512]{1,0:T(8,128)(2,1)S(1)}, bf16[1024,512]{1,0:T(8,128)(2,1)S(1)}, u32[]{:S(2)}, u32[]{:S(2)}) collective-permute-start(bf16[1024,512]{1,0:T(8,128)(2,1)S(1)} %add_convert_fusion.2), channel_id=1, source_target_pairs={{0,16},{8,24},{16,0},{24,8},{1,17},{9,25},{17,1},{25,9},{2,18},{10... | collective-permute-start | bytes 3145736 | tf_op jit(solution)/shard_map/ppermute | solution.py:120
  258.8 23.5 %collective-permute-start.44 = (bf16[2,2,48,2048]{3,2,1,0:T(8,128)(2,1)S(1)}, bf16[2,2,48,2048]{3,2,1,0:T(8,128)(2,1)S(1)}, u32[]{:S(2)}, u32[]{:S(2)}) collective-permute-start(bf16[2,2,48,2048]{3,2,1,0:T(8,128)(2,1)S(1)} %get-tuple-element.595), channel_id=1, source_target_pairs={{0,1},{1,0},{2,3},{3,2},{4,5},{5,4},{6,7},{7,6},{8,9},{9,8},{10,11... | collective-permute-start | bytes 2359304 | tf_op jit(solution)/shard_map/ppermute | solution.py:120
  261.5 20.8 %collective-permute-start.45 = (bf16[48,2048]{1,0:T(8,128)(2,1)S(1)}, bf16[48,2048]{1,0:T(8,128)(2,1)S(1)}, u32[]{:S(2)}, u32[]{:S(2)}) collective-permute-start(bf16[48,2048]{1,0:T(8,128)(2,1)S(1)} %get-tuple-element.637), channel_id=1, source_target_pairs={{0,1},{1,0},{2,3},{3,2},{4,5},{5,4},{6,7},{7,6},{8,9},{9,8},{10,11... | collective-permute-start | bytes 589832 | tf_op jit(solution)/shard_map/ppermute | solution.py:120
  282.9 25.9 %collective-permute-start.47 = (bf16[1,384,512]{2,1,0:T(8,128)(2,1)}, bf16[1,384,512]{2,1,0:T(8,128)(2,1)}, u32[]{:S(2)}, u32[]{:S(2)}) collective-permute-start(bf16[1,384,512]{2,1,0:T(8,128)(2,1)} %get-tuple-element.436), channel_id=1, source_target_pairs={{0,16},{8,24},{16,0},{24,8},{1,17},{9,25},{17,1},{25,9},{2,18},{10... | collective-permute-start | bytes 1179656 | tf_op jit(solution)/shard_map/ppermute | solution.py:120
  283.8 25.1 %collective-permute-start.48 = (bf16[1,384,512]{2,1,0:T(8,128)(2,1)}, bf16[1,384,512]{2,1,0:T(8,128)(2,1)}, u32[]{:S(2)}, u32[]{:S(2)}) collective-permute-start(bf16[1,384,512]{2,1,0:T(8,128)(2,1)} %get-tuple-element.437), channel_id=1, source_target_pairs={{0,24},{8,16},{16,8},{24,0},{1,25},{9,17},{17,9},{25,1},{2,26},{10... | collective-permute-start | bytes 1179656 | tf_op jit(solution)/shard_map/ppermute | solution.py:120
  286.4 21.4 %collective-permute-start.49 = (bf16[2,48,2048]{2,1,0:T(8,128)(2,1)}, bf16[2,48,2048]{2,1,0:T(8,128)(2,1)}, u32[]{:S(2)}, u32[]{:S(2)}) collective-permute-start(bf16[2,48,2048]{2,1,0:T(8,128)(2,1)} %pad_maximum_fusion.12), channel_id=1, source_target_pairs={{0,4},{1,5},{2,6},{3,7},{4,0},{5,1},{6,2},{7,3},{8,12},{9,13},{10,... | collective-permute-start | bytes 1179656 | tf_op jit(solution)/shard_map/ppermute | solution.py:120
  289.8 19.5 %collective-permute-start.50 = (bf16[2,48,2048]{2,1,0:T(8,128)(2,1)}, bf16[2,48,2048]{2,1,0:T(8,128)(2,1)}, u32[]{:S(2)}, u32[]{:S(2)}) collective-permute-start(bf16[2,48,2048]{2,1,0:T(8,128)(2,1)} %get-tuple-element.615), channel_id=1, source_target_pairs={{0,2},{1,3},{2,0},{3,1},{4,6},{5,7},{6,4},{7,5},{8,10},{9,11},{10,... | collective-permute-start | bytes 1179656 | tf_op jit(solution)/shard_map/ppermute | solution.py:120
  291.4 20.5 %collective-permute-start.51 = (bf16[2,2,48,2048]{3,2,1,0:T(8,128)(2,1)}, bf16[2,2,48,2048]{3,2,1,0:T(8,128)(2,1)}, u32[]{:S(2)}, u32[]{:S(2)}) collective-permute-start(bf16[2,2,48,2048]{3,2,1,0:T(8,128)(2,1)} %get-tuple-element.593), channel_id=1, source_target_pairs={{0,1},{1,0},{2,3},{3,2},{4,5},{5,4},{6,7},{7,6},{8,9},{9,8},{10,11... | collective-permute-start | bytes 2359304 | tf_op jit(solution)/shard_map/ppermute | solution.py:120
  314.3 32.9 %collective-permute-start.52 = (bf16[2,48,2048]{2,1,0:T(8,128)(2,1)S(1)}, bf16[2,48,2048]{2,1,0:T(8,128)(2,1)S(1)}, u32[]{:S(2)}, u32[]{:S(2)}) collective-permute-start(bf16[2,48,2048]{2,1,0:T(8,128)(2,1)S(1)} %pad_maximum_fusion.13), channel_id=1, source_target_pairs={{0,4},{1,5},{2,6},{3,7},{4,0},{5,1},{6,2},{7,3},{8,12},{9,13},{10,... | collective-permute-start | bytes 1179656 | tf_op jit(solution)/shard_map/ppermute | solution.py:120
  318.1 29.2 %collective-permute-start.53 = (bf16[2,2,48,2048]{3,2,1,0:T(8,128)(2,1)S(1)}, bf16[2,2,48,2048]{3,2,1,0:T(8,128)(2,1)S(1)}, u32[]{:S(2)}, u32[]{:S(2)}) collective-permute-start(bf16[2,2,48,2048]{3,2,1,0:T(8,128)(2,1)S(1)} %pad_maximum_fusion.10), channel_id=1, source_target_pairs={{0,2},{1,3},{2,0},{3,1},{4,6},{5,7},{6,4},{7,5},{8,10},{9,11},{10,... | collective-permute-start | bytes 2359304 | tf_op jit(solution)/shard_map/ppermute | solution.py:120
  319.2 28.2 %collective-permute-start.54 = (bf16[2,2,48,2048]{3,2,1,0:T(8,128)(2,1)S(1)}, bf16[2,2,48,2048]{3,2,1,0:T(8,128)(2,1)S(1)}, u32[]{:S(2)}, u32[]{:S(2)}) collective-permute-start(bf16[2,2,48,2048]{3,2,1,0:T(8,128)(2,1)S(1)} %broadcast_select_fusion.5), channel_id=1, source_target_pairs={{0,1},{1,0},{2,3},{3,2},{4,5},{5,4},{6,7},{7,6},{8,9},{9,8},{10,11... | collective-permute-start | bytes 2359304 | tf_op jit(solution)/shard_map/ppermute | solution.py:120
  320.7 26.6 %collective-permute-start.55 = (bf16[512,1024]{1,0:T(8,128)(2,1)S(1)}, bf16[512,1024]{1,0:T(8,128)(2,1)S(1)}, u32[]{:S(2)}, u32[]{:S(2)}) collective-permute-start(bf16[512,1024]{1,0:T(8,128)(2,1)S(1)} %copy-done.100), channel_id=1, source_target_pairs={{0,16},{8,24},{16,0},{24,8},{1,17},{9,25},{17,1},{25,9},{2,18},{10... | collective-permute-start | bytes 3145736 | tf_op jit(solution)/shard_map/ppermute | solution.py:120
  328.2 19.0 %collective-permute-start.57 = (f32[46,512]{1,0:T(8,128)S(1)}, f32[46,512]{1,0:T(8,128)S(1)}, u32[]{:S(2)}, u32[]{:S(2)}) collective-permute-start(f32[46,512]{1,0:T(8,128)S(1)} %slice.363), channel_id=1, source_target_pairs={{0,16},{8,24},{16,0},{24,8},{1,17},{9,25},{17,1},{25,9},{2,18},{10... | collective-permute-start | bytes 282632 | tf_op jit(solution)/shard_map/ppermute | solution.py:120
  349.1 21.0 %collective-permute-start.58 = (bf16[2,48,2048]{2,1,0:T(8,128)(2,1)S(1)}, bf16[2,48,2048]{2,1,0:T(8,128)(2,1)S(1)}, u32[]{:S(2)}, u32[]{:S(2)}) collective-permute-start(bf16[2,48,2048]{2,1,0:T(8,128)(2,1)S(1)} %pad_maximum_fusion.14), channel_id=1, source_target_pairs={{0,4},{1,5},{2,6},{3,7},{4,0},{5,1},{6,2},{7,3},{8,12},{9,13},{10,... | collective-permute-start | bytes 1179656 | tf_op jit(solution)/shard_map/ppermute | solution.py:120
  350.7 19.5 %collective-permute-start.60 = (bf16[2,2,48,2048]{3,2,1,0:T(8,128)(2,1)S(1)}, bf16[2,2,48,2048]{3,2,1,0:T(8,128)(2,1)S(1)}, u32[]{:S(2)}, u32[]{:S(2)}) collective-permute-start(bf16[2,2,48,2048]{3,2,1,0:T(8,128)(2,1)S(1)} %broadcast_select_fusion.4), channel_id=1, source_target_pairs={{0,1},{1,0},{2,3},{3,2},{4,5},{5,4},{6,7},{7,6},{8,9},{9,8},{10,11... | collective-permute-start | bytes 2359304 | tf_op jit(solution)/shard_map/ppermute | solution.py:120
  351.5 22.6 %collective-permute-start.61 = (bf16[4,512,256]{2,1,0:T(8,128)(2,1)S(1)}, bf16[4,512,256]{2,1,0:T(8,128)(2,1)S(1)}, u32[]{:S(2)}, u32[]{:S(2)}) collective-permute-start(bf16[4,512,256]{2,1,0:T(8,128)(2,1)S(1)} %add_convert_fusion), channel_id=1, source_target_pairs={{0,16},{8,24},{16,0},{24,8},{1,17},{9,25},{17,1},{25,9},{2,18},{10... | collective-permute-start | bytes 3145736 | tf_op jit(solution)/shard_map/ppermute | solution.py:120
  352.3 18.0 %collective-permute-start.59 = (bf16[2,48,2048]{2,1,0:T(8,128)(2,1)S(1)}, bf16[2,48,2048]{2,1,0:T(8,128)(2,1)S(1)}, u32[]{:S(2)}, u32[]{:S(2)}) collective-permute-start(bf16[2,48,2048]{2,1,0:T(8,128)(2,1)S(1)} %broadcast_select_fusion.12), channel_id=1, source_target_pairs={{0,2},{1,3},{2,0},{3,1},{4,6},{5,7},{6,4},{7,5},{8,10},{9,11},{10,... | collective-permute-start | bytes 1179656 | tf_op jit(solution)/shard_map/ppermute | solution.py:120
  353.4 16.8 %collective-permute-start.62 = (f32[46,512]{1,0:T(8,128)S(1)}, f32[46,512]{1,0:T(8,128)S(1)}, u32[]{:S(2)}, u32[]{:S(2)}) collective-permute-start(f32[46,512]{1,0:T(8,128)S(1)} %slice_add_fusion.1), channel_id=1, source_target_pairs={{0,1},{1,0},{2,3},{3,2},{4,5},{5,4},{6,7},{7,6},{8,9},{9,8},{10,11... | collective-permute-start | bytes 282632 | tf_op jit(solution)/shard_map/ppermute | solution.py:120
  375.2 26.1 %collective-permute-start.63 = (bf16[384,512]{1,0:T(8,128)(2,1)}, bf16[384,512]{1,0:T(8,128)(2,1)}, u32[]{:S(2)}, u32[]{:S(2)}) collective-permute-start(bf16[384,512]{1,0:T(8,128)(2,1)} %get-tuple-element.591), channel_id=1, source_target_pairs={{0,16},{8,24},{16,0},{24,8},{1,17},{9,25},{17,1},{25,9},{2,18},{10... | collective-permute-start | bytes 1179656 | tf_op jit(solution)/shard_map/ppermute | solution.py:120
  376.7 24.6 %collective-permute-start.64 = (bf16[2,2,48,2048]{3,2,1,0:T(8,128)(2,1)}, bf16[2,2,48,2048]{3,2,1,0:T(8,128)(2,1)}, u32[]{:S(2)}, u32[]{:S(2)}) collective-permute-start(bf16[2,2,48,2048]{3,2,1,0:T(8,128)(2,1)} %broadcast_select_fusion.3), channel_id=1, source_target_pairs={{0,1},{1,0},{2,3},{3,2},{4,5},{5,4},{6,7},{7,6},{8,9},{9,8},{10,11... | collective-permute-start | bytes 2359304 | tf_op jit(solution)/shard_map/ppermute | solution.py:120
  378.9 22.4 %collective-permute-start.65 = (bf16[2,48,2048]{2,1,0:T(8,128)(2,1)}, bf16[2,48,2048]{2,1,0:T(8,128)(2,1)}, u32[]{:S(2)}, u32[]{:S(2)}) collective-permute-start(bf16[2,48,2048]{2,1,0:T(8,128)(2,1)} %broadcast_select_fusion.11), channel_id=1, source_target_pairs={{0,2},{1,3},{2,0},{3,1},{4,6},{5,7},{6,4},{7,5},{8,10},{9,11},{10,... | collective-permute-start | bytes 1179656 | tf_op jit(solution)/shard_map/ppermute | solution.py:120
  381.3 20.0 %collective-permute-start.66 = (bf16[48,2048]{1,0:T(8,128)(2,1)S(1)}, bf16[48,2048]{1,0:T(8,128)(2,1)}, u32[]{:S(2)}, u32[]{:S(2)}) collective-permute-start(bf16[48,2048]{1,0:T(8,128)(2,1)S(1)} %shard_map.514), channel_id=1, source_target_pairs={{0,4},{1,5},{2,6},{3,7},{4,0},{5,1},{6,2},{7,3},{8,12},{9,13},{10,... | collective-permute-start | bytes 589832 | tf_op jit(solution)/shard_map/ppermute | solution.py:120
  405.2 23.2 %collective-permute-start.74 = (bf16[384,512]{1,0:T(8,128)(2,1)}, bf16[384,512]{1,0:T(8,128)(2,1)S(1)}, u32[]{:S(2)}, u32[]{:S(2)}) collective-permute-start(bf16[384,512]{1,0:T(8,128)(2,1)} %get-tuple-element.523), channel_id=1, source_target_pairs={{0,8},{8,0},{16,24},{24,16},{1,9},{9,1},{17,25},{25,17},{2,10},{10... | collective-permute-start | bytes 1179656 | tf_op jit(solution)/shard_map/ppermute | solution.py:120
  405.7 22.8 %collective-permute-start.75 = (bf16[384,512]{1,0:T(8,128)(2,1)}, bf16[384,512]{1,0:T(8,128)(2,1)S(1)}, u32[]{:S(2)}, u32[]{:S(2)}) collective-permute-start(bf16[384,512]{1,0:T(8,128)(2,1)} %get-tuple-element.524), channel_id=1, source_target_pairs={{0,24},{8,16},{16,8},{24,0},{1,25},{9,17},{17,9},{25,1},{2,26},{10... | collective-permute-start | bytes 1179656 | tf_op jit(solution)/shard_map/ppermute | solution.py:120
  408.4 20.1 %collective-permute-start.76 = (bf16[2,2,48,2048]{3,2,1,0:T(8,128)(2,1)S(1)}, bf16[2,2,48,2048]{3,2,1,0:T(8,128)(2,1)S(1)}, u32[]{:S(2)}, u32[]{:S(2)}) collective-permute-start(bf16[2,2,48,2048]{3,2,1,0:T(8,128)(2,1)S(1)} %broadcast_select_fusion.2), channel_id=1, source_target_pairs={{0,1},{1,0},{2,3},{3,2},{4,5},{5,4},{6,7},{7,6},{8,9},{9,8},{10,11... | collective-permute-start | bytes 2359304 | tf_op jit(solution)/shard_map/ppermute | solution.py:120
  432.6 24.8 %collective-permute-start.78 = (bf16[2,2,48,2048]{3,2,1,0:T(8,128)(2,1)}, bf16[2,2,48,2048]{3,2,1,0:T(8,128)(2,1)}, u32[]{:S(2)}, u32[]{:S(2)}) collective-permute-start(bf16[2,2,48,2048]{3,2,1,0:T(8,128)(2,1)} %broadcast_select_fusion.1), channel_id=1, source_target_pairs={{0,1},{1,0},{2,3},{3,2},{4,5},{5,4},{6,7},{7,6},{8,9},{9,8},{10,11... | collective-permute-start | bytes 2359304 | tf_op jit(solution)/shard_map/ppermute | solution.py:120
  (179 other events, 1959.1 us)

commit v4 on v3

--- a/solution.py
+++ b/solution.py
@@ -295,6 +295,13 @@
         )
         self.moved = None
 
+    def place_new(self, count, index):
+        spot = bits_of(lax.axis_size(self.axis)).index(self.bit)
+        side = (lax.axis_index(self.axis) & self.bit) // self.bit
+        whole = place_first(self.values, self.moved, side, spot, count, index)
+        shape = self.values.shape[:spot] + (2,) + self.values.shape[spot:]
+        return whole.reshape((count,) + shape)
+
     def place_last(self, whole, index):
         spot = bits_of(lax.axis_size(self.axis)).index(self.bit)
         side = (lax.axis_index(self.axis) & self.bit) // self.bit
@@ -336,6 +343,41 @@
         ),
         cost_estimate=light(),
     )(*blocks)
+
+
+def place_kernel(side_ref, values_ref, moved_ref, out_ref):
+    @pl.when(pl.program_id(1) == 0)
+    def own():
+        out_ref[0, 0, 0] = values_ref[0]
+
+    @pl.when(pl.program_id(1) == 1)
+    def other():
+        out_ref[0, 0, 0] = moved_ref[0]
+
+
+def place_first(values, moved, side, spot, count, index):
+    front = 2**spot
+    rows, width = values.size // values.shape[-1] // front, values.shape[-1]
+    part = pl.BlockSpec((1, rows, width), lambda a, g, side_ref: (a, 0, 0))
+    return pl.pallas_call(
+        place_kernel,
+        grid_spec=pltpu.PrefetchScalarGridSpec(
+            num_scalar_prefetch=1,
+            grid=(front, 2),
+            in_specs=[part, part],
+            out_specs=pl.BlockSpec(
+                (1, 1, 1, rows, width),
+                lambda a, g, side_ref: (index, a, (side_ref[0] + g) % 2, 0, 0),
+            ),
+        ),
+        out_shape=jax.ShapeDtypeStruct((count, front, 2, rows, width), values.dtype),
+        compiler_params=pltpu.CompilerParams(vmem_limit_bytes=12 << 20),
+        cost_estimate=light(),
+    )(
+        side.reshape(1).astype(jnp.int32),
+        values.reshape(front, rows, width),
+        moved.reshape(front, rows, width),
+    )
 
 
 def outer_kernel(pairs, *refs):
@@ -828,12 +870,15 @@
     )(place, grads, layer_inputs)
 
 
-def back_kernel(owners, place_ref, grads_ref, inputs_ref, gain_ref, extra_ref, out_ref):
+def back_kernel(
+    owners, place_ref, grads_ref, moved_ref, inputs_ref, gain_ref, extra_ref, out_ref
+):
     cols = inputs_ref.shape[1] // owners
     values = inputs_ref[...].astype(jnp.float32)
     centred = values - jnp.mean(values, axis=-1, keepdims=True)
     inverse = lax.rsqrt(jnp.mean(centred * centred, axis=-1, keepdims=True) + norm_epsilon)
-    back = norm_back(grads_ref[...], centred * inverse, inverse, gain_ref[...])
+    grads = grads_ref[...].astype(jnp.float32) + moved_ref[...].astype(jnp.float32)
+    back = norm_back(grads, centred * inverse, inverse, gain_ref[...])
     if extra_ref is not None:
         back = back + extra_ref[...]
     for index in range(owners):
@@ -841,21 +886,21 @@
         out_ref[:, lane_block(place_ref, index, cols)] = back[:, spot].astype(jnp.bfloat16)
 
 
-def back_share(grads, inputs, gain, extra, place, owners):
+def back_share(grads, moved, inputs, gain, extra, place, owners):
     rows, width = grads.shape
     kernel = functools.partial(back_kernel, owners)
     if extra is None:
-        kernel = lambda place_ref, grads_ref, inputs_ref, gain_ref, out_ref: back_kernel(
-            owners, place_ref, grads_ref, inputs_ref, gain_ref, None, out_ref
+        kernel = lambda place_ref, grads_ref, moved_ref, inputs_ref, gain_ref, out_ref: back_kernel(
+            owners, place_ref, grads_ref, moved_ref, inputs_ref, gain_ref, None, out_ref
         )
     whole = pl.BlockSpec((rows, width), lambda i, place_ref: (0, 0))
-    given = [grads, inputs, gain] + ([] if extra is None else [extra])
+    given = [grads, moved, inputs, gain] + ([] if extra is None else [extra])
     return pl.pallas_call(
         kernel,
         grid_spec=pltpu.PrefetchScalarGridSpec(
             num_scalar_prefetch=1,
             grid=(1,),
-            in_specs=[whole, whole, pl.BlockSpec((1, width), lambda i, place_ref: (0, 0))]
+            in_specs=[whole, whole, whole, pl.BlockSpec((1, width), lambda i, place_ref: (0, 0))]
             + ([] if extra is None else [whole]),
             out_specs=whole,
         ),
@@ -1172,7 +1217,6 @@
 
     summed = [None, None, None, Scatter(grad_normed_ffn, "tensor", in_first)]
     summed[3].step(0)
-    newest_all.step(1)
     send_far(history_front, first_far)
     send_far(history_front, near_spots)
     grad_project.near()
@@ -1191,12 +1235,17 @@
         )
         for index in range(3)
     ]
+    grad_proj_late, upper_late, near_pieces = sync(
+        [grad_proj, grad_upper, [history_front[spot] for spot in near_spots]], []
+    )
+    for spot, piece in zip(near_spots, near_pieces):
+        history_front[spot] = piece
     grad_attend = Reduce(
-        *attend_grads_call(normed_kept, normed_given, grad_proj, grad_kept, grad_given, heads_out),
+        *attend_grads_call(normed_kept, normed_given, grad_proj_late, grad_kept, grad_given, heads_out),
         "dp",
         1,
     )
-    grad_expand = Reduce(*expand_grads(normed_kept, normed_given, grad_upper), "dp", 0)
+    grad_expand = Reduce(*expand_grads(normed_kept, normed_given, upper_late), "dp", 0)
     grad_normed_attend, grad_normed_ffn, history_front, history_last, layer_late = sync(
         [grad_normed_attend, grad_normed_ffn, history_front, history_last, layer_late],
         [grad_attend, grad_expand, grad_project, newest_all, summed[3]] + stored_pair,
@@ -1207,8 +1256,9 @@
     summed[0].step(0)
     summed[3].step(1)
     send_far(history_front, last_far)
-    grad_attend.near()
     grad_expand.near()
+    newest_all.step(1)
+    (layer_late,) = sync([layer_late], [grad_expand])
     all_grads = list(enumerate(grad_normed_attend + [grad_normed_ffn]))
     sums = [
         norm_sums(grads[None], layer_late, index, place, owners)[0] for index, grads in all_grads[:2]
@@ -1227,6 +1277,7 @@
     summed[3].step(2)
     summed[0].step(1)
     grad_project.far()
+    grad_attend.near()
     sums, history_front, history_last = sync(
         [sums, history_front, history_last], summed + [grad_project, grad_expand, grad_attend]
     )
@@ -1234,7 +1285,8 @@
     def back(index):
         return Gather(
             back_share(
-                summed[index].result(),
+                summed[index].values,
+                summed[index].moved,
                 input_share[index],
                 norm_vals[index][None],
                 grad_newest if index == 3 else None,
@@ -1286,9 +1338,6 @@
     grad_attend.prepare()
     pack.near()
     pack.far()
-    grad_inputs = jnp.zeros(
-        (4,) + (2,) * len(bits_of(tensor_size)) + (share_rows, width), bf16_type
-    )
     grad_history = jnp.zeros(history.shape, bf16_type)
     for spot, index in enumerate(order):
         first_row = (me ^ index) * tokens_here
@@ -1297,8 +1346,8 @@
                 grad_history = lax.dynamic_update_slice(
                     grad_history, pieces[spot], (layer, first_row, 0)
                 )
-    grad_history, grad_inputs = sync(
-        [grad_history, grad_inputs],
+    (grad_history,) = sync(
+        [grad_history],
         summed[1:3] + [gathered[0], gathered[3], newest_all, grad_attend, grad_expand, pack],
     )
 
@@ -1324,7 +1373,7 @@
     pack.rows("tensor", far)
     entry_pieces = [newest_whole[:, spot * cols : (spot + 1) * cols] for spot in range(owners)]
     send_far(entry_pieces, first_far)
-    grad_inputs = gathered[3].place_last(grad_inputs, 3)
+    grad_inputs = gathered[3].place_new(4, 3)
     shard_squares = project_squares + expand_squares + grad_attend.squares()
     shard_squares, entry_pieces, grad_inputs = sync(
         [shard_squares, entry_pieces, grad_inputs],
@@ -1339,12 +1388,11 @@
         square_sum(norm_grad) + square_sum(grad_mixer_in) + square_sum(grad_mixer_out)
     )
     total_squares = jnp.full((1, 128), shard_squares + shared_squares / tensor_size)
-    for axis, bits in (
-        ("dp", bits_of(owners)[:1]),
-        ("tensor", side_bits + far),
-        ("dp", bits_of(owners)[1:]),
-        ("tensor", near),
-    ):
+    for axis, bits in (("dp", bits_of(owners)[:1]), ("tensor", side_bits + far)):
+        for bit in bits:
+            total_squares = total_squares + swap(total_squares, axis, bit)
+    (total_squares,) = sync([total_squares], [gathered[2]])
+    for axis, bits in (("dp", bits_of(owners)[1:]), ("tensor", near)):
         for bit in bits:
             total_squares = total_squares + swap(total_squares, axis, bit)
     gathered[1].step(2)
@@ -1352,8 +1400,16 @@
     send_far(entry_pieces, last_far)
     send_far(entry_pieces, near_spots)
     grad_inputs = gathered[0].place_last(grad_inputs, 0)
-    total_squares, entry_pieces, grad_inputs = sync(
-        [total_squares, entry_pieces, grad_inputs], [gathered[1], gathered[2]]
+    new_entry = jnp.zeros(grad_entry.shape, bf16_type)
+    entry_late = last_far + near_spots
+    for spot in range(owners):
+        if spot not in entry_late:
+            first_row = (me ^ order[spot]) * tokens_here
+            new_entry = lax.dynamic_update_slice_in_dim(
+                new_entry, entry_pieces[spot], first_row, 0
+            )
+    total_squares, entry_pieces, grad_inputs, new_entry = sync(
+        [total_squares, entry_pieces, grad_inputs, new_entry], [gathered[1], gathered[2]]
     )
     total_squares = total_squares[0, 0]
 
@@ -1420,9 +1476,8 @@
         2.0 / math.sqrt(FF),
         weight_decay,
     )
-    new_entry = jnp.zeros(grad_entry.shape, bf16_type)
-    for spot, index in enumerate(order):
-        first_row = (me ^ index) * tokens_here
+    for spot in entry_late:
+        first_row = (me ^ order[spot]) * tokens_here
         new_entry = lax.dynamic_update_slice_in_dim(new_entry, entry_pieces[spot], first_row, 0)
     for index in (1, 2):
         grad_inputs = gathered[index].place_last(grad_inputs, index)

time: 465 us -> 456 us (0.981)
  local copies, waits for them, and re-layouts: 69.3 us -> 62.1 us
    unnamed x300 -> x316, local copies, waits for them, and re-layouts: 20.8 us -> 16 us
    dynamic_update_slice x7 -> x5, local copies, waits for them, and re-layouts: 10.1 us -> 8.2 us  [place_last(): whole = lax.dynamic_update_slice(whole, block, starts)]
  transfers between devices with their start and end apart: 79 -> 79, of which waited for: 31 -> 30; matrix products, arithmetic and copies ran while one was open for 25% -> 25% of each run, Pallas kernels for 10% -> 10%
where the time goes in v4:
time: 456 us; the launch traced here: 452 us
  waiting for transfers between devices  161 us (35%)
  starting transfers between devices  80.9 us (18%)
  other arithmetic  67.8 us (15%)
  local copies, waits for them, and re-layouts  62.1 us (14%)
  Pallas kernels  57.9 us (13%)
  matrix products  13.5 us (3%)
  between operations  8.92 us (2%)
    ppermute x79, waiting for transfers between devices, swap(): lax.ppermute(values, axis, [(source, source ^ mask) for source in range(s...  161 us
    ppermute x79, starting transfers between devices, swap(): lax.ppermute(values, axis, [(source, source ^ mask) for source in range(s...  80.9 us
    unnamed x316, local copies, waits for them, and re-layouts  16 us
    pallas_call x4, Pallas kernels, norm_sums(): pl.pallas_call(functools.partial(sums_kernel, owners), grid_spec=pltpu.Pr...  11.6 us
    select_n x23, other arithmetic, settle(): jnp.where(lax.broadcasted_iota(jnp.int32, shape, dim) == side, jnp.expand...  10.7 us
    reduce_sum x6, other arithmetic, square_sum(): return jnp.sum(values * values)  9.55 us
  transfers between devices with their start and end apart: 79, of which 30 were waited for; matrix products, arithmetic and copies ran while one was open for 25% of the time, Pallas kernels for 10%

profile of v4, /device:TPU:0, one launch (start us, length us, event | category | flops | bytes accessed | tf_op | source)
XLA Modules:
  0.0 451.8 jit_solution(5300487421019219777)
XLA Ops:
  1.6 3.0 collective-permute-start
  22.7 2.7 collective-permute-start.7
  27.8 2.8 copy-done
  30.6 7.0 %shard_map.497 = (bf16[4,384,1024]{2,1,0:T(8,128)(2,1)S(1)}, bf16[4,384,1024]{2,1,0:T(8,128)(2,1)S(1)}) custom-call(s32[4]{0:T(128)S(1)} %pad_add_fusion.place_ref, bf16[4,384,2048]{2,1,0:T(8,128)(2,1)S(1)} %copy-done, f32[4,1,2048]{2,1,0:T(1,128)S(1)} %copy.83.gains_ref, f32[4,1,2048]{2,1,0:T(1,128)S(1)} %copy.84.biases_ref), custom_call_target="tpu_custom_call" | custom-call | flops 1 | bytes 1 | tf_op jit(solution)/shard_map/pallas_call | solution.py:538
  37.6 5.3 %collective-permute-done.5 = bf16[4,512,256]{2,1,0:T(8,128)(2,1)} collective-permute-done((bf16[4,512,256]{2,1,0:T(8,128)(2,1)}, bf16[4,512,256]{2,1,0:T(8,128)(2,1)}, u32[]{:S(2)}, u32[]{:S(2)}) %collective-permute-start.5) | collective-permute-done | bytes 1048608 | tf_op jit(solution)/shard_map/ppermute | solution.py:120
  51.2 21.3 %collective-permute-done.9 = bf16[512,1024]{1,0:T(8,128)(2,1)S(1)} collective-permute-done((bf16[512,1024]{1,0:T(8,128)(2,1)S(1)}, bf16[512,1024]{1,0:T(8,128)(2,1)S(1)}, u32[]{:S(2)}, u32[]{:S(2)}) %collective-permute-start.9) | collective-permute-done | bytes 1048608 | tf_op jit(solution)/shard_map/ppermute | solution.py:120
  75.7 2.7 collective-permute-start.15
  81.1 3.0 constant_dynamic-slice_fusion.13
  87.5 12.1 %collective-permute-done.13 = bf16[1024,512]{1,0:T(8,128)(2,1)S(1)} collective-permute-done((bf16[1024,512]{1,0:T(8,128)(2,1)S(1)}, bf16[1024,512]{1,0:T(8,128)(2,1)S(1)}, u32[]{:S(2)}, u32[]{:S(2)}) %collective-permute-start.13) | collective-permute-done | bytes 1048608 | tf_op jit(solution)/shard_map/ppermute | solution.py:120
  101.3 4.9 %fusion.8 = (f32[384,1024]{1,0:T(8,128)}, bf16[384,1024]{1,0:T(8,128)(2,1)S(1)}) fusion(f32[384,1024]{1,0:T(8,128)S(1)} %fusion.26, f32[384,1024]{1,0:T(8,128)S(1)} %fusion.24), kind=kLoop, calls=%fused_computation.29 | loop fusion | flops 29097984 | bytes 5505024 | tf_op jit(solution)/shard_map/add | solution.py:1115
  113.6 5.5 %collective-permute-done.17 = bf16[2,2,48,1024]{3,2,1,0:T(8,128)(2,1)S(1)} collective-permute-done((bf16[2,2,48,1024]{3,2,1,0:T(8,128)(2,1)S(1)}, bf16[2,2,48,1024]{3,2,1,0:T(8,128)(2,1)S(1)}, u32[]{:S(2)}, u32[]{:S(2)}) %collective-permute-start.17) | collective-permute-done | bytes 393248 | tf_op jit(solution)/shard_map/ppermute | solution.py:120
  123.2 2.6 collective-permute-start.22
  125.8 3.6 collective-permute-done.18
  129.9 7.3 %collective-permute-done.22 = bf16[2,48,1024]{2,1,0:T(8,128)(2,1)S(1)} collective-permute-done((bf16[2,48,1024]{2,1,0:T(8,128)(2,1)S(1)}, bf16[2,48,1024]{2,1,0:T(8,128)(2,1)S(1)}, u32[]{:S(2)}, u32[]{:S(2)}) %collective-permute-start.22) | collective-permute-done | bytes 196640 | tf_op jit(solution)/shard_map/ppermute | solution.py:120
  138.3 3.7 collective-permute-done.23
  146.2 6.3 %collective-permute-done.24 = bf16[48,1024]{1,0:T(8,128)(2,1)} collective-permute-done((bf16[48,1024]{1,0:T(8,128)(2,1)S(1)}, bf16[48,1024]{1,0:T(8,128)(2,1)}, u32[]{:S(2)}, u32[]{:S(2)}) %collective-permute-start.24) | collective-permute-done | bytes 98336 | tf_op jit(solution)/shard_map/ppermute | solution.py:120
  154.4 2.6 collective-permute-start.28
  157.0 5.9 %collective-permute-done.25 = bf16[2,48,1024]{2,1,0:T(8,128)(2,1)S(1)} collective-permute-done((bf16[2,48,1024]{2,1,0:T(8,128)(2,1)S(1)}, bf16[2,48,1024]{2,1,0:T(8,128)(2,1)S(1)}, u32[]{:S(2)}, u32[]{:S(2)}) %collective-permute-start.25) | collective-permute-done | bytes 196640 | tf_op jit(solution)/shard_map/ppermute | solution.py:120
  166.2 4.7 %collective-permute-done.26 = bf16[2,2,48,1024]{3,2,1,0:T(8,128)(2,1)S(1)} collective-permute-done((bf16[2,2,48,1024]{3,2,1,0:T(8,128)(2,1)S(1)}, bf16[2,2,48,1024]{3,2,1,0:T(8,128)(2,1)S(1)}, u32[]{:S(2)}, u32[]{:S(2)}) %collective-permute-start.26) | collective-permute-done | bytes 393248 | tf_op jit(solution)/shard_map/ppermute | solution.py:120
  172.6 5.2 %shard_map.501 = (bf16[3,384,512]{2,1,0:T(8,128)(2,1)S(1)}, bf16[2,384,512]{2,1,0:T(8,128)(2,1)S(1)}, bf16[1,384,512]{2,1,0:T(8,128)(2,1)}, bf16[3,384,512]{2,1,...) custom-call(s32[4]{0:T(128)S(1)} %pad_add_fusion.place_ref, ...), custom_call_target="tpu_custom_call" | custom-call | flops 1 | bytes 1 | tf_op jit(solution)/shard_map/pallas_call | solution.py:771
  177.8 2.5 collective-permute-start.30
  182.8 3.3 shard_map.502
  193.3 4.1 collective-permute-done.31
  198.2 2.4 shard_map.503.back_ref
  208.6 4.7 %shard_map.504 = (bf16[4,1024,256]{2,1,0:T(8,128)(2,1)S(1)}, bf16[4,1024,256]{2,1,0:T(8,128)(2,1)}) custom-call(bf16[4,384,1024]{2,1,0:T(8,128)(2,1)S(1)} %copy-done.3, bf16[4,384,1024]{2,1,0:T(8,128)(2,1)S(1)} %copy-done.5, bf16[3,384,256]{2,1,0:T(8,128)(2,1)S(1)} %shard_map.503.back_ref, bf16[384,1024]{1,0:T(8,128)(2,1)S(1)} %bitcast_select_fusion.5.refs_1_.out_kept_ref, ...), custom_call_target="tpu_custom_call" | custom-call | flops 1 | bytes 1 | tf_op jit(solution)/shard_map/pallas_call | solution.py:459
  213.3 3.2 shard_map.505
  216.7 7.3 %collective-permute-done.36 = bf16[2,2,48,2048]{3,2,1,0:T(8,128)(2,1)S(1)} collective-permute-done((bf16[2,2,48,2048]{3,2,1,0:T(8,128)(2,1)S(1)}, bf16[2,2,48,2048]{3,2,1,0:T(8,128)(2,1)S(1)}, u32[]{:S(2)}, u32[]{:S(2)}) %collective-permute-start.36) | collective-permute-done | bytes 786464 | tf_op jit(solution)/shard_map/ppermute | solution.py:120
  232.0 3.2 shard_map.506
  235.3 2.8 shard_map.507
  238.1 9.7 %collective-permute-done.40 = bf16[2,48,2048]{2,1,0:T(8,128)(2,1)S(1)} collective-permute-done((bf16[2,48,2048]{2,1,0:T(8,128)(2,1)S(1)}, bf16[2,48,2048]{2,1,0:T(8,128)(2,1)S(1)}, u32[]{:S(2)}, u32[]{:S(2)}) %collective-permute-start.40) | collective-permute-done | bytes 393248 | tf_op jit(solution)/shard_map/ppermute | solution.py:120
  259.4 2.8 shard_map.508
  262.2 2.8 shard_map.509
  265.0 14.1 %collective-permute-done.44.moved_ref = bf16[48,2048]{1,0:T(8,128)(2,1)S(1)} collective-permute-done((bf16[48,2048]{1,0:T(8,128)(2,1)S(1)}, bf16[48,2048]{1,0:T(8,128)(2,1)S(1)}, u32[]{:S(2)}, u32[]{:S(2)}) %collective-permute-start.44) | collective-permute-done | bytes 196640 | tf_op jit(solution)/shard_map/ppermute | solution.py:120
  290.8 2.6 broadcast_in_dim.510
  296.0 2.7 multiply_reduce_fusion.2
  298.7 5.6 %collective-permute-done.49 = bf16[2,48,2048]{2,1,0:T(8,128)(2,1)} collective-permute-done((bf16[2,48,2048]{2,1,0:T(8,128)(2,1)}, bf16[2,48,2048]{2,1,0:T(8,128)(2,1)}, u32[]{:S(2)}, u32[]{:S(2)}) %collective-permute-start.49) | collective-permute-done | bytes 393248 | tf_op jit(solution)/shard_map/ppermute | solution.py:120
  305.5 2.5 collective-permute-done.51
  327.5 15.8 %collective-permute-done.57 = f32[46,512]{1,0:T(8,128)S(1)} collective-permute-done((f32[46,512]{1,0:T(8,128)S(1)}, f32[46,512]{1,0:T(8,128)S(1)}, u32[]{:S(2)}, u32[]{:S(2)}) %collective-permute-start.57) | collective-permute-done | bytes 94240 | tf_op jit(solution)/shard_map/ppermute | solution.py:120
  354.0 6.6 %shard_map.512 = bf16[4,384,2048]{2,1,0:T(8,128)(2,1)} custom-call(s32[4]{0:T(128)S(1)} %pad_add_fusion.place_ref, f32[384,16]{1,0:T(8,128)S(1)} %convert_add_fusion.8.weights_ref, bf16[384,2048]{1,0:T(8,128)(2,1)S(1)} %get-tuple-element.521.newest_ref, bf16[384,2048]{1,0:T(8,128)(2,1)S(1)} %get-tuple-element.670.refs_0_, ...), custom_call_target="tpu_custom_call" | custom-call | flops 1 | bytes 1 | tf_op jit(solution)/shard_map/pallas_call | solution.py:816
  360.6 5.6 %collective-permute-done.62 = f32[46,512]{1,0:T(8,128)S(1)} collective-permute-done((f32[46,512]{1,0:T(8,128)S(1)}, f32[46,512]{1,0:T(8,128)S(1)}, u32[]{:S(2)}, u32[]{:S(2)}) %collective-permute-start.62) | collective-permute-done | bytes 94240 | tf_op jit(solution)/shard_map/ppermute | solution.py:120
  366.3 3.6 collective-permute-done.61.refs_2_
  380.4 2.4 collective-permute-done.67
  383.1 3.7 multiply_reduce_fusion
  414.6 4.8 %collective-permute-done.73 = f32[1,128]{1,0:T(1,128)S(1)} collective-permute-done((f32[1,128]{1,0:T(1,128)S(1)}, f32[1,128]{1,0:T(1,128)S(1)}, u32[]{:S(2)}, u32[]{:S(2)}) %collective-permute-start.73) | collective-permute-done | bytes 544 | tf_op jit(solution)/shard_map/ppermute | solution.py:120
  428.7 6.8 %fusion.59 = (bf16[512,1024]{1,0:T(8,128)(2,1)}, f32[512,1024]{1,0:T(8,128)}, f32[512,1024]{1,0:T(8,128)}, f32[512,1024]{1,0:T(8,128)}) fusion(f32[512,1024]{1,0:T(8,128)} %param.38, f32[]{:T(128)} %min.3, bf16[512,1024]{1,0:T(8,128)(2,1)S(1)} %copy-done.73, bf16[1024,1024]{1,0:T(8,128)(2,1)} %copy-done.67, bf16[1024,1024]{1,0:T(8,128)(2,1)} %copy-done.12, ...), kind=kLoop, calls=%fused_computation.296 | loop fusion | flops 11534336 | bytes 16777220 | tf_op jit(solution)/shard_map/convert_element_type | solution.py:1504
  436.9 3.4 fusion.61
  440.4 3.3 shard_map.516
  444.6 3.8 fusion.57
  (659 shorter events, 194.9 us)
Async XLA Ops:
  1.6 14.1 %collective-permute-start = (bf16[9,512]{1,0:T(8,128)(2,1)S(1)}, bf16[9,512]{1,0:T(8,128)(2,1)}, u32[]{:S(2)}, u32[]{:S(2)}) collective-permute-start(bf16[9,512]{1,0:T(8,128)(2,1)S(1)} %convert_element_type.309), channel_id=1, source_target_pairs={{0,16},{8,24},{16,0},{24,8},{1,17},{9,25},{17,1},{25,9},{2,18},{10... | collective-permute-start | bytes 27656 | tf_op jit(solution)/shard_map/ppermute | solution.py:120
  16.8 26.2 %collective-permute-start.5 = (bf16[4,512,256]{2,1,0:T(8,128)(2,1)}, bf16[4,512,256]{2,1,0:T(8,128)(2,1)}, u32[]{:S(2)}, u32[]{:S(2)}) collective-permute-start(bf16[4,512,256]{2,1,0:T(8,128)(2,1)} %pad_maximum_fusion.7), channel_id=1, source_target_pairs={{0,16},{8,24},{16,0},{24,8},{1,17},{9,25},{17,1},{25,9},{2,18},{10... | collective-permute-start | bytes 3145736 | tf_op jit(solution)/shard_map/ppermute | solution.py:120
  22.7 21.6 %collective-permute-start.7 = (bf16[2,48,2048]{2,1,0:T(8,128)(2,1)S(1)}, bf16[2,48,2048]{2,1,0:T(8,128)(2,1)S(1)}, u32[]{:S(2)}, u32[]{:S(2)}) collective-permute-start(bf16[2,48,2048]{2,1,0:T(8,128)(2,1)S(1)} %slice.340), channel_id=1, source_target_pairs={{0,4},{1,5},{2,6},{3,7},{4,0},{5,1},{6,2},{7,3},{8,12},{9,13},{10,... | collective-permute-start | bytes 1179656 | tf_op jit(solution)/shard_map/ppermute | solution.py:120
  25.4 18.9 %collective-permute-start.8 = (bf16[1,48,2048]{2,1,0:T(8,128)(2,1)S(1)}, bf16[1,48,2048]{2,1,0:T(8,128)(2,1)S(1)}, u32[]{:S(2)}, u32[]{:S(2)}) collective-permute-start(bf16[1,48,2048]{2,1,0:T(8,128)(2,1)S(1)} %get-tuple-element.330), channel_id=1, source_target_pairs={{0,1},{1,0},{2,3},{3,2},{4,5},{5,4},{6,7},{7,6},{8,9},{9,8},{10,11... | collective-permute-start | bytes 589832 | tf_op jit(solution)/shard_map/ppermute | solution.py:120
  44.4 28.4 %collective-permute-start.10 = (bf16[4,1024,256]{2,1,0:T(8,128)(2,1)S(1)}, bf16[4,1024,256]{2,1,0:T(8,128)(2,1)S(1)}, u32[]{:S(2)}, u32[]{:S(2)}) collective-permute-start(bf16[4,1024,256]{2,1,0:T(8,128)(2,1)S(1)} %pad_maximum_fusion), channel_id=1, source_target_pairs={{0,8},{8,0},{16,24},{24,16},{1,9},{9,1},{17,25},{25,17},{2,10},{10... | collective-permute-start | bytes 6291464 | tf_op jit(solution)/shard_map/ppermute | solution.py:120
  47.2 25.3 %collective-permute-start.9 = (bf16[512,1024]{1,0:T(8,128)(2,1)S(1)}, bf16[512,1024]{1,0:T(8,128)(2,1)S(1)}, u32[]{:S(2)}, u32[]{:S(2)}) collective-permute-start(bf16[512,1024]{1,0:T(8,128)(2,1)S(1)} %convert_element_type.313), channel_id=1, source_target_pairs={{0,16},{8,24},{16,0},{24,8},{1,17},{9,25},{17,1},{25,9},{2,18},{10... | collective-permute-start | bytes 3145736 | tf_op jit(solution)/shard_map/ppermute | solution.py:120
  48.8 24.0 %collective-permute-start.11 = (bf16[2,2,48,2048]{3,2,1,0:T(8,128)(2,1)S(1)}, bf16[2,2,48,2048]{3,2,1,0:T(8,128)(2,1)S(1)}, u32[]{:S(2)}, u32[]{:S(2)}) collective-permute-start(bf16[2,2,48,2048]{3,2,1,0:T(8,128)(2,1)S(1)} %broadcast_select_fusion.7), channel_id=1, source_target_pairs={{0,2},{1,3},{2,0},{3,1},{4,6},{5,7},{6,4},{7,5},{8,10},{9,11},{10,... | collective-permute-start | bytes 2359304 | tf_op jit(solution)/shard_map/ppermute | solution.py:120
  72.8 27.2 %collective-permute-start.14 = (bf16[1024,1024]{1,0:T(8,128)(2,1)S(1)}, bf16[1024,1024]{1,0:T(8,128)(2,1)S(1)}, u32[]{:S(2)}, u32[]{:S(2)}) collective-permute-start(bf16[1024,1024]{1,0:T(8,128)(2,1)S(1)} %pad_maximum_fusion.1), channel_id=1, source_target_pairs={{0,8},{8,0},{16,24},{24,16},{1,9},{9,1},{17,25},{25,17},{2,10},{10... | collective-permute-start | bytes 6291464 | tf_op jit(solution)/shard_map/ppermute | solution.py:120
  74.4 25.2 %collective-permute-start.13 = (bf16[1024,512]{1,0:T(8,128)(2,1)S(1)}, bf16[1024,512]{1,0:T(8,128)(2,1)S(1)}, u32[]{:S(2)}, u32[]{:S(2)}) collective-permute-start(bf16[1024,512]{1,0:T(8,128)(2,1)S(1)} %convert_element_type.314), channel_id=1, source_target_pairs={{0,16},{8,24},{16,0},{24,8},{1,17},{9,25},{17,1},{25,9},{2,18},{10... | collective-permute-start | bytes 3145736 | tf_op jit(solution)/shard_map/ppermute | solution.py:120
  75.7 24.3 %collective-permute-start.15 = (bf16[1,2,48,2048]{3,2,1,0:T(8,128)(2,1)S(1)}, bf16[1,2,48,2048]{3,2,1,0:T(8,128)(2,1)S(1)}, u32[]{:S(2)}, u32[]{:S(2)}) collective-permute-start(bf16[1,2,48,2048]{3,2,1,0:T(8,128)(2,1)S(1)} %broadcast_select_fusion.16), channel_id=1, source_target_pairs={{0,4},{1,5},{2,6},{3,7},{4,0},{5,1},{6,2},{7,3},{8,12},{9,13},{10,... | collective-permute-start | bytes 1179656 | tf_op jit(solution)/shard_map/ppermute | solution.py:120
  79.6 20.4 %collective-permute-start.16 = (bf16[1,2,2,48,2048]{4,3,2,1,0:T(8,128)(2,1)S(1)}, bf16[1,2,2,48,2048]{4,3,2,1,0:T(8,128)(2,1)S(1)}, u32[]{:S(2)}, u32[]{:S(2)}) collective-permute-start(bf16[1,2,2,48,2048]{4,3,2,1,0:T(8,128)(2,1)S(1)} %get-tuple-element.497), channel_id=1, source_target_pairs={{0,1},{1,0},{2,3},{3,2},{4,5},{5,4},{6,7},{7,6},{8,9},{9,8},{10,11... | collective-permute-start | bytes 2359304 | tf_op jit(solution)/shard_map/ppermute | solution.py:120
  177.8 15.5 %collective-permute-start.30 = (bf16[48,2048]{1,0:T(8,128)(2,1)S(1)}, bf16[48,2048]{1,0:T(8,128)(2,1)S(1)}, u32[]{:S(2)}, u32[]{:S(2)}) collective-permute-start(bf16[48,2048]{1,0:T(8,128)(2,1)S(1)} %copy-done.40), channel_id=1, source_target_pairs={{0,4},{1,5},{2,6},{3,7},{4,0},{5,1},{6,2},{7,3},{8,12},{9,13},{10,... | collective-permute-start | bytes 589832 | tf_op jit(solution)/shard_map/ppermute | solution.py:120
  180.4 17.0 %collective-permute-start.31 = (bf16[1,2,2,48,2048]{4,3,2,1,0:T(8,128)(2,1)S(1)}, bf16[1,2,2,48,2048]{4,3,2,1,0:T(8,128)(2,1)S(1)}, u32[]{:S(2)}, u32[]{:S(2)}) collective-permute-start(bf16[1,2,2,48,2048]{4,3,2,1,0:T(8,128)(2,1)S(1)} %broadcast_select_fusion.6), channel_id=1, source_target_pairs={{0,2},{1,3},{2,0},{3,1},{4,6},{5,7},{6,4},{7,5},{8,10},{9,11},{10,... | collective-permute-start | bytes 2359304 | tf_op jit(solution)/shard_map/ppermute | solution.py:120
  180.8 16.6 %collective-permute-start.32 = (bf16[1,2,2,48,2048]{4,3,2,1,0:T(8,128)(2,1)S(1)}, bf16[1,2,2,48,2048]{4,3,2,1,0:T(8,128)(2,1)S(1)}, u32[]{:S(2)}, u32[]{:S(2)}) collective-permute-start(bf16[1,2,2,48,2048]{4,3,2,1,0:T(8,128)(2,1)S(1)} %copy-done.77), channel_id=1, source_target_pairs={{0,1},{1,0},{2,3},{3,2},{4,5},{5,4},{6,7},{7,6},{8,9},{9,8},{10,11... | collective-permute-start | bytes 2359304 | tf_op jit(solution)/shard_map/ppermute | solution.py:120
  201.5 15.2 %collective-permute-start.33 = (bf16[2,384,512]{2,1,0:T(8,128)(2,1)S(1)}, bf16[2,384,512]{2,1,0:T(8,128)(2,1)S(1)}, u32[]{:S(2)}, u32[]{:S(2)}) collective-permute-start(bf16[2,384,512]{2,1,0:T(8,128)(2,1)S(1)} %get-tuple-element.376), channel_id=1, source_target_pairs={{0,16},{8,24},{16,0},{24,8},{1,17},{9,25},{17,1},{25,9},{2,18},{10... | collective-permute-start | bytes 2359304 | tf_op jit(solution)/shard_map/ppermute | solution.py:120
  202.6 21.4 %collective-permute-start.35 = (bf16[1024,1024]{1,0:T(8,128)(2,1)S(1)}, bf16[1024,1024]{1,0:T(8,128)(2,1)S(1)}, u32[]{:S(2)}, u32[]{:S(2)}) collective-permute-start(bf16[1024,1024]{1,0:T(8,128)(2,1)S(1)} %get-tuple-element.390), channel_id=1, source_target_pairs={{0,8},{8,0},{16,24},{24,16},{1,9},{9,1},{17,25},{25,17},{2,10},{10... | collective-permute-start | bytes 6291464 | tf_op jit(solution)/shard_map/ppermute | solution.py:120
  204.5 19.5 %collective-permute-start.36 = (bf16[2,2,48,2048]{3,2,1,0:T(8,128)(2,1)S(1)}, bf16[2,2,48,2048]{3,2,1,0:T(8,128)(2,1)S(1)}, u32[]{:S(2)}, u32[]{:S(2)}) collective-permute-start(bf16[2,2,48,2048]{3,2,1,0:T(8,128)(2,1)S(1)} %get-tuple-element.613), channel_id=1, source_target_pairs={{0,2},{1,3},{2,0},{3,1},{4,6},{5,7},{6,4},{7,5},{8,10},{9,11},{10,... | collective-permute-start | bytes 2359304 | tf_op jit(solution)/shard_map/ppermute | solution.py:120
  224.0 23.8 %collective-permute-start.38 = (bf16[2,384,512]{2,1,0:T(8,128)(2,1)S(1)}, bf16[2,384,512]{2,1,0:T(8,128)(2,1)S(1)}, u32[]{:S(2)}, u32[]{:S(2)}) collective-permute-start(bf16[2,384,512]{2,1,0:T(8,128)(2,1)S(1)} %get-tuple-element.408), channel_id=1, source_target_pairs={{0,24},{8,16},{16,8},{24,0},{1,25},{9,17},{17,9},{25,1},{2,26},{10... | collective-permute-start | bytes 2359304 | tf_op jit(solution)/shard_map/ppermute | solution.py:120
  226.2 22.6 %collective-permute-start.39 = (bf16[2,2,48,2048]{3,2,1,0:T(8,128)(2,1)S(1)}, bf16[2,2,48,2048]{3,2,1,0:T(8,128)(2,1)S(1)}, u32[]{:S(2)}, u32[]{:S(2)}) collective-permute-start(bf16[2,2,48,2048]{3,2,1,0:T(8,128)(2,1)S(1)} %get-tuple-element.611), channel_id=1, source_target_pairs={{0,1},{1,0},{2,3},{3,2},{4,5},{5,4},{6,7},{7,6},{8,9},{9,8},{10,11... | collective-permute-start | bytes 2359304 | tf_op jit(solution)/shard_map/ppermute | solution.py:120
  227.9 19.9 %collective-permute-start.40 = (bf16[2,48,2048]{2,1,0:T(8,128)(2,1)S(1)}, bf16[2,48,2048]{2,1,0:T(8,128)(2,1)S(1)}, u32[]{:S(2)}, u32[]{:S(2)}) collective-permute-start(bf16[2,48,2048]{2,1,0:T(8,128)(2,1)S(1)} %get-tuple-element.633), channel_id=1, source_target_pairs={{0,4},{1,5},{2,6},{3,7},{4,0},{5,1},{6,2},{7,3},{8,12},{9,13},{10,... | collective-permute-start | bytes 1179656 | tf_op jit(solution)/shard_map/ppermute | solution.py:120
  228.7 19.1 %collective-permute-start.41 = (bf16[2,48,2048]{2,1,0:T(8,128)(2,1)S(1)}, bf16[2,48,2048]{2,1,0:T(8,128)(2,1)S(1)}, u32[]{:S(2)}, u32[]{:S(2)}) collective-permute-start(bf16[2,48,2048]{2,1,0:T(8,128)(2,1)S(1)} %broadcast_select_fusion.14), channel_id=1, source_target_pairs={{0,2},{1,3},{2,0},{3,1},{4,6},{5,7},{6,4},{7,5},{8,10},{9,11},{10,... | collective-permute-start | bytes 1179656 | tf_op jit(solution)/shard_map/ppermute | solution.py:120
  249.7 29.4 %collective-permute-start.46 = (bf16[4,1024,256]{2,1,0:T(8,128)(2,1)}, bf16[4,1024,256]{2,1,0:T(8,128)(2,1)}, u32[]{:S(2)}, u32[]{:S(2)}) collective-permute-start(bf16[4,1024,256]{2,1,0:T(8,128)(2,1)} %get-tuple-element.443), channel_id=1, source_target_pairs={{0,8},{8,0},{16,24},{24,16},{1,9},{9,1},{17,25},{25,17},{2,10},{10... | collective-permute-start | bytes 6291464 | tf_op jit(solution)/shard_map/ppermute | solution.py:120
  252.4 26.7 %collective-permute-start.42 = (bf16[2,48,2048]{2,1,0:T(8,128)(2,1)S(1)}, bf16[2,48,2048]{2,1,0:T(8,128)(2,1)S(1)}, u32[]{:S(2)}, u32[]{:S(2)}) collective-permute-start(bf16[2,48,2048]{2,1,0:T(8,128)(2,1)S(1)} %get-tuple-element.631), channel_id=1, source_target_pairs={{0,2},{1,3},{2,0},{3,1},{4,6},{5,7},{6,4},{7,5},{8,10},{9,11},{10,... | collective-permute-start | bytes 1179656 | tf_op jit(solution)/shard_map/ppermute | solution.py:120
  252.5 26.6 %collective-permute-start.45 = (bf16[1024,512]{1,0:T(8,128)(2,1)}, bf16[1024,512]{1,0:T(8,128)(2,1)S(1)}, u32[]{:S(2)}, u32[]{:S(2)}) collective-permute-start(bf16[1024,512]{1,0:T(8,128)(2,1)} %add_convert_fusion.2), channel_id=1, source_target_pairs={{0,16},{8,24},{16,0},{24,8},{1,17},{9,25},{17,1},{25,9},{2,18},{10... | collective-permute-start | bytes 3145736 | tf_op jit(solution)/shard_map/ppermute | solution.py:120
  255.0 24.0 %collective-permute-start.43 = (bf16[2,2,48,2048]{3,2,1,0:T(8,128)(2,1)S(1)}, bf16[2,2,48,2048]{3,2,1,0:T(8,128)(2,1)S(1)}, u32[]{:S(2)}, u32[]{:S(2)}) collective-permute-start(bf16[2,2,48,2048]{3,2,1,0:T(8,128)(2,1)S(1)} %get-tuple-element.609), channel_id=1, source_target_pairs={{0,1},{1,0},{2,3},{3,2},{4,5},{5,4},{6,7},{7,6},{8,9},{9,8},{10,11... | collective-permute-start | bytes 2359304 | tf_op jit(solution)/shard_map/ppermute | solution.py:120
  256.9 22.2 %collective-permute-start.44 = (bf16[48,2048]{1,0:T(8,128)(2,1)S(1)}, bf16[48,2048]{1,0:T(8,128)(2,1)S(1)}, u32[]{:S(2)}, u32[]{:S(2)}) collective-permute-start(bf16[48,2048]{1,0:T(8,128)(2,1)S(1)} %get-tuple-element.651), channel_id=1, source_target_pairs={{0,1},{1,0},{2,3},{3,2},{4,5},{5,4},{6,7},{7,6},{8,9},{9,8},{10,11... | collective-permute-start | bytes 589832 | tf_op jit(solution)/shard_map/ppermute | solution.py:120
  279.1 26.3 %collective-permute-start.47 = (bf16[1,384,512]{2,1,0:T(8,128)(2,1)}, bf16[1,384,512]{2,1,0:T(8,128)(2,1)}, u32[]{:S(2)}, u32[]{:S(2)}) collective-permute-start(bf16[1,384,512]{2,1,0:T(8,128)(2,1)} %get-tuple-element.449), channel_id=1, source_target_pairs={{0,16},{8,24},{16,0},{24,8},{1,17},{9,25},{17,1},{25,9},{2,18},{10... | collective-permute-start | bytes 1179656 | tf_op jit(solution)/shard_map/ppermute | solution.py:120
  280.2 25.2 %collective-permute-start.48 = (bf16[1,384,512]{2,1,0:T(8,128)(2,1)}, bf16[1,384,512]{2,1,0:T(8,128)(2,1)}, u32[]{:S(2)}, u32[]{:S(2)}) collective-permute-start(bf16[1,384,512]{2,1,0:T(8,128)(2,1)} %get-tuple-element.450), channel_id=1, source_target_pairs={{0,24},{8,16},{16,8},{24,0},{1,25},{9,17},{17,9},{25,1},{2,26},{10... | collective-permute-start | bytes 1179656 | tf_op jit(solution)/shard_map/ppermute | solution.py:120
  282.7 21.6 %collective-permute-start.49 = (bf16[2,48,2048]{2,1,0:T(8,128)(2,1)}, bf16[2,48,2048]{2,1,0:T(8,128)(2,1)}, u32[]{:S(2)}, u32[]{:S(2)}) collective-permute-start(bf16[2,48,2048]{2,1,0:T(8,128)(2,1)} %pad_maximum_fusion.12), channel_id=1, source_target_pairs={{0,4},{1,5},{2,6},{3,7},{4,0},{5,1},{6,2},{7,3},{8,12},{9,13},{10,... | collective-permute-start | bytes 1179656 | tf_op jit(solution)/shard_map/ppermute | solution.py:120
  286.0 19.5 %collective-permute-start.50 = (bf16[2,48,2048]{2,1,0:T(8,128)(2,1)}, bf16[2,48,2048]{2,1,0:T(8,128)(2,1)}, u32[]{:S(2)}, u32[]{:S(2)}) collective-permute-start(bf16[2,48,2048]{2,1,0:T(8,128)(2,1)} %get-tuple-element.629), channel_id=1, source_target_pairs={{0,2},{1,3},{2,0},{3,1},{4,6},{5,7},{6,4},{7,5},{8,10},{9,11},{10,... | collective-permute-start | bytes 1179656 | tf_op jit(solution)/shard_map/ppermute | solution.py:120
  287.7 20.3 %collective-permute-start.51 = (bf16[2,2,48,2048]{3,2,1,0:T(8,128)(2,1)}, bf16[2,2,48,2048]{3,2,1,0:T(8,128)(2,1)}, u32[]{:S(2)}, u32[]{:S(2)}) collective-permute-start(bf16[2,2,48,2048]{3,2,1,0:T(8,128)(2,1)} %get-tuple-element.607), channel_id=1, source_target_pairs={{0,1},{1,0},{2,3},{3,2},{4,5},{5,4},{6,7},{7,6},{8,9},{9,8},{10,11... | collective-permute-start | bytes 2359304 | tf_op jit(solution)/shard_map/ppermute | solution.py:120
  310.5 32.8 %collective-permute-start.52 = (bf16[2,48,2048]{2,1,0:T(8,128)(2,1)S(1)}, bf16[2,48,2048]{2,1,0:T(8,128)(2,1)S(1)}, u32[]{:S(2)}, u32[]{:S(2)}) collective-permute-start(bf16[2,48,2048]{2,1,0:T(8,128)(2,1)S(1)} %pad_maximum_fusion.13), channel_id=1, source_target_pairs={{0,4},{1,5},{2,6},{3,7},{4,0},{5,1},{6,2},{7,3},{8,12},{9,13},{10,... | collective-permute-start | bytes 1179656 | tf_op jit(solution)/shard_map/ppermute | solution.py:120
  314.2 29.2 %collective-permute-start.53 = (bf16[2,2,48,2048]{3,2,1,0:T(8,128)(2,1)S(1)}, bf16[2,2,48,2048]{3,2,1,0:T(8,128)(2,1)S(1)}, u32[]{:S(2)}, u32[]{:S(2)}) collective-permute-start(bf16[2,2,48,2048]{3,2,1,0:T(8,128)(2,1)S(1)} %pad_maximum_fusion.10), channel_id=1, source_target_pairs={{0,2},{1,3},{2,0},{3,1},{4,6},{5,7},{6,4},{7,5},{8,10},{9,11},{10,... | collective-permute-start | bytes 2359304 | tf_op jit(solution)/shard_map/ppermute | solution.py:120
  315.2 28.2 %collective-permute-start.54 = (bf16[2,2,48,2048]{3,2,1,0:T(8,128)(2,1)S(1)}, bf16[2,2,48,2048]{3,2,1,0:T(8,128)(2,1)S(1)}, u32[]{:S(2)}, u32[]{:S(2)}) collective-permute-start(bf16[2,2,48,2048]{3,2,1,0:T(8,128)(2,1)S(1)} %broadcast_select_fusion.5), channel_id=1, source_target_pairs={{0,1},{1,0},{2,3},{3,2},{4,5},{5,4},{6,7},{7,6},{8,9},{9,8},{10,11... | collective-permute-start | bytes 2359304 | tf_op jit(solution)/shard_map/ppermute | solution.py:120
  316.9 26.6 %collective-permute-start.55 = (bf16[512,1024]{1,0:T(8,128)(2,1)S(1)}, bf16[512,1024]{1,0:T(8,128)(2,1)S(1)}, u32[]{:S(2)}, u32[]{:S(2)}) collective-permute-start(bf16[512,1024]{1,0:T(8,128)(2,1)S(1)} %copy-done.98), channel_id=1, source_target_pairs={{0,16},{8,24},{16,0},{24,8},{1,17},{9,25},{17,1},{25,9},{2,18},{10... | collective-permute-start | bytes 3145736 | tf_op jit(solution)/shard_map/ppermute | solution.py:120
  324.7 18.6 %collective-permute-start.57 = (f32[46,512]{1,0:T(8,128)S(1)}, f32[46,512]{1,0:T(8,128)S(1)}, u32[]{:S(2)}, u32[]{:S(2)}) collective-permute-start(f32[46,512]{1,0:T(8,128)S(1)} %slice.363), channel_id=1, source_target_pairs={{0,16},{8,24},{16,0},{24,8},{1,17},{9,25},{17,1},{25,9},{2,18},{10... | collective-permute-start | bytes 282632 | tf_op jit(solution)/shard_map/ppermute | solution.py:120
  345.2 21.0 %collective-permute-start.58 = (bf16[2,48,2048]{2,1,0:T(8,128)(2,1)S(1)}, bf16[2,48,2048]{2,1,0:T(8,128)(2,1)S(1)}, u32[]{:S(2)}, u32[]{:S(2)}) collective-permute-start(bf16[2,48,2048]{2,1,0:T(8,128)(2,1)S(1)} %pad_maximum_fusion.14), channel_id=1, source_target_pairs={{0,4},{1,5},{2,6},{3,7},{4,0},{5,1},{6,2},{7,3},{8,12},{9,13},{10,... | collective-permute-start | bytes 1179656 | tf_op jit(solution)/shard_map/ppermute | solution.py:120
  346.8 19.5 %collective-permute-start.60 = (bf16[2,2,48,2048]{3,2,1,0:T(8,128)(2,1)S(1)}, bf16[2,2,48,2048]{3,2,1,0:T(8,128)(2,1)S(1)}, u32[]{:S(2)}, u32[]{:S(2)}) collective-permute-start(bf16[2,2,48,2048]{3,2,1,0:T(8,128)(2,1)S(1)} %broadcast_select_fusion.4), channel_id=1, source_target_pairs={{0,1},{1,0},{2,3},{3,2},{4,5},{5,4},{6,7},{7,6},{8,9},{9,8},{10,11... | collective-permute-start | bytes 2359304 | tf_op jit(solution)/shard_map/ppermute | solution.py:120
  347.4 22.5 %collective-permute-start.61 = (bf16[4,512,256]{2,1,0:T(8,128)(2,1)S(1)}, bf16[4,512,256]{2,1,0:T(8,128)(2,1)S(1)}, u32[]{:S(2)}, u32[]{:S(2)}) collective-permute-start(bf16[4,512,256]{2,1,0:T(8,128)(2,1)S(1)} %add_convert_fusion), channel_id=1, source_target_pairs={{0,16},{8,24},{16,0},{24,8},{1,17},{9,25},{17,1},{25,9},{2,18},{10... | collective-permute-start | bytes 3145736 | tf_op jit(solution)/shard_map/ppermute | solution.py:120
  348.5 17.8 %collective-permute-start.59 = (bf16[2,48,2048]{2,1,0:T(8,128)(2,1)S(1)}, bf16[2,48,2048]{2,1,0:T(8,128)(2,1)S(1)}, u32[]{:S(2)}, u32[]{:S(2)}) collective-permute-start(bf16[2,48,2048]{2,1,0:T(8,128)(2,1)S(1)} %broadcast_select_fusion.12), channel_id=1, source_target_pairs={{0,2},{1,3},{2,0},{3,1},{4,6},{5,7},{6,4},{7,5},{8,10},{9,11},{10,... | collective-permute-start | bytes 1179656 | tf_op jit(solution)/shard_map/ppermute | solution.py:120
  349.7 16.5 %collective-permute-start.62 = (f32[46,512]{1,0:T(8,128)S(1)}, f32[46,512]{1,0:T(8,128)S(1)}, u32[]{:S(2)}, u32[]{:S(2)}) collective-permute-start(f32[46,512]{1,0:T(8,128)S(1)} %slice_add_fusion.1), channel_id=1, source_target_pairs={{0,1},{1,0},{2,3},{3,2},{4,5},{5,4},{6,7},{7,6},{8,9},{9,8},{10,11... | collective-permute-start | bytes 282632 | tf_op jit(solution)/shard_map/ppermute | solution.py:120
  371.1 19.7 %collective-permute-start.63 = (bf16[384,512]{1,0:T(8,128)(2,1)}, bf16[384,512]{1,0:T(8,128)(2,1)}, u32[]{:S(2)}, u32[]{:S(2)}) collective-permute-start(bf16[384,512]{1,0:T(8,128)(2,1)} %get-tuple-element.605), channel_id=1, source_target_pairs={{0,16},{8,24},{16,0},{24,8},{1,17},{9,25},{17,1},{25,9},{2,18},{10... | collective-permute-start | bytes 1179656 | tf_op jit(solution)/shard_map/ppermute | solution.py:120
  373.1 18.5 %collective-permute-start.64 = (bf16[2,2,48,2048]{3,2,1,0:T(8,128)(2,1)}, bf16[2,2,48,2048]{3,2,1,0:T(8,128)(2,1)}, u32[]{:S(2)}, u32[]{:S(2)}) collective-permute-start(bf16[2,2,48,2048]{3,2,1,0:T(8,128)(2,1)} %broadcast_select_fusion.3), channel_id=1, source_target_pairs={{0,1},{1,0},{2,3},{3,2},{4,5},{5,4},{6,7},{7,6},{8,9},{9,8},{10,11... | collective-permute-start | bytes 2359304 | tf_op jit(solution)/shard_map/ppermute | solution.py:120
  376.9 14.7 %collective-permute-start.65 = (bf16[2,48,2048]{2,1,0:T(8,128)(2,1)}, bf16[2,48,2048]{2,1,0:T(8,128)(2,1)}, u32[]{:S(2)}, u32[]{:S(2)}) collective-permute-start(bf16[2,48,2048]{2,1,0:T(8,128)(2,1)} %broadcast_select_fusion.11), channel_id=1, source_target_pairs={{0,2},{1,3},{2,0},{3,1},{4,6},{5,7},{6,4},{7,5},{8,10},{9,11},{10,... | collective-permute-start | bytes 1179656 | tf_op jit(solution)/shard_map/ppermute | solution.py:120
  395.5 24.0 %collective-permute-start.74 = (bf16[384,512]{1,0:T(8,128)(2,1)}, bf16[384,512]{1,0:T(8,128)(2,1)S(1)}, u32[]{:S(2)}, u32[]{:S(2)}) collective-permute-start(bf16[384,512]{1,0:T(8,128)(2,1)} %get-tuple-element.538), channel_id=1, source_target_pairs={{0,8},{8,0},{16,24},{24,16},{1,9},{9,1},{17,25},{25,17},{2,10},{10... | collective-permute-start | bytes 1179656 | tf_op jit(solution)/shard_map/ppermute | solution.py:120
  396.0 23.5 %collective-permute-start.75 = (bf16[384,512]{1,0:T(8,128)(2,1)}, bf16[384,512]{1,0:T(8,128)(2,1)S(1)}, u32[]{:S(2)}, u32[]{:S(2)}) collective-permute-start(bf16[384,512]{1,0:T(8,128)(2,1)} %get-tuple-element.539), channel_id=1, source_target_pairs={{0,24},{8,16},{16,8},{24,0},{1,25},{9,17},{17,9},{25,1},{2,26},{10... | collective-permute-start | bytes 1179656 | tf_op jit(solution)/shard_map/ppermute | solution.py:120
  399.8 19.7 %collective-permute-start.76 = (bf16[2,2,48,2048]{3,2,1,0:T(8,128)(2,1)S(1)}, bf16[2,2,48,2048]{3,2,1,0:T(8,128)(2,1)S(1)}, u32[]{:S(2)}, u32[]{:S(2)}) collective-permute-start(bf16[2,2,48,2048]{3,2,1,0:T(8,128)(2,1)S(1)} %broadcast_select_fusion.2), channel_id=1, source_target_pairs={{0,1},{1,0},{2,3},{3,2},{4,5},{5,4},{6,7},{7,6},{8,9},{9,8},{10,11... | collective-permute-start | bytes 2359304 | tf_op jit(solution)/shard_map/ppermute | solution.py:120
  423.6 24.8 %collective-permute-start.78 = (bf16[2,2,48,2048]{3,2,1,0:T(8,128)(2,1)}, bf16[2,2,48,2048]{3,2,1,0:T(8,128)(2,1)}, u32[]{:S(2)}, u32[]{:S(2)}) collective-permute-start(bf16[2,2,48,2048]{3,2,1,0:T(8,128)(2,1)} %broadcast_select_fusion.1), channel_id=1, source_target_pairs={{0,1},{1,0},{2,3},{3,2},{4,5},{5,4},{6,7},{7,6},{8,9},{9,8},{10,11... | collective-permute-start | bytes 2359304 | tf_op jit(solution)/shard_map/ppermute | solution.py:120
  (187 other events, 1736.0 us)

commit v5 on v4

--- a/solution.py
+++ b/solution.py
@@ -494,7 +494,7 @@
     own = pl.BlockSpec(block, lambda *steps: steps[: len(grid)])
     if flip:
         term_specs = [
-            pl.BlockSpec((1,) + master.shape[::-1], lambda *steps: (spot, 0, 0)) for term in terms
+            pl.BlockSpec((1,) + block[::-1], lambda *steps: (spot, steps[1], 0)) for term in terms
         ]
     else:
         term_specs = [own] * len(terms)
@@ -1454,8 +1454,8 @@
         attend_out_second,
         factor,
         wide,
-        (1, 1),
-        attend_out_master.shape,
+        (1, attend_out_master.shape[1] // 128),
+        (attend_out_master.shape[0], 128),
         parts,
     )
     expand_out = adam_step(

time: 456 us -> 457 us (level)
  transfers between devices with their start and end apart: 79 -> 79, of which waited for: 30 -> 30; matrix products, arithmetic and copies ran while one was open for 25% -> 25% of each run, Pallas kernels for 10% -> 11%
where the time goes in v5:
time: 457 us; the launch traced here: 453 us
  waiting for transfers between devices  161 us (35%)
  starting transfers between devices  80.9 us (18%)
  other arithmetic  67.8 us (15%)
  local copies, waits for them, and re-layouts  61.8 us (14%)
  Pallas kernels  59.4 us (13%)
  matrix products  13.5 us (3%)
  between operations  8.93 us (2%)
    ppermute x79, waiting for transfers between devices, swap(): lax.ppermute(values, axis, [(source, source ^ mask) for source in range(s...  161 us
    ppermute x79, starting transfers between devices, swap(): lax.ppermute(values, axis, [(source, source ^ mask) for source in range(s...  80.9 us
    unnamed x316, local copies, waits for them, and re-layouts  15.7 us
    pallas_call x4, Pallas kernels, norm_sums(): pl.pallas_call(functools.partial(sums_kernel, owners), grid_spec=pltpu.Pr...  11.6 us
    select_n x23, other arithmetic, settle(): jnp.where(lax.broadcasted_iota(jnp.int32, shape, dim) == side, jnp.expand...  10.7 us
    reduce_sum x6, other arithmetic, square_sum(): return jnp.sum(values * values)  9.55 us
  transfers between devices with their start and end apart: 79, of which 30 were waited for; matrix products, arithmetic and copies ran while one was open for 25% of the time, Pallas kernels for 11%

profile of v5, /device:TPU:0, one launch (start us, length us, event | category | flops | bytes accessed | tf_op | source)
XLA Modules:
  0.0 453.0 jit_solution(3939582247437454411)
XLA Ops:
  1.6 3.0 collective-permute-start
  22.7 2.7 collective-permute-start.7
  27.8 2.8 copy-done
  30.6 7.0 %shard_map.497 = (bf16[4,384,1024]{2,1,0:T(8,128)(2,1)S(1)}, bf16[4,384,1024]{2,1,0:T(8,128)(2,1)S(1)}) custom-call(s32[4]{0:T(128)S(1)} %pad_add_fusion.place_ref, bf16[4,384,2048]{2,1,0:T(8,128)(2,1)S(1)} %copy-done, f32[4,1,2048]{2,1,0:T(1,128)S(1)} %copy.83.gains_ref, f32[4,1,2048]{2,1,0:T(1,128)S(1)} %copy.84.biases_ref), custom_call_target="tpu_custom_call" | custom-call | flops 1 | bytes 1 | tf_op jit(solution)/shard_map/pallas_call | solution.py:538
  37.6 5.3 %collective-permute-done.5 = bf16[4,512,256]{2,1,0:T(8,128)(2,1)} collective-permute-done((bf16[4,512,256]{2,1,0:T(8,128)(2,1)}, bf16[4,512,256]{2,1,0:T(8,128)(2,1)}, u32[]{:S(2)}, u32[]{:S(2)}) %collective-permute-start.5) | collective-permute-done | bytes 1048608 | tf_op jit(solution)/shard_map/ppermute | solution.py:120
  51.2 21.3 %collective-permute-done.9 = bf16[512,1024]{1,0:T(8,128)(2,1)S(1)} collective-permute-done((bf16[512,1024]{1,0:T(8,128)(2,1)S(1)}, bf16[512,1024]{1,0:T(8,128)(2,1)S(1)}, u32[]{:S(2)}, u32[]{:S(2)}) %collective-permute-start.9) | collective-permute-done | bytes 1048608 | tf_op jit(solution)/shard_map/ppermute | solution.py:120
  75.7 2.7 collective-permute-start.15
  81.1 3.0 constant_dynamic-slice_fusion.13
  87.5 12.1 %collective-permute-done.13 = bf16[1024,512]{1,0:T(8,128)(2,1)S(1)} collective-permute-done((bf16[1024,512]{1,0:T(8,128)(2,1)S(1)}, bf16[1024,512]{1,0:T(8,128)(2,1)S(1)}, u32[]{:S(2)}, u32[]{:S(2)}) %collective-permute-start.13) | collective-permute-done | bytes 1048608 | tf_op jit(solution)/shard_map/ppermute | solution.py:120
  101.3 4.9 %fusion.8 = (f32[384,1024]{1,0:T(8,128)}, bf16[384,1024]{1,0:T(8,128)(2,1)S(1)}) fusion(f32[384,1024]{1,0:T(8,128)S(1)} %fusion.26, f32[384,1024]{1,0:T(8,128)S(1)} %fusion.24), kind=kLoop, calls=%fused_computation.29 | loop fusion | flops 29097984 | bytes 5505024 | tf_op jit(solution)/shard_map/add | solution.py:1115
  113.6 5.5 %collective-permute-done.17 = bf16[2,2,48,1024]{3,2,1,0:T(8,128)(2,1)S(1)} collective-permute-done((bf16[2,2,48,1024]{3,2,1,0:T(8,128)(2,1)S(1)}, bf16[2,2,48,1024]{3,2,1,0:T(8,128)(2,1)S(1)}, u32[]{:S(2)}, u32[]{:S(2)}) %collective-permute-start.17) | collective-permute-done | bytes 393248 | tf_op jit(solution)/shard_map/ppermute | solution.py:120
  123.2 2.6 collective-permute-start.22
  125.8 3.6 collective-permute-done.18
  129.9 7.3 %collective-permute-done.22 = bf16[2,48,1024]{2,1,0:T(8,128)(2,1)S(1)} collective-permute-done((bf16[2,48,1024]{2,1,0:T(8,128)(2,1)S(1)}, bf16[2,48,1024]{2,1,0:T(8,128)(2,1)S(1)}, u32[]{:S(2)}, u32[]{:S(2)}) %collective-permute-start.22) | collective-permute-done | bytes 196640 | tf_op jit(solution)/shard_map/ppermute | solution.py:120
  138.3 3.7 collective-permute-done.23
  146.2 6.3 %collective-permute-done.24 = bf16[48,1024]{1,0:T(8,128)(2,1)} collective-permute-done((bf16[48,1024]{1,0:T(8,128)(2,1)S(1)}, bf16[48,1024]{1,0:T(8,128)(2,1)}, u32[]{:S(2)}, u32[]{:S(2)}) %collective-permute-start.24) | collective-permute-done | bytes 98336 | tf_op jit(solution)/shard_map/ppermute | solution.py:120
  154.4 2.6 collective-permute-start.28
  157.0 5.9 %collective-permute-done.25 = bf16[2,48,1024]{2,1,0:T(8,128)(2,1)S(1)} collective-permute-done((bf16[2,48,1024]{2,1,0:T(8,128)(2,1)S(1)}, bf16[2,48,1024]{2,1,0:T(8,128)(2,1)S(1)}, u32[]{:S(2)}, u32[]{:S(2)}) %collective-permute-start.25) | collective-permute-done | bytes 196640 | tf_op jit(solution)/shard_map/ppermute | solution.py:120
  166.2 4.7 %collective-permute-done.26 = bf16[2,2,48,1024]{3,2,1,0:T(8,128)(2,1)S(1)} collective-permute-done((bf16[2,2,48,1024]{3,2,1,0:T(8,128)(2,1)S(1)}, bf16[2,2,48,1024]{3,2,1,0:T(8,128)(2,1)S(1)}, u32[]{:S(2)}, u32[]{:S(2)}) %collective-permute-start.26) | collective-permute-done | bytes 393248 | tf_op jit(solution)/shard_map/ppermute | solution.py:120
  172.6 5.2 %shard_map.501 = (bf16[3,384,512]{2,1,0:T(8,128)(2,1)S(1)}, bf16[2,384,512]{2,1,0:T(8,128)(2,1)S(1)}, bf16[1,384,512]{2,1,0:T(8,128)(2,1)}, bf16[3,384,512]{2,1,...) custom-call(s32[4]{0:T(128)S(1)} %pad_add_fusion.place_ref, ...), custom_call_target="tpu_custom_call" | custom-call | flops 1 | bytes 1 | tf_op jit(solution)/shard_map/pallas_call | solution.py:771
  177.8 2.5 collective-permute-start.30
  182.8 3.3 shard_map.502
  193.3 4.1 collective-permute-done.31
  198.2 2.4 shard_map.503.back_ref
  208.6 4.7 %shard_map.504 = (bf16[4,1024,256]{2,1,0:T(8,128)(2,1)S(1)}, bf16[4,1024,256]{2,1,0:T(8,128)(2,1)}) custom-call(bf16[4,384,1024]{2,1,0:T(8,128)(2,1)S(1)} %copy-done.3, bf16[4,384,1024]{2,1,0:T(8,128)(2,1)S(1)} %copy-done.5, bf16[3,384,256]{2,1,0:T(8,128)(2,1)S(1)} %shard_map.503.back_ref, bf16[384,1024]{1,0:T(8,128)(2,1)S(1)} %bitcast_select_fusion.5.refs_1_.out_kept_ref, ...), custom_call_target="tpu_custom_call" | custom-call | flops 1 | bytes 1 | tf_op jit(solution)/shard_map/pallas_call | solution.py:459
  213.3 3.2 shard_map.505
  216.7 7.3 %collective-permute-done.36 = bf16[2,2,48,2048]{3,2,1,0:T(8,128)(2,1)S(1)} collective-permute-done((bf16[2,2,48,2048]{3,2,1,0:T(8,128)(2,1)S(1)}, bf16[2,2,48,2048]{3,2,1,0:T(8,128)(2,1)S(1)}, u32[]{:S(2)}, u32[]{:S(2)}) %collective-permute-start.36) | collective-permute-done | bytes 786464 | tf_op jit(solution)/shard_map/ppermute | solution.py:120
  232.0 3.2 shard_map.506
  235.3 2.8 shard_map.507
  238.1 9.7 %collective-permute-done.40 = bf16[2,48,2048]{2,1,0:T(8,128)(2,1)S(1)} collective-permute-done((bf16[2,48,2048]{2,1,0:T(8,128)(2,1)S(1)}, bf16[2,48,2048]{2,1,0:T(8,128)(2,1)S(1)}, u32[]{:S(2)}, u32[]{:S(2)}) %collective-permute-start.40) | collective-permute-done | bytes 393248 | tf_op jit(solution)/shard_map/ppermute | solution.py:120
  259.4 2.8 shard_map.508
  262.2 2.8 shard_map.509
  265.0 14.1 %collective-permute-done.44.moved_ref = bf16[48,2048]{1,0:T(8,128)(2,1)S(1)} collective-permute-done((bf16[48,2048]{1,0:T(8,128)(2,1)S(1)}, bf16[48,2048]{1,0:T(8,128)(2,1)S(1)}, u32[]{:S(2)}, u32[]{:S(2)}) %collective-permute-start.44) | collective-permute-done | bytes 196640 | tf_op jit(solution)/shard_map/ppermute | solution.py:120
  290.8 2.6 broadcast_in_dim.510
  296.0 2.7 multiply_reduce_fusion.2
  298.7 5.6 %collective-permute-done.49 = bf16[2,48,2048]{2,1,0:T(8,128)(2,1)} collective-permute-done((bf16[2,48,2048]{2,1,0:T(8,128)(2,1)}, bf16[2,48,2048]{2,1,0:T(8,128)(2,1)}, u32[]{:S(2)}, u32[]{:S(2)}) %collective-permute-start.49) | collective-permute-done | bytes 393248 | tf_op jit(solution)/shard_map/ppermute | solution.py:120
  305.5 2.5 collective-permute-done.51
  327.5 15.8 %collective-permute-done.57 = f32[46,512]{1,0:T(8,128)S(1)} collective-permute-done((f32[46,512]{1,0:T(8,128)S(1)}, f32[46,512]{1,0:T(8,128)S(1)}, u32[]{:S(2)}, u32[]{:S(2)}) %collective-permute-start.57) | collective-permute-done | bytes 94240 | tf_op jit(solution)/shard_map/ppermute | solution.py:120
  354.0 6.6 %shard_map.512 = bf16[4,384,2048]{2,1,0:T(8,128)(2,1)} custom-call(s32[4]{0:T(128)S(1)} %pad_add_fusion.place_ref, f32[384,16]{1,0:T(8,128)S(1)} %convert_add_fusion.8.weights_ref, bf16[384,2048]{1,0:T(8,128)(2,1)S(1)} %get-tuple-element.521.newest_ref, bf16[384,2048]{1,0:T(8,128)(2,1)S(1)} %get-tuple-element.670.refs_0_, ...), custom_call_target="tpu_custom_call" | custom-call | flops 1 | bytes 1 | tf_op jit(solution)/shard_map/pallas_call | solution.py:816
  360.6 5.6 %collective-permute-done.62 = f32[46,512]{1,0:T(8,128)S(1)} collective-permute-done((f32[46,512]{1,0:T(8,128)S(1)}, f32[46,512]{1,0:T(8,128)S(1)}, u32[]{:S(2)}, u32[]{:S(2)}) %collective-permute-start.62) | collective-permute-done | bytes 94240 | tf_op jit(solution)/shard_map/ppermute | solution.py:120
  366.3 3.6 collective-permute-done.61.refs_2_
  380.4 2.4 collective-permute-done.67
  383.1 3.7 multiply_reduce_fusion
  414.6 4.8 %collective-permute-done.73 = f32[1,128]{1,0:T(1,128)S(1)} collective-permute-done((f32[1,128]{1,0:T(1,128)S(1)}, f32[1,128]{1,0:T(1,128)S(1)}, u32[]{:S(2)}, u32[]{:S(2)}) %collective-permute-start.73) | collective-permute-done | bytes 544 | tf_op jit(solution)/shard_map/ppermute | solution.py:120
  428.7 6.8 %fusion.59 = (bf16[512,1024]{1,0:T(8,128)(2,1)}, f32[512,1024]{1,0:T(8,128)}, f32[512,1024]{1,0:T(8,128)}, f32[512,1024]{1,0:T(8,128)}) fusion(f32[512,1024]{1,0:T(8,128)} %param.38, f32[]{:T(128)} %min.3, bf16[512,1024]{1,0:T(8,128)(2,1)S(1)} %copy-done.73, bf16[1024,1024]{1,0:T(8,128)(2,1)} %copy-done.67, bf16[1024,1024]{1,0:T(8,128)(2,1)} %copy-done.12, ...), kind=kLoop, calls=%fused_computation.296 | loop fusion | flops 11534336 | bytes 16777220 | tf_op jit(solution)/shard_map/convert_element_type | solution.py:1504
  436.9 3.4 fusion.61
  440.4 4.7 %shard_map.516 = (f32[256,512]{1,0:T(8,128)}, f32[256,512]{1,0:T(8,128)}, f32[256,512]{1,0:T(8,128)}, bf16[256,512]{1,0:T(8,128)(2,1)}) custom-call(f32[1]{0:T(128)} %bitcast.131.factor_ref, bf16[4,1024,256]{2,1,0:T(8,128)(2,1)S(1)} %copy-done.7, bf16[4,1024,256]{2,1,0:T(8,128)(2,1)} %collective-permute-done.46.refs_1_, ...), custom_call_target="tpu_custom_call" | custom-call | flops 1 | bytes 1 | tf_op jit(solution)/shard_map/pallas_call | solution.py:502
  445.8 3.8 fusion.57
  (659 shorter events, 194.6 us)
Async XLA Ops:
  1.6 14.1 %collective-permute-start = (bf16[9,512]{1,0:T(8,128)(2,1)S(1)}, bf16[9,512]{1,0:T(8,128)(2,1)}, u32[]{:S(2)}, u32[]{:S(2)}) collective-permute-start(bf16[9,512]{1,0:T(8,128)(2,1)S(1)} %convert_element_type.309), channel_id=1, source_target_pairs={{0,16},{8,24},{16,0},{24,8},{1,17},{9,25},{17,1},{25,9},{2,18},{10... | collective-permute-start | bytes 27656 | tf_op jit(solution)/shard_map/ppermute | solution.py:120
  16.8 26.2 %collective-permute-start.5 = (bf16[4,512,256]{2,1,0:T(8,128)(2,1)}, bf16[4,512,256]{2,1,0:T(8,128)(2,1)}, u32[]{:S(2)}, u32[]{:S(2)}) collective-permute-start(bf16[4,512,256]{2,1,0:T(8,128)(2,1)} %pad_maximum_fusion.7), channel_id=1, source_target_pairs={{0,16},{8,24},{16,0},{24,8},{1,17},{9,25},{17,1},{25,9},{2,18},{10... | collective-permute-start | bytes 3145736 | tf_op jit(solution)/shard_map/ppermute | solution.py:120
  22.7 21.6 %collective-permute-start.7 = (bf16[2,48,2048]{2,1,0:T(8,128)(2,1)S(1)}, bf16[2,48,2048]{2,1,0:T(8,128)(2,1)S(1)}, u32[]{:S(2)}, u32[]{:S(2)}) collective-permute-start(bf16[2,48,2048]{2,1,0:T(8,128)(2,1)S(1)} %slice.340), channel_id=1, source_target_pairs={{0,4},{1,5},{2,6},{3,7},{4,0},{5,1},{6,2},{7,3},{8,12},{9,13},{10,... | collective-permute-start | bytes 1179656 | tf_op jit(solution)/shard_map/ppermute | solution.py:120
  25.4 18.9 %collective-permute-start.8 = (bf16[1,48,2048]{2,1,0:T(8,128)(2,1)S(1)}, bf16[1,48,2048]{2,1,0:T(8,128)(2,1)S(1)}, u32[]{:S(2)}, u32[]{:S(2)}) collective-permute-start(bf16[1,48,2048]{2,1,0:T(8,128)(2,1)S(1)} %get-tuple-element.330), channel_id=1, source_target_pairs={{0,1},{1,0},{2,3},{3,2},{4,5},{5,4},{6,7},{7,6},{8,9},{9,8},{10,11... | collective-permute-start | bytes 589832 | tf_op jit(solution)/shard_map/ppermute | solution.py:120
  44.4 28.4 %collective-permute-start.10 = (bf16[4,1024,256]{2,1,0:T(8,128)(2,1)S(1)}, bf16[4,1024,256]{2,1,0:T(8,128)(2,1)S(1)}, u32[]{:S(2)}, u32[]{:S(2)}) collective-permute-start(bf16[4,1024,256]{2,1,0:T(8,128)(2,1)S(1)} %pad_maximum_fusion), channel_id=1, source_target_pairs={{0,8},{8,0},{16,24},{24,16},{1,9},{9,1},{17,25},{25,17},{2,10},{10... | collective-permute-start | bytes 6291464 | tf_op jit(solution)/shard_map/ppermute | solution.py:120
  47.2 25.3 %collective-permute-start.9 = (bf16[512,1024]{1,0:T(8,128)(2,1)S(1)}, bf16[512,1024]{1,0:T(8,128)(2,1)S(1)}, u32[]{:S(2)}, u32[]{:S(2)}) collective-permute-start(bf16[512,1024]{1,0:T(8,128)(2,1)S(1)} %convert_element_type.313), channel_id=1, source_target_pairs={{0,16},{8,24},{16,0},{24,8},{1,17},{9,25},{17,1},{25,9},{2,18},{10... | collective-permute-start | bytes 3145736 | tf_op jit(solution)/shard_map/ppermute | solution.py:120
  48.8 24.0 %collective-permute-start.11 = (bf16[2,2,48,2048]{3,2,1,0:T(8,128)(2,1)S(1)}, bf16[2,2,48,2048]{3,2,1,0:T(8,128)(2,1)S(1)}, u32[]{:S(2)}, u32[]{:S(2)}) collective-permute-start(bf16[2,2,48,2048]{3,2,1,0:T(8,128)(2,1)S(1)} %broadcast_select_fusion.7), channel_id=1, source_target_pairs={{0,2},{1,3},{2,0},{3,1},{4,6},{5,7},{6,4},{7,5},{8,10},{9,11},{10,... | collective-permute-start | bytes 2359304 | tf_op jit(solution)/shard_map/ppermute | solution.py:120
  72.8 27.2 %collective-permute-start.14 = (bf16[1024,1024]{1,0:T(8,128)(2,1)S(1)}, bf16[1024,1024]{1,0:T(8,128)(2,1)S(1)}, u32[]{:S(2)}, u32[]{:S(2)}) collective-permute-start(bf16[1024,1024]{1,0:T(8,128)(2,1)S(1)} %pad_maximum_fusion.1), channel_id=1, source_target_pairs={{0,8},{8,0},{16,24},{24,16},{1,9},{9,1},{17,25},{25,17},{2,10},{10... | collective-permute-start | bytes 6291464 | tf_op jit(solution)/shard_map/ppermute | solution.py:120
  74.4 25.2 %collective-permute-start.13 = (bf16[1024,512]{1,0:T(8,128)(2,1)S(1)}, bf16[1024,512]{1,0:T(8,128)(2,1)S(1)}, u32[]{:S(2)}, u32[]{:S(2)}) collective-permute-start(bf16[1024,512]{1,0:T(8,128)(2,1)S(1)} %convert_element_type.314), channel_id=1, source_target_pairs={{0,16},{8,24},{16,0},{24,8},{1,17},{9,25},{17,1},{25,9},{2,18},{10... | collective-permute-start | bytes 3145736 | tf_op jit(solution)/shard_map/ppermute | solution.py:120
  75.7 24.3 %collective-permute-start.15 = (bf16[1,2,48,2048]{3,2,1,0:T(8,128)(2,1)S(1)}, bf16[1,2,48,2048]{3,2,1,0:T(8,128)(2,1)S(1)}, u32[]{:S(2)}, u32[]{:S(2)}) collective-permute-start(bf16[1,2,48,2048]{3,2,1,0:T(8,128)(2,1)S(1)} %broadcast_select_fusion.16), channel_id=1, source_target_pairs={{0,4},{1,5},{2,6},{3,7},{4,0},{5,1},{6,2},{7,3},{8,12},{9,13},{10,... | collective-permute-start | bytes 1179656 | tf_op jit(solution)/shard_map/ppermute | solution.py:120
  79.6 20.4 %collective-permute-start.16 = (bf16[1,2,2,48,2048]{4,3,2,1,0:T(8,128)(2,1)S(1)}, bf16[1,2,2,48,2048]{4,3,2,1,0:T(8,128)(2,1)S(1)}, u32[]{:S(2)}, u32[]{:S(2)}) collective-permute-start(bf16[1,2,2,48,2048]{4,3,2,1,0:T(8,128)(2,1)S(1)} %get-tuple-element.497), channel_id=1, source_target_pairs={{0,1},{1,0},{2,3},{3,2},{4,5},{5,4},{6,7},{7,6},{8,9},{9,8},{10,11... | collective-permute-start | bytes 2359304 | tf_op jit(solution)/shard_map/ppermute | solution.py:120
  177.8 15.5 %collective-permute-start.30 = (bf16[48,2048]{1,0:T(8,128)(2,1)S(1)}, bf16[48,2048]{1,0:T(8,128)(2,1)S(1)}, u32[]{:S(2)}, u32[]{:S(2)}) collective-permute-start(bf16[48,2048]{1,0:T(8,128)(2,1)S(1)} %copy-done.40), channel_id=1, source_target_pairs={{0,4},{1,5},{2,6},{3,7},{4,0},{5,1},{6,2},{7,3},{8,12},{9,13},{10,... | collective-permute-start | bytes 589832 | tf_op jit(solution)/shard_map/ppermute | solution.py:120
  180.4 17.0 %collective-permute-start.31 = (bf16[1,2,2,48,2048]{4,3,2,1,0:T(8,128)(2,1)S(1)}, bf16[1,2,2,48,2048]{4,3,2,1,0:T(8,128)(2,1)S(1)}, u32[]{:S(2)}, u32[]{:S(2)}) collective-permute-start(bf16[1,2,2,48,2048]{4,3,2,1,0:T(8,128)(2,1)S(1)} %broadcast_select_fusion.6), channel_id=1, source_target_pairs={{0,2},{1,3},{2,0},{3,1},{4,6},{5,7},{6,4},{7,5},{8,10},{9,11},{10,... | collective-permute-start | bytes 2359304 | tf_op jit(solution)/shard_map/ppermute | solution.py:120
  180.8 16.6 %collective-permute-start.32 = (bf16[1,2,2,48,2048]{4,3,2,1,0:T(8,128)(2,1)S(1)}, bf16[1,2,2,48,2048]{4,3,2,1,0:T(8,128)(2,1)S(1)}, u32[]{:S(2)}, u32[]{:S(2)}) collective-permute-start(bf16[1,2,2,48,2048]{4,3,2,1,0:T(8,128)(2,1)S(1)} %copy-done.77), channel_id=1, source_target_pairs={{0,1},{1,0},{2,3},{3,2},{4,5},{5,4},{6,7},{7,6},{8,9},{9,8},{10,11... | collective-permute-start | bytes 2359304 | tf_op jit(solution)/shard_map/ppermute | solution.py:120
  201.5 15.2 %collective-permute-start.33 = (bf16[2,384,512]{2,1,0:T(8,128)(2,1)S(1)}, bf16[2,384,512]{2,1,0:T(8,128)(2,1)S(1)}, u32[]{:S(2)}, u32[]{:S(2)}) collective-permute-start(bf16[2,384,512]{2,1,0:T(8,128)(2,1)S(1)} %get-tuple-element.376), channel_id=1, source_target_pairs={{0,16},{8,24},{16,0},{24,8},{1,17},{9,25},{17,1},{25,9},{2,18},{10... | collective-permute-start | bytes 2359304 | tf_op jit(solution)/shard_map/ppermute | solution.py:120
  202.6 21.4 %collective-permute-start.35 = (bf16[1024,1024]{1,0:T(8,128)(2,1)S(1)}, bf16[1024,1024]{1,0:T(8,128)(2,1)S(1)}, u32[]{:S(2)}, u32[]{:S(2)}) collective-permute-start(bf16[1024,1024]{1,0:T(8,128)(2,1)S(1)} %get-tuple-element.390), channel_id=1, source_target_pairs={{0,8},{8,0},{16,24},{24,16},{1,9},{9,1},{17,25},{25,17},{2,10},{10... | collective-permute-start | bytes 6291464 | tf_op jit(solution)/shard_map/ppermute | solution.py:120
  204.5 19.5 %collective-permute-start.36 = (bf16[2,2,48,2048]{3,2,1,0:T(8,128)(2,1)S(1)}, bf16[2,2,48,2048]{3,2,1,0:T(8,128)(2,1)S(1)}, u32[]{:S(2)}, u32[]{:S(2)}) collective-permute-start(bf16[2,2,48,2048]{3,2,1,0:T(8,128)(2,1)S(1)} %get-tuple-element.613), channel_id=1, source_target_pairs={{0,2},{1,3},{2,0},{3,1},{4,6},{5,7},{6,4},{7,5},{8,10},{9,11},{10,... | collective-permute-start | bytes 2359304 | tf_op jit(solution)/shard_map/ppermute | solution.py:120
  224.0 23.8 %collective-permute-start.38 = (bf16[2,384,512]{2,1,0:T(8,128)(2,1)S(1)}, bf16[2,384,512]{2,1,0:T(8,128)(2,1)S(1)}, u32[]{:S(2)}, u32[]{:S(2)}) collective-permute-start(bf16[2,384,512]{2,1,0:T(8,128)(2,1)S(1)} %get-tuple-element.408), channel_id=1, source_target_pairs={{0,24},{8,16},{16,8},{24,0},{1,25},{9,17},{17,9},{25,1},{2,26},{10... | collective-permute-start | bytes 2359304 | tf_op jit(solution)/shard_map/ppermute | solution.py:120
  226.2 22.6 %collective-permute-start.39 = (bf16[2,2,48,2048]{3,2,1,0:T(8,128)(2,1)S(1)}, bf16[2,2,48,2048]{3,2,1,0:T(8,128)(2,1)S(1)}, u32[]{:S(2)}, u32[]{:S(2)}) collective-permute-start(bf16[2,2,48,2048]{3,2,1,0:T(8,128)(2,1)S(1)} %get-tuple-element.611), channel_id=1, source_target_pairs={{0,1},{1,0},{2,3},{3,2},{4,5},{5,4},{6,7},{7,6},{8,9},{9,8},{10,11... | collective-permute-start | bytes 2359304 | tf_op jit(solution)/shard_map/ppermute | solution.py:120
  227.9 19.9 %collective-permute-start.40 = (bf16[2,48,2048]{2,1,0:T(8,128)(2,1)S(1)}, bf16[2,48,2048]{2,1,0:T(8,128)(2,1)S(1)}, u32[]{:S(2)}, u32[]{:S(2)}) collective-permute-start(bf16[2,48,2048]{2,1,0:T(8,128)(2,1)S(1)} %get-tuple-element.633), channel_id=1, source_target_pairs={{0,4},{1,5},{2,6},{3,7},{4,0},{5,1},{6,2},{7,3},{8,12},{9,13},{10,... | collective-permute-start | bytes 1179656 | tf_op jit(solution)/shard_map/ppermute | solution.py:120
  228.7 19.1 %collective-permute-start.41 = (bf16[2,48,2048]{2,1,0:T(8,128)(2,1)S(1)}, bf16[2,48,2048]{2,1,0:T(8,128)(2,1)S(1)}, u32[]{:S(2)}, u32[]{:S(2)}) collective-permute-start(bf16[2,48,2048]{2,1,0:T(8,128)(2,1)S(1)} %broadcast_select_fusion.14), channel_id=1, source_target_pairs={{0,2},{1,3},{2,0},{3,1},{4,6},{5,7},{6,4},{7,5},{8,10},{9,11},{10,... | collective-permute-start | bytes 1179656 | tf_op jit(solution)/shard_map/ppermute | solution.py:120
  249.7 29.4 %collective-permute-start.46 = (bf16[4,1024,256]{2,1,0:T(8,128)(2,1)}, bf16[4,1024,256]{2,1,0:T(8,128)(2,1)}, u32[]{:S(2)}, u32[]{:S(2)}) collective-permute-start(bf16[4,1024,256]{2,1,0:T(8,128)(2,1)} %get-tuple-element.443), channel_id=1, source_target_pairs={{0,8},{8,0},{16,24},{24,16},{1,9},{9,1},{17,25},{25,17},{2,10},{10... | collective-permute-start | bytes 6291464 | tf_op jit(solution)/shard_map/ppermute | solution.py:120
  252.4 26.7 %collective-permute-start.42 = (bf16[2,48,2048]{2,1,0:T(8,128)(2,1)S(1)}, bf16[2,48,2048]{2,1,0:T(8,128)(2,1)S(1)}, u32[]{:S(2)}, u32[]{:S(2)}) collective-permute-start(bf16[2,48,2048]{2,1,0:T(8,128)(2,1)S(1)} %get-tuple-element.631), channel_id=1, source_target_pairs={{0,2},{1,3},{2,0},{3,1},{4,6},{5,7},{6,4},{7,5},{8,10},{9,11},{10,... | collective-permute-start | bytes 1179656 | tf_op jit(solution)/shard_map/ppermute | solution.py:120
  252.5 26.6 %collective-permute-start.45 = (bf16[1024,512]{1,0:T(8,128)(2,1)}, bf16[1024,512]{1,0:T(8,128)(2,1)S(1)}, u32[]{:S(2)}, u32[]{:S(2)}) collective-permute-start(bf16[1024,512]{1,0:T(8,128)(2,1)} %add_convert_fusion.2), channel_id=1, source_target_pairs={{0,16},{8,24},{16,0},{24,8},{1,17},{9,25},{17,1},{25,9},{2,18},{10... | collective-permute-start | bytes 3145736 | tf_op jit(solution)/shard_map/ppermute | solution.py:120
  255.0 24.0 %collective-permute-start.43 = (bf16[2,2,48,2048]{3,2,1,0:T(8,128)(2,1)S(1)}, bf16[2,2,48,2048]{3,2,1,0:T(8,128)(2,1)S(1)}, u32[]{:S(2)}, u32[]{:S(2)}) collective-permute-start(bf16[2,2,48,2048]{3,2,1,0:T(8,128)(2,1)S(1)} %get-tuple-element.609), channel_id=1, source_target_pairs={{0,1},{1,0},{2,3},{3,2},{4,5},{5,4},{6,7},{7,6},{8,9},{9,8},{10,11... | collective-permute-start | bytes 2359304 | tf_op jit(solution)/shard_map/ppermute | solution.py:120
  256.9 22.2 %collective-permute-start.44 = (bf16[48,2048]{1,0:T(8,128)(2,1)S(1)}, bf16[48,2048]{1,0:T(8,128)(2,1)S(1)}, u32[]{:S(2)}, u32[]{:S(2)}) collective-permute-start(bf16[48,2048]{1,0:T(8,128)(2,1)S(1)} %get-tuple-element.651), channel_id=1, source_target_pairs={{0,1},{1,0},{2,3},{3,2},{4,5},{5,4},{6,7},{7,6},{8,9},{9,8},{10,11... | collective-permute-start | bytes 589832 | tf_op jit(solution)/shard_map/ppermute | solution.py:120
  279.1 26.3 %collective-permute-start.47 = (bf16[1,384,512]{2,1,0:T(8,128)(2,1)}, bf16[1,384,512]{2,1,0:T(8,128)(2,1)}, u32[]{:S(2)}, u32[]{:S(2)}) collective-permute-start(bf16[1,384,512]{2,1,0:T(8,128)(2,1)} %get-tuple-element.449), channel_id=1, source_target_pairs={{0,16},{8,24},{16,0},{24,8},{1,17},{9,25},{17,1},{25,9},{2,18},{10... | collective-permute-start | bytes 1179656 | tf_op jit(solution)/shard_map/ppermute | solution.py:120
  280.2 25.2 %collective-permute-start.48 = (bf16[1,384,512]{2,1,0:T(8,128)(2,1)}, bf16[1,384,512]{2,1,0:T(8,128)(2,1)}, u32[]{:S(2)}, u32[]{:S(2)}) collective-permute-start(bf16[1,384,512]{2,1,0:T(8,128)(2,1)} %get-tuple-element.450), channel_id=1, source_target_pairs={{0,24},{8,16},{16,8},{24,0},{1,25},{9,17},{17,9},{25,1},{2,26},{10... | collective-permute-start | bytes 1179656 | tf_op jit(solution)/shard_map/ppermute | solution.py:120
  282.7 21.6 %collective-permute-start.49 = (bf16[2,48,2048]{2,1,0:T(8,128)(2,1)}, bf16[2,48,2048]{2,1,0:T(8,128)(2,1)}, u32[]{:S(2)}, u32[]{:S(2)}) collective-permute-start(bf16[2,48,2048]{2,1,0:T(8,128)(2,1)} %pad_maximum_fusion.12), channel_id=1, source_target_pairs={{0,4},{1,5},{2,6},{3,7},{4,0},{5,1},{6,2},{7,3},{8,12},{9,13},{10,... | collective-permute-start | bytes 1179656 | tf_op jit(solution)/shard_map/ppermute | solution.py:120
  286.0 19.5 %collective-permute-start.50 = (bf16[2,48,2048]{2,1,0:T(8,128)(2,1)}, bf16[2,48,2048]{2,1,0:T(8,128)(2,1)}, u32[]{:S(2)}, u32[]{:S(2)}) collective-permute-start(bf16[2,48,2048]{2,1,0:T(8,128)(2,1)} %get-tuple-element.629), channel_id=1, source_target_pairs={{0,2},{1,3},{2,0},{3,1},{4,6},{5,7},{6,4},{7,5},{8,10},{9,11},{10,... | collective-permute-start | bytes 1179656 | tf_op jit(solution)/shard_map/ppermute | solution.py:120
  287.7 20.3 %collective-permute-start.51 = (bf16[2,2,48,2048]{3,2,1,0:T(8,128)(2,1)}, bf16[2,2,48,2048]{3,2,1,0:T(8,128)(2,1)}, u32[]{:S(2)}, u32[]{:S(2)}) collective-permute-start(bf16[2,2,48,2048]{3,2,1,0:T(8,128)(2,1)} %get-tuple-element.607), channel_id=1, source_target_pairs={{0,1},{1,0},{2,3},{3,2},{4,5},{5,4},{6,7},{7,6},{8,9},{9,8},{10,11... | collective-permute-start | bytes 2359304 | tf_op jit(solution)/shard_map/ppermute | solution.py:120
  310.5 32.8 %collective-permute-start.52 = (bf16[2,48,2048]{2,1,0:T(8,128)(2,1)S(1)}, bf16[2,48,2048]{2,1,0:T(8,128)(2,1)S(1)}, u32[]{:S(2)}, u32[]{:S(2)}) collective-permute-start(bf16[2,48,2048]{2,1,0:T(8,128)(2,1)S(1)} %pad_maximum_fusion.13), channel_id=1, source_target_pairs={{0,4},{1,5},{2,6},{3,7},{4,0},{5,1},{6,2},{7,3},{8,12},{9,13},{10,... | collective-permute-start | bytes 1179656 | tf_op jit(solution)/shard_map/ppermute | solution.py:120
  314.2 29.2 %collective-permute-start.53 = (bf16[2,2,48,2048]{3,2,1,0:T(8,128)(2,1)S(1)}, bf16[2,2,48,2048]{3,2,1,0:T(8,128)(2,1)S(1)}, u32[]{:S(2)}, u32[]{:S(2)}) collective-permute-start(bf16[2,2,48,2048]{3,2,1,0:T(8,128)(2,1)S(1)} %pad_maximum_fusion.10), channel_id=1, source_target_pairs={{0,2},{1,3},{2,0},{3,1},{4,6},{5,7},{6,4},{7,5},{8,10},{9,11},{10,... | collective-permute-start | bytes 2359304 | tf_op jit(solution)/shard_map/ppermute | solution.py:120
  315.2 28.2 %collective-permute-start.54 = (bf16[2,2,48,2048]{3,2,1,0:T(8,128)(2,1)S(1)}, bf16[2,2,48,2048]{3,2,1,0:T(8,128)(2,1)S(1)}, u32[]{:S(2)}, u32[]{:S(2)}) collective-permute-start(bf16[2,2,48,2048]{3,2,1,0:T(8,128)(2,1)S(1)} %broadcast_select_fusion.5), channel_id=1, source_target_pairs={{0,1},{1,0},{2,3},{3,2},{4,5},{5,4},{6,7},{7,6},{8,9},{9,8},{10,11... | collective-permute-start | bytes 2359304 | tf_op jit(solution)/shard_map/ppermute | solution.py:120
  316.9 26.6 %collective-permute-start.55 = (bf16[512,1024]{1,0:T(8,128)(2,1)S(1)}, bf16[512,1024]{1,0:T(8,128)(2,1)S(1)}, u32[]{:S(2)}, u32[]{:S(2)}) collective-permute-start(bf16[512,1024]{1,0:T(8,128)(2,1)S(1)} %copy-done.98), channel_id=1, source_target_pairs={{0,16},{8,24},{16,0},{24,8},{1,17},{9,25},{17,1},{25,9},{2,18},{10... | collective-permute-start | bytes 3145736 | tf_op jit(solution)/shard_map/ppermute | solution.py:120
  324.7 18.6 %collective-permute-start.57 = (f32[46,512]{1,0:T(8,128)S(1)}, f32[46,512]{1,0:T(8,128)S(1)}, u32[]{:S(2)}, u32[]{:S(2)}) collective-permute-start(f32[46,512]{1,0:T(8,128)S(1)} %slice.363), channel_id=1, source_target_pairs={{0,16},{8,24},{16,0},{24,8},{1,17},{9,25},{17,1},{25,9},{2,18},{10... | collective-permute-start | bytes 282632 | tf_op jit(solution)/shard_map/ppermute | solution.py:120
  345.2 21.0 %collective-permute-start.58 = (bf16[2,48,2048]{2,1,0:T(8,128)(2,1)S(1)}, bf16[2,48,2048]{2,1,0:T(8,128)(2,1)S(1)}, u32[]{:S(2)}, u32[]{:S(2)}) collective-permute-start(bf16[2,48,2048]{2,1,0:T(8,128)(2,1)S(1)} %pad_maximum_fusion.14), channel_id=1, source_target_pairs={{0,4},{1,5},{2,6},{3,7},{4,0},{5,1},{6,2},{7,3},{8,12},{9,13},{10,... | collective-permute-start | bytes 1179656 | tf_op jit(solution)/shard_map/ppermute | solution.py:120
  346.8 19.5 %collective-permute-start.60 = (bf16[2,2,48,2048]{3,2,1,0:T(8,128)(2,1)S(1)}, bf16[2,2,48,2048]{3,2,1,0:T(8,128)(2,1)S(1)}, u32[]{:S(2)}, u32[]{:S(2)}) collective-permute-start(bf16[2,2,48,2048]{3,2,1,0:T(8,128)(2,1)S(1)} %broadcast_select_fusion.4), channel_id=1, source_target_pairs={{0,1},{1,0},{2,3},{3,2},{4,5},{5,4},{6,7},{7,6},{8,9},{9,8},{10,11... | collective-permute-start | bytes 2359304 | tf_op jit(solution)/shard_map/ppermute | solution.py:120
  347.4 22.5 %collective-permute-start.61 = (bf16[4,512,256]{2,1,0:T(8,128)(2,1)S(1)}, bf16[4,512,256]{2,1,0:T(8,128)(2,1)S(1)}, u32[]{:S(2)}, u32[]{:S(2)}) collective-permute-start(bf16[4,512,256]{2,1,0:T(8,128)(2,1)S(1)} %add_convert_fusion), channel_id=1, source_target_pairs={{0,16},{8,24},{16,0},{24,8},{1,17},{9,25},{17,1},{25,9},{2,18},{10... | collective-permute-start | bytes 3145736 | tf_op jit(solution)/shard_map/ppermute | solution.py:120
  348.5 17.8 %collective-permute-start.59 = (bf16[2,48,2048]{2,1,0:T(8,128)(2,1)S(1)}, bf16[2,48,2048]{2,1,0:T(8,128)(2,1)S(1)}, u32[]{:S(2)}, u32[]{:S(2)}) collective-permute-start(bf16[2,48,2048]{2,1,0:T(8,128)(2,1)S(1)} %broadcast_select_fusion.12), channel_id=1, source_target_pairs={{0,2},{1,3},{2,0},{3,1},{4,6},{5,7},{6,4},{7,5},{8,10},{9,11},{10,... | collective-permute-start | bytes 1179656 | tf_op jit(solution)/shard_map/ppermute | solution.py:120
  349.7 16.5 %collective-permute-start.62 = (f32[46,512]{1,0:T(8,128)S(1)}, f32[46,512]{1,0:T(8,128)S(1)}, u32[]{:S(2)}, u32[]{:S(2)}) collective-permute-start(f32[46,512]{1,0:T(8,128)S(1)} %slice_add_fusion.1), channel_id=1, source_target_pairs={{0,1},{1,0},{2,3},{3,2},{4,5},{5,4},{6,7},{7,6},{8,9},{9,8},{10,11... | collective-permute-start | bytes 282632 | tf_op jit(solution)/shard_map/ppermute | solution.py:120
  371.1 19.7 %collective-permute-start.63 = (bf16[384,512]{1,0:T(8,128)(2,1)}, bf16[384,512]{1,0:T(8,128)(2,1)}, u32[]{:S(2)}, u32[]{:S(2)}) collective-permute-start(bf16[384,512]{1,0:T(8,128)(2,1)} %get-tuple-element.605), channel_id=1, source_target_pairs={{0,16},{8,24},{16,0},{24,8},{1,17},{9,25},{17,1},{25,9},{2,18},{10... | collective-permute-start | bytes 1179656 | tf_op jit(solution)/shard_map/ppermute | solution.py:120
  373.1 18.5 %collective-permute-start.64 = (bf16[2,2,48,2048]{3,2,1,0:T(8,128)(2,1)}, bf16[2,2,48,2048]{3,2,1,0:T(8,128)(2,1)}, u32[]{:S(2)}, u32[]{:S(2)}) collective-permute-start(bf16[2,2,48,2048]{3,2,1,0:T(8,128)(2,1)} %broadcast_select_fusion.3), channel_id=1, source_target_pairs={{0,1},{1,0},{2,3},{3,2},{4,5},{5,4},{6,7},{7,6},{8,9},{9,8},{10,11... | collective-permute-start | bytes 2359304 | tf_op jit(solution)/shard_map/ppermute | solution.py:120
  376.9 14.7 %collective-permute-start.65 = (bf16[2,48,2048]{2,1,0:T(8,128)(2,1)}, bf16[2,48,2048]{2,1,0:T(8,128)(2,1)}, u32[]{:S(2)}, u32[]{:S(2)}) collective-permute-start(bf16[2,48,2048]{2,1,0:T(8,128)(2,1)} %broadcast_select_fusion.11), channel_id=1, source_target_pairs={{0,2},{1,3},{2,0},{3,1},{4,6},{5,7},{6,4},{7,5},{8,10},{9,11},{10,... | collective-permute-start | bytes 1179656 | tf_op jit(solution)/shard_map/ppermute | solution.py:120
  395.5 24.0 %collective-permute-start.74 = (bf16[384,512]{1,0:T(8,128)(2,1)}, bf16[384,512]{1,0:T(8,128)(2,1)S(1)}, u32[]{:S(2)}, u32[]{:S(2)}) collective-permute-start(bf16[384,512]{1,0:T(8,128)(2,1)} %get-tuple-element.538), channel_id=1, source_target_pairs={{0,8},{8,0},{16,24},{24,16},{1,9},{9,1},{17,25},{25,17},{2,10},{10... | collective-permute-start | bytes 1179656 | tf_op jit(solution)/shard_map/ppermute | solution.py:120
  396.0 23.5 %collective-permute-start.75 = (bf16[384,512]{1,0:T(8,128)(2,1)}, bf16[384,512]{1,0:T(8,128)(2,1)S(1)}, u32[]{:S(2)}, u32[]{:S(2)}) collective-permute-start(bf16[384,512]{1,0:T(8,128)(2,1)} %get-tuple-element.539), channel_id=1, source_target_pairs={{0,24},{8,16},{16,8},{24,0},{1,25},{9,17},{17,9},{25,1},{2,26},{10... | collective-permute-start | bytes 1179656 | tf_op jit(solution)/shard_map/ppermute | solution.py:120
  399.8 19.7 %collective-permute-start.76 = (bf16[2,2,48,2048]{3,2,1,0:T(8,128)(2,1)S(1)}, bf16[2,2,48,2048]{3,2,1,0:T(8,128)(2,1)S(1)}, u32[]{:S(2)}, u32[]{:S(2)}) collective-permute-start(bf16[2,2,48,2048]{3,2,1,0:T(8,128)(2,1)S(1)} %broadcast_select_fusion.2), channel_id=1, source_target_pairs={{0,1},{1,0},{2,3},{3,2},{4,5},{5,4},{6,7},{7,6},{8,9},{9,8},{10,11... | collective-permute-start | bytes 2359304 | tf_op jit(solution)/shard_map/ppermute | solution.py:120
  423.6 26.0 %collective-permute-start.78 = (bf16[2,2,48,2048]{3,2,1,0:T(8,128)(2,1)}, bf16[2,2,48,2048]{3,2,1,0:T(8,128)(2,1)}, u32[]{:S(2)}, u32[]{:S(2)}) collective-permute-start(bf16[2,2,48,2048]{3,2,1,0:T(8,128)(2,1)} %broadcast_select_fusion.1), channel_id=1, source_target_pairs={{0,1},{1,0},{2,3},{3,2},{4,5},{5,4},{6,7},{7,6},{8,9},{9,8},{10,11... | collective-permute-start | bytes 2359304 | tf_op jit(solution)/shard_map/ppermute | solution.py:120
  (187 other events, 1748.7 us)
